TPU v7x, 256 devices: a whole 4x4x8 slice. The times are simulated.
256 devices in a mesh: dp: 32 (over x, y, core), tensor: 8 (over z).
Axes of the slice: x: 4, y: 4, z: 8, core: 2. Of those that a mesh axis runs over, the one named last changes fastest.
Arguments:
- activations: bfloat16 [4096, 16384], P('dp', 'tensor'), may hold values from -1 to 1
- weight: bfloat16 [16384, 12288], P('dp', 'tensor'), may hold values from -0.046875 to 0.046875
- grad_out: bfloat16 [4096, 12288], P('dp', 'tensor'), may hold values from -6 to 6
Outputs:
- grad_input: bfloat16 [4096, 16384], P('dp', 'tensor')
- grad_weight: float32 [16384, 12288], P('dp', 'tensor')
All inputs are finite; a program needn't handle non-finite values.
Results may differ from a plain program's by a relative error of at most 0.02.
Values may be sent and summed in bfloat16 or wider, within the bound.
No kernel may reach another device: no remote copies, remote signals or barrier semaphores. Data moves between devices by JAX's collectives and lax.ppermute only.
A program may use at most 128 MiB of HBM per device.

v0:
```python
import math

import jax
import jax.numpy as jnp
from jax import lax
from jax.sharding import PartitionSpec as P

BLOCK = 1024
WIDTH = 16384


levels = 127.0
ripple = 0.5
epsilon = 1e-06


def swapped(block, axis, distance):
    count = lax.axis_size(axis)
    route = []
    for low in range(count):
        high = low | 1 << distance
        if high != low and high < count:
            route += [(low, high), (high, low)]
    return lax.ppermute(block, axis, route)


def hadamard_table(length, number_type):
    row_ids = lax.broadcasted_iota(jnp.int32, (length, length), 0)
    column_ids = lax.broadcasted_iota(jnp.int32, (length, length), 1)
    common = jnp.bitwise_and(row_ids, column_ids)
    parity = jnp.zeros((length, length), jnp.int32)
    for bit_index in range(length.bit_length() - 1):
        parity = parity + jnp.bitwise_and(jnp.right_shift(common, bit_index), 1)
    parity = parity % 2
    return (1 - 2 * parity).astype(number_type)


def inner_mix(values, blocks):
    row_count = values.shape[0]
    inner = jnp.dot(
        values.reshape(row_count * blocks, BLOCK),
        hadamard_table(BLOCK, jnp.bfloat16),
        preferred_element_type=jnp.float32,
    )
    inner = inner.reshape(row_count, blocks, BLOCK)
    combined = jnp.einsum(
        "ab,rbf->raf", hadamard_table(blocks, jnp.float32), inner, precision=lax.Precision.HIGHEST
    )
    return combined.reshape(row_count, blocks * BLOCK)


def cross_mix(values):
    position = lax.axis_index("tensor")
    for bit_index in range(lax.axis_size("tensor").bit_length() - 1):
        partner = swapped(values, "tensor", bit_index)
        upper = jnp.bitwise_and(jnp.right_shift(position, bit_index), 1) == 1
        values = jnp.where(upper, partner - values, values + partner)
    return values


def quantize(transformed, peak):
    scale = (peak + epsilon) / levels
    phase = 2.0 * math.pi * (transformed / scale)
    quantized = (transformed - ripple / (2.0 * math.pi) * scale * jnp.sin(phase)).astype(
        jnp.bfloat16
    )
    slope = 1.0 - ripple * jnp.cos(phase)
    return (quantized, slope)


def shards(activations, weight, grad_out):
    norm_factor = 1.0 / math.sqrt(WIDTH)
    local_blocks = activations.shape[1] // BLOCK
    transformed = cross_mix(inner_mix(activations, local_blocks)) * norm_factor
    local_peak = jnp.max(jnp.abs(transformed), axis=1, keepdims=True)
    peak = lax.pmax(local_peak, "tensor")
    quantized, slope = quantize(transformed, peak)
    full_rows = lax.all_gather(quantized, "tensor", axis=1, tiled=True)
    q_block = lax.all_to_all(full_rows, "dp", split_axis=1, concat_axis=0, tiled=True)
    shard_rows = lax.all_gather(grad_out, "dp", axis=0, tiled=True)
    weight_sum = lax.dot_general(
        q_block, shard_rows, (((0,), (0,)), ((), ())), preferred_element_type=jnp.float32
    )
    product = lax.dot_general(
        shard_rows, weight, (((1,), (1,)), ((), ())), preferred_element_type=jnp.float32
    )
    partial_rows = product.astype(jnp.bfloat16)
    homed = lax.all_to_all(partial_rows, "dp", split_axis=0, concat_axis=1, tiled=True)
    summed = lax.psum_scatter(
        homed.astype(jnp.float32).astype(jnp.bfloat16), "tensor", scatter_dimension=1, tiled=True
    ).astype(jnp.float32)
    upstream = (summed * slope).astype(jnp.bfloat16)
    grad_input = (cross_mix(inner_mix(upstream, local_blocks)) * norm_factor).astype(jnp.bfloat16)
    return (grad_input, weight_sum)


def solution(mesh):
    return jax.shard_map(
        shards,
        mesh=mesh,
        in_specs=(P("dp", "tensor"), P("dp", "tensor"), P("dp", "tensor")),
        out_specs=(P("dp", "tensor"), P("dp", "tensor")),
        check_vma=False,
    )
```

profile of v0, /device:TPU:1, one launch (start us, length us, event | category | flops | bytes accessed | tf_op | source)
XLA Modules:
  0.0 555.8 jit_solution(5980058065239631978)
XLA Ops:
  7.2 0.0 copy-start
  7.2 0.0 all-gather.3.cloned.1.call-start
  7.2 0.7 all-gather.3.cloned.1.call-update
  7.9 0.0 reduce-scatter.2.cloned.1.call-start
  8.0 74.8 %all-gather.3.cloned.1.call-done = bf16[4096,1536]{1,0:T(8,128)(2,1)} async-done(((bf16[128,1536]{1,0:T(8,128)(2,1)}), bf16[4096,1536]{1,0:T(8,128)(2,1)}) %all-gather.3.cloned.1.call-update) | async-done | bytes 12582928 | tf_op jit(solution)/shard_map/all_gather | solution.py:80
  82.7 9.7 %convolution_convert_fusion = bf16[4096,512]{1,0:T(8,128)(2,1)S(1)} fusion(bf16[4096,1536]{1,0:T(8,128)(2,1)} %all-gather.3.cloned.1.call-done, bf16[512,1536]{1,0:T(8,128)(2,1)S(1)} %copy-done), kind=kOutput, calls=%fused_computation.3 | convolution fusion | flops 6444548096 | bytes 18350080 | tf_op jit(solution)/shard_map/dot_general | solution.py:84
  92.5 55.9 %all_to_all.38 = bf16[32,128,512]{2,1,0:T(8,128)(2,1)} all-to-all(bf16[32,128,512]{2,1,0:T(8,128)(2,1)S(1)} %bitcast.40), channel_id=1, replica_groups=mesh['dp'=32,'tensor'=8] {'dp'}, dimensions={0} | all-to-all | bytes 8388608 | tf_op jit(solution)/shard_map/all_to_all | solution.py:88
  148.4 6.4 %copy.7 = bf16[128,32,512]{0,2,1:T(8,128)(2,1)} copy(bf16[128,32,512]{2,0,1:T(8,128)(2,1)} %bitcast.37) | data formatting | bytes 8388608 | tf_op jit(solution)/shard_map/all_to_all | solution.py:88
  154.9 0.0 reduce-scatter.2.cloned.1.call-update
  154.9 0.0 all-gather.5.cloned.1.call-start
  155.0 1.0 copy-done.2
  155.9 0.2 reshape.26
  156.1 7.5 %fusion.9 = f32[256,1024]{1,0:T(8,128)} fusion(bf16[256,1024]{1,0:T(8,128)(2,1)S(1)} %reshape.26), kind=kOutput, calls=%fused_computation.13 | convolution fusion | flops 583008256 | bytes 1572864 | tf_op jit(solution)/shard_map/dot_general | solution.py:40
  163.6 2.1 reshape.27
  165.7 4.6 convolution_bitcast_fusion.1
  170.3 1.5 copy.19
  171.8 1.3 collective-permute-start
  173.1 46.6 %collective-permute-done = f32[128,2048]{0,1:T(8,128)} collective-permute-done((f32[128,2048]{0,1:T(8,128)S(1)}, f32[128,2048]{0,1:T(8,128)}, u32[]{:S(2)}, u32[]{:S(2)}) %collective-permute-start) | collective-permute-done | bytes 1048608 | tf_op jit(solution)/shard_map/ppermute | solution.py:24
  219.7 2.3 add_select_fusion.4
  222.0 1.7 collective-permute-start.1
  223.8 48.5 %collective-permute-done.1 = f32[128,2048]{0,1:T(8,128)} collective-permute-done((f32[128,2048]{0,1:T(8,128)}, f32[128,2048]{0,1:T(8,128)}, u32[]{:S(2)}, u32[]{:S(2)}) %collective-permute-start.1) | collective-permute-done | bytes 1048608 | tf_op jit(solution)/shard_map/ppermute | solution.py:24
  272.3 1.7 add_select_fusion.3
  273.9 0.0 copy-start.1
  274.0 3.2 collective-permute-start.2
  277.1 48.5 %collective-permute-done.2 = f32[128,2048]{0,1:T(8,128)} collective-permute-done((f32[128,2048]{0,1:T(8,128)S(1)}, f32[128,2048]{0,1:T(8,128)}, u32[]{:S(2)}, u32[]{:S(2)}) %collective-permute-start.2) | collective-permute-done | bytes 1048608 | tf_op jit(solution)/shard_map/ppermute | solution.py:24
  325.6 1.7 abs_reduce_fusion
  327.3 11.1 %pmax.7 = f32[128,1]{0,1:T(1,128)S(1)} all-reduce(f32[128,1]{0,1:T(1,128)S(1)} %bitcast.44), channel_id=1, replica_groups=mesh['dp'=32,'tensor'=8] {'tensor'}, use_global_device_ids=true, to_apply=%region_2.3 | all-reduce | flops 128 | bytes 1024 | tf_op jit(solution)/shard_map/pmax | solution.py:76
  338.4 0.0 reduce-scatter.2.cloned.1.call-done
  338.4 5.6 %subtract_convert_fusion = (bf16[128,2048]{0,1:T(8,128)(2,1)}, bf16[128,2048]{0,1:T(8,128)(2,1)S(1)}) fusion(f32[128,2048]{0,1:T(8,128)S(1)} %get-tuple-element.5, f32[128]{0:T(128)S(1)} %get-tuple-element.8, f32[128]{0:T(128)S(1)} %get-tuple-element.9, bf16[128,2048]{0,1:T(8,128)(2,1)} %reduce-scatter.2.cloned.1.call-done), kind=kLoop, calls=%fused_computation.14 | loop fusion | flops 2621440 | bytes 2622464 | tf_op jit(solution)/shard_map/convert_element_type | solution.py:64
  344.0 0.0 all-gather.5.cloned.1.call-update
  344.1 6.8 %fusion.4 = f32[128,2,1024]{2,0,1:T(8,128)S(1)} fusion(bf16[128,2,1024]{0,2,1:T(8,128)(2,1)S(1)} %bitcast.43), kind=kOutput, calls=%fused_computation.8 | convolution fusion | flops 583008256 | bytes 1572864 | tf_op jit(solution)/shard_map/dot_general | solution.py:40
  350.9 4.8 convolution_bitcast_fusion
  355.6 1.5 copy.20
  357.1 1.3 collective-permute-start.3
  358.4 63.4 %all-gather.5.cloned.1.call-done = bf16[128,16384]{0,1:T(8,128)(2,1)} async-done(((bf16[128,2048]{0,1:T(8,128)(2,1)}), bf16[128,16384]{0,1:T(8,128)(2,1)}) %all-gather.5.cloned.1.call-update) | async-done | bytes 4194320 | tf_op jit(solution)/shard_map/all_gather | solution.py:78
  421.8 7.4 %all-to-all-start.1 = ((bf16[128,32,512]{0,2,1:T(8,128)(2,1)}), bf16[128,32,512]{0,2,1:T(8,128)(2,1)}, u32[]{:S(2)}, u32[]{:S(2)}) async-start(bf16[128,32,512]{0,2,1:T(8,128)(2,1)} %bitcast.38), calls=%async_computation.2 | async-start | bytes 8388608 | tf_op jit(solution)/shard_map/all_to_all | solution.py:79
  429.2 0.0 collective-permute-done.3
  429.2 1.3 add_select_fusion.2
  430.6 0.3 collective-permute-start.4
  430.9 48.2 %collective-permute-done.4 = f32[128,2048]{0,1:T(8,128)S(1)} collective-permute-done((f32[128,2048]{0,1:T(8,128)S(1)}, f32[128,2048]{0,1:T(8,128)S(1)}, u32[]{:S(2)}, u32[]{:S(2)}) %collective-permute-start.4) | collective-permute-done | bytes 1048608 | tf_op jit(solution)/shard_map/ppermute | solution.py:24
  479.0 0.1 add_select_fusion.1
  479.2 2.0 collective-permute-start.5
  481.2 48.3 %collective-permute-done.5 = f32[128,2048]{0,1:T(8,128)S(1)} collective-permute-done((f32[128,2048]{0,1:T(8,128)S(1)}, f32[128,2048]{0,1:T(8,128)S(1)}, u32[]{:S(2)}, u32[]{:S(2)}) %collective-permute-start.5) | collective-permute-done | bytes 1048608 | tf_op jit(solution)/shard_map/ppermute | solution.py:24
  529.4 0.2 multiply_convert_fusion
  529.6 1.0 copy.17
  530.6 0.0 all-to-all-done.1
  530.6 6.5 %copy.16 = bf16[32,128,512]{2,1,0:T(8,128)(2,1)} copy(bf16[32,128,512]{1,2,0:T(8,128)(2,1)} %bitcast.13) | data formatting | bytes 8388608 | tf_op jit(solution)/shard_map/all_to_all | solution.py:79
  537.1 12.1 %fusion.52 = f32[512,1536]{1,0:T(8,128)} fusion(bf16[4096,512]{1,0:T(8,128)(2,1)} %bitcast.39, bf16[4096,1536]{1,0:T(8,128)(2,1)} %all-gather.3.cloned.1.call-done), kind=kOutput, calls=%fused_computation.67 | convolution fusion | flops 6442450944 | bytes 19922944 | tf_op jit(solution)/shard_map/dot_general | solution.py:81
  (4 shorter events, 0.0 us)
Async XLA Ops:
  7.2 75.6 %copy-start = (bf16[512,1536]{1,0:T(8,128)(2,1)S(1)}, bf16[512,1536]{1,0:T(8,128)(2,1)}, u32[]{:S(2)}) copy-start(bf16[512,1536]{1,0:T(8,128)(2,1)} %param.4) | copy-start | bytes 4718596
  7.2 75.6 %all-gather.3.cloned.1.call-start = ((), (), s32[]{:S(2)}) async-start(), calls=%async_computation.3 | async-start | bytes 12976128 | tf_op jit(solution)/shard_map/all_gather | solution.py:80
  7.9 330.5 %reduce-scatter.2.cloned.1.call-start = ((), (), s32[]{:S(2)}) async-start(), calls=%async_computation.4 | async-start | bytes 4718592 | tf_op jit(solution)/shard_map/reduce_scatter | solution.py:89
  154.9 1.0 copy-start.2
  154.9 266.9 %all-gather.5.cloned.1.call-start = ((), (), s32[]{:S(2)}) async-start(), calls=%async_computation.5 | async-start | bytes 4718592 | tf_op jit(solution)/shard_map/all_gather | solution.py:78
  171.8 47.9 %collective-permute-start = (f32[128,2048]{0,1:T(8,128)S(1)}, f32[128,2048]{0,1:T(8,128)}, u32[]{:S(2)}, u32[]{:S(2)}) collective-permute-start(f32[128,2048]{0,1:T(8,128)S(1)} %bitcast.41), channel_id=1, source_target_pairs={{0,1},{1,0},{2,3},{3,2},{4,5},{5,4},{6,7},{7,6},{8,9},{9,8},{10,11... | collective-permute-start | bytes 3145736 | tf_op jit(solution)/shard_map/ppermute | solution.py:24
  222.0 50.2 %collective-permute-start.1 = (f32[128,2048]{0,1:T(8,128)}, f32[128,2048]{0,1:T(8,128)}, u32[]{:S(2)}, u32[]{:S(2)}) collective-permute-start(f32[128,2048]{0,1:T(8,128)} %add_select_fusion.4), channel_id=1, source_target_pairs={{0,2},{2,0},{1,3},{3,1},{4,6},{6,4},{5,7},{7,5},{8,10},{10,8},{9,1... | collective-permute-start | bytes 3145736 | tf_op jit(solution)/shard_map/ppermute | solution.py:24
  273.9 3.2 copy-start.1
  274.0 51.6 %collective-permute-start.2 = (f32[128,2048]{0,1:T(8,128)S(1)}, f32[128,2048]{0,1:T(8,128)}, u32[]{:S(2)}, u32[]{:S(2)}) collective-permute-start(f32[128,2048]{0,1:T(8,128)S(1)} %add_select_fusion.3), channel_id=1, source_target_pairs={{0,4},{4,0},{1,5},{5,1},{2,6},{6,2},{3,7},{7,3},{8,12},{12,8},{9,1... | collective-permute-start | bytes 3145736 | tf_op jit(solution)/shard_map/ppermute | solution.py:24
  357.1 72.1 %collective-permute-start.3 = (f32[128,2048]{0,1:T(8,128)S(1)}, f32[128,2048]{0,1:T(8,128)}, u32[]{:S(2)}, u32[]{:S(2)}) collective-permute-start(f32[128,2048]{0,1:T(8,128)S(1)} %bitcast.42), channel_id=1, source_target_pairs={{0,1},{1,0},{2,3},{3,2},{4,5},{5,4},{6,7},{7,6},{8,9},{9,8},{10,11... | collective-permute-start | bytes 3145736 | tf_op jit(solution)/shard_map/ppermute | solution.py:24
  421.8 108.8 %all-to-all-start.1 = ((bf16[128,32,512]{0,2,1:T(8,128)(2,1)}), bf16[128,32,512]{0,2,1:T(8,128)(2,1)}, u32[]{:S(2)}, u32[]{:S(2)}) async-start(bf16[128,32,512]{0,2,1:T(8,128)(2,1)} %bitcast.38), calls=%async_computation.2 | async-start | bytes 8388608 | tf_op jit(solution)/shard_map/all_to_all | solution.py:79
  430.6 48.5 %collective-permute-start.4 = (f32[128,2048]{0,1:T(8,128)S(1)}, f32[128,2048]{0,1:T(8,128)S(1)}, u32[]{:S(2)}, u32[]{:S(2)}) collective-permute-start(f32[128,2048]{0,1:T(8,128)S(1)} %add_select_fusion.2), channel_id=1, source_target_pairs={{0,2},{2,0},{1,3},{3,1},{4,6},{6,4},{5,7},{7,5},{8,10},{10,8},{9,1... | collective-permute-start | bytes 3145736 | tf_op jit(solution)/shard_map/ppermute | solution.py:24
  479.2 50.3 %collective-permute-start.5 = (f32[128,2048]{0,1:T(8,128)S(1)}, f32[128,2048]{0,1:T(8,128)S(1)}, u32[]{:S(2)}, u32[]{:S(2)}) collective-permute-start(f32[128,2048]{0,1:T(8,128)S(1)} %add_select_fusion.1), channel_id=1, source_target_pairs={{0,4},{4,0},{1,5},{5,1},{2,6},{6,2},{3,7},{7,3},{8,12},{12,8},{9,1... | collective-permute-start | bytes 3145736 | tf_op jit(solution)/shard_map/ppermute | solution.py:24
Sparse Core Ops, SparseCore 0:
  10.6 72.1 all-gather.2
  155.0 74.7 reduce-scatter.1
  344.2 77.5 all-gather.4
where the time goes:
time: 557 us; the launch traced here: 556 us
  waiting for transfers between devices  379 us (68%)
  blocking collectives  67 us (12%)
  matrix products  45.6 us (8%)
  local copies, waits for them, and re-layouts  20.1 us (4%)
  starting transfers between devices  17.4 us (3%)
  between operations  13.8 us (2%)
  other arithmetic  12.9 us (2%)
    ppermute x6, waiting for transfers between devices, swapped(): return lax.ppermute(block, axis, route)  240 us
    all_gather x1, waiting for transfers between devices, shards(): shard_rows = lax.all_gather(grad_out, 'dp', axis=0, tiled=True)  74.8 us
    all_gather x1, waiting for transfers between devices, shards(): full_rows = lax.all_gather(quantized, 'tensor', axis=1, tiled=True)  63.4 us
    all_to_all x1, blocking collectives, shards(): lax.all_to_all(partial_rows, 'dp', split_axis=0, concat_axis=1, tiled=True)  55.9 us
    dot_general x2, matrix products, inner_mix(): jnp.dot(values.reshape(row_count * blocks, BLOCK), hadamard_table(BLOCK,...  14.3 us
    dot_general x1, matrix products, shards(): lax.dot_general(q_block, shard_rows, (((0,), (0,)), ((), ())), preferred_...  12.1 us
  transfers between devices with their start and end apart: 10, of which 7 were waited for; matrix products, arithmetic and copies ran while one was open for 7% of the time, Pallas kernels for 0%

commit v1 on v0

v1 whole, which is shorter than its diff:
```python
import math

import jax
import jax.numpy as jnp
import numpy as np
from jax import lax
from jax.experimental import pallas as pl
from jax.experimental.pallas import tpu as pltpu
from jax.sharding import PartitionSpec as P

BLOCK = 1024
WIDTH = 16384
BLOCKS = WIDTH // BLOCK
LANES = 128
NORM = 1.0 / math.sqrt(WIDTH)

levels = 127.0
ripple = 0.5
epsilon = 1e-06


def hadamard_table(length):
    table = np.ones((1, 1), np.float32)
    while table.shape[0] < length:
        table = np.block([[table, table], [table, -table]])
    return jnp.asarray(table, jnp.bfloat16)


def fit(odd, terms):
    nodes = 0.5 * np.cos(np.pi * (np.arange(400) + 0.5) / 800.0)
    squares = nodes * nodes
    values = np.sin(2.0 * np.pi * nodes) / nodes if odd else np.cos(2.0 * np.pi * nodes)
    scaled = np.polynomial.chebyshev.Chebyshev.fit(squares, values, terms - 1, domain=[0.0, 0.25])
    return [float(c) for c in scaled.convert(kind=np.polynomial.Polynomial).coef]


SINE = fit(True, 8)
COSINE = fit(False, 9)


def horner(coefficients, square):
    total = jnp.full_like(square, coefficients[-1])
    for coefficient in coefficients[-2::-1]:
        total = total * square + coefficient
    return total


def butterfly(parts):
    distance = 1
    while distance < len(parts):
        mixed = list(parts)
        for low in range(len(parts)):
            if not low & distance:
                mixed[low] = parts[low] + parts[low | distance]
                mixed[low | distance] = parts[low] - parts[low | distance]
        parts = mixed
        distance *= 2
    return parts


def quantize_kernel(place, rows_ref, table_ref, quantized_ref, slope_ref, inner, mixed):
    tokens = rows_ref.shape[1]
    per_shard = rows_ref.shape[2] // BLOCK
    stacked = jnp.concatenate(
        [
            rows_ref[b // per_shard, :, (b % per_shard) * BLOCK : (b % per_shard + 1) * BLOCK]
            for b in range(BLOCKS)
        ],
        axis=0,
    )
    inner[...] = jnp.dot(stacked, table_ref[...], preferred_element_type=jnp.float32)
    largest = jnp.zeros((tokens, LANES), jnp.float32)
    for chunk in range(BLOCK // LANES):
        lanes = slice(chunk * LANES, (chunk + 1) * LANES)
        parts = butterfly([inner[b * tokens : (b + 1) * tokens, lanes] for b in range(BLOCKS)])
        for b in range(BLOCKS):
            value = parts[b] * NORM
            mixed[b * tokens : (b + 1) * tokens, lanes] = value
            largest = jnp.maximum(largest, jnp.abs(value))
    peak = jnp.max(largest, axis=1, keepdims=True)
    scale = (peak + epsilon) / levels
    inverse = 1.0 / scale
    depth = (ripple / (2.0 * math.pi)) * scale
    width = quantized_ref.shape[2]
    per_block = BLOCK // width

    def remainder(value):
        turns = value * inverse
        return turns - jnp.round(turns)

    for b in range(BLOCKS):
        value = mixed[b * tokens : (b + 1) * tokens, :]
        rest = remainder(value)
        sine = rest * horner(SINE, rest * rest)
        result = (value - depth * sine).astype(jnp.bfloat16)
        for k in range(per_block):
            quantized_ref[b * per_block + k] = result[:, k * width : (k + 1) * width]

    @pl.when(pl.program_id(0) == place[0])
    def _():
        for b in range(BLOCKS):
            rest = remainder(mixed[b * tokens : (b + 1) * tokens, :])
            slope = 1.0 - ripple * horner(COSINE, rest * rest)
            for k in range(per_block):
                slope_ref[b * per_block + k] = slope[:, k * width : (k + 1) * width]


def quantize(rows, table, place, dp, width):
    shards, tokens, features = rows.shape
    step = tokens // shards
    return pl.pallas_call(
        quantize_kernel,
        grid_spec=pltpu.PrefetchScalarGridSpec(
            num_scalar_prefetch=1,
            grid=(shards,),
            in_specs=[
                pl.BlockSpec((shards, step, features), lambda i, place: (0, i, 0)),
                pl.BlockSpec((BLOCK, BLOCK), lambda i, place: (0, 0)),
            ],
            out_specs=[
                pl.BlockSpec((dp, step, width), lambda i, place: (0, i, 0)),
                pl.BlockSpec((dp, step, width), lambda i, place: (0, 0, 0)),
            ],
            scratch_shapes=[
                pltpu.VMEM((BLOCKS * step, BLOCK), jnp.float32),
                pltpu.VMEM((BLOCKS * step, BLOCK), jnp.float32),
            ],
        ),
        out_shape=[
            jax.ShapeDtypeStruct((dp, tokens, width), jnp.bfloat16),
            jax.ShapeDtypeStruct((dp, step, width), jnp.float32),
        ],
        compiler_params=pltpu.CompilerParams(vmem_limit_bytes=32 * 1024 * 1024),
        cost_estimate=pl.CostEstimate(
            flops=2 * tokens * WIDTH * BLOCK, bytes_accessed=4 * tokens * WIDTH, transcendentals=0
        ),
    )(place, rows, table)


def product_kernel(rows_ref, weight_ref, out_ref):
    devices, tokens, depth = rows_ref.shape
    out_ref[0] = lax.dot_general(
        rows_ref[...].reshape(devices * tokens, depth),
        weight_ref[...],
        (((1,), (1,)), ((), ())),
        preferred_element_type=jnp.float32,
    ).astype(out_ref.dtype)


def product(rows, weight, shards):
    devices, tokens, depth = rows.shape
    step = tokens // shards
    width = weight.shape[0]
    return pl.pallas_call(
        product_kernel,
        grid=(shards,),
        in_specs=[
            pl.BlockSpec((devices, step, depth), lambda i: (0, i, 0)),
            pl.BlockSpec((width, depth), lambda i: (0, 0)),
        ],
        out_specs=pl.BlockSpec((1, devices * step, width), lambda i: (i, 0, 0)),
        out_shape=jax.ShapeDtypeStruct((shards, devices * step, width), jnp.bfloat16),
        compiler_params=pltpu.CompilerParams(vmem_limit_bytes=32 * 1024 * 1024),
        cost_estimate=pl.CostEstimate(
            flops=2 * devices * tokens * depth * width,
            bytes_accessed=2 * devices * tokens * (depth + width),
            transcendentals=0,
        ),
    )(rows, weight)


def finish_kernel(summed_ref, slope_ref, table_ref, out_ref, inner):
    tokens, width = summed_ref.shape[1:]
    per_block = BLOCK // width
    per_shard = out_ref.shape[2] // BLOCK
    upstream = (summed_ref[...].astype(jnp.float32) * slope_ref[...]).astype(jnp.bfloat16)
    stacked = jnp.concatenate(
        [
            jnp.concatenate([upstream[b * per_block + k] for k in range(per_block)], axis=1)
            for b in range(BLOCKS)
        ],
        axis=0,
    )
    inner[...] = jnp.dot(stacked, table_ref[...], preferred_element_type=jnp.float32)
    for chunk in range(BLOCK // LANES):
        lanes = slice(chunk * LANES, (chunk + 1) * LANES)
        parts = butterfly([inner[b * tokens : (b + 1) * tokens, lanes] for b in range(BLOCKS)])
        for b in range(BLOCKS):
            start = (b % per_shard) * BLOCK + chunk * LANES
            out_ref[b // per_shard, :, start : start + LANES] = (parts[b] * NORM).astype(
                out_ref.dtype
            )


def finish(summed, slope, table, shards):
    devices, tokens, width = summed.shape
    return pl.pallas_call(
        finish_kernel,
        out_shape=jax.ShapeDtypeStruct((shards, tokens, WIDTH // shards), jnp.bfloat16),
        scratch_shapes=[pltpu.VMEM((BLOCKS * tokens, BLOCK), jnp.float32)],
        compiler_params=pltpu.CompilerParams(vmem_limit_bytes=32 * 1024 * 1024),
        cost_estimate=pl.CostEstimate(
            flops=2 * tokens * WIDTH * BLOCK, bytes_accessed=8 * tokens * WIDTH, transcendentals=0
        ),
    )(summed, slope, table)


def shards(activations, weight, grad_out):
    dp = lax.axis_size("dp")
    members = lax.axis_size("tensor")
    tokens, features = activations.shape
    width, depth = weight.shape
    place = lax.axis_index("tensor").astype(jnp.int32).reshape(1)
    table = hadamard_table(BLOCK)
    wide_rows = lax.all_gather(activations, "tensor", axis=0, tiled=False)
    all_rows = lax.all_gather(grad_out, "dp", axis=0, tiled=False)
    quantized, slope = quantize(wide_rows, table, place, dp, width)
    q_block = lax.all_to_all(quantized, "dp", split_axis=0, concat_axis=0, tiled=True)
    partial_rows = product(all_rows, weight, members)
    summed = lax.psum_scatter(partial_rows, "tensor", scatter_dimension=0, tiled=False)
    homed = lax.all_to_all(
        summed.reshape(dp, tokens // members, width), "dp", split_axis=0, concat_axis=0, tiled=True
    )
    mixed = finish(homed, slope, table, members)
    grad_input = lax.all_to_all(mixed, "tensor", split_axis=0, concat_axis=0, tiled=True)
    weight_sum = lax.dot_general(
        q_block.reshape(dp * tokens, width),
        all_rows.reshape(dp * tokens, depth),
        (((0,), (0,)), ((), ())),
        preferred_element_type=jnp.float32,
    )
    return (grad_input.reshape(tokens, features), weight_sum)


def solution(mesh):
    return jax.shard_map(
        shards,
        mesh=mesh,
        in_specs=(P("dp", "tensor"), P("dp", "tensor"), P("dp", "tensor")),
        out_specs=(P("dp", "tensor"), P("dp", "tensor")),
        check_vma=False,
    )
```

time: 557 us -> 320 us (0.57)
  waiting for transfers between devices: 379 us -> 233 us
  blocking collectives: 67 us -> 0 us
  matrix products: 45.6 us -> 12.1 us
  Pallas kernels: 0 us -> 25.7 us
  other arithmetic: 12.9 us -> 0 us
    ppermute x6 -> x0, waiting for transfers between devices: 240 us -> none  [swapped(): return lax.ppermute(block, axis, route)]
    all_to_all x1 -> x0, blocking collectives: 55.9 us -> none  [shards(): lax.all_to_all(partial_rows, 'dp', split_axis=0, concat_axis=1, tiled=True)]
    all_to_all x1 -> x3, waiting for transfers between devices: 0.01 us -> 54.8 us  [the longest x1 49.3 us: shards(): lax.all_to_all(quantized, 'dp', split_axis=0, concat_axis=0, tiled=True)]
    reduce_scatter x1, waiting for transfers between devices: 0.01 us -> 53.9 us  [shards(): lax.psum_scatter(partial_rows, 'tensor', scatter_dimension=0, tiled=False)]
    dot_general x6 -> x1, matrix products: 45.6 us -> 12.1 us  [shards(): lax.dot_general(q_block.reshape(dp * tokens, width), all_rows.reshape(dp...]
    pallas_call x0 -> x3, Pallas kernels: none -> 25.7 us  [the longest x1 15 us: quantize(): pl.pallas_call(quantize_kernel, grid_spec=pltpu.PrefetchScalarGridSpec(nu...]
    all_gather x2, waiting for transfers between devices: 138 us -> 123 us  [the longest x1 74.8 us: shards(): all_rows = lax.all_gather(grad_out, 'dp', axis=0, tiled=False)]
    unnamed x7 -> x17, local copies, waits for them, and re-layouts: 1.99 us -> 15 us
  transfers between devices with their start and end apart: 10 -> 6, of which waited for: 7 -> 5; matrix products, arithmetic and copies ran while one was open for 7% -> 4% of each run, Pallas kernels for 0% -> 5%
where the time goes in v1:
time: 320 us; the launch traced here: 318 us
  waiting for transfers between devices  233 us (73%)
  Pallas kernels  25.7 us (8%)
  starting transfers between devices  19.2 us (6%)
  local copies, waits for them, and re-layouts  15 us (5%)
  between operations  13.8 us (4%)
  matrix products  12.1 us (4%)
    all_gather x1, waiting for transfers between devices, shards(): all_rows = lax.all_gather(grad_out, 'dp', axis=0, tiled=False)  74.8 us
    reduce_scatter x1, waiting for transfers between devices, shards(): lax.psum_scatter(partial_rows, 'tensor', scatter_dimension=0, tiled=False)  53.9 us
    all_to_all x1, waiting for transfers between devices, shards(): lax.all_to_all(quantized, 'dp', split_axis=0, concat_axis=0, tiled=True)  49.3 us
    all_gather x1, waiting for transfers between devices, shards(): wide_rows = lax.all_gather(activations, 'tensor', axis=0, tiled=False)  47.7 us
    pallas_call x1, Pallas kernels, quantize(): pl.pallas_call(quantize_kernel, grid_spec=pltpu.PrefetchScalarGridSpec(nu...  15 us
    unnamed x17, local copies, waits for them, and re-layouts  15 us
    dot_general x1, matrix products, shards(): lax.dot_general(q_block.reshape(dp * tokens, width), all_rows.reshape(dp...  12.1 us
    pallas_call x1, Pallas kernels, product(): pl.pallas_call(product_kernel, grid=(shards,), in_specs=[pl.BlockSpec((de...  8.97 us
  transfers between devices with their start and end apart: 6, of which 5 were waited for; matrix products, arithmetic and copies ran while one was open for 4% of the time, Pallas kernels for 5%

profile of v1, /device:TPU:1, one launch (start us, length us, event | category | flops | bytes accessed | tf_op | source)
XLA Modules:
  0.0 318.5 jit_solution(7971229339586990114)
XLA Ops:
  7.2 0.0 all-gather.5.cloned.1.call-start
  7.2 0.7 all-gather.5.cloned.1.call-update
  7.9 0.0 reduce-scatter.2.cloned.1.call-start
  7.9 74.8 %all-gather.5.cloned.1.call-done = bf16[4096,1536]{1,0:T(8,128)(2,1)} async-done(((bf16[128,1536]{1,0:T(8,128)(2,1)}), bf16[4096,1536]{1,0:T(8,128)(2,1)}) %all-gather.5.cloned.1.call-update) | async-done | bytes 12582928 | tf_op jit(solution)/shard_map/all_gather | solution.py:216
  82.7 0.0 copy-start.5
  82.7 4.6 %copy-done.5 = bf16[4096,1536]{1,0:T(8,128)(2,1)S(1)} copy-done((bf16[4096,1536]{1,0:T(8,128)(2,1)S(1)}, bf16[4096,1536]{1,0:T(8,128)(2,1)}, u32[]{:S(2)}) %copy-start.5) | copy-done | bytes 12582936
  87.3 0.0 copy-start.7
  87.3 1.4 copy-done.7
  88.7 9.0 %shard_map.59 = bf16[8,512,512]{2,1,0:T(8,128)(2,1)S(1)} custom-call(bf16[32,128,1536]{2,1,0:T(8,128)(2,1)S(1)} %bitcast.10, bf16[512,1536]{1,0:T(8,128)(2,1)S(1)} %copy-done.7), custom_call_target="tpu_custom_call" | custom-call | flops 6442450944 | bytes 16777216 | tf_op jit(solution)/shard_map/pallas_call | solution.py:154
  97.7 0.0 copy-start.1
  97.7 1.9 copy-done.1
  99.6 0.0 copy-start.2
  99.6 0.0 reduce-scatter.2.cloned.1.call-update
  99.6 0.0 all-gather.7.cloned.1.call-start
  99.7 0.7 all-gather.7.cloned.1.call-update
  100.4 53.9 %reduce-scatter.2.cloned.1.call-done = bf16[1,512,512]{2,1,0:T(8,128)(2,1)} async-done(((bf16[8,512,512]{2,1,0:T(8,128)(2,1)}), bf16[1,512,512]{2,1,0:T(8,128)(2,1)}) %reduce-scatter.2.cloned.1.call-update) | async-done | bytes 524304 | tf_op jit(solution)/shard_map/reduce_scatter | solution.py:220
  154.3 7.5 %all-to-all-start = ((bf16[32,16,512]{2,1,0:T(8,128)(2,1)}), bf16[32,16,512]{2,1,0:T(8,128)(2,1)S(1)}, u32[]{:S(2)}, u32[]{:S(2)}) async-start(bf16[32,16,512]{2,1,0:T(8,128)(2,1)} %bitcast.13), calls=%async_computation.1 | async-start | bytes 1048576 | tf_op jit(solution)/shard_map/all_to_all | solution.py:221
  161.8 47.7 %all-gather.7.cloned.1.call-done = bf16[1024,2048]{1,0:T(8,128)(2,1)} async-done(((bf16[128,2048]{1,0:T(8,128)(2,1)}), bf16[1024,2048]{1,0:T(8,128)(2,1)}) %all-gather.7.cloned.1.call-update) | async-done | bytes 4194320 | tf_op jit(solution)/shard_map/all_gather | solution.py:215
  209.6 0.0 copy-done.2
  209.6 0.0 copy-start.6
  209.6 2.2 copy-done.6
  211.8 15.0 %shard_map.60 = (bf16[32,128,512]{2,1,0:T(8,128)(2,1)S(1)}, f32[32,16,512]{2,1,0:T(8,128)S(1)}) custom-call(s32[1]{0:T(128)} %bitcast.2.place, bf16[8,128,2048]{2,1,0:T(8,128)(2,1)S(1)} %bitcast.11, bf16[1024,1024]{1,0:T(8,128)(2,1)S(1)} %copy-done.2), custom_call_target="tpu_custom_call" | custom-call | flops 4294967296 | bytes 8388608 | tf_op jit(solution)/shard_map/pallas_call | solution.py:111
  226.8 0.0 copy-start
  226.8 1.9 copy-done
  228.7 0.0 copy-start.3
  228.7 1.0 copy-done.3
  229.7 0.0 all-to-all-done.summed_ref
  229.7 7.6 %all-to-all-start.2 = ((bf16[32,128,512]{2,1,0:T(8,128)(2,1)}), bf16[32,128,512]{2,1,0:T(8,128)(2,1)}, u32[]{:S(2)}, u32[]{:S(2)}) async-start(bf16[32,128,512]{2,1,0:T(8,128)(2,1)} %copy-done), calls=%async_computation.3 | async-start | bytes 8388608 | tf_op jit(solution)/shard_map/all_to_all | solution.py:218
  237.3 0.0 copy-start.4
  237.3 1.2 copy-done.4
  238.5 1.7 shard_map.61
  240.2 49.3 %all-to-all-done.2 = bf16[32,128,512]{2,1,0:T(8,128)(2,1)} async-done(((bf16[32,128,512]{2,1,0:T(8,128)(2,1)}), bf16[32,128,512]{2,1,0:T(8,128)(2,1)}, u32[]{:S(2)}, u32[]{:S(2)}) %all-to-all-start.2) | async-done | bytes 4194336 | tf_op jit(solution)/shard_map/all_to_all | solution.py:218
  289.5 4.0 %all-to-all-start.1 = ((bf16[8,16,2048]{2,1,0:T(8,128)(2,1)}), bf16[8,16,2048]{2,1,0:T(8,128)(2,1)S(1)}, u32[]{:S(2)}, u32[]{:S(2)}) async-start(bf16[8,16,2048]{2,1,0:T(8,128)(2,1)} %shard_map.61), calls=%async_computation.2 | async-start | bytes 1048576 | tf_op jit(solution)/shard_map/all_to_all | solution.py:225
  293.6 12.1 %convolution_bitcast_fusion = f32[512,1536]{1,0:T(8,128)} fusion(bf16[32,128,512]{2,1,0:T(8,128)(2,1)} %all-to-all-done.2, bf16[32,128,1536]{2,1,0:T(8,128)(2,1)} %bitcast.9), kind=kOutput, calls=%fused_computation | convolution fusion | flops 6442450944 | bytes 19922944 | tf_op jit(solution)/shard_map/dot_general | solution.py:226
  305.7 5.4 %all-to-all-done.1 = bf16[8,16,2048]{2,1,0:T(8,128)(2,1)S(1)} async-done(((bf16[8,16,2048]{2,1,0:T(8,128)(2,1)}), bf16[8,16,2048]{2,1,0:T(8,128)(2,1)S(1)}, u32[]{:S(2)}, u32[]{:S(2)}) %all-to-all-start.1) | async-done | bytes 524320 | tf_op jit(solution)/shard_map/all_to_all | solution.py:225
  311.1 0.8 copy.9
Async XLA Ops:
  7.2 75.6 %all-gather.5.cloned.1.call-start = ((), (), s32[]{:S(2)}) async-start(), calls=%async_computation.5 | async-start | bytes 12976128 | tf_op jit(solution)/shard_map/all_gather | solution.py:216
  7.9 146.4 %reduce-scatter.2.cloned.1.call-start = ((), (), s32[]{:S(2)}) async-start(), calls=%async_computation.4 | async-start | bytes 4718592 | tf_op jit(solution)/shard_map/reduce_scatter | solution.py:220
  82.7 4.6 %copy-start.5 = (bf16[4096,1536]{1,0:T(8,128)(2,1)S(1)}, bf16[4096,1536]{1,0:T(8,128)(2,1)}, u32[]{:S(2)}) copy-start(bf16[4096,1536]{1,0:T(8,128)(2,1)} %all-gather.5.cloned.1.call-done) | copy-start | bytes 37748740
  87.3 1.4 copy-start.7
  97.7 1.9 copy-start.1
  99.6 109.9 %copy-start.2 = (bf16[1024,1024]{1,0:T(8,128)(2,1)S(1)}, bf16[1024,1024]{1,0:T(8,128)(2,1)}, u32[]{:S(2)}) copy-start(bf16[1024,1024]{1,0:T(8,128)(2,1)} %constant.6.clone.table_ref) | copy-start | bytes 6291460
  99.6 109.9 %all-gather.7.cloned.1.call-start = ((), (), s32[]{:S(2)}) async-start(), calls=%async_computation.6 | async-start | bytes 4718592 | tf_op jit(solution)/shard_map/all_gather | solution.py:215
  154.3 75.4 %all-to-all-start = ((bf16[32,16,512]{2,1,0:T(8,128)(2,1)}), bf16[32,16,512]{2,1,0:T(8,128)(2,1)S(1)}, u32[]{:S(2)}, u32[]{:S(2)}) async-start(bf16[32,16,512]{2,1,0:T(8,128)(2,1)} %bitcast.13), calls=%async_computation.1 | async-start | bytes 1048576 | tf_op jit(solution)/shard_map/all_to_all | solution.py:221
  209.6 2.2 copy-start.6
  226.8 1.9 copy-start
  228.7 1.0 copy-start.3
  229.7 59.8 %all-to-all-start.2 = ((bf16[32,128,512]{2,1,0:T(8,128)(2,1)}), bf16[32,128,512]{2,1,0:T(8,128)(2,1)}, u32[]{:S(2)}, u32[]{:S(2)}) async-start(bf16[32,128,512]{2,1,0:T(8,128)(2,1)} %copy-done), calls=%async_computation.3 | async-start | bytes 8388608 | tf_op jit(solution)/shard_map/all_to_all | solution.py:218
  237.3 1.2 copy-start.4
  289.5 21.6 %all-to-all-start.1 = ((bf16[8,16,2048]{2,1,0:T(8,128)(2,1)}), bf16[8,16,2048]{2,1,0:T(8,128)(2,1)S(1)}, u32[]{:S(2)}, u32[]{:S(2)}) async-start(bf16[8,16,2048]{2,1,0:T(8,128)(2,1)} %shard_map.61), calls=%async_computation.2 | async-start | bytes 1048576 | tf_op jit(solution)/shard_map/all_to_all | solution.py:225
Sparse Core Ops, SparseCore 0:
  10.5 72.1 all-gather.4
  99.8 54.5 reduce-scatter.1
  156.1 53.4 all-gather.6

commit v2 on v1

--- a/solution.py
+++ b/solution.py
@@ -13,6 +13,9 @@
 BLOCKS = WIDTH // BLOCK
 LANES = 128
 NORM = 1.0 / math.sqrt(WIDTH)
+SIDE = 4
+PIECES = 4
+OFFSETS = (0, -1, 1, -2)
 
 levels = 127.0
 ripple = 0.5
@@ -137,36 +140,139 @@
     )(place, rows, table)
 
 
-def product_kernel(rows_ref, weight_ref, out_ref):
-    devices, tokens, depth = rows_ref.shape
-    out_ref[0] = lax.dot_general(
-        rows_ref[...].reshape(devices * tokens, depth),
-        weight_ref[...],
-        (((1,), (1,)), ((), ())),
-        preferred_element_type=jnp.float32,
-    ).astype(out_ref.dtype)
-
-
-def product(rows, weight, shards):
-    devices, tokens, depth = rows.shape
-    step = tokens // shards
-    width = weight.shape[0]
+def product_kernel(*refs):
+    weight_ref, out_ref = refs[-2:]
+    pieces = [ref for ref in refs[:-2] if len(ref.shape) == 2]
+    members, step = out_ref.shape[0], out_ref.shape[1] // PIECES // 2
+    done = 0
+    for piece_ref in pieces:
+        rows, depth = piece_ref.shape
+        result = lax.dot_general(
+            piece_ref[...],
+            weight_ref[...],
+            (((1,), (1,)), ((), ())),
+            preferred_element_type=jnp.float32,
+        ).astype(out_ref.dtype)
+        for k in range(rows // (members * step)):
+            for t in range(members):
+                start = (k * members + t) * step
+                out_ref[t, done * step : (done + 1) * step, :] = result[start : start + step]
+            done += 1
+
+
+def product(held, pieces, weight, position, members):
+    rows = sum(piece.shape[0] for piece in pieces)
+    width, depth = weight.shape
+    whole = [pl.BlockSpec(memory_space=pltpu.VMEM)] * (len(pieces) + 1)
+    earlier = [] if held is None else [held]
     return pl.pallas_call(
         product_kernel,
-        grid=(shards,),
-        in_specs=[
-            pl.BlockSpec((devices, step, depth), lambda i: (0, i, 0)),
-            pl.BlockSpec((width, depth), lambda i: (0, 0)),
-        ],
-        out_specs=pl.BlockSpec((1, devices * step, width), lambda i: (i, 0, 0)),
-        out_shape=jax.ShapeDtypeStruct((shards, devices * step, width), jnp.bfloat16),
+        grid=(1,),
+        in_specs=[pl.BlockSpec(memory_space=pl.ANY)] * len(earlier) + whole,
+        out_specs=pl.BlockSpec((members, rows // members, width), lambda i: (0, position, 0)),
+        out_shape=jax.ShapeDtypeStruct((members, 4 * rows // members, width), jnp.bfloat16),
+        input_output_aliases={0: 0} if earlier else {},
         compiler_params=pltpu.CompilerParams(vmem_limit_bytes=32 * 1024 * 1024),
         cost_estimate=pl.CostEstimate(
-            flops=2 * devices * tokens * depth * width,
-            bytes_accessed=2 * devices * tokens * (depth + width),
+            flops=2 * rows * depth * width,
+            bytes_accessed=2 * rows * (depth + width),
             transcendentals=0,
         ),
-    )(rows, weight)
+    )(*earlier, *pieces, weight)
+
+
+def order_kernel(sources, rows_ref, out_ref):
+    for slot in range(rows_ref.shape[0]):
+        out_ref[sources[slot]] = rows_ref[slot]
+
+
+def order(rows, sources):
+    return pl.pallas_call(
+        order_kernel,
+        in_specs=[
+            pl.BlockSpec(memory_space=pltpu.SMEM),
+            pl.BlockSpec(memory_space=pltpu.VMEM),
+        ],
+        out_specs=pl.BlockSpec(memory_space=pltpu.VMEM),
+        out_shape=jax.ShapeDtypeStruct(rows.shape, rows.dtype),
+    )(sources, rows)
+
+
+def gradient_kernel(sources, quantized_ref, *refs):
+    out_ref = refs[-1]
+    pieces = refs[:-1]
+    tokens = quantized_ref.shape[1]
+    slot = 0
+    for number, piece_ref in enumerate(pieces):
+        count = piece_ref.shape[0] // tokens
+        block = jnp.concatenate(
+            [quantized_ref[sources[slot + k]] for k in range(count)], axis=0
+        )
+        slot += count
+        term = lax.dot_general(
+            block, piece_ref[...], (((0,), (0,)), ((), ())), preferred_element_type=jnp.float32
+        )
+        out_ref[...] = term if number == 0 else out_ref[...] + term
+
+
+def gradient(sources, quantized, pieces):
+    width, depth = quantized.shape[2], pieces[0].shape[1]
+    rows = sum(piece.shape[0] for piece in pieces)
+    return pl.pallas_call(
+        gradient_kernel,
+        in_specs=[pl.BlockSpec(memory_space=pltpu.SMEM)]
+        + [pl.BlockSpec(memory_space=pltpu.VMEM)] * (len(pieces) + 1),
+        out_specs=pl.BlockSpec(memory_space=pltpu.VMEM),
+        out_shape=jax.ShapeDtypeStruct((width, depth), jnp.float32),
+        compiler_params=pltpu.CompilerParams(vmem_limit_bytes=48 * 1024 * 1024),
+        cost_estimate=pl.CostEstimate(
+            flops=2 * rows * depth * width,
+            bytes_accessed=2 * rows * (depth + width) + 4 * width * depth,
+            transcendentals=0,
+        ),
+    )(sources, quantized, *pieces)
+
+
+def chip_core(x, y, core):
+    return (x % SIDE * SIDE + y % SIDE) * 2 + core
+
+
+def route(turn, sign):
+    pairs = []
+    for x in range(SIDE):
+        for y in range(SIDE):
+            for core in range(2):
+                along = (sign, 0) if core == turn else (0, sign)
+                pairs.append(
+                    (chip_core(x, y, core), chip_core(x + along[0], y + along[1], core))
+                )
+    return pairs
+
+
+def around(block, turn):
+    half = block.shape[0] // 2
+    below = lax.ppermute(block, "dp", route(turn, 1))
+    above = lax.ppermute(block, "dp", route(turn, -1))
+    first = lax.ppermute(below[:half], "dp", route(turn, 1))
+    second = lax.ppermute(above[half:], "dp", route(turn, -1))
+    return below, above, first, second
+
+
+def other_core(block):
+    return lax.ppermute(block, "dp", [(d, d ^ 1) for d in range(2 * SIDE * SIDE)])
+
+
+def sources_of(device):
+    x, y, core = device // (2 * SIDE), device // 2 % SIDE, device % 2
+    found = []
+    for outer in OFFSETS:
+        for chain in range(2):
+            sender = core ^ chain
+            for inner in OFFSETS:
+                at_x = (x + jnp.where(sender == 0, inner, outer) + SIDE) % SIDE
+                at_y = (y + jnp.where(sender == 0, outer, inner) + SIDE) % SIDE
+                found.append((at_x * SIDE + at_y) * 2 + sender)
+    return jnp.stack(found).astype(jnp.int32)
 
 
 def finish_kernel(summed_ref, slope_ref, table_ref, out_ref, inner):
@@ -209,26 +315,28 @@
     dp = lax.axis_size("dp")
     members = lax.axis_size("tensor")
     tokens, features = activations.shape
-    width, depth = weight.shape
+    width = weight.shape[0]
     place = lax.axis_index("tensor").astype(jnp.int32).reshape(1)
+    sources = sources_of(lax.axis_index("dp").astype(jnp.int32))
     table = hadamard_table(BLOCK)
     wide_rows = lax.all_gather(activations, "tensor", axis=0, tiled=False)
-    all_rows = lax.all_gather(grad_out, "dp", axis=0, tiled=False)
+    near = jnp.concatenate([grad_out, *around(grad_out, 0)], axis=0)
+    below, above, first, second = around(near, 1)
+    groups = []
+    for block in (near, below, above):
+        groups.append([block, other_core(block)])
+    groups.append([first, second, other_core(first), other_core(second)])
+    partial_rows = None
+    for position, group in enumerate(groups):
+        partial_rows = product(partial_rows, group, weight, position, members)
+    summed = lax.psum_scatter(partial_rows, "tensor", scatter_dimension=0, tiled=False)
     quantized, slope = quantize(wide_rows, table, place, dp, width)
     q_block = lax.all_to_all(quantized, "dp", split_axis=0, concat_axis=0, tiled=True)
-    partial_rows = product(all_rows, weight, members)
-    summed = lax.psum_scatter(partial_rows, "tensor", scatter_dimension=0, tiled=False)
-    homed = lax.all_to_all(
-        summed.reshape(dp, tokens // members, width), "dp", split_axis=0, concat_axis=0, tiled=True
-    )
+    ordered = order(summed.reshape(dp, tokens // members, width), sources)
+    homed = lax.all_to_all(ordered, "dp", split_axis=0, concat_axis=0, tiled=True)
     mixed = finish(homed, slope, table, members)
     grad_input = lax.all_to_all(mixed, "tensor", split_axis=0, concat_axis=0, tiled=True)
-    weight_sum = lax.dot_general(
-        q_block.reshape(dp * tokens, width),
-        all_rows.reshape(dp * tokens, depth),
-        (((0,), (0,)), ((), ())),
-        preferred_element_type=jnp.float32,
-    )
+    weight_sum = gradient(sources, q_block, [block for group in groups for block in group])
     return (grad_input.reshape(tokens, features), weight_sum)
 
 

time: 320 us -> 297 us (0.928)
  waiting for transfers between devices: 233 us -> 178 us
  starting transfers between devices: 19.2 us -> 43.7 us
  Pallas kernels: 25.7 us -> 38.7 us
  matrix products: 12.1 us -> 0 us
  local copies, waits for them, and re-layouts: 15 us -> 19 us
    all_gather x1 -> x0, waiting for transfers between devices: 74.8 us -> none  [shards(): all_rows = lax.all_gather(grad_out, 'dp', axis=0, tiled=False)]
    ppermute x0 -> x13, waiting for transfers between devices: none -> 32.5 us  [the longest x2 17.7 us: around(): below = lax.ppermute(block, 'dp', route(turn, 1))]
    ppermute x0 -> x13, starting transfers between devices: none -> 24.2 us  [the longest x5 11.5 us: other_core(): lax.ppermute(block, 'dp', [(d, d ^ 1) for d in range(2 * SIDE * SIDE)])]
    pallas_call x1 -> x6, Pallas kernels: 8.97 us -> 22 us  [the longest x1 12.8 us: gradient(): pl.pallas_call(gradient_kernel, in_specs=[pl.BlockSpec(memory_space=pltpu...]
    dot_general x1 -> x0, matrix products: 12.1 us -> none  [shards(): lax.dot_general(q_block.reshape(dp * tokens, width), all_rows.reshape(dp...]
    all_to_all x1, waiting for transfers between devices: 5.45 us -> 0.68 us  [shards(): lax.all_to_all(mixed, 'tensor', split_axis=0, concat_axis=0, tiled=True)]
    unnamed x17 -> x53, local copies, waits for them, and re-layouts: 15 us -> 18.2 us
  transfers between devices with their start and end apart: 6 -> 18, of which waited for: 5 -> 9; matrix products, arithmetic and copies ran while one was open for 4% -> 1% of each run, Pallas kernels for 5% -> 12%
where the time goes in v2:
time: 297 us; the launch traced here: 296 us
  waiting for transfers between devices  178 us (60%)
  starting transfers between devices  43.7 us (15%)
  Pallas kernels  38.7 us (13%)
  local copies, waits for them, and re-layouts  19 us (6%)
  between operations  15.7 us (5%)
    reduce_scatter x1, waiting for transfers between devices, shards(): lax.psum_scatter(partial_rows, 'tensor', scatter_dimension=0, tiled=False)  51.1 us
    all_to_all x1, waiting for transfers between devices, shards(): lax.all_to_all(quantized, 'dp', split_axis=0, concat_axis=0, tiled=True)  47.7 us
    all_gather x1, waiting for transfers between devices, shards(): wide_rows = lax.all_gather(activations, 'tensor', axis=0, tiled=False)  45.9 us
    unnamed x53, local copies, waits for them, and re-layouts  18.2 us
    ppermute x2, waiting for transfers between devices, around(): below = lax.ppermute(block, 'dp', route(turn, 1))  17.7 us
    pallas_call x1, Pallas kernels, quantize(): pl.pallas_call(quantize_kernel, grid_spec=pltpu.PrefetchScalarGridSpec(nu...  15 us
    pallas_call x1, Pallas kernels, gradient(): pl.pallas_call(gradient_kernel, in_specs=[pl.BlockSpec(memory_space=pltpu...  12.8 us
    ppermute x5, starting transfers between devices, other_core(): lax.ppermute(block, 'dp', [(d, d ^ 1) for d in range(2 * SIDE * SIDE)])  11.5 us
  transfers between devices with their start and end apart: 18, of which 9 were waited for; matrix products, arithmetic and copies ran while one was open for 1% of the time, Pallas kernels for 12%

profile of v2, /device:TPU:1, one launch (start us, length us, event | category | flops | bytes accessed | tf_op | source)
XLA Modules:
  0.0 295.6 jit_solution(13265565496175896629)
XLA Ops:
  7.2 2.2 collective-permute-start
  9.4 1.5 collective-permute-start.1
  10.9 1.1 constant_dynamic-update-slice_fusion.4
  12.0 4.5 %collective-permute-done = bf16[128,1536]{1,0:T(8,128)(2,1)S(1)} collective-permute-done((bf16[128,1536]{1,0:T(8,128)(2,1)}, bf16[128,1536]{1,0:T(8,128)(2,1)S(1)}, u32[]{:S(2)}, u32[]{:S(2)}) %collective-permute-start) | collective-permute-done | bytes 393248 | tf_op jit(solution)/shard_map/ppermute | solution.py:254
  16.5 0.1 collective-permute-start.2
  16.7 2.7 collective-permute-start.3
  19.5 2.9 collective-permute-done.2
  22.4 1.0 collective-permute-start.5
  23.4 1.8 collective-permute-start.7
  25.2 4.9 %collective-permute-start.4 = (bf16[512,1536]{1,0:T(8,128)(2,1)S(1)}, bf16[512,1536]{1,0:T(8,128)(2,1)S(1)}, u32[]{:S(2)}, u32[]{:S(2)}) collective-permute-start(bf16[512,1536]{1,0:T(8,128)(2,1)S(1)} %constant_dynamic-update-slice_fusion.refs_0_), channel_id=1, source_target_pairs={{0,8},{8,0},{16,24},{24,16},{32,40},{40,32},{48,56},{56,48},{64,72... | collective-permute-start | bytes 4718600 | tf_op jit(solution)/shard_map/ppermute | solution.py:262
  30.1 13.2 %collective-permute-done.5.refs_1_.refs_2_ = bf16[512,1536]{1,0:T(8,128)(2,1)S(1)} collective-permute-done((bf16[512,1536]{1,0:T(8,128)(2,1)S(1)}, bf16[512,1536]{1,0:T(8,128)(2,1)S(1)}, u32[]{:S(2)}, u32[]{:S(2)}) %collective-permute-start.5) | collective-permute-done | bytes 1572896 | tf_op jit(solution)/shard_map/ppermute | solution.py:254
  43.3 5.2 %collective-permute-start.6 = (bf16[512,1536]{1,0:T(8,128)(2,1)S(1)}, bf16[512,1536]{1,0:T(8,128)(2,1)S(1)}, u32[]{:S(2)}, u32[]{:S(2)}) collective-permute-start(bf16[512,1536]{1,0:T(8,128)(2,1)S(1)} %collective-permute-done.5.refs_1_.refs_2_), channel_id=1, source_target_pairs={{0,8},{8,0},{16,24},{24,16},{32,40},{40,32},{48,56},{56,48},{64,72... | collective-permute-start | bytes 4718600 | tf_op jit(solution)/shard_map/ppermute | solution.py:262
  48.5 0.1 collective-permute-start.8
  48.6 3.3 %collective-permute-start.10 = (bf16[256,1536]{1,0:T(8,128)(2,1)S(1)}, bf16[256,1536]{1,0:T(8,128)(2,1)S(1)}, u32[]{:S(2)}, u32[]{:S(2)}) collective-permute-start(bf16[256,1536]{1,0:T(8,128)(2,1)S(1)} %slice.19), channel_id=1, source_target_pairs={{0,48},{8,200},{16,0},{24,216},{32,16},{40,232},{48,32},{56,248},{... | collective-permute-start | bytes 2359304 | tf_op jit(solution)/shard_map/ppermute | solution.py:257
  52.0 0.1 collective-permute-start.9
  52.1 8.8 %collective-permute-done.10.refs_2_.refs_7_ = bf16[256,1536]{1,0:T(8,128)(2,1)S(1)} collective-permute-done((bf16[256,1536]{1,0:T(8,128)(2,1)S(1)}, bf16[256,1536]{1,0:T(8,128)(2,1)S(1)}, u32[]{:S(2)}, u32[]{:S(2)}) %collective-permute-start.10) | collective-permute-done | bytes 786464 | tf_op jit(solution)/shard_map/ppermute | solution.py:257
  60.9 0.5 collective-permute-start.12
  61.4 3.1 %collective-permute-done.9.refs_1_.refs_6_ = bf16[256,1536]{1,0:T(8,128)(2,1)S(1)} collective-permute-done((bf16[256,1536]{1,0:T(8,128)(2,1)S(1)}, bf16[256,1536]{1,0:T(8,128)(2,1)S(1)}, u32[]{:S(2)}, u32[]{:S(2)}) %collective-permute-start.9) | collective-permute-done | bytes 786464 | tf_op jit(solution)/shard_map/ppermute | solution.py:256
  64.4 0.8 collective-permute-start.11
  65.2 1.8 shard_map.59.refs_0_
  67.1 1.8 shard_map.60.refs_0_
  68.9 1.8 shard_map.61.refs_0_
  70.8 1.8 shard_map.62
  72.7 2.0 copy-done
  74.6 0.9 copy-done.18
  75.5 0.9 copy-done.20
  76.4 0.7 all-gather.3.cloned.1.call-update
  78.5 0.7 stack.131.sources
  79.2 51.1 %reduce-scatter.2.cloned.1.call-done = bf16[1,512,512]{2,1,0:T(8,128)(2,1)} async-done(((bf16[8,512,512]{2,1,0:T(8,128)(2,1)}), bf16[1,512,512]{2,1,0:T(8,128)(2,1)}) %reduce-scatter.2.cloned.1.call-update) | async-done | bytes 524304 | tf_op jit(solution)/shard_map/reduce_scatter | solution.py:332
  130.3 1.9 shard_map.63
  132.1 7.5 %all-to-all-start = ((bf16[32,16,512]{2,1,0:T(8,128)(2,1)}), bf16[32,16,512]{2,1,0:T(8,128)(2,1)S(1)}, u32[]{:S(2)}, u32[]{:S(2)}) async-start(bf16[32,16,512]{2,1,0:T(8,128)(2,1)} %shard_map.63), calls=%async_computation.1 | async-start | bytes 1048576 | tf_op jit(solution)/shard_map/all_to_all | solution.py:336
  139.6 45.9 %all-gather.3.cloned.1.call-done = bf16[1024,2048]{1,0:T(8,128)(2,1)} async-done(((bf16[128,2048]{1,0:T(8,128)(2,1)}), bf16[1024,2048]{1,0:T(8,128)(2,1)}) %all-gather.3.cloned.1.call-update) | async-done | bytes 4194320 | tf_op jit(solution)/shard_map/all_gather | solution.py:322
  185.5 2.2 copy-done.23
  187.7 15.0 %shard_map.64 = (bf16[32,128,512]{2,1,0:T(8,128)(2,1)S(1)}, f32[32,16,512]{2,1,0:T(8,128)S(1)}) custom-call(s32[1]{0:T(128)} %bitcast.33.place, bf16[8,128,2048]{2,1,0:T(8,128)(2,1)S(1)} %bitcast.36, bf16[1024,1024]{1,0:T(8,128)(2,1)S(1)} %copy-done.7), custom_call_target="tpu_custom_call" | custom-call | flops 4294967296 | bytes 8388608 | tf_op jit(solution)/shard_map/pallas_call | solution.py:114
  202.7 2.0 copy-done.2
  204.8 1.0 copy-done.12
  205.8 7.6 %all-to-all-start.2 = ((bf16[32,128,512]{2,1,0:T(8,128)(2,1)}), bf16[32,128,512]{2,1,0:T(8,128)(2,1)}, u32[]{:S(2)}, u32[]{:S(2)}) async-start(bf16[32,128,512]{2,1,0:T(8,128)(2,1)} %copy-done.2), calls=%async_computation.3 | async-start | bytes 8388608 | tf_op jit(solution)/shard_map/all_to_all | solution.py:334
  213.3 1.6 copy-done.8
  214.9 1.2 copy-done.13
  216.2 1.7 shard_map.65
  217.8 47.7 %all-to-all-done.2.quantized_ref = bf16[32,128,512]{2,1,0:T(8,128)(2,1)} async-done(((bf16[32,128,512]{2,1,0:T(8,128)(2,1)}), bf16[32,128,512]{2,1,0:T(8,128)(2,1)}, u32[]{:S(2)}, u32[]{:S(2)}) %all-to-all-start.2) | async-done | bytes 4194336 | tf_op jit(solution)/shard_map/all_to_all | solution.py:334
  265.5 4.4 %all-to-all-start.1 = ((bf16[8,16,2048]{2,1,0:T(8,128)(2,1)}), bf16[8,16,2048]{2,1,0:T(8,128)(2,1)}, u32[]{:S(2)}, u32[]{:S(2)}) async-start(bf16[8,16,2048]{2,1,0:T(8,128)(2,1)} %shard_map.65), calls=%async_computation.2 | async-start | bytes 1048576 | tf_op jit(solution)/shard_map/all_to_all | solution.py:338
  270.0 1.1 copy-done.17
  271.1 1.1 copy-done.19
  272.2 1.1 copy-done.21
  273.3 12.8 %shard_map.66 = f32[512,1536]{1,0:T(8,128)} custom-call(s32[32]{0:T(128)S(1)} %copy-done.22, bf16[32,128,512]{2,1,0:T(8,128)(2,1)} %all-to-all-done.2.quantized_ref, bf16[512,1536]{1,0:T(8,128)(2,1)S(1)} %copy-done.6, bf16[512,1536]{1,0:T(8,128)(2,1)} %copy-done.11, bf16[512,1536]{1,0:T(8,128)(2,1)} %copy-done.3, bf16[512,1536]{1,0:T(8,128)(2,1)} %copy-done.9, ...), custom_call_target="tpu_custom_call" | custom-call | flops 6442450944 | bytes 19922944 | tf_op jit(solution)/shard_map/pallas_call | solution.py:221
  286.2 0.7 all-to-all-done.1
  286.9 1.9 copy.17
  (57 shorter events, 0.4 us)
Async XLA Ops:
  7.2 123.1 %reduce-scatter.2.cloned.1.call-start = ((), (), s32[]{:S(2)}) async-start(), calls=%async_computation.4 | async-start | bytes 4718592 | tf_op jit(solution)/shard_map/reduce_scatter | solution.py:332
  7.2 9.3 %collective-permute-start = (bf16[128,1536]{1,0:T(8,128)(2,1)}, bf16[128,1536]{1,0:T(8,128)(2,1)S(1)}, u32[]{:S(2)}, u32[]{:S(2)}) collective-permute-start(bf16[128,1536]{1,0:T(8,128)(2,1)} %param.6), channel_id=1, source_target_pairs={{0,64},{8,24},{16,80},{24,40},{32,96},{40,56},{48,112},{56,8},{64,... | collective-permute-start | bytes 1179656 | tf_op jit(solution)/shard_map/ppermute | solution.py:254
  9.4 7.2 %collective-permute-start.1 = (bf16[128,1536]{1,0:T(8,128)(2,1)}, bf16[128,1536]{1,0:T(8,128)(2,1)S(1)}, u32[]{:S(2)}, u32[]{:S(2)}) collective-permute-start(bf16[128,1536]{1,0:T(8,128)(2,1)} %param.6), channel_id=1, source_target_pairs={{0,192},{8,56},{16,208},{24,8},{32,224},{40,24},{48,240},{56,40},{... | collective-permute-start | bytes 1179656 | tf_op jit(solution)/shard_map/ppermute | solution.py:255
  16.5 5.8 %collective-permute-start.2 = (bf16[64,1536]{1,0:T(8,128)(2,1)S(1)}, bf16[64,1536]{1,0:T(8,128)(2,1)S(1)}, u32[]{:S(2)}, u32[]{:S(2)}) collective-permute-start(bf16[64,1536]{1,0:T(8,128)(2,1)S(1)} %slice.16), channel_id=1, source_target_pairs={{0,64},{8,24},{16,80},{24,40},{32,96},{40,56},{48,112},{56,8},{64,... | collective-permute-start | bytes 589832 | tf_op jit(solution)/shard_map/ppermute | solution.py:256
  16.7 5.7 %collective-permute-start.3 = (bf16[64,1536]{1,0:T(8,128)(2,1)S(1)}, bf16[64,1536]{1,0:T(8,128)(2,1)S(1)}, u32[]{:S(2)}, u32[]{:S(2)}) collective-permute-start(bf16[64,1536]{1,0:T(8,128)(2,1)S(1)} %slice.17), channel_id=1, source_target_pairs={{0,192},{8,56},{16,208},{24,8},{32,224},{40,24},{48,240},{56,40},{... | collective-permute-start | bytes 589832 | tf_op jit(solution)/shard_map/ppermute | solution.py:257
  22.4 42.8 %copy-start.5 = (bf16[512,1536]{1,0:T(8,128)(2,1)}, bf16[512,1536]{1,0:T(8,128)(2,1)S(1)}, u32[]{:S(2)}) copy-start(bf16[512,1536]{1,0:T(8,128)(2,1)S(1)} %constant_dynamic-update-slice_fusion.refs_0_) | copy-start | bytes 4718596
  22.4 42.8 %copy-start.1 = (bf16[512,1536]{1,0:T(8,128)(2,1)S(1)}, bf16[512,1536]{1,0:T(8,128)(2,1)}, u32[]{:S(2)}) copy-start(bf16[512,1536]{1,0:T(8,128)(2,1)} %refs_5_.1) | copy-start | bytes 4718596
  22.4 20.8 %collective-permute-start.5 = (bf16[512,1536]{1,0:T(8,128)(2,1)S(1)}, bf16[512,1536]{1,0:T(8,128)(2,1)S(1)}, u32[]{:S(2)}, u32[]{:S(2)}) collective-permute-start(bf16[512,1536]{1,0:T(8,128)(2,1)S(1)} %constant_dynamic-update-slice_fusion.refs_0_), channel_id=1, source_target_pairs={{0,16},{8,72},{16,32},{24,88},{32,48},{40,104},{48,0},{56,120},{64... | collective-permute-start | bytes 4718600 | tf_op jit(solution)/shard_map/ppermute | solution.py:254
  23.4 25.1 %collective-permute-start.7 = (bf16[512,1536]{1,0:T(8,128)(2,1)S(1)}, bf16[512,1536]{1,0:T(8,128)(2,1)S(1)}, u32[]{:S(2)}, u32[]{:S(2)}) collective-permute-start(bf16[512,1536]{1,0:T(8,128)(2,1)S(1)} %constant_dynamic-update-slice_fusion.refs_0_), channel_id=1, source_target_pairs={{0,48},{8,200},{16,0},{24,216},{32,16},{40,232},{48,32},{56,248},{... | collective-permute-start | bytes 4718600 | tf_op jit(solution)/shard_map/ppermute | solution.py:255
  25.2 40.0 %collective-permute-start.4 = (bf16[512,1536]{1,0:T(8,128)(2,1)S(1)}, bf16[512,1536]{1,0:T(8,128)(2,1)S(1)}, u32[]{:S(2)}, u32[]{:S(2)}) collective-permute-start(bf16[512,1536]{1,0:T(8,128)(2,1)S(1)} %constant_dynamic-update-slice_fusion.refs_0_), channel_id=1, source_target_pairs={{0,8},{8,0},{16,24},{24,16},{32,40},{40,32},{48,56},{56,48},{64,72... | collective-permute-start | bytes 4718600 | tf_op jit(solution)/shard_map/ppermute | solution.py:262
  43.3 23.8 %copy-start.3 = (bf16[512,1536]{1,0:T(8,128)(2,1)}, bf16[512,1536]{1,0:T(8,128)(2,1)S(1)}, u32[]{:S(2)}) copy-start(bf16[512,1536]{1,0:T(8,128)(2,1)S(1)} %collective-permute-done.5.refs_1_.refs_2_) | copy-start | bytes 4718596
  43.3 23.8 %collective-permute-start.6 = (bf16[512,1536]{1,0:T(8,128)(2,1)S(1)}, bf16[512,1536]{1,0:T(8,128)(2,1)S(1)}, u32[]{:S(2)}, u32[]{:S(2)}) collective-permute-start(bf16[512,1536]{1,0:T(8,128)(2,1)S(1)} %collective-permute-done.5.refs_1_.refs_2_), channel_id=1, source_target_pairs={{0,8},{8,0},{16,24},{24,16},{32,40},{40,32},{48,56},{56,48},{64,72... | collective-permute-start | bytes 4718600 | tf_op jit(solution)/shard_map/ppermute | solution.py:262
  48.5 20.4 %copy-start.4 = (bf16[512,1536]{1,0:T(8,128)(2,1)}, bf16[512,1536]{1,0:T(8,128)(2,1)S(1)}, u32[]{:S(2)}) copy-start(bf16[512,1536]{1,0:T(8,128)(2,1)S(1)} %collective-permute-done.7.refs_1_.refs_4_) | copy-start | bytes 4718596
  48.5 20.4 %collective-permute-start.8 = (bf16[512,1536]{1,0:T(8,128)(2,1)S(1)}, bf16[512,1536]{1,0:T(8,128)(2,1)S(1)}, u32[]{:S(2)}, u32[]{:S(2)}) collective-permute-start(bf16[512,1536]{1,0:T(8,128)(2,1)S(1)} %collective-permute-done.7.refs_1_.refs_4_), channel_id=1, source_target_pairs={{0,8},{8,0},{16,24},{24,16},{32,40},{40,32},{48,56},{56,48},{64,72... | collective-permute-start | bytes 4718600 | tf_op jit(solution)/shard_map/ppermute | solution.py:262
  48.6 12.2 %collective-permute-start.10 = (bf16[256,1536]{1,0:T(8,128)(2,1)S(1)}, bf16[256,1536]{1,0:T(8,128)(2,1)S(1)}, u32[]{:S(2)}, u32[]{:S(2)}) collective-permute-start(bf16[256,1536]{1,0:T(8,128)(2,1)S(1)} %slice.19), channel_id=1, source_target_pairs={{0,48},{8,200},{16,0},{24,216},{32,16},{40,232},{48,32},{56,248},{... | collective-permute-start | bytes 2359304 | tf_op jit(solution)/shard_map/ppermute | solution.py:257
  52.0 12.4 %collective-permute-start.9 = (bf16[256,1536]{1,0:T(8,128)(2,1)S(1)}, bf16[256,1536]{1,0:T(8,128)(2,1)S(1)}, u32[]{:S(2)}, u32[]{:S(2)}) collective-permute-start(bf16[256,1536]{1,0:T(8,128)(2,1)S(1)} %slice.18), channel_id=1, source_target_pairs={{0,16},{8,72},{16,32},{24,88},{32,48},{40,104},{48,0},{56,120},{64... | collective-permute-start | bytes 2359304 | tf_op jit(solution)/shard_map/ppermute | solution.py:256
  60.9 9.9 %copy-start.14 = (bf16[256,1536]{1,0:T(8,128)(2,1)}, bf16[256,1536]{1,0:T(8,128)(2,1)S(1)}, u32[]{:S(2)}) copy-start(bf16[256,1536]{1,0:T(8,128)(2,1)S(1)} %collective-permute-done.10.refs_2_.refs_7_) | copy-start | bytes 2359300
  60.9 9.9 %collective-permute-start.12 = (bf16[256,1536]{1,0:T(8,128)(2,1)S(1)}, bf16[256,1536]{1,0:T(8,128)(2,1)S(1)}, u32[]{:S(2)}, u32[]{:S(2)}) collective-permute-start(bf16[256,1536]{1,0:T(8,128)(2,1)S(1)} %collective-permute-done.10.refs_2_.refs_7_), channel_id=1, source_target_pairs={{0,8},{8,0},{16,24},{24,16},{32,40},{40,32},{48,56},{56,48},{64,72... | collective-permute-start | bytes 2359304 | tf_op jit(solution)/shard_map/ppermute | solution.py:262
  64.4 6.4 %copy-start.16 = (bf16[256,1536]{1,0:T(8,128)(2,1)}, bf16[256,1536]{1,0:T(8,128)(2,1)S(1)}, u32[]{:S(2)}) copy-start(bf16[256,1536]{1,0:T(8,128)(2,1)S(1)} %collective-permute-done.9.refs_1_.refs_6_) | copy-start | bytes 2359300
  64.4 6.4 %collective-permute-start.11 = (bf16[256,1536]{1,0:T(8,128)(2,1)S(1)}, bf16[256,1536]{1,0:T(8,128)(2,1)S(1)}, u32[]{:S(2)}, u32[]{:S(2)}) collective-permute-start(bf16[256,1536]{1,0:T(8,128)(2,1)S(1)} %collective-permute-done.9.refs_1_.refs_6_), channel_id=1, source_target_pairs={{0,8},{8,0},{16,24},{24,16},{32,40},{40,32},{48,56},{56,48},{64,72... | collective-permute-start | bytes 2359304 | tf_op jit(solution)/shard_map/ppermute | solution.py:262
  65.2 1.8 copy-start.11
  67.1 1.8 copy-start.9
  68.9 1.8 copy-start.10
  72.6 2.0 copy-start
  74.6 0.9 copy-start.18
  75.5 0.9 copy-start.20
  76.4 109.1 %all-gather.3.cloned.1.call-start = ((), (), s32[]{:S(2)}) async-start(), calls=%async_computation.5 | async-start | bytes 4718592 | tf_op jit(solution)/shard_map/all_gather | solution.py:322
  77.6 107.9 %copy-start.7 = (bf16[1024,1024]{1,0:T(8,128)(2,1)S(1)}, bf16[1024,1024]{1,0:T(8,128)(2,1)}, u32[]{:S(2)}) copy-start(bf16[1024,1024]{1,0:T(8,128)(2,1)} %constant.313.clone.table_ref) | copy-start | bytes 6291460
  132.1 73.6 %all-to-all-start = ((bf16[32,16,512]{2,1,0:T(8,128)(2,1)}), bf16[32,16,512]{2,1,0:T(8,128)(2,1)S(1)}, u32[]{:S(2)}, u32[]{:S(2)}) async-start(bf16[32,16,512]{2,1,0:T(8,128)(2,1)} %shard_map.63), calls=%async_computation.1 | async-start | bytes 1048576 | tf_op jit(solution)/shard_map/all_to_all | solution.py:336
  185.5 2.2 copy-start.23
  202.7 2.0 copy-start.2
  204.8 1.0 copy-start.12
  205.8 59.8 %all-to-all-start.2 = ((bf16[32,128,512]{2,1,0:T(8,128)(2,1)}), bf16[32,128,512]{2,1,0:T(8,128)(2,1)}, u32[]{:S(2)}, u32[]{:S(2)}) async-start(bf16[32,128,512]{2,1,0:T(8,128)(2,1)} %copy-done.2), calls=%async_computation.3 | async-start | bytes 8388608 | tf_op jit(solution)/shard_map/all_to_all | solution.py:334
  213.3 1.6 copy-start.8
  214.9 1.2 copy-start.13
  216.2 53.8 %copy-start.6 = (bf16[512,1536]{1,0:T(8,128)(2,1)S(1)}, bf16[512,1536]{1,0:T(8,128)(2,1)}, u32[]{:S(2)}) copy-start(bf16[512,1536]{1,0:T(8,128)(2,1)} %copy-done.5) | copy-start | bytes 4718596
  216.2 53.8 %copy-start.15 = (bf16[256,1536]{1,0:T(8,128)(2,1)S(1)}, bf16[256,1536]{1,0:T(8,128)(2,1)}, u32[]{:S(2)}) copy-start(bf16[256,1536]{1,0:T(8,128)(2,1)} %copy-done.14) | copy-start | bytes 2359300
  216.2 53.8 %copy-start.22 = (s32[32]{0:T(128)S(1)}, s32[32]{0:T(128)}, u32[]{:S(2)}) copy-start(s32[32]{0:T(128)} %stack.131.sources) | copy-start | bytes 388
  265.5 21.3 %all-to-all-start.1 = ((bf16[8,16,2048]{2,1,0:T(8,128)(2,1)}), bf16[8,16,2048]{2,1,0:T(8,128)(2,1)}, u32[]{:S(2)}, u32[]{:S(2)}) async-start(bf16[8,16,2048]{2,1,0:T(8,128)(2,1)} %shard_map.65), calls=%async_computation.2 | async-start | bytes 1048576 | tf_op jit(solution)/shard_map/all_to_all | solution.py:338
  269.9 1.1 copy-start.17
  271.1 1.1 copy-start.19
  272.2 1.1 copy-start.21
Sparse Core Ops, SparseCore 0:
  76.5 53.6 reduce-scatter.1
  132.1 53.4 all-gather.2

commit v3 on v2

--- a/solution.py
+++ b/solution.py
@@ -262,17 +262,19 @@
     return lax.ppermute(block, "dp", [(d, d ^ 1) for d in range(2 * SIDE * SIDE)])
 
 
-def sources_of(device):
-    x, y, core = device // (2 * SIDE), device // 2 % SIDE, device % 2
-    found = []
-    for outer in OFFSETS:
-        for chain in range(2):
-            sender = core ^ chain
-            for inner in OFFSETS:
-                at_x = (x + jnp.where(sender == 0, inner, outer) + SIDE) % SIDE
-                at_y = (y + jnp.where(sender == 0, outer, inner) + SIDE) % SIDE
-                found.append((at_x * SIDE + at_y) * 2 + sender)
-    return jnp.stack(found).astype(jnp.int32)
+def sources_table():
+    table = []
+    for x in range(SIDE):
+        for y in range(SIDE):
+            for core in range(2):
+                found = []
+                for outer in OFFSETS:
+                    for sender in (core, 1 - core):
+                        for inner in OFFSETS:
+                            along = (inner, outer) if sender == 0 else (outer, inner)
+                            found.append(chip_core(x + along[0], y + along[1], sender))
+                table.append(found)
+    return np.asarray(table, np.int32)
 
 
 def finish_kernel(summed_ref, slope_ref, table_ref, out_ref, inner):
@@ -317,7 +319,7 @@
     tokens, features = activations.shape
     width = weight.shape[0]
     place = lax.axis_index("tensor").astype(jnp.int32).reshape(1)
-    sources = sources_of(lax.axis_index("dp").astype(jnp.int32))
+    sources = jnp.asarray(sources_table())[lax.axis_index("dp")]
     table = hadamard_table(BLOCK)
     wide_rows = lax.all_gather(activations, "tensor", axis=0, tiled=False)
     near = jnp.concatenate([grad_out, *around(grad_out, 0)], axis=0)
@@ -329,6 +331,7 @@
     partial_rows = None
     for position, group in enumerate(groups):
         partial_rows = product(partial_rows, group, weight, position, members)
+    partial_rows, wide_rows = lax.optimization_barrier((partial_rows, wide_rows))
     summed = lax.psum_scatter(partial_rows, "tensor", scatter_dimension=0, tiled=False)
     quantized, slope = quantize(wide_rows, table, place, dp, width)
     q_block = lax.all_to_all(quantized, "dp", split_axis=0, concat_axis=0, tiled=True)

time: 297 us -> 252 us (0.85)
  waiting for transfers between devices: 178 us -> 134 us
    all_gather x1, waiting for transfers between devices: 45.9 us -> 0.01 us  [shards(): wide_rows = lax.all_gather(activations, 'tensor', axis=0, tiled=False)]
    ppermute x2, waiting for transfers between devices: 8.79 us -> 0.01 us  [around(): second = lax.ppermute(above[half:], 'dp', route(turn, -1))]
    ppermute x2, waiting for transfers between devices: 5.94 us -> 12.5 us  [around(): first = lax.ppermute(below[:half], 'dp', route(turn, 1))]
    reduce_scatter x1, waiting for transfers between devices: 51.1 us -> 54.9 us  [shards(): lax.psum_scatter(partial_rows, 'tensor', scatter_dimension=0, tiled=False)]
  transfers between devices with their start and end apart: 18 -> 18, of which waited for: 9 -> 7; matrix products, arithmetic and copies ran while one was open for 1% -> 1% of each run, Pallas kernels for 12% -> 15%
where the time goes in v3:
time: 252 us; the launch traced here: 250 us
  waiting for transfers between devices  134 us (53%)
  starting transfers between devices  43.1 us (17%)
  Pallas kernels  38.7 us (15%)
  local copies, waits for them, and re-layouts  19.8 us (8%)
  between operations  14.4 us (6%)
    reduce_scatter x1, waiting for transfers between devices, shards(): lax.psum_scatter(partial_rows, 'tensor', scatter_dimension=0, tiled=False)  54.9 us
    all_to_all x1, waiting for transfers between devices, shards(): lax.all_to_all(quantized, 'dp', split_axis=0, concat_axis=0, tiled=True)  47.7 us
    unnamed x53, local copies, waits for them, and re-layouts  18.2 us
    ppermute x2, waiting for transfers between devices, around(): below = lax.ppermute(block, 'dp', route(turn, 1))  17.8 us
    pallas_call x1, Pallas kernels, quantize(): pl.pallas_call(quantize_kernel, grid_spec=pltpu.PrefetchScalarGridSpec(nu...  15 us
    pallas_call x1, Pallas kernels, gradient(): pl.pallas_call(gradient_kernel, in_specs=[pl.BlockSpec(memory_space=pltpu...  12.8 us
    ppermute x2, waiting for transfers between devices, around(): first = lax.ppermute(below[:half], 'dp', route(turn, 1))  12.5 us
    ppermute x5, starting transfers between devices, other_core(): lax.ppermute(block, 'dp', [(d, d ^ 1) for d in range(2 * SIDE * SIDE)])  11 us
  transfers between devices with their start and end apart: 18, of which 7 were waited for; matrix products, arithmetic and copies ran while one was open for 1% of the time, Pallas kernels for 15%

profile of v3, /device:TPU:1, one launch (start us, length us, event | category | flops | bytes accessed | tf_op | source)
XLA Modules:
  0.0 250.4 jit_solution(9974618347439349907)
XLA Ops:
  7.2 0.7 all-gather.3.cloned.1.call-update
  7.9 2.2 collective-permute-start
  10.1 1.5 collective-permute-start.1
  11.7 1.1 constant_dynamic-update-slice_fusion.4
  12.7 4.5 %collective-permute-done = bf16[128,1536]{1,0:T(8,128)(2,1)S(1)} collective-permute-done((bf16[128,1536]{1,0:T(8,128)(2,1)}, bf16[128,1536]{1,0:T(8,128)(2,1)S(1)}, u32[]{:S(2)}, u32[]{:S(2)}) %collective-permute-start) | collective-permute-done | bytes 393248 | tf_op jit(solution)/shard_map/ppermute | solution.py:254
  17.3 0.1 collective-permute-start.2
  17.4 2.7 %collective-permute-start.3 = (bf16[64,1536]{1,0:T(8,128)(2,1)S(1)}, bf16[64,1536]{1,0:T(8,128)(2,1)S(1)}, u32[]{:S(2)}, u32[]{:S(2)}) collective-permute-start(bf16[64,1536]{1,0:T(8,128)(2,1)S(1)} %slice.17), channel_id=1, source_target_pairs={{0,192},{8,56},{16,208},{24,8},{32,224},{40,24},{48,240},{56,40},{... | collective-permute-start | bytes 589832 | tf_op jit(solution)/shard_map/ppermute | solution.py:257
  20.2 2.9 %collective-permute-done.2 = bf16[64,1536]{1,0:T(8,128)(2,1)S(1)} collective-permute-done((bf16[64,1536]{1,0:T(8,128)(2,1)S(1)}, bf16[64,1536]{1,0:T(8,128)(2,1)S(1)}, u32[]{:S(2)}, u32[]{:S(2)}) %collective-permute-start.2) | collective-permute-done | bytes 196640 | tf_op jit(solution)/shard_map/ppermute | solution.py:256
  23.2 1.0 collective-permute-start.5
  24.2 1.8 collective-permute-start.7
  25.9 4.9 %collective-permute-start.4 = (bf16[512,1536]{1,0:T(8,128)(2,1)S(1)}, bf16[512,1536]{1,0:T(8,128)(2,1)S(1)}, u32[]{:S(2)}, u32[]{:S(2)}) collective-permute-start(bf16[512,1536]{1,0:T(8,128)(2,1)S(1)} %constant_dynamic-update-slice_fusion.refs_0_), channel_id=1, source_target_pairs={{0,8},{8,0},{16,24},{24,16},{32,40},{40,32},{48,56},{56,48},{64,72... | collective-permute-start | bytes 4718600 | tf_op jit(solution)/shard_map/ppermute | solution.py:262
  30.8 13.3 %collective-permute-done.5.refs_1_.refs_2_ = bf16[512,1536]{1,0:T(8,128)(2,1)S(1)} collective-permute-done((bf16[512,1536]{1,0:T(8,128)(2,1)S(1)}, bf16[512,1536]{1,0:T(8,128)(2,1)S(1)}, u32[]{:S(2)}, u32[]{:S(2)}) %collective-permute-start.5) | collective-permute-done | bytes 1572896 | tf_op jit(solution)/shard_map/ppermute | solution.py:254
  44.1 5.1 %collective-permute-start.6 = (bf16[512,1536]{1,0:T(8,128)(2,1)S(1)}, bf16[512,1536]{1,0:T(8,128)(2,1)S(1)}, u32[]{:S(2)}, u32[]{:S(2)}) collective-permute-start(bf16[512,1536]{1,0:T(8,128)(2,1)S(1)} %collective-permute-done.5.refs_1_.refs_2_), channel_id=1, source_target_pairs={{0,8},{8,0},{16,24},{24,16},{32,40},{40,32},{48,56},{56,48},{64,72... | collective-permute-start | bytes 4718600 | tf_op jit(solution)/shard_map/ppermute | solution.py:262
  49.2 0.1 collective-permute-start.8
  49.3 0.1 slice.18
  49.4 0.1 collective-permute-start.9
  49.5 0.1 slice.19
  49.5 3.3 %collective-permute-start.10 = (bf16[256,1536]{1,0:T(8,128)(2,1)S(1)}, bf16[256,1536]{1,0:T(8,128)(2,1)S(1)}, u32[]{:S(2)}, u32[]{:S(2)}) collective-permute-start(bf16[256,1536]{1,0:T(8,128)(2,1)S(1)} %slice.19), channel_id=1, source_target_pairs={{0,48},{8,200},{16,0},{24,216},{32,16},{40,232},{48,32},{56,248},{... | collective-permute-start | bytes 2359304 | tf_op jit(solution)/shard_map/ppermute | solution.py:257
  52.8 9.6 %collective-permute-done.9.refs_1_.refs_6_ = bf16[256,1536]{1,0:T(8,128)(2,1)S(1)} collective-permute-done((bf16[256,1536]{1,0:T(8,128)(2,1)S(1)}, bf16[256,1536]{1,0:T(8,128)(2,1)S(1)}, u32[]{:S(2)}, u32[]{:S(2)}) %collective-permute-start.9) | collective-permute-done | bytes 786464 | tf_op jit(solution)/shard_map/ppermute | solution.py:256
  62.5 0.6 collective-permute-start.11
  63.1 0.3 collective-permute-start.12
  63.4 1.8 shard_map.68.refs_0_
  65.2 1.8 shard_map.69.refs_0_
  67.1 1.8 shard_map.70.refs_0_
  69.0 1.8 shard_map.71
  70.8 2.0 copy-done
  72.8 0.9 copy-done.18
  73.7 0.9 copy-done.20
  74.6 1.4 dynamic-slice_bitcast_fusion.sources
  76.1 54.9 %reduce-scatter.2.cloned.1.call-done = bf16[1,512,512]{2,1,0:T(8,128)(2,1)} async-done(((bf16[8,512,512]{2,1,0:T(8,128)(2,1)}), bf16[1,512,512]{2,1,0:T(8,128)(2,1)}) %reduce-scatter.2.cloned.1.call-update) | async-done | bytes 524304 | tf_op jit(solution)/shard_map/reduce_scatter | solution.py:335
  131.0 1.9 shard_map.72
  132.9 7.5 %all-to-all-start = ((bf16[32,16,512]{2,1,0:T(8,128)(2,1)}), bf16[32,16,512]{2,1,0:T(8,128)(2,1)S(1)}, u32[]{:S(2)}, u32[]{:S(2)}) async-start(bf16[32,16,512]{2,1,0:T(8,128)(2,1)} %shard_map.72), calls=%async_computation.1 | async-start | bytes 1048576 | tf_op jit(solution)/shard_map/all_to_all | solution.py:339
  140.4 2.2 copy-done.23
  142.6 15.0 %shard_map.73 = (bf16[32,128,512]{2,1,0:T(8,128)(2,1)S(1)}, f32[32,16,512]{2,1,0:T(8,128)S(1)}) custom-call(s32[1]{0:T(128)} %bitcast.3.place, bf16[8,128,2048]{2,1,0:T(8,128)(2,1)S(1)} %bitcast.6, bf16[1024,1024]{1,0:T(8,128)(2,1)S(1)} %copy-done.7), custom_call_target="tpu_custom_call" | custom-call | flops 4294967296 | bytes 8388608 | tf_op jit(solution)/shard_map/pallas_call | solution.py:114
  157.6 2.0 copy-done.2
  159.6 1.0 copy-done.12
  160.6 7.4 %all-to-all-start.2 = ((bf16[32,128,512]{2,1,0:T(8,128)(2,1)}), bf16[32,128,512]{2,1,0:T(8,128)(2,1)}, u32[]{:S(2)}, u32[]{:S(2)}) async-start(bf16[32,128,512]{2,1,0:T(8,128)(2,1)} %copy-done.2), calls=%async_computation.3 | async-start | bytes 8388608 | tf_op jit(solution)/shard_map/all_to_all | solution.py:337
  168.1 1.6 copy-done.8
  169.7 1.2 copy-done.13
  170.9 1.7 shard_map.74
  172.6 47.7 %all-to-all-done.2.quantized_ref = bf16[32,128,512]{2,1,0:T(8,128)(2,1)} async-done(((bf16[32,128,512]{2,1,0:T(8,128)(2,1)}), bf16[32,128,512]{2,1,0:T(8,128)(2,1)}, u32[]{:S(2)}, u32[]{:S(2)}) %all-to-all-start.2) | async-done | bytes 4194336 | tf_op jit(solution)/shard_map/all_to_all | solution.py:337
  220.3 4.4 %all-to-all-start.1 = ((bf16[8,16,2048]{2,1,0:T(8,128)(2,1)}), bf16[8,16,2048]{2,1,0:T(8,128)(2,1)}, u32[]{:S(2)}, u32[]{:S(2)}) async-start(bf16[8,16,2048]{2,1,0:T(8,128)(2,1)} %shard_map.74), calls=%async_computation.2 | async-start | bytes 1048576 | tf_op jit(solution)/shard_map/all_to_all | solution.py:341
  224.7 1.1 copy-done.17
  225.8 1.1 copy-done.19
  227.0 1.1 copy-done.21
  228.1 12.8 %shard_map.75 = f32[512,1536]{1,0:T(8,128)} custom-call(s32[32]{0:T(128)S(1)} %copy-done.22, bf16[32,128,512]{2,1,0:T(8,128)(2,1)} %all-to-all-done.2.quantized_ref, bf16[512,1536]{1,0:T(8,128)(2,1)S(1)} %copy-done.6, bf16[512,1536]{1,0:T(8,128)(2,1)} %copy-done.11, bf16[512,1536]{1,0:T(8,128)(2,1)} %copy-done.3, bf16[512,1536]{1,0:T(8,128)(2,1)} %copy-done.9, ...), custom_call_target="tpu_custom_call" | custom-call | flops 6442450944 | bytes 19922944 | tf_op jit(solution)/shard_map/pallas_call | solution.py:221
  240.9 0.7 all-to-all-done.1
  241.6 1.9 copy.18
  (57 shorter events, 0.3 us)
Async XLA Ops:
  7.2 67.4 %all-gather.3.cloned.1.call-start = ((), (), s32[]{:S(2)}) async-start(), calls=%async_computation.5 | async-start | bytes 4718592 | tf_op jit(solution)/shard_map/all_gather | solution.py:324
  7.9 123.1 %reduce-scatter.2.cloned.1.call-start = ((), (), s32[]{:S(2)}) async-start(), calls=%async_computation.4 | async-start | bytes 4718592 | tf_op jit(solution)/shard_map/reduce_scatter | solution.py:335
  7.9 9.3 %collective-permute-start = (bf16[128,1536]{1,0:T(8,128)(2,1)}, bf16[128,1536]{1,0:T(8,128)(2,1)S(1)}, u32[]{:S(2)}, u32[]{:S(2)}) collective-permute-start(bf16[128,1536]{1,0:T(8,128)(2,1)} %param.7), channel_id=1, source_target_pairs={{0,64},{8,24},{16,80},{24,40},{32,96},{40,56},{48,112},{56,8},{64,... | collective-permute-start | bytes 1179656 | tf_op jit(solution)/shard_map/ppermute | solution.py:254
  10.1 7.2 %collective-permute-start.1 = (bf16[128,1536]{1,0:T(8,128)(2,1)}, bf16[128,1536]{1,0:T(8,128)(2,1)S(1)}, u32[]{:S(2)}, u32[]{:S(2)}) collective-permute-start(bf16[128,1536]{1,0:T(8,128)(2,1)} %param.7), channel_id=1, source_target_pairs={{0,192},{8,56},{16,208},{24,8},{32,224},{40,24},{48,240},{56,40},{... | collective-permute-start | bytes 1179656 | tf_op jit(solution)/shard_map/ppermute | solution.py:255
  17.3 5.8 %collective-permute-start.2 = (bf16[64,1536]{1,0:T(8,128)(2,1)S(1)}, bf16[64,1536]{1,0:T(8,128)(2,1)S(1)}, u32[]{:S(2)}, u32[]{:S(2)}) collective-permute-start(bf16[64,1536]{1,0:T(8,128)(2,1)S(1)} %slice.16), channel_id=1, source_target_pairs={{0,64},{8,24},{16,80},{24,40},{32,96},{40,56},{48,112},{56,8},{64,... | collective-permute-start | bytes 589832 | tf_op jit(solution)/shard_map/ppermute | solution.py:256
  17.4 5.7 %collective-permute-start.3 = (bf16[64,1536]{1,0:T(8,128)(2,1)S(1)}, bf16[64,1536]{1,0:T(8,128)(2,1)S(1)}, u32[]{:S(2)}, u32[]{:S(2)}) collective-permute-start(bf16[64,1536]{1,0:T(8,128)(2,1)S(1)} %slice.17), channel_id=1, source_target_pairs={{0,192},{8,56},{16,208},{24,8},{32,224},{40,24},{48,240},{56,40},{... | collective-permute-start | bytes 589832 | tf_op jit(solution)/shard_map/ppermute | solution.py:257
  23.1 40.2 %copy-start.5 = (bf16[512,1536]{1,0:T(8,128)(2,1)}, bf16[512,1536]{1,0:T(8,128)(2,1)S(1)}, u32[]{:S(2)}) copy-start(bf16[512,1536]{1,0:T(8,128)(2,1)S(1)} %constant_dynamic-update-slice_fusion.refs_0_) | copy-start | bytes 4718596
  23.1 40.2 %copy-start.1 = (bf16[512,1536]{1,0:T(8,128)(2,1)S(1)}, bf16[512,1536]{1,0:T(8,128)(2,1)}, u32[]{:S(2)}) copy-start(bf16[512,1536]{1,0:T(8,128)(2,1)} %refs_5_.1) | copy-start | bytes 4718596
  23.2 21.0 %collective-permute-start.5 = (bf16[512,1536]{1,0:T(8,128)(2,1)S(1)}, bf16[512,1536]{1,0:T(8,128)(2,1)S(1)}, u32[]{:S(2)}, u32[]{:S(2)}) collective-permute-start(bf16[512,1536]{1,0:T(8,128)(2,1)S(1)} %constant_dynamic-update-slice_fusion.refs_0_), channel_id=1, source_target_pairs={{0,16},{8,72},{16,32},{24,88},{32,48},{40,104},{48,0},{56,120},{64... | collective-permute-start | bytes 4718600 | tf_op jit(solution)/shard_map/ppermute | solution.py:254
  24.2 25.1 %collective-permute-start.7 = (bf16[512,1536]{1,0:T(8,128)(2,1)S(1)}, bf16[512,1536]{1,0:T(8,128)(2,1)S(1)}, u32[]{:S(2)}, u32[]{:S(2)}) collective-permute-start(bf16[512,1536]{1,0:T(8,128)(2,1)S(1)} %constant_dynamic-update-slice_fusion.refs_0_), channel_id=1, source_target_pairs={{0,48},{8,200},{16,0},{24,216},{32,16},{40,232},{48,32},{56,248},{... | collective-permute-start | bytes 4718600 | tf_op jit(solution)/shard_map/ppermute | solution.py:255
  25.9 37.4 %collective-permute-start.4 = (bf16[512,1536]{1,0:T(8,128)(2,1)S(1)}, bf16[512,1536]{1,0:T(8,128)(2,1)S(1)}, u32[]{:S(2)}, u32[]{:S(2)}) collective-permute-start(bf16[512,1536]{1,0:T(8,128)(2,1)S(1)} %constant_dynamic-update-slice_fusion.refs_0_), channel_id=1, source_target_pairs={{0,8},{8,0},{16,24},{24,16},{32,40},{40,32},{48,56},{56,48},{64,72... | collective-permute-start | bytes 4718600 | tf_op jit(solution)/shard_map/ppermute | solution.py:262
  44.1 21.1 %copy-start.3 = (bf16[512,1536]{1,0:T(8,128)(2,1)}, bf16[512,1536]{1,0:T(8,128)(2,1)S(1)}, u32[]{:S(2)}) copy-start(bf16[512,1536]{1,0:T(8,128)(2,1)S(1)} %collective-permute-done.5.refs_1_.refs_2_) | copy-start | bytes 4718596
  44.1 21.1 %collective-permute-start.6 = (bf16[512,1536]{1,0:T(8,128)(2,1)S(1)}, bf16[512,1536]{1,0:T(8,128)(2,1)S(1)}, u32[]{:S(2)}, u32[]{:S(2)}) collective-permute-start(bf16[512,1536]{1,0:T(8,128)(2,1)S(1)} %collective-permute-done.5.refs_1_.refs_2_), channel_id=1, source_target_pairs={{0,8},{8,0},{16,24},{24,16},{32,40},{40,32},{48,56},{56,48},{64,72... | collective-permute-start | bytes 4718600 | tf_op jit(solution)/shard_map/ppermute | solution.py:262
  49.2 17.9 %copy-start.4 = (bf16[512,1536]{1,0:T(8,128)(2,1)}, bf16[512,1536]{1,0:T(8,128)(2,1)S(1)}, u32[]{:S(2)}) copy-start(bf16[512,1536]{1,0:T(8,128)(2,1)S(1)} %collective-permute-done.7.refs_1_.refs_4_) | copy-start | bytes 4718596
  49.2 17.9 %collective-permute-start.8 = (bf16[512,1536]{1,0:T(8,128)(2,1)S(1)}, bf16[512,1536]{1,0:T(8,128)(2,1)S(1)}, u32[]{:S(2)}, u32[]{:S(2)}) collective-permute-start(bf16[512,1536]{1,0:T(8,128)(2,1)S(1)} %collective-permute-done.7.refs_1_.refs_4_), channel_id=1, source_target_pairs={{0,8},{8,0},{16,24},{24,16},{32,40},{40,32},{48,56},{56,48},{64,72... | collective-permute-start | bytes 4718600 | tf_op jit(solution)/shard_map/ppermute | solution.py:262
  49.4 13.1 %collective-permute-start.9 = (bf16[256,1536]{1,0:T(8,128)(2,1)S(1)}, bf16[256,1536]{1,0:T(8,128)(2,1)S(1)}, u32[]{:S(2)}, u32[]{:S(2)}) collective-permute-start(bf16[256,1536]{1,0:T(8,128)(2,1)S(1)} %slice.18), channel_id=1, source_target_pairs={{0,16},{8,72},{16,32},{24,88},{32,48},{40,104},{48,0},{56,120},{64... | collective-permute-start | bytes 2359304 | tf_op jit(solution)/shard_map/ppermute | solution.py:256
  49.5 13.5 %collective-permute-start.10 = (bf16[256,1536]{1,0:T(8,128)(2,1)S(1)}, bf16[256,1536]{1,0:T(8,128)(2,1)S(1)}, u32[]{:S(2)}, u32[]{:S(2)}) collective-permute-start(bf16[256,1536]{1,0:T(8,128)(2,1)S(1)} %slice.19), channel_id=1, source_target_pairs={{0,48},{8,200},{16,0},{24,216},{32,16},{40,232},{48,32},{56,248},{... | collective-permute-start | bytes 2359304 | tf_op jit(solution)/shard_map/ppermute | solution.py:257
  62.5 6.5 %copy-start.14 = (bf16[256,1536]{1,0:T(8,128)(2,1)}, bf16[256,1536]{1,0:T(8,128)(2,1)S(1)}, u32[]{:S(2)}) copy-start(bf16[256,1536]{1,0:T(8,128)(2,1)S(1)} %collective-permute-done.9.refs_1_.refs_6_) | copy-start | bytes 2359300
  62.5 6.5 %collective-permute-start.11 = (bf16[256,1536]{1,0:T(8,128)(2,1)S(1)}, bf16[256,1536]{1,0:T(8,128)(2,1)S(1)}, u32[]{:S(2)}, u32[]{:S(2)}) collective-permute-start(bf16[256,1536]{1,0:T(8,128)(2,1)S(1)} %collective-permute-done.9.refs_1_.refs_6_), channel_id=1, source_target_pairs={{0,8},{8,0},{16,24},{24,16},{32,40},{40,32},{48,56},{56,48},{64,72... | collective-permute-start | bytes 2359304 | tf_op jit(solution)/shard_map/ppermute | solution.py:262
  63.1 5.9 %copy-start.16 = (bf16[256,1536]{1,0:T(8,128)(2,1)}, bf16[256,1536]{1,0:T(8,128)(2,1)S(1)}, u32[]{:S(2)}) copy-start(bf16[256,1536]{1,0:T(8,128)(2,1)S(1)} %collective-permute-done.10.refs_2_.refs_7_) | copy-start | bytes 2359300
  63.1 5.9 %collective-permute-start.12 = (bf16[256,1536]{1,0:T(8,128)(2,1)S(1)}, bf16[256,1536]{1,0:T(8,128)(2,1)S(1)}, u32[]{:S(2)}, u32[]{:S(2)}) collective-permute-start(bf16[256,1536]{1,0:T(8,128)(2,1)S(1)} %collective-permute-done.10.refs_2_.refs_7_), channel_id=1, source_target_pairs={{0,8},{8,0},{16,24},{24,16},{32,40},{40,32},{48,56},{56,48},{64,72... | collective-permute-start | bytes 2359304 | tf_op jit(solution)/shard_map/ppermute | solution.py:262
  63.4 1.8 copy-start.11
  65.2 1.8 copy-start.9
  67.1 1.8 copy-start.10
  70.8 2.0 copy-start
  72.8 0.9 copy-start.18
  73.7 0.9 copy-start.20
  74.6 65.8 %copy-start.7 = (bf16[1024,1024]{1,0:T(8,128)(2,1)S(1)}, bf16[1024,1024]{1,0:T(8,128)(2,1)}, u32[]{:S(2)}) copy-start(bf16[1024,1024]{1,0:T(8,128)(2,1)} %constant.18.clone.table_ref) | copy-start | bytes 6291460
  132.9 27.7 %all-to-all-start = ((bf16[32,16,512]{2,1,0:T(8,128)(2,1)}), bf16[32,16,512]{2,1,0:T(8,128)(2,1)S(1)}, u32[]{:S(2)}, u32[]{:S(2)}) async-start(bf16[32,16,512]{2,1,0:T(8,128)(2,1)} %shard_map.72), calls=%async_computation.1 | async-start | bytes 1048576 | tf_op jit(solution)/shard_map/all_to_all | solution.py:339
  140.4 2.2 copy-start.23
  157.6 2.0 copy-start.2
  159.6 1.0 copy-start.12
  160.6 59.7 %all-to-all-start.2 = ((bf16[32,128,512]{2,1,0:T(8,128)(2,1)}), bf16[32,128,512]{2,1,0:T(8,128)(2,1)}, u32[]{:S(2)}, u32[]{:S(2)}) async-start(bf16[32,128,512]{2,1,0:T(8,128)(2,1)} %copy-done.2), calls=%async_computation.3 | async-start | bytes 8388608 | tf_op jit(solution)/shard_map/all_to_all | solution.py:337
  168.1 1.6 copy-start.8
  169.7 1.2 copy-start.13
  170.9 53.8 %copy-start.6 = (bf16[512,1536]{1,0:T(8,128)(2,1)S(1)}, bf16[512,1536]{1,0:T(8,128)(2,1)}, u32[]{:S(2)}) copy-start(bf16[512,1536]{1,0:T(8,128)(2,1)} %copy-done.5) | copy-start | bytes 4718596
  170.9 53.8 %copy-start.15 = (bf16[256,1536]{1,0:T(8,128)(2,1)S(1)}, bf16[256,1536]{1,0:T(8,128)(2,1)}, u32[]{:S(2)}) copy-start(bf16[256,1536]{1,0:T(8,128)(2,1)} %copy-done.14) | copy-start | bytes 2359300
  170.9 53.8 %copy-start.22 = (s32[32]{0:T(128)S(1)}, s32[32]{0:T(128)}, u32[]{:S(2)}) copy-start(s32[32]{0:T(128)} %dynamic-slice_bitcast_fusion.sources) | copy-start | bytes 388
  220.3 21.3 %all-to-all-start.1 = ((bf16[8,16,2048]{2,1,0:T(8,128)(2,1)}), bf16[8,16,2048]{2,1,0:T(8,128)(2,1)}, u32[]{:S(2)}, u32[]{:S(2)}) async-start(bf16[8,16,2048]{2,1,0:T(8,128)(2,1)} %shard_map.74), calls=%async_computation.2 | async-start | bytes 1048576 | tf_op jit(solution)/shard_map/all_to_all | solution.py:341
  224.7 1.1 copy-start.17
  225.8 1.1 copy-start.19
  227.0 1.1 copy-start.21
Sparse Core Ops, SparseCore 0:
  9.8 58.6 all-gather.2
  74.7 56.2 reduce-scatter.1

commit v4 on v3

--- a/solution.py
+++ b/solution.py
@@ -10,8 +10,9 @@
 
 BLOCK = 1024
 WIDTH = 16384
-BLOCKS = WIDTH // BLOCK
+TABLE = 256
 LANES = 128
+VMEM_BYTES = 60 * 1024 * 1024
 NORM = 1.0 / math.sqrt(WIDTH)
 SIDE = 4
 PIECES = 4
@@ -37,8 +38,8 @@
     return [float(c) for c in scaled.convert(kind=np.polynomial.Polynomial).coef]
 
 
-SINE = fit(True, 8)
-COSINE = fit(False, 9)
+SINE = fit(True, 6)
+COSINE = fit(False, 7)
 
 
 def horner(coefficients, square):
@@ -62,78 +63,94 @@
 
 
 def quantize_kernel(place, rows_ref, table_ref, quantized_ref, slope_ref, inner, mixed):
-    tokens = rows_ref.shape[1]
-    per_shard = rows_ref.shape[2] // BLOCK
-    stacked = jnp.concatenate(
-        [
-            rows_ref[b // per_shard, :, (b % per_shard) * BLOCK : (b % per_shard + 1) * BLOCK]
-            for b in range(BLOCKS)
-        ],
-        axis=0,
-    )
-    inner[...] = jnp.dot(stacked, table_ref[...], preferred_element_type=jnp.float32)
-    largest = jnp.zeros((tokens, LANES), jnp.float32)
-    for chunk in range(BLOCK // LANES):
-        lanes = slice(chunk * LANES, (chunk + 1) * LANES)
-        parts = butterfly([inner[b * tokens : (b + 1) * tokens, lanes] for b in range(BLOCKS)])
-        for b in range(BLOCKS):
-            value = parts[b] * NORM
-            mixed[b * tokens : (b + 1) * tokens, lanes] = value
-            largest = jnp.maximum(largest, jnp.abs(value))
-    peak = jnp.max(largest, axis=1, keepdims=True)
-    scale = (peak + epsilon) / levels
-    inverse = 1.0 / scale
-    depth = (ripple / (2.0 * math.pi)) * scale
-    width = quantized_ref.shape[2]
-    per_block = BLOCK // width
-
-    def remainder(value):
-        turns = value * inverse
-        return turns - jnp.round(turns)
-
-    for b in range(BLOCKS):
-        value = mixed[b * tokens : (b + 1) * tokens, :]
-        rest = remainder(value)
-        sine = rest * horner(SINE, rest * rest)
-        result = (value - depth * sine).astype(jnp.bfloat16)
-        for k in range(per_block):
-            quantized_ref[b * per_block + k] = result[:, k * width : (k + 1) * width]
-
-    @pl.when(pl.program_id(0) == place[0])
-    def _():
-        for b in range(BLOCKS):
-            rest = remainder(mixed[b * tokens : (b + 1) * tokens, :])
-            slope = 1.0 - ripple * horner(COSINE, rest * rest)
-            for k in range(per_block):
-                slope_ref[b * per_block + k] = slope[:, k * width : (k + 1) * width]
+    members, count, features = rows_ref.shape
+    step, width = slope_ref.shape[1:]
+    chunks, per_shard, per_width = features // TABLE, features // width, width // TABLE
+    rows = rows_ref[...].reshape(members * count, features)
+    for c in range(chunks):
+        inner[c] = jnp.dot(
+            rows[:, c * TABLE : (c + 1) * TABLE],
+            table_ref[...],
+            preferred_element_type=jnp.float32,
+        )
+    halves = [slice(l * LANES, (l + 1) * LANES) for l in range(TABLE // LANES)]
+    for group in range(count // step):
+        spans = [
+            slice(t * count + group * step, t * count + (group + 1) * step)
+            for t in range(members)
+        ]
+        here = slice(group * step, (group + 1) * step)
+        for span in spans:
+            for lanes in halves:
+                parts = butterfly([inner[c, span, lanes] for c in range(chunks)])
+                for c in range(chunks):
+                    inner[c, span, lanes] = parts[c]
+        largest = jnp.zeros((step, LANES), jnp.float32)
+        for c in range(chunks):
+            for lanes in halves:
+                parts = butterfly([inner[c, span, lanes] for span in spans])
+                for span, part in zip(spans, parts):
+                    mixed[c, span, lanes] = part
+                    largest = jnp.maximum(largest, jnp.abs(part))
+        peak = jnp.max(largest, axis=1, keepdims=True) * NORM
+        scale = (peak + epsilon) / levels
+        inverse = jnp.broadcast_to(NORM / scale, (step, LANES))
+        depth = jnp.broadcast_to((ripple / (2.0 * math.pi)) * scale, (step, LANES))
+
+        def remainder(value):
+            turns = value * inverse
+            return turns - jnp.round(turns)
+
+        def places():
+            for t, span in enumerate(spans):
+                for c in range(chunks):
+                    for l, lanes in enumerate(halves):
+                        start = (c % per_width) * TABLE + l * LANES
+                        yield t * per_shard + c // per_width, start, mixed[c, span, lanes]
+
+        for block, start, value in places():
+            rest = remainder(value)
+            sine = rest * horner(SINE, rest * rest)
+            quantized_ref[block, here, start : start + LANES] = (
+                value * NORM - depth * sine
+            ).astype(jnp.bfloat16)
+
+        @pl.when(pl.program_id(0) * (count // step) + group == place[0])
+        def _():
+            for block, start, value in places():
+                rest = remainder(value)
+                slope_ref[block, :, start : start + LANES] = 1.0 - ripple * horner(
+                    COSINE, rest * rest
+                )
 
 
 def quantize(rows, table, place, dp, width):
-    shards, tokens, features = rows.shape
-    step = tokens // shards
+    members, tokens, features = rows.shape
+    step = tokens // members
+    count = 2 * step
     return pl.pallas_call(
         quantize_kernel,
         grid_spec=pltpu.PrefetchScalarGridSpec(
             num_scalar_prefetch=1,
-            grid=(shards,),
+            grid=(tokens // count,),
             in_specs=[
-                pl.BlockSpec((shards, step, features), lambda i, place: (0, i, 0)),
-                pl.BlockSpec((BLOCK, BLOCK), lambda i, place: (0, 0)),
+                pl.BlockSpec((members, count, features), lambda i, place: (0, i, 0)),
+                pl.BlockSpec((TABLE, TABLE), lambda i, place: (0, 0)),
             ],
             out_specs=[
-                pl.BlockSpec((dp, step, width), lambda i, place: (0, i, 0)),
+                pl.BlockSpec((dp, count, width), lambda i, place: (0, i, 0)),
                 pl.BlockSpec((dp, step, width), lambda i, place: (0, 0, 0)),
             ],
             scratch_shapes=[
-                pltpu.VMEM((BLOCKS * step, BLOCK), jnp.float32),
-                pltpu.VMEM((BLOCKS * step, BLOCK), jnp.float32),
+                pltpu.VMEM((features // TABLE, members * count, TABLE), jnp.float32),
+                pltpu.VMEM((features // TABLE, members * count, TABLE), jnp.float32),
             ],
         ),
         out_shape=[
             jax.ShapeDtypeStruct((dp, tokens, width), jnp.bfloat16),
             jax.ShapeDtypeStruct((dp, step, width), jnp.float32),
         ],
-        compiler_params=pltpu.CompilerParams(vmem_limit_bytes=32 * 1024 * 1024),
+        compiler_params=pltpu.CompilerParams(vmem_limit_bytes=VMEM_BYTES),
         cost_estimate=pl.CostEstimate(
             flops=2 * tokens * WIDTH * BLOCK, bytes_accessed=4 * tokens * WIDTH, transcendentals=0
         ),
@@ -172,7 +189,7 @@
         out_specs=pl.BlockSpec((members, rows // members, width), lambda i: (0, position, 0)),
         out_shape=jax.ShapeDtypeStruct((members, 4 * rows // members, width), jnp.bfloat16),
         input_output_aliases={0: 0} if earlier else {},
-        compiler_params=pltpu.CompilerParams(vmem_limit_bytes=32 * 1024 * 1024),
+        compiler_params=pltpu.CompilerParams(vmem_limit_bytes=VMEM_BYTES),
         cost_estimate=pl.CostEstimate(
             flops=2 * rows * depth * width,
             bytes_accessed=2 * rows * (depth + width),
@@ -195,6 +212,7 @@
         ],
         out_specs=pl.BlockSpec(memory_space=pltpu.VMEM),
         out_shape=jax.ShapeDtypeStruct(rows.shape, rows.dtype),
+        compiler_params=pltpu.CompilerParams(vmem_limit_bytes=VMEM_BYTES),
     )(sources, rows)
 
 
@@ -224,7 +242,7 @@
         + [pl.BlockSpec(memory_space=pltpu.VMEM)] * (len(pieces) + 1),
         out_specs=pl.BlockSpec(memory_space=pltpu.VMEM),
         out_shape=jax.ShapeDtypeStruct((width, depth), jnp.float32),
-        compiler_params=pltpu.CompilerParams(vmem_limit_bytes=48 * 1024 * 1024),
+        compiler_params=pltpu.CompilerParams(vmem_limit_bytes=VMEM_BYTES),
         cost_estimate=pl.CostEstimate(
             flops=2 * rows * depth * width,
             bytes_accessed=2 * rows * (depth + width) + 4 * width * depth,
@@ -249,13 +267,17 @@
     return pairs
 
 
-def around(block, turn):
-    half = block.shape[0] // 2
+def hops(block, turn):
     below = lax.ppermute(block, "dp", route(turn, 1))
     above = lax.ppermute(block, "dp", route(turn, -1))
+    return below, above
+
+
+def far_hops(below, above, turn):
+    half = below.shape[0] // 2
     first = lax.ppermute(below[:half], "dp", route(turn, 1))
     second = lax.ppermute(above[half:], "dp", route(turn, -1))
-    return below, above, first, second
+    return first, second
 
 
 def other_core(block):
@@ -278,37 +300,43 @@
 
 
 def finish_kernel(summed_ref, slope_ref, table_ref, out_ref, inner):
-    tokens, width = summed_ref.shape[1:]
-    per_block = BLOCK // width
-    per_shard = out_ref.shape[2] // BLOCK
+    devices, step, width = summed_ref.shape
+    members, per_width = out_ref.shape[0], width // TABLE
+    per_shard = devices // members
     upstream = (summed_ref[...].astype(jnp.float32) * slope_ref[...]).astype(jnp.bfloat16)
-    stacked = jnp.concatenate(
-        [
-            jnp.concatenate([upstream[b * per_block + k] for k in range(per_block)], axis=1)
-            for b in range(BLOCKS)
-        ],
-        axis=0,
-    )
-    inner[...] = jnp.dot(stacked, table_ref[...], preferred_element_type=jnp.float32)
-    for chunk in range(BLOCK // LANES):
-        lanes = slice(chunk * LANES, (chunk + 1) * LANES)
-        parts = butterfly([inner[b * tokens : (b + 1) * tokens, lanes] for b in range(BLOCKS)])
-        for b in range(BLOCKS):
-            start = (b % per_shard) * BLOCK + chunk * LANES
-            out_ref[b // per_shard, :, start : start + LANES] = (parts[b] * NORM).astype(
-                out_ref.dtype
-            )
-
-
-def finish(summed, slope, table, shards):
-    devices, tokens, width = summed.shape
+    upstream = upstream.reshape(devices * step, width)
+    for c in range(per_width):
+        inner[c] = jnp.dot(
+            upstream[:, c * TABLE : (c + 1) * TABLE],
+            table_ref[...],
+            preferred_element_type=jnp.float32,
+        )
+    span = lambda d: slice(d * step, (d + 1) * step)
+    for l in range(TABLE // LANES):
+        lanes = slice(l * LANES, (l + 1) * LANES)
+        for t in range(members):
+            near = [(c, span(t * per_shard + k)) for k in range(per_shard) for c in range(per_width)]
+            parts = butterfly([inner[c, rows, lanes] for c, rows in near])
+            for (c, rows), part in zip(near, parts):
+                inner[c, rows, lanes] = part
+        for k in range(per_shard):
+            for c in range(per_width):
+                far = [span(t * per_shard + k) for t in range(members)]
+                parts = butterfly([inner[c, rows, lanes] for rows in far])
+                start = (k * per_width + c) * TABLE + l * LANES
+                for t in range(members):
+                    out_ref[t, :, start : start + LANES] = (parts[t] * NORM).astype(out_ref.dtype)
+
+
+def finish(summed, slope, table, members):
+    devices, step, width = summed.shape
     return pl.pallas_call(
         finish_kernel,
-        out_shape=jax.ShapeDtypeStruct((shards, tokens, WIDTH // shards), jnp.bfloat16),
-        scratch_shapes=[pltpu.VMEM((BLOCKS * tokens, BLOCK), jnp.float32)],
-        compiler_params=pltpu.CompilerParams(vmem_limit_bytes=32 * 1024 * 1024),
+        out_shape=jax.ShapeDtypeStruct((members, step, WIDTH // members), jnp.bfloat16),
+        scratch_shapes=[pltpu.VMEM((width // TABLE, devices * step, TABLE), jnp.float32)],
+        compiler_params=pltpu.CompilerParams(vmem_limit_bytes=VMEM_BYTES),
         cost_estimate=pl.CostEstimate(
-            flops=2 * tokens * WIDTH * BLOCK, bytes_accessed=8 * tokens * WIDTH, transcendentals=0
+            flops=2 * step * WIDTH * BLOCK, bytes_accessed=8 * step * WIDTH, transcendentals=0
         ),
     )(summed, slope, table)
 
@@ -320,26 +348,32 @@
     width = weight.shape[0]
     place = lax.axis_index("tensor").astype(jnp.int32).reshape(1)
     sources = jnp.asarray(sources_table())[lax.axis_index("dp")]
-    table = hadamard_table(BLOCK)
+    table = hadamard_table(TABLE)
     wide_rows = lax.all_gather(activations, "tensor", axis=0, tiled=False)
-    near = jnp.concatenate([grad_out, *around(grad_out, 0)], axis=0)
-    below, above, first, second = around(near, 1)
-    groups = []
-    for block in (near, below, above):
-        groups.append([block, other_core(block)])
-    groups.append([first, second, other_core(first), other_core(second)])
-    partial_rows = None
-    for position, group in enumerate(groups):
-        partial_rows = product(partial_rows, group, weight, position, members)
+    below, above = hops(grad_out, 0)
+    near = jnp.concatenate([grad_out, below, above, *far_hops(below, above, 0)], axis=0)
+    below, above = hops(near, 1)
+    near_pair = [near, other_core(near)]
+    partial_rows = product(None, near_pair, weight, 0, members)
+    below, above, partial_rows = lax.optimization_barrier((below, above, partial_rows))
+    first, second = far_hops(below, above, 1)
+    below_pair = [below, other_core(below)]
+    above_pair = [above, other_core(above)]
+    partial_rows = product(partial_rows, below_pair, weight, 1, members)
+    partial_rows = product(partial_rows, above_pair, weight, 2, members)
+    first, second, partial_rows = lax.optimization_barrier((first, second, partial_rows))
+    far_pair = [first, second, other_core(first), other_core(second)]
+    partial_rows = product(partial_rows, far_pair, weight, 3, members)
     partial_rows, wide_rows = lax.optimization_barrier((partial_rows, wide_rows))
     summed = lax.psum_scatter(partial_rows, "tensor", scatter_dimension=0, tiled=False)
     quantized, slope = quantize(wide_rows, table, place, dp, width)
     q_block = lax.all_to_all(quantized, "dp", split_axis=0, concat_axis=0, tiled=True)
+    summed, q_block = lax.optimization_barrier((summed, q_block))
     ordered = order(summed.reshape(dp, tokens // members, width), sources)
     homed = lax.all_to_all(ordered, "dp", split_axis=0, concat_axis=0, tiled=True)
     mixed = finish(homed, slope, table, members)
     grad_input = lax.all_to_all(mixed, "tensor", split_axis=0, concat_axis=0, tiled=True)
-    weight_sum = gradient(sources, q_block, [block for group in groups for block in group])
+    weight_sum = gradient(sources, q_block, near_pair + below_pair + above_pair + far_pair)
     return (grad_input.reshape(tokens, features), weight_sum)
 
 

time: 252 us -> 206 us (0.82)
  waiting for transfers between devices: 134 us -> 77.1 us
  blocking collectives: 0 us -> 18.8 us
  Pallas kernels: 38.7 us -> 53.3 us
  starting transfers between devices: 43.1 us -> 32.8 us
  local copies, waits for them, and re-layouts: 19.8 us -> 9.83 us
    reduce_scatter x1, waiting for transfers between devices: 54.9 us -> 0.01 us  [shards(): lax.psum_scatter(partial_rows, 'tensor', scatter_dimension=0, tiled=False)]
    all_to_all x0 -> x1, blocking collectives: none -> 18.8 us  [shards(): lax.all_to_all(ordered, 'dp', split_axis=0, concat_axis=0, tiled=True)]
    pallas_call x4, Pallas kernels: 7.28 us -> 20.9 us  [product(): pl.pallas_call(product_kernel, grid=(1,), in_specs=[pl.BlockSpec(memory_s...]
    ppermute x8, waiting for transfers between devices: 30.3 us -> 17.6 us  [the longest x2 16.3 us: hops(): below = lax.ppermute(block, 'dp', route(turn, 1))]
    unnamed x53 -> x15, local copies, waits for them, and re-layouts: 18.2 us -> 5.89 us
    all_to_all x1 -> x0, starting transfers between devices: 7.48 us -> none  [shards(): lax.all_to_all(ordered, 'dp', split_axis=0, concat_axis=0, tiled=True)]
    ppermute x5, starting transfers between devices: 11 us -> 6.97 us  [other_core(): lax.ppermute(block, 'dp', [(d, d ^ 1) for d in range(2 * SIDE * SIDE)])]
    ppermute x5, waiting for transfers between devices: 0.01 us -> 3.85 us  [other_core(): lax.ppermute(block, 'dp', [(d, d ^ 1) for d in range(2 * SIDE * SIDE)])]
  transfers between devices with their start and end apart: 18 -> 17, of which waited for: 7 -> 8; matrix products, arithmetic and copies ran while one was open for 1% -> 4% of each run, Pallas kernels for 15% -> 24%
where the time goes in v4:
time: 206 us
  waiting for transfers between devices  77.1 us (37%)
  Pallas kernels  53.3 us (26%)
  starting transfers between devices  32.8 us (16%)
  blocking collectives  18.8 us (9%)
  between operations  14.1 us (7%)
  local copies, waits for them, and re-layouts  9.83 us (5%)
    all_to_all x1, waiting for transfers between devices, shards(): lax.all_to_all(quantized, 'dp', split_axis=0, concat_axis=0, tiled=True)  51 us
    pallas_call x4, Pallas kernels, product(): pl.pallas_call(product_kernel, grid=(1,), in_specs=[pl.BlockSpec(memory_s...  20.9 us
    all_to_all x1, blocking collectives, shards(): lax.all_to_all(ordered, 'dp', split_axis=0, concat_axis=0, tiled=True)  18.8 us
    ppermute x2, waiting for transfers between devices, hops(): below = lax.ppermute(block, 'dp', route(turn, 1))  16.3 us
    pallas_call x1, Pallas kernels, gradient(): pl.pallas_call(gradient_kernel, in_specs=[pl.BlockSpec(memory_space=pltpu...  14.2 us
    pallas_call x1, Pallas kernels, quantize(): pl.pallas_call(quantize_kernel, grid_spec=pltpu.PrefetchScalarGridSpec(nu...  13.6 us
    all_to_all x1, starting transfers between devices, shards(): lax.all_to_all(quantized, 'dp', split_axis=0, concat_axis=0, tiled=True)  7.35 us
    ppermute x5, starting transfers between devices, other_core(): lax.ppermute(block, 'dp', [(d, d ^ 1) for d in range(2 * SIDE * SIDE)])  6.97 us
  transfers between devices with their start and end apart: 17, of which 8 were waited for; matrix products, arithmetic and copies ran while one was open for 4% of the time, Pallas kernels for 24%

profile of v4, /device:TPU:1, one launch (start us, length us, event | category | flops | bytes accessed | tf_op | source)
XLA Modules:
  0.0 205.9 jit_solution(9407002857462574408)
XLA Ops:
  7.2 0.0 all-gather.3.cloned.1.call-start
  7.2 0.7 all-gather.3.cloned.1.call-update
  7.9 0.0 reduce-scatter.2.cloned.1.call-start
  7.9 2.2 %collective-permute-start = (bf16[128,1536]{1,0:T(8,128)(2,1)}, bf16[128,1536]{1,0:T(8,128)(2,1)S(1)}, u32[]{:S(2)}, u32[]{:S(2)}) collective-permute-start(bf16[128,1536]{1,0:T(8,128)(2,1)} %param.7), channel_id=1, source_target_pairs={{0,64},{8,24},{16,80},{24,40},{32,96},{40,56},{48,112},{56,8},{64,... | collective-permute-start | bytes 1179656 | tf_op jit(solution)/shard_map/ppermute | solution.py:271
  10.1 1.5 collective-permute-start.1
  11.7 1.8 constant_dynamic-update-slice_fusion.4
  13.5 3.8 %collective-permute-done = bf16[128,1536]{1,0:T(8,128)(2,1)S(1)} collective-permute-done((bf16[128,1536]{1,0:T(8,128)(2,1)}, bf16[128,1536]{1,0:T(8,128)(2,1)S(1)}, u32[]{:S(2)}, u32[]{:S(2)}) %collective-permute-start) | collective-permute-done | bytes 393248 | tf_op jit(solution)/shard_map/ppermute | solution.py:271
  17.3 0.1 collective-permute-start.2
  17.4 0.0 collective-permute-done.1
  17.4 2.7 %collective-permute-start.3 = (bf16[64,1536]{1,0:T(8,128)(2,1)S(1)}, bf16[64,1536]{1,0:T(8,128)(2,1)S(1)}, u32[]{:S(2)}, u32[]{:S(2)}) collective-permute-start(bf16[64,1536]{1,0:T(8,128)(2,1)S(1)} %slice.17), channel_id=1, source_target_pairs={{0,192},{8,56},{16,208},{24,8},{32,224},{40,24},{48,240},{56,40},{... | collective-permute-start | bytes 589832 | tf_op jit(solution)/shard_map/ppermute | solution.py:279
  20.1 0.8 constant_dynamic-update-slice_fusion.3
  20.9 0.8 constant_dynamic-update-slice_fusion.2
  21.7 1.4 collective-permute-done.2
  23.1 0.7 constant_dynamic-update-slice_fusion.1
  23.8 0.0 collective-permute-done.3
  23.8 0.7 constant_dynamic-update-slice_fusion.refs_0_
  24.5 4.4 %collective-permute-start.6 = (bf16[512,1536]{1,0:T(8,128)(2,1)}, bf16[512,1536]{1,0:T(8,128)(2,1)}, u32[]{:S(2)}, u32[]{:S(2)}) collective-permute-start(bf16[512,1536]{1,0:T(8,128)(2,1)} %constant_dynamic-update-slice_fusion.refs_0_), channel_id=1, source_target_pairs={{0,8},{8,0},{16,24},{24,16},{32,40},{40,32},{48,56},{56,48},{64,72... | collective-permute-start | bytes 4718600 | tf_op jit(solution)/shard_map/ppermute | solution.py:284
  28.8 2.7 %collective-permute-start.5 = (bf16[512,1536]{1,0:T(8,128)(2,1)}, bf16[512,1536]{1,0:T(8,128)(2,1)S(1)}, u32[]{:S(2)}, u32[]{:S(2)}) collective-permute-start(bf16[512,1536]{1,0:T(8,128)(2,1)} %constant_dynamic-update-slice_fusion.refs_0_), channel_id=1, source_target_pairs={{0,48},{8,200},{16,0},{24,216},{32,16},{40,232},{48,32},{56,248},{... | collective-permute-start | bytes 4718600 | tf_op jit(solution)/shard_map/ppermute | solution.py:272
  31.5 0.7 collective-permute-done.6.refs_1_
  32.2 5.2 %shard_map.68.refs_0_ = bf16[8,512,512]{2,1,0:T(8,128)(2,1)} custom-call(bf16[512,1536]{1,0:T(8,128)(2,1)} %constant_dynamic-update-slice_fusion.refs_0_, bf16[512,1536]{1,0:T(8,128)(2,1)} %collective-permute-done.6.refs_1_, bf16[512,1536]{1,0:T(8,128)(2,1)} %refs_5_.1), custom_call_target="tpu_custom_call" | custom-call | flops 1610612736 | bytes 4194304 | tf_op jit(solution)/shard_map/pallas_call | solution.py:185
  37.4 12.5 %collective-permute-done.4.refs_1_.refs_2_ = bf16[512,1536]{1,0:T(8,128)(2,1)S(1)} collective-permute-done((bf16[512,1536]{1,0:T(8,128)(2,1)}, bf16[512,1536]{1,0:T(8,128)(2,1)S(1)}, u32[]{:S(2)}, u32[]{:S(2)}) %collective-permute-start.4) | collective-permute-done | bytes 1572896 | tf_op jit(solution)/shard_map/ppermute | solution.py:271
  49.9 0.0 collective-permute-done.5.refs_1_.refs_4_
  49.9 0.8 collective-permute-start.9
  50.8 0.1 collective-permute-start.10
  50.9 1.0 slice.14
  51.8 1.0 slice.15
  52.9 0.1 collective-permute-start.7
  53.0 2.6 %collective-permute-start.8 = (bf16[256,1536]{1,0:T(8,128)(2,1)}, bf16[256,1536]{1,0:T(8,128)(2,1)}, u32[]{:S(2)}, u32[]{:S(2)}) collective-permute-start(bf16[256,1536]{1,0:T(8,128)(2,1)} %slice.15), channel_id=1, source_target_pairs={{0,48},{8,200},{16,0},{24,216},{32,16},{40,232},{48,32},{56,248},{... | collective-permute-start | bytes 2359304 | tf_op jit(solution)/shard_map/ppermute | solution.py:279
  55.5 5.2 %shard_map.69.refs_0_ = bf16[8,512,512]{2,1,0:T(8,128)(2,1)} custom-call(bf16[8,512,512]{2,1,0:T(8,128)(2,1)} %shard_map.68.refs_0_, bf16[512,1536]{1,0:T(8,128)(2,1)} %copy-done, bf16[512,1536]{1,0:T(8,128)(2,1)} %collective-permute-done.9.refs_2_.refs_3_, bf16[512,1536]{1,0:T(8,128)(2,1)} %refs_5_.1), custom_call_target="tpu_custom_call", output_to_operand_aliasing={{}: (0, {})} | custom-call | flops 1610612736 | bytes 4194304 | tf_op jit(solution)/shard_map/pallas_call | solution.py:185
  60.8 5.2 %shard_map.70.refs_0_ = bf16[8,512,512]{2,1,0:T(8,128)(2,1)} custom-call(bf16[8,512,512]{2,1,0:T(8,128)(2,1)} %shard_map.69.refs_0_, bf16[512,1536]{1,0:T(8,128)(2,1)} %copy-done.1, bf16[512,1536]{1,0:T(8,128)(2,1)} %collective-permute-done.10.refs_2_.refs_5_, bf16[512,1536]{1,0:T(8,128)(2,1)} %refs_5_.1), custom_call_target="tpu_custom_call", output_to_operand_aliasing={{}: (0, {})} | custom-call | flops 1610612736 | bytes 4194304 | tf_op jit(solution)/shard_map/pallas_call | solution.py:185
  66.0 1.6 collective-permute-start.11
  67.6 0.1 collective-permute-start.12
  67.7 1.9 collective-permute-done.11.refs_3_.refs_8_
  69.7 1.2 collective-permute-done.12.refs_4_.refs_9_
  70.9 1.0 copy-done.4
  71.9 5.3 %shard_map.71 = bf16[8,512,512]{2,1,0:T(8,128)(2,1)} custom-call(bf16[8,512,512]{2,1,0:T(8,128)(2,1)} %shard_map.70.refs_0_, bf16[256,1536]{1,0:T(8,128)(2,1)} %copy-done.2, bf16[256,1536]{1,0:T(8,128)(2,1)} %collective-permute-done.8.refs_2_.refs_7_, bf16[256,1536]{1,0:T(8,128)(2,1)} %copy-done.3, ...), custom_call_target="tpu_custom_call", output_to_operand_aliasing={{}: (0, {})} | custom-call | flops 1610612736 | bytes 4194304 | tf_op jit(solution)/shard_map/pallas_call | solution.py:185
  77.1 0.0 reduce-scatter.2.cloned.1.call-update
  77.2 13.6 %shard_map.72 = (bf16[32,128,512]{2,1,0:T(8,128)(2,1)}, f32[32,16,512]{2,1,0:T(8,128)}) custom-call(s32[1]{0:T(128)} %bitcast.3.place, bf16[8,128,2048]{2,1,0:T(8,128)(2,1)} %bitcast.9, bf16[256,256]{1,0:T(8,128)(2,1)} %constant.18.clone.table_ref), custom_call_target="tpu_custom_call" | custom-call | flops 4294967296 | bytes 8388608 | tf_op jit(solution)/shard_map/pallas_call | solution.py:131
  90.8 7.3 %all-to-all-start = ((bf16[32,128,512]{2,1,0:T(8,128)(2,1)}), bf16[32,128,512]{2,1,0:T(8,128)(2,1)}, u32[]{:S(2)}, u32[]{:S(2)}) async-start(bf16[32,128,512]{2,1,0:T(8,128)(2,1)} %get-tuple-element.22), calls=%async_computation.1 | async-start | bytes 8388608 | tf_op jit(solution)/shard_map/all_to_all | solution.py:370
  98.1 1.2 dynamic-slice_bitcast_fusion.sources
  99.4 51.0 %all-to-all-done.quantized_ref = bf16[32,128,512]{2,1,0:T(8,128)(2,1)} async-done(((bf16[32,128,512]{2,1,0:T(8,128)(2,1)}), bf16[32,128,512]{2,1,0:T(8,128)(2,1)}, u32[]{:S(2)}, u32[]{:S(2)}) %all-to-all-start) | async-done | bytes 4194336 | tf_op jit(solution)/shard_map/all_to_all | solution.py:370
  150.4 1.9 shard_map.73
  152.2 18.8 %all_to_all.15.summed_ref = bf16[32,16,512]{2,1,0:T(8,128)(2,1)} all-to-all(bf16[32,16,512]{2,1,0:T(8,128)(2,1)} %shard_map.73), channel_id=1, replica_groups=mesh['dp'=32,'tensor'=8] {'dp'}, dimensions={0} | all-to-all | bytes 1048576 | tf_op jit(solution)/shard_map/all_to_all | solution.py:373
  171.1 2.7 %shard_map.74 = bf16[8,16,2048]{2,1,0:T(8,128)(2,1)} custom-call(bf16[32,16,512]{2,1,0:T(8,128)(2,1)} %all_to_all.15.summed_ref, f32[32,16,512]{2,1,0:T(8,128)} %get-tuple-element.24.slope_ref, bf16[256,256]{1,0:T(8,128)(2,1)} %constant.18.clone.table_ref), custom_call_target="tpu_custom_call" | custom-call | flops 536870912 | bytes 2097152 | tf_op jit(solution)/shard_map/pallas_call | solution.py:333
  173.7 6.5 %all-to-all-start.2 = ((bf16[8,16,2048]{2,1,0:T(8,128)(2,1)}), bf16[8,16,2048]{2,1,0:T(8,128)(2,1)S(1)}, u32[]{:S(2)}, u32[]{:S(2)}) async-start(bf16[8,16,2048]{2,1,0:T(8,128)(2,1)} %shard_map.74), calls=%async_computation.3 | async-start | bytes 1048576 | tf_op jit(solution)/shard_map/all_to_all | solution.py:375
  180.2 14.2 %shard_map.75 = f32[512,1536]{1,0:T(8,128)} custom-call(s32[32]{0:T(128)} %dynamic-slice_bitcast_fusion.sources, bf16[32,128,512]{2,1,0:T(8,128)(2,1)} %all-to-all-done.quantized_ref, bf16[512,1536]{1,0:T(8,128)(2,1)} %constant_dynamic-update-slice_fusion.refs_0_, bf16[512,1536]{1,0:T(8,128)(2,1)} %collective-permute-done.6.refs_1_, ...), custom_call_target="tpu_custom_call" | custom-call | flops 6442450944 | bytes 19922944 | tf_op jit(solution)/shard_map/pallas_call | solution.py:239
  194.4 3.9 %all-to-all-done.2 = bf16[8,16,2048]{2,1,0:T(8,128)(2,1)S(1)} async-done(((bf16[8,16,2048]{2,1,0:T(8,128)(2,1)}), bf16[8,16,2048]{2,1,0:T(8,128)(2,1)S(1)}, u32[]{:S(2)}, u32[]{:S(2)}) %all-to-all-start.2) | async-done | bytes 524320 | tf_op jit(solution)/shard_map/all_to_all | solution.py:375
  198.3 0.8 copy.18
  (18 shorter events, 0.1 us)
Async XLA Ops:
  7.2 70.0 %all-gather.3.cloned.1.call-start = ((), (), s32[]{:S(2)}) async-start(), calls=%async_computation.5 | async-start | bytes 4718592 | tf_op jit(solution)/shard_map/all_gather | solution.py:352
  7.9 142.5 %reduce-scatter.2.cloned.1.call-start = ((), (), s32[]{:S(2)}) async-start(), calls=%async_computation.4 | async-start | bytes 4718592 | tf_op jit(solution)/shard_map/reduce_scatter | solution.py:368
  7.9 9.3 %collective-permute-start = (bf16[128,1536]{1,0:T(8,128)(2,1)}, bf16[128,1536]{1,0:T(8,128)(2,1)S(1)}, u32[]{:S(2)}, u32[]{:S(2)}) collective-permute-start(bf16[128,1536]{1,0:T(8,128)(2,1)} %param.7), channel_id=1, source_target_pairs={{0,64},{8,24},{16,80},{24,40},{32,96},{40,56},{48,112},{56,8},{64,... | collective-permute-start | bytes 1179656 | tf_op jit(solution)/shard_map/ppermute | solution.py:271
  10.1 7.2 %collective-permute-start.1 = (bf16[128,1536]{1,0:T(8,128)(2,1)}, bf16[128,1536]{1,0:T(8,128)(2,1)S(1)}, u32[]{:S(2)}, u32[]{:S(2)}) collective-permute-start(bf16[128,1536]{1,0:T(8,128)(2,1)} %param.7), channel_id=1, source_target_pairs={{0,192},{8,56},{16,208},{24,8},{32,224},{40,24},{48,240},{56,40},{... | collective-permute-start | bytes 1179656 | tf_op jit(solution)/shard_map/ppermute | solution.py:272
  17.3 5.8 %collective-permute-start.2 = (bf16[64,1536]{1,0:T(8,128)(2,1)S(1)}, bf16[64,1536]{1,0:T(8,128)(2,1)S(1)}, u32[]{:S(2)}, u32[]{:S(2)}) collective-permute-start(bf16[64,1536]{1,0:T(8,128)(2,1)S(1)} %slice.16), channel_id=1, source_target_pairs={{0,64},{8,24},{16,80},{24,40},{32,96},{40,56},{48,112},{56,8},{64,... | collective-permute-start | bytes 589832 | tf_op jit(solution)/shard_map/ppermute | solution.py:278
  17.4 6.4 %collective-permute-start.3 = (bf16[64,1536]{1,0:T(8,128)(2,1)S(1)}, bf16[64,1536]{1,0:T(8,128)(2,1)S(1)}, u32[]{:S(2)}, u32[]{:S(2)}) collective-permute-start(bf16[64,1536]{1,0:T(8,128)(2,1)S(1)} %slice.17), channel_id=1, source_target_pairs={{0,192},{8,56},{16,208},{24,8},{32,224},{40,24},{48,240},{56,40},{... | collective-permute-start | bytes 589832 | tf_op jit(solution)/shard_map/ppermute | solution.py:279
  24.5 7.7 %collective-permute-start.6 = (bf16[512,1536]{1,0:T(8,128)(2,1)}, bf16[512,1536]{1,0:T(8,128)(2,1)}, u32[]{:S(2)}, u32[]{:S(2)}) collective-permute-start(bf16[512,1536]{1,0:T(8,128)(2,1)} %constant_dynamic-update-slice_fusion.refs_0_), channel_id=1, source_target_pairs={{0,8},{8,0},{16,24},{24,16},{32,40},{40,32},{48,56},{56,48},{64,72... | collective-permute-start | bytes 4718600 | tf_op jit(solution)/shard_map/ppermute | solution.py:284
  28.8 21.1 %collective-permute-start.4 = (bf16[512,1536]{1,0:T(8,128)(2,1)}, bf16[512,1536]{1,0:T(8,128)(2,1)S(1)}, u32[]{:S(2)}, u32[]{:S(2)}) collective-permute-start(bf16[512,1536]{1,0:T(8,128)(2,1)} %constant_dynamic-update-slice_fusion.refs_0_), channel_id=1, source_target_pairs={{0,16},{8,72},{16,32},{24,88},{32,48},{40,104},{48,0},{56,120},{64... | collective-permute-start | bytes 4718600 | tf_op jit(solution)/shard_map/ppermute | solution.py:271
  28.8 21.1 %collective-permute-start.5 = (bf16[512,1536]{1,0:T(8,128)(2,1)}, bf16[512,1536]{1,0:T(8,128)(2,1)S(1)}, u32[]{:S(2)}, u32[]{:S(2)}) collective-permute-start(bf16[512,1536]{1,0:T(8,128)(2,1)} %constant_dynamic-update-slice_fusion.refs_0_), channel_id=1, source_target_pairs={{0,48},{8,200},{16,0},{24,216},{32,16},{40,232},{48,32},{56,248},{... | collective-permute-start | bytes 4718600 | tf_op jit(solution)/shard_map/ppermute | solution.py:272
  49.9 3.0 %copy-start = (bf16[512,1536]{1,0:T(8,128)(2,1)}, bf16[512,1536]{1,0:T(8,128)(2,1)S(1)}, u32[]{:S(2)}) copy-start(bf16[512,1536]{1,0:T(8,128)(2,1)S(1)} %collective-permute-done.4.refs_1_.refs_2_) | copy-start | bytes 4718596
  49.9 2.9 %copy-start.1 = (bf16[512,1536]{1,0:T(8,128)(2,1)}, bf16[512,1536]{1,0:T(8,128)(2,1)S(1)}, u32[]{:S(2)}) copy-start(bf16[512,1536]{1,0:T(8,128)(2,1)S(1)} %collective-permute-done.5.refs_1_.refs_4_) | copy-start | bytes 4718596
  49.9 5.6 %collective-permute-start.9 = (bf16[512,1536]{1,0:T(8,128)(2,1)S(1)}, bf16[512,1536]{1,0:T(8,128)(2,1)}, u32[]{:S(2)}, u32[]{:S(2)}) collective-permute-start(bf16[512,1536]{1,0:T(8,128)(2,1)S(1)} %collective-permute-done.4.refs_1_.refs_2_), channel_id=1, source_target_pairs={{0,8},{8,0},{16,24},{24,16},{32,40},{40,32},{48,56},{56,48},{64,72... | collective-permute-start | bytes 4718600 | tf_op jit(solution)/shard_map/ppermute | solution.py:284
  50.8 10.0 %collective-permute-start.10 = (bf16[512,1536]{1,0:T(8,128)(2,1)S(1)}, bf16[512,1536]{1,0:T(8,128)(2,1)}, u32[]{:S(2)}, u32[]{:S(2)}) collective-permute-start(bf16[512,1536]{1,0:T(8,128)(2,1)S(1)} %collective-permute-done.5.refs_1_.refs_4_), channel_id=1, source_target_pairs={{0,8},{8,0},{16,24},{24,16},{32,40},{40,32},{48,56},{56,48},{64,72... | collective-permute-start | bytes 4718600 | tf_op jit(solution)/shard_map/ppermute | solution.py:284
  52.9 13.2 %collective-permute-start.7 = (bf16[256,1536]{1,0:T(8,128)(2,1)}, bf16[256,1536]{1,0:T(8,128)(2,1)S(1)}, u32[]{:S(2)}, u32[]{:S(2)}) collective-permute-start(bf16[256,1536]{1,0:T(8,128)(2,1)} %slice.14), channel_id=1, source_target_pairs={{0,16},{8,72},{16,32},{24,88},{32,48},{40,104},{48,0},{56,120},{64... | collective-permute-start | bytes 2359304 | tf_op jit(solution)/shard_map/ppermute | solution.py:278
  53.0 13.0 %collective-permute-start.8 = (bf16[256,1536]{1,0:T(8,128)(2,1)}, bf16[256,1536]{1,0:T(8,128)(2,1)}, u32[]{:S(2)}, u32[]{:S(2)}) collective-permute-start(bf16[256,1536]{1,0:T(8,128)(2,1)} %slice.15), channel_id=1, source_target_pairs={{0,48},{8,200},{16,0},{24,216},{32,16},{40,232},{48,32},{56,248},{... | collective-permute-start | bytes 2359304 | tf_op jit(solution)/shard_map/ppermute | solution.py:279
  66.0 4.8 %copy-start.2 = (bf16[256,1536]{1,0:T(8,128)(2,1)}, bf16[256,1536]{1,0:T(8,128)(2,1)S(1)}, u32[]{:S(2)}) copy-start(bf16[256,1536]{1,0:T(8,128)(2,1)S(1)} %collective-permute-done.7.refs_1_.refs_6_) | copy-start | bytes 2359300
  66.0 3.6 %collective-permute-start.11 = (bf16[256,1536]{1,0:T(8,128)(2,1)S(1)}, bf16[256,1536]{1,0:T(8,128)(2,1)S(1)}, u32[]{:S(2)}, u32[]{:S(2)}) collective-permute-start(bf16[256,1536]{1,0:T(8,128)(2,1)S(1)} %collective-permute-done.7.refs_1_.refs_6_), channel_id=1, source_target_pairs={{0,8},{8,0},{16,24},{24,16},{32,40},{40,32},{48,56},{56,48},{64,72... | collective-permute-start | bytes 2359304 | tf_op jit(solution)/shard_map/ppermute | solution.py:284
  67.6 3.2 %collective-permute-start.12 = (bf16[256,1536]{1,0:T(8,128)(2,1)}, bf16[256,1536]{1,0:T(8,128)(2,1)S(1)}, u32[]{:S(2)}, u32[]{:S(2)}) collective-permute-start(bf16[256,1536]{1,0:T(8,128)(2,1)} %collective-permute-done.8.refs_2_.refs_7_), channel_id=1, source_target_pairs={{0,8},{8,0},{16,24},{24,16},{32,40},{40,32},{48,56},{56,48},{64,72... | collective-permute-start | bytes 2359304 | tf_op jit(solution)/shard_map/ppermute | solution.py:284
  69.7 1.2 copy-start.3
  70.9 1.0 copy-start.4
  90.8 59.6 %all-to-all-start = ((bf16[32,128,512]{2,1,0:T(8,128)(2,1)}), bf16[32,128,512]{2,1,0:T(8,128)(2,1)}, u32[]{:S(2)}, u32[]{:S(2)}) async-start(bf16[32,128,512]{2,1,0:T(8,128)(2,1)} %get-tuple-element.22), calls=%async_computation.1 | async-start | bytes 8388608 | tf_op jit(solution)/shard_map/all_to_all | solution.py:370
  173.7 24.5 %all-to-all-start.2 = ((bf16[8,16,2048]{2,1,0:T(8,128)(2,1)}), bf16[8,16,2048]{2,1,0:T(8,128)(2,1)S(1)}, u32[]{:S(2)}, u32[]{:S(2)}) async-start(bf16[8,16,2048]{2,1,0:T(8,128)(2,1)} %shard_map.74), calls=%async_computation.3 | async-start | bytes 1048576 | tf_op jit(solution)/shard_map/all_to_all | solution.py:375
Sparse Core Ops, SparseCore 0:
  9.8 58.6 all-gather.2
  77.3 56.1 reduce-scatter.1

commit v5 on v4

--- a/solution.py
+++ b/solution.py
@@ -17,6 +17,7 @@
 SIDE = 4
 PIECES = 4
 OFFSETS = (0, -1, 1, -2)
+RING = (0, 1, 2, -1)
 
 levels = 127.0
 ripple = 0.5
@@ -62,7 +63,9 @@
     return parts
 
 
-def quantize_kernel(place, rows_ref, table_ref, quantized_ref, slope_ref, inner, mixed):
+def quantize_kernel(
+    place, targets, rows_ref, table_ref, stay_ref, up_ref, down_ref, slope_ref, inner, mixed
+):
     members, count, features = rows_ref.shape
     step, width = slope_ref.shape[1:]
     chunks, per_shard, per_width = features // TABLE, features // width, width // TABLE
@@ -89,8 +92,8 @@
         for c in range(chunks):
             for lanes in halves:
                 parts = butterfly([inner[c, span, lanes] for span in spans])
-                for span, part in zip(spans, parts):
-                    mixed[c, span, lanes] = part
+                for t, part in enumerate(parts):
+                    mixed[c, t, here, lanes] = part
                     largest = jnp.maximum(largest, jnp.abs(part))
         peak = jnp.max(largest, axis=1, keepdims=True) * NORM
         scale = (peak + epsilon) / levels
@@ -101,60 +104,62 @@
             turns = value * inverse
             return turns - jnp.round(turns)
 
-        def places():
-            for t, span in enumerate(spans):
+        sent = [
+            (ref, slot) for ref in (stay_ref, up_ref, down_ref) for slot in range(ref.shape[0])
+        ]
+        for number, (ref, slot) in enumerate(sent):
+            block = targets[number]
+            t, c = block // per_shard, block % per_shard * per_width
+            for k in range(per_width):
+                for l, lanes in enumerate(halves):
+                    value = mixed[c + k, t, here, lanes]
+                    rest = remainder(value)
+                    sine = rest * horner(SINE, rest * rest)
+                    start = k * TABLE + l * LANES
+                    ref[slot, here, start : start + LANES] = (
+                        value * NORM - depth * sine
+                    ).astype(jnp.bfloat16)
+
+        @pl.when(pl.program_id(0) * (count // step) + group == place[0])
+        def _():
+            for t in range(members):
                 for c in range(chunks):
                     for l, lanes in enumerate(halves):
+                        rest = remainder(mixed[c, t, here, lanes])
                         start = (c % per_width) * TABLE + l * LANES
-                        yield t * per_shard + c // per_width, start, mixed[c, span, lanes]
-
-        for block, start, value in places():
-            rest = remainder(value)
-            sine = rest * horner(SINE, rest * rest)
-            quantized_ref[block, here, start : start + LANES] = (
-                value * NORM - depth * sine
-            ).astype(jnp.bfloat16)
-
-        @pl.when(pl.program_id(0) * (count // step) + group == place[0])
-        def _():
-            for block, start, value in places():
-                rest = remainder(value)
-                slope_ref[block, :, start : start + LANES] = 1.0 - ripple * horner(
-                    COSINE, rest * rest
-                )
-
-
-def quantize(rows, table, place, dp, width):
+                        slope_ref[t * per_shard + c // per_width, :, start : start + LANES] = (
+                            1.0 - ripple * horner(COSINE, rest * rest)
+                        )
+
+
+def quantize(rows, table, place, targets, dp, width):
     members, tokens, features = rows.shape
     step = tokens // members
     count = 2 * step
+    sizes = (dp // SIDE, dp * 3 // (2 * SIDE), dp * 3 // (2 * SIDE))
     return pl.pallas_call(
         quantize_kernel,
         grid_spec=pltpu.PrefetchScalarGridSpec(
-            num_scalar_prefetch=1,
+            num_scalar_prefetch=2,
             grid=(tokens // count,),
             in_specs=[
-                pl.BlockSpec((members, count, features), lambda i, place: (0, i, 0)),
-                pl.BlockSpec((TABLE, TABLE), lambda i, place: (0, 0)),
+                pl.BlockSpec((members, count, features), lambda i, *_: (0, i, 0)),
+                pl.BlockSpec((TABLE, TABLE), lambda i, *_: (0, 0)),
             ],
-            out_specs=[
-                pl.BlockSpec((dp, count, width), lambda i, place: (0, i, 0)),
-                pl.BlockSpec((dp, step, width), lambda i, place: (0, 0, 0)),
-            ],
+            out_specs=[pl.BlockSpec((n, count, width), lambda i, *_: (0, i, 0)) for n in sizes]
+            + [pl.BlockSpec((dp, step, width), lambda i, *_: (0, 0, 0))],
             scratch_shapes=[
                 pltpu.VMEM((features // TABLE, members * count, TABLE), jnp.float32),
-                pltpu.VMEM((features // TABLE, members * count, TABLE), jnp.float32),
+                pltpu.VMEM((features // TABLE, members, count, TABLE), jnp.float32),
             ],
         ),
-        out_shape=[
-            jax.ShapeDtypeStruct((dp, tokens, width), jnp.bfloat16),
-            jax.ShapeDtypeStruct((dp, step, width), jnp.float32),
-        ],
+        out_shape=[jax.ShapeDtypeStruct((n, tokens, width), jnp.bfloat16) for n in sizes]
+        + [jax.ShapeDtypeStruct((dp, step, width), jnp.float32)],
         compiler_params=pltpu.CompilerParams(vmem_limit_bytes=VMEM_BYTES),
         cost_estimate=pl.CostEstimate(
             flops=2 * tokens * WIDTH * BLOCK, bytes_accessed=4 * tokens * WIDTH, transcendentals=0
         ),
-    )(place, rows, table)
+    )(place, targets, rows, table)
 
 
 def product_kernel(*refs):
@@ -216,30 +221,32 @@
     )(sources, rows)
 
 
-def gradient_kernel(sources, quantized_ref, *refs):
+def gradient_kernel(*refs):
     out_ref = refs[-1]
-    pieces = refs[:-1]
+    quantized_ref = refs[-2]
+    pieces = [ref for ref in refs[:-2] if ref.dtype == quantized_ref.dtype]
+    held = [ref for ref in refs[:-2] if ref.dtype != quantized_ref.dtype]
     tokens = quantized_ref.shape[1]
+    total = held[0][...] if held else None
     slot = 0
-    for number, piece_ref in enumerate(pieces):
+    for piece_ref in pieces:
         count = piece_ref.shape[0] // tokens
-        block = jnp.concatenate(
-            [quantized_ref[sources[slot + k]] for k in range(count)], axis=0
-        )
+        block = quantized_ref[slot : slot + count].reshape(count * tokens, quantized_ref.shape[2])
         slot += count
         term = lax.dot_general(
             block, piece_ref[...], (((0,), (0,)), ((), ())), preferred_element_type=jnp.float32
         )
-        out_ref[...] = term if number == 0 else out_ref[...] + term
-
-
-def gradient(sources, quantized, pieces):
+        total = term if total is None else total + term
+    out_ref[...] = total
+
+
+def gradient(held, quantized, pieces):
     width, depth = quantized.shape[2], pieces[0].shape[1]
     rows = sum(piece.shape[0] for piece in pieces)
+    earlier = [] if held is None else [held]
     return pl.pallas_call(
         gradient_kernel,
-        in_specs=[pl.BlockSpec(memory_space=pltpu.SMEM)]
-        + [pl.BlockSpec(memory_space=pltpu.VMEM)] * (len(pieces) + 1),
+        in_specs=[pl.BlockSpec(memory_space=pltpu.VMEM)] * (len(earlier) + len(pieces) + 1),
         out_specs=pl.BlockSpec(memory_space=pltpu.VMEM),
         out_shape=jax.ShapeDtypeStruct((width, depth), jnp.float32),
         compiler_params=pltpu.CompilerParams(vmem_limit_bytes=VMEM_BYTES),
@@ -248,7 +255,7 @@
             bytes_accessed=2 * rows * (depth + width) + 4 * width * depth,
             transcendentals=0,
         ),
-    )(sources, quantized, *pieces)
+    )(*earlier, *pieces, quantized)
 
 
 def chip_core(x, y, core):
@@ -297,6 +304,34 @@
                             found.append(chip_core(x + along[0], y + along[1], sender))
                 table.append(found)
     return np.asarray(table, np.int32)
+
+
+def targets_table():
+    table = []
+    for x in range(SIDE):
+        for y in range(SIDE):
+            for core in range(2):
+                def block(first, second, swap):
+                    along = (first, second) if core == 0 else (second, first)
+                    return chip_core(x + along[0], y + along[1], core ^ swap)
+
+                pairs = [(0, s) for s in RING] + [(1, s) for s in RING]
+                pairs += [(2, s) for s in RING] + [(-1, s) for s in RING]
+                table.append([block(p, s, swap) for p, s in pairs for swap in range(2)])
+    return np.asarray(table, np.int32)
+
+
+def spread_once(up, down, turn):
+    below = lax.ppermute(up, "dp", route(turn, 1))
+    above = lax.ppermute(down, "dp", route(turn, -1))
+    return below, above
+
+
+def spread_far(below, above, turn):
+    half = below.shape[0] // 3
+    first = lax.ppermute(below[2 * half :], "dp", route(turn, 1))
+    second = lax.ppermute(above[:half], "dp", route(turn, -1))
+    return first, second
 
 
 def finish_kernel(summed_ref, slope_ref, table_ref, out_ref, inner):
@@ -348,6 +383,7 @@
     width = weight.shape[0]
     place = lax.axis_index("tensor").astype(jnp.int32).reshape(1)
     sources = jnp.asarray(sources_table())[lax.axis_index("dp")]
+    targets = jnp.asarray(targets_table())[lax.axis_index("dp")]
     table = hadamard_table(TABLE)
     wide_rows = lax.all_gather(activations, "tensor", axis=0, tiled=False)
     below, above = hops(grad_out, 0)
@@ -366,14 +402,27 @@
     partial_rows = product(partial_rows, far_pair, weight, 3, members)
     partial_rows, wide_rows = lax.optimization_barrier((partial_rows, wide_rows))
     summed = lax.psum_scatter(partial_rows, "tensor", scatter_dimension=0, tiled=False)
-    quantized, slope = quantize(wide_rows, table, place, dp, width)
-    q_block = lax.all_to_all(quantized, "dp", split_axis=0, concat_axis=0, tiled=True)
-    summed, q_block = lax.optimization_barrier((summed, q_block))
+    stay, up, down, slope = quantize(wide_rows, table, place, targets, dp, width)
+    below, above = spread_once(up, down, 0)
+    first, second = spread_far(below, above, 0)
+    lines = [stay, below[:8], above[4:], jnp.concatenate([first, second], axis=0)]
+    up = jnp.concatenate([line[2:4] for line in lines] + [lines[0][4:6], lines[1][4:6]], axis=0)
+    down = jnp.concatenate([lines[2][4:6], lines[3][4:6]] + [line[6:] for line in lines], axis=0)
+    below, above = spread_once(up, down, 1)
     ordered = order(summed.reshape(dp, tokens // members, width), sources)
     homed = lax.all_to_all(ordered, "dp", split_axis=0, concat_axis=0, tiled=True)
+    below, above, homed = lax.optimization_barrier((below, above, homed))
+    first, second = spread_far(below, above, 1)
     mixed = finish(homed, slope, table, members)
     grad_input = lax.all_to_all(mixed, "tensor", split_axis=0, concat_axis=0, tiled=True)
-    weight_sum = gradient(sources, q_block, near_pair + below_pair + above_pair + far_pair)
+    arrived = jnp.concatenate(
+        [line[:2] for line in lines] + [below[:8], above[4:], first, second], axis=0
+    ).reshape(dp // 2, 2, tokens, width)
+    crossed = other_core(arrived[:, 1])
+    own = [near_pair[0], below_pair[0], above_pair[0], *far_pair[:2]]
+    other = [near_pair[1], below_pair[1], above_pair[1], *far_pair[2:]]
+    weight_sum = gradient(None, arrived[:, 0], own)
+    weight_sum = gradient(weight_sum, crossed, other)
     return (grad_input.reshape(tokens, features), weight_sum)
 
 

time: 206 us -> 231 us (1.12)
  local copies, waits for them, and re-layouts: 9.83 us -> 36.2 us
  blocking collectives: 18.8 us -> 0 us
  starting transfers between devices: 32.8 us -> 44.3 us
  Pallas kernels: 53.3 us -> 57.8 us
    all_to_all x1, waiting for transfers between devices: 51 us -> 3.72 us  [shards(): lax.all_to_all(ordered, 'dp', split_axis=0, concat_axis=0, tiled=True)]
    ppermute x0 -> x8, waiting for transfers between devices: none -> 40.9 us  [the longest x2 21.5 us: spread_once(): above = lax.ppermute(down, 'dp', route(turn, -1))]
    all_to_all x1 -> x0, blocking collectives: 18.8 us -> none  [shards(): lax.all_to_all(ordered, 'dp', split_axis=0, concat_axis=0, tiled=True)]
    unnamed x15 -> x37, local copies, waits for them, and re-layouts: 5.89 us -> 21.6 us
    ppermute x0 -> x8, starting transfers between devices: none -> 11.6 us  [the longest x2 7.25 us: spread_far(): second = lax.ppermute(above[:half], 'dp', route(turn, -1))]
    ppermute x2, waiting for transfers between devices: 0.01 us -> 10.4 us  [hops(): above = lax.ppermute(block, 'dp', route(turn, -1))]
    ppermute x2, waiting for transfers between devices: 16.3 us -> 6.05 us  [hops(): below = lax.ppermute(block, 'dp', route(turn, 1))]
    squeeze x0 -> x2, local copies, waits for them, and re-layouts: none -> 5.91 us  [the longest x1 4.72 us: shards(): crossed = other_core(arrived[:, 1])]
  transfers between devices with their start and end apart: 17 -> 26, of which waited for: 8 -> 15; matrix products, arithmetic and copies ran while one was open for 4% -> 9% of each run, Pallas kernels for 24% -> 21%
where the time goes in v5:
time: 231 us
  waiting for transfers between devices  78.2 us (34%)
  Pallas kernels  57.8 us (25%)
  starting transfers between devices  44.3 us (19%)
  local copies, waits for them, and re-layouts  36.2 us (16%)
  between operations  14.1 us (6%)
    unnamed x37, local copies, waits for them, and re-layouts  21.6 us
    ppermute x2, waiting for transfers between devices, spread_once(): above = lax.ppermute(down, 'dp', route(turn, -1))  21.5 us
    pallas_call x4, Pallas kernels, product(): pl.pallas_call(product_kernel, grid=(1,), in_specs=[pl.BlockSpec(memory_s...  20.8 us
    pallas_call x2, Pallas kernels, gradient(): pl.pallas_call(gradient_kernel, in_specs=[pl.BlockSpec(memory_space=pltpu...  18.1 us
    pallas_call x1, Pallas kernels, quantize(): pl.pallas_call(quantize_kernel, grid_spec=pltpu.PrefetchScalarGridSpec(nu...  14.4 us
    ppermute x2, waiting for transfers between devices, hops(): above = lax.ppermute(block, 'dp', route(turn, -1))  10.4 us
    all_to_all x1, waiting for transfers between devices, shards(): lax.all_to_all(mixed, 'tensor', split_axis=0, concat_axis=0, tiled=True)  9.37 us
    all_to_all x1, starting transfers between devices, shards(): lax.all_to_all(ordered, 'dp', split_axis=0, concat_axis=0, tiled=True)  8.27 us
  transfers between devices with their start and end apart: 26, of which 15 were waited for; matrix products, arithmetic and copies ran while one was open for 9% of the time, Pallas kernels for 21%

profile of v5, /device:TPU:1, one launch (start us, length us, event | category | flops | bytes accessed | tf_op | source)
XLA Modules:
  0.0 230.6 jit_solution(8513819736617939928)
XLA Ops:
  7.9 2.2 collective-permute-start
  10.1 1.5 collective-permute-start.1
  11.7 1.8 constant_dynamic-update-slice_fusion.4
  13.5 3.8 %collective-permute-done = bf16[128,1536]{1,0:T(8,128)(2,1)S(1)} collective-permute-done((bf16[128,1536]{1,0:T(8,128)(2,1)}, bf16[128,1536]{1,0:T(8,128)(2,1)S(1)}, u32[]{:S(2)}, u32[]{:S(2)}) %collective-permute-start) | collective-permute-done | bytes 393248 | tf_op jit(solution)/shard_map/ppermute | solution.py:278
  17.4 2.7 %collective-permute-start.3 = (bf16[64,1536]{1,0:T(8,128)(2,1)S(1)}, bf16[64,1536]{1,0:T(8,128)(2,1)S(1)}, u32[]{:S(2)}, u32[]{:S(2)}) collective-permute-start(bf16[64,1536]{1,0:T(8,128)(2,1)S(1)} %slice.123), channel_id=1, source_target_pairs={{0,192},{8,56},{16,208},{24,8},{32,224},{40,24},{48,240},{56,40},{... | collective-permute-start | bytes 589832 | tf_op jit(solution)/shard_map/ppermute | solution.py:286
  21.7 1.4 collective-permute-done.2
  24.5 4.4 %collective-permute-start.6 = (bf16[512,1536]{1,0:T(8,128)(2,1)}, bf16[512,1536]{1,0:T(8,128)(2,1)S(1)}, u32[]{:S(2)}, u32[]{:S(2)}) collective-permute-start(bf16[512,1536]{1,0:T(8,128)(2,1)} %constant_dynamic-update-slice_fusion.refs_0_), channel_id=1, source_target_pairs={{0,8},{8,0},{16,24},{24,16},{32,40},{40,32},{48,56},{56,48},{64,72... | collective-permute-start | bytes 4718600 | tf_op jit(solution)/shard_map/ppermute | solution.py:291
  28.8 2.4 %collective-permute-start.5 = (bf16[512,1536]{1,0:T(8,128)(2,1)}, bf16[512,1536]{1,0:T(8,128)(2,1)S(1)}, u32[]{:S(2)}, u32[]{:S(2)}) collective-permute-start(bf16[512,1536]{1,0:T(8,128)(2,1)} %constant_dynamic-update-slice_fusion.refs_0_), channel_id=1, source_target_pairs={{0,48},{8,200},{16,0},{24,216},{32,16},{40,232},{48,32},{56,248},{... | collective-permute-start | bytes 4718600 | tf_op jit(solution)/shard_map/ppermute | solution.py:279
  32.1 1.2 copy-done.2
  33.2 5.2 %shard_map.77.refs_0_ = bf16[8,512,512]{2,1,0:T(8,128)(2,1)} custom-call(bf16[512,1536]{1,0:T(8,128)(2,1)} %constant_dynamic-update-slice_fusion.refs_0_, bf16[512,1536]{1,0:T(8,128)(2,1)} %copy-done.2, bf16[512,1536]{1,0:T(8,128)(2,1)} %refs_5_.1), custom_call_target="tpu_custom_call" | custom-call | flops 1610612736 | bytes 4194304 | tf_op jit(solution)/shard_map/pallas_call | solution.py:190
  38.5 10.4 %collective-permute-done.5.refs_1_.refs_2_ = bf16[512,1536]{1,0:T(8,128)(2,1)S(1)} collective-permute-done((bf16[512,1536]{1,0:T(8,128)(2,1)}, bf16[512,1536]{1,0:T(8,128)(2,1)S(1)}, u32[]{:S(2)}, u32[]{:S(2)}) %collective-permute-start.5) | collective-permute-done | bytes 1572896 | tf_op jit(solution)/shard_map/ppermute | solution.py:279
  48.9 1.1 copy-done.3
  50.0 2.3 collective-permute-done.4.refs_1_
  52.8 2.1 slice.96
  54.9 1.0 slice.97
  55.8 1.6 collective-permute-start.8
  57.5 1.1 copy-done
  58.6 5.2 %shard_map.78.refs_0_ = bf16[8,512,512]{2,1,0:T(8,128)(2,1)} custom-call(bf16[8,512,512]{2,1,0:T(8,128)(2,1)} %shard_map.77.refs_0_, bf16[512,1536]{1,0:T(8,128)(2,1)} %collective-permute-done.4.refs_1_, bf16[512,1536]{1,0:T(8,128)(2,1)} %copy-done, bf16[512,1536]{1,0:T(8,128)(2,1)} %refs_5_.1), custom_call_target="tpu_custom_call", output_to_operand_aliasing={{}: (0, {})} | custom-call | flops 1610612736 | bytes 4194304 | tf_op jit(solution)/shard_map/pallas_call | solution.py:190
  63.9 1.1 copy-done.1
  65.0 5.2 %shard_map.79.refs_0_ = bf16[8,512,512]{2,1,0:T(8,128)(2,1)} custom-call(bf16[8,512,512]{2,1,0:T(8,128)(2,1)} %shard_map.78.refs_0_, bf16[512,1536]{1,0:T(8,128)(2,1)} %copy-done.3, bf16[512,1536]{1,0:T(8,128)(2,1)} %copy-done.1, bf16[512,1536]{1,0:T(8,128)(2,1)} %refs_5_.1), custom_call_target="tpu_custom_call", output_to_operand_aliasing={{}: (0, {})} | custom-call | flops 1610612736 | bytes 4194304 | tf_op jit(solution)/shard_map/pallas_call | solution.py:190
  70.9 2.1 collective-permute-done.11.refs_3_.refs_4_
  74.8 5.2 %shard_map.80 = bf16[8,512,512]{2,1,0:T(8,128)(2,1)} custom-call(bf16[8,512,512]{2,1,0:T(8,128)(2,1)} %shard_map.79.refs_0_, bf16[256,1536]{1,0:T(8,128)(2,1)} %collective-permute-done.7.refs_1_.refs_3_, bf16[256,1536]{1,0:T(8,128)(2,1)} %copy-done.10, bf16[256,1536]{1,0:T(8,128)(2,1)} %copy-done.5, ...), custom_call_target="tpu_custom_call", output_to_operand_aliasing={{}: (0, {})} | custom-call | flops 1610612736 | bytes 4194304 | tf_op jit(solution)/shard_map/pallas_call | solution.py:190
  80.0 1.2 dynamic-slice_bitcast_fusion.1.targets
  81.1 14.4 %shard_map.81 = (bf16[8,128,512]{2,1,0:T(8,128)(2,1)}, bf16[12,128,512]{2,1,0:T(8,128)(2,1)}, bf16[12,128,512]{2,1,0:T(8,128)(2,1)}, f32[32,16,512]{2,1,0:T(8,128)}) custom-call(s32[1]{0:T(128)} %bitcast.place, s32[32]{0:T(128)} %dynamic-slice_bitcast_fusion.1.targets, bf16[8,128,2048]{2,1,0:T(8,128)(2,1)} %bitcast.19, bf16[256,256]{1,0:T(8,128)(2,1)} %constant.21.clone.table_ref), custom_call_target="tpu_custom_call" | custom-call | flops 4294967296 | bytes 8388608 | tf_op jit(solution)/shard_map/pallas_call | solution.py:140
  95.6 2.4 %collective-permute-start.14 = (bf16[12,128,512]{2,1,0:T(8,128)(2,1)}, bf16[12,128,512]{2,1,0:T(8,128)(2,1)S(1)}, u32[]{:S(2)}, u32[]{:S(2)}) collective-permute-start(bf16[12,128,512]{2,1,0:T(8,128)(2,1)} %get-tuple-element.26), channel_id=1, source_target_pairs={{0,192},{8,56},{16,208},{24,8},{32,224},{40,24},{48,240},{56,40},{... | collective-permute-start | bytes 4718600 | tf_op jit(solution)/shard_map/ppermute | solution.py:326
  97.9 17.7 %collective-permute-done.14 = bf16[12,128,512]{2,1,0:T(8,128)(2,1)S(1)} collective-permute-done((bf16[12,128,512]{2,1,0:T(8,128)(2,1)}, bf16[12,128,512]{2,1,0:T(8,128)(2,1)S(1)}, u32[]{:S(2)}, u32[]{:S(2)}) %collective-permute-start.14) | collective-permute-done | bytes 1572896 | tf_op jit(solution)/shard_map/ppermute | solution.py:326
  115.7 3.5 %collective-permute-start.17 = (bf16[4,128,512]{2,1,0:T(8,128)(2,1)S(1)}, bf16[4,128,512]{2,1,0:T(8,128)(2,1)S(1)}, u32[]{:S(2)}, u32[]{:S(2)}) collective-permute-start(bf16[4,128,512]{2,1,0:T(8,128)(2,1)S(1)} %slice.130), channel_id=1, source_target_pairs={{0,192},{8,56},{16,208},{24,8},{32,224},{40,24},{48,240},{56,40},{... | collective-permute-start | bytes 1572872 | tf_op jit(solution)/shard_map/ppermute | solution.py:333
  120.0 5.3 %collective-permute-done.17 = bf16[4,128,512]{2,1,0:T(8,128)(2,1)S(1)} collective-permute-done((bf16[4,128,512]{2,1,0:T(8,128)(2,1)S(1)}, bf16[4,128,512]{2,1,0:T(8,128)(2,1)S(1)}, u32[]{:S(2)}, u32[]{:S(2)}) %collective-permute-start.17) | collective-permute-done | bytes 524320 | tf_op jit(solution)/shard_map/ppermute | solution.py:333
  129.4 1.9 collective-permute-start.18
  133.6 1.3 dynamic-slice_bitcast_fusion.sources
  134.9 1.8 reduce-scatter.2.cloned.1.call-done
  136.7 1.9 shard_map.82
  138.5 8.3 %all-to-all-start = ((bf16[32,16,512]{2,1,0:T(8,128)(2,1)}), bf16[32,16,512]{2,1,0:T(8,128)(2,1)S(1)}, u32[]{:S(2)}, u32[]{:S(2)}) async-start(bf16[32,16,512]{2,1,0:T(8,128)(2,1)} %shard_map.82), calls=%async_computation.1 | async-start | bytes 1048576 | tf_op jit(solution)/shard_map/all_to_all | solution.py:413
  146.8 3.8 %collective-permute-done.18 = bf16[12,128,512]{2,1,0:T(8,128)(2,1)S(1)} collective-permute-done((bf16[12,128,512]{2,1,0:T(8,128)(2,1)}, bf16[12,128,512]{2,1,0:T(8,128)(2,1)S(1)}, u32[]{:S(2)}, u32[]{:S(2)}) %collective-permute-start.18) | collective-permute-done | bytes 1572896 | tf_op jit(solution)/shard_map/ppermute | solution.py:326
  150.7 8.3 %collective-permute-done.16 = bf16[12,128,512]{2,1,0:T(8,128)(2,1)} collective-permute-done((bf16[12,128,512]{2,1,0:T(8,128)(2,1)}, bf16[12,128,512]{2,1,0:T(8,128)(2,1)}, u32[]{:S(2)}, u32[]{:S(2)}) %collective-permute-start.16) | collective-permute-done | bytes 1572896 | tf_op jit(solution)/shard_map/ppermute | solution.py:325
  158.9 3.7 %all-to-all-done.summed_ref = bf16[32,16,512]{2,1,0:T(8,128)(2,1)S(1)} async-done(((bf16[32,16,512]{2,1,0:T(8,128)(2,1)}), bf16[32,16,512]{2,1,0:T(8,128)(2,1)S(1)}, u32[]{:S(2)}, u32[]{:S(2)}) %all-to-all-start) | async-done | bytes 524320 | tf_op jit(solution)/shard_map/all_to_all | solution.py:413
  162.6 1.3 slice.118
  163.9 3.8 %collective-permute-start.20 = (bf16[4,128,512]{2,1,0:T(8,128)(2,1)S(1)}, bf16[4,128,512]{2,1,0:T(8,128)(2,1)S(1)}, u32[]{:S(2)}, u32[]{:S(2)}) collective-permute-start(bf16[4,128,512]{2,1,0:T(8,128)(2,1)S(1)} %slice.119), channel_id=1, source_target_pairs={{0,48},{8,200},{16,0},{24,216},{32,16},{40,232},{48,32},{56,248},{... | collective-permute-start | bytes 1572872 | tf_op jit(solution)/shard_map/ppermute | solution.py:333
  167.7 2.3 slice_dynamic-update-slice_fusion.1
  170.0 1.1 slice_dynamic-update-slice_fusion
  171.1 5.9 %collective-permute-done.19 = bf16[4,128,512]{2,1,0:T(8,128)(2,1)S(1)} collective-permute-done((bf16[4,128,512]{2,1,0:T(8,128)(2,1)S(1)}, bf16[4,128,512]{2,1,0:T(8,128)(2,1)S(1)}, u32[]{:S(2)}, u32[]{:S(2)}) %collective-permute-start.19) | collective-permute-done | bytes 524320 | tf_op jit(solution)/shard_map/ppermute | solution.py:332
  178.6 4.7 %slice_bitcast_fusion = (bf16[16,128,512]{2,1,0:T(8,128)(2,1)}, bf16[16,128,512]{2,1,0:T(8,128)(2,1)}) fusion(bf16[16,2,128,512]{3,2,1,0:T(8,128)(2,1)} %bitcast.6), kind=kLoop, calls=%fused_computation | loop fusion | bytes 8388608 | tf_op jit(solution)/shard_map/squeeze | solution.py:421
  183.3 2.7 %shard_map.83 = bf16[8,16,2048]{2,1,0:T(8,128)(2,1)} custom-call(bf16[32,16,512]{2,1,0:T(8,128)(2,1)} %copy-done.8, f32[32,16,512]{2,1,0:T(8,128)} %get-tuple-element.29.slope_ref, bf16[256,256]{1,0:T(8,128)(2,1)} %constant.21.clone.table_ref), custom_call_target="tpu_custom_call" | custom-call | flops 536870912 | bytes 2097152 | tf_op jit(solution)/shard_map/pallas_call | solution.py:368
  186.0 8.2 %all-to-all-start.1 = ((bf16[8,16,2048]{2,1,0:T(8,128)(2,1)}), bf16[8,16,2048]{2,1,0:T(8,128)(2,1)S(1)}, u32[]{:S(2)}, u32[]{:S(2)}) async-start(bf16[8,16,2048]{2,1,0:T(8,128)(2,1)} %shard_map.83), calls=%async_computation.2 | async-start | bytes 1048576 | tf_op jit(solution)/shard_map/all_to_all | solution.py:417
  194.2 8.6 %shard_map.84.refs_0_ = f32[512,1536]{1,0:T(8,128)} custom-call(bf16[512,1536]{1,0:T(8,128)(2,1)} %constant_dynamic-update-slice_fusion.refs_0_, bf16[512,1536]{1,0:T(8,128)(2,1)} %collective-permute-done.4.refs_1_, bf16[512,1536]{1,0:T(8,128)(2,1)} %copy-done.3, bf16[256,1536]{1,0:T(8,128)(2,1)} %collective-permute-done.7.refs_1_.refs_3_, ...), custom_call_target="tpu_custom_call" | custom-call | flops 3221225472 | bytes 11534336 | tf_op jit(solution)/shard_map/pallas_call | solution.py:247
  202.8 9.4 %all-to-all-done.1 = bf16[8,16,2048]{2,1,0:T(8,128)(2,1)S(1)} async-done(((bf16[8,16,2048]{2,1,0:T(8,128)(2,1)}), bf16[8,16,2048]{2,1,0:T(8,128)(2,1)S(1)}, u32[]{:S(2)}, u32[]{:S(2)}) %all-to-all-start.1) | async-done | bytes 524320 | tf_op jit(solution)/shard_map/all_to_all | solution.py:417
  212.2 1.3 copy-done.7
  213.5 9.5 %shard_map.85 = f32[512,1536]{1,0:T(8,128)} custom-call(f32[512,1536]{1,0:T(8,128)} %shard_map.84.refs_0_, bf16[512,1536]{1,0:T(8,128)(2,1)} %copy-done.2, bf16[512,1536]{1,0:T(8,128)(2,1)} %copy-done, bf16[512,1536]{1,0:T(8,128)(2,1)} %copy-done.1, bf16[256,1536]{1,0:T(8,128)(2,1)} %copy-done.5, bf16[256,1536]{1,0:T(8,128)(2,1)} %copy-done.6, ...), custom_call_target="tpu_custom_call" | custom-call | flops 3221225472 | bytes 11534336 | tf_op jit(solution)/shard_map/pallas_call | solution.py:247
  (67 shorter events, 17.7 us)
Async XLA Ops:
  7.2 72.8 %all-gather.3.cloned.1.call-start = ((), (), s32[]{:S(2)}) async-start(), calls=%async_computation.4 | async-start | bytes 4718592 | tf_op jit(solution)/shard_map/all_gather | solution.py:388
  7.9 128.8 %reduce-scatter.2.cloned.1.call-start = ((), (), s32[]{:S(2)}) async-start(), calls=%async_computation.3 | async-start | bytes 4718592 | tf_op jit(solution)/shard_map/reduce_scatter | solution.py:404
  7.9 9.3 %collective-permute-start = (bf16[128,1536]{1,0:T(8,128)(2,1)}, bf16[128,1536]{1,0:T(8,128)(2,1)S(1)}, u32[]{:S(2)}, u32[]{:S(2)}) collective-permute-start(bf16[128,1536]{1,0:T(8,128)(2,1)} %param.8), channel_id=1, source_target_pairs={{0,64},{8,24},{16,80},{24,40},{32,96},{40,56},{48,112},{56,8},{64,... | collective-permute-start | bytes 1179656 | tf_op jit(solution)/shard_map/ppermute | solution.py:278
  10.1 7.2 %collective-permute-start.1 = (bf16[128,1536]{1,0:T(8,128)(2,1)}, bf16[128,1536]{1,0:T(8,128)(2,1)S(1)}, u32[]{:S(2)}, u32[]{:S(2)}) collective-permute-start(bf16[128,1536]{1,0:T(8,128)(2,1)} %param.8), channel_id=1, source_target_pairs={{0,192},{8,56},{16,208},{24,8},{32,224},{40,24},{48,240},{56,40},{... | collective-permute-start | bytes 1179656 | tf_op jit(solution)/shard_map/ppermute | solution.py:279
  17.3 5.8 %collective-permute-start.2 = (bf16[64,1536]{1,0:T(8,128)(2,1)S(1)}, bf16[64,1536]{1,0:T(8,128)(2,1)S(1)}, u32[]{:S(2)}, u32[]{:S(2)}) collective-permute-start(bf16[64,1536]{1,0:T(8,128)(2,1)S(1)} %slice.122), channel_id=1, source_target_pairs={{0,64},{8,24},{16,80},{24,40},{32,96},{40,56},{48,112},{56,8},{64,... | collective-permute-start | bytes 589832 | tf_op jit(solution)/shard_map/ppermute | solution.py:285
  17.4 6.4 %collective-permute-start.3 = (bf16[64,1536]{1,0:T(8,128)(2,1)S(1)}, bf16[64,1536]{1,0:T(8,128)(2,1)S(1)}, u32[]{:S(2)}, u32[]{:S(2)}) collective-permute-start(bf16[64,1536]{1,0:T(8,128)(2,1)S(1)} %slice.123), channel_id=1, source_target_pairs={{0,192},{8,56},{16,208},{24,8},{32,224},{40,24},{48,240},{56,40},{... | collective-permute-start | bytes 589832 | tf_op jit(solution)/shard_map/ppermute | solution.py:286
  24.5 7.6 %collective-permute-start.6 = (bf16[512,1536]{1,0:T(8,128)(2,1)}, bf16[512,1536]{1,0:T(8,128)(2,1)S(1)}, u32[]{:S(2)}, u32[]{:S(2)}) collective-permute-start(bf16[512,1536]{1,0:T(8,128)(2,1)} %constant_dynamic-update-slice_fusion.refs_0_), channel_id=1, source_target_pairs={{0,8},{8,0},{16,24},{24,16},{32,40},{40,32},{48,56},{56,48},{64,72... | collective-permute-start | bytes 4718600 | tf_op jit(solution)/shard_map/ppermute | solution.py:291
  28.8 20.0 %collective-permute-start.5 = (bf16[512,1536]{1,0:T(8,128)(2,1)}, bf16[512,1536]{1,0:T(8,128)(2,1)S(1)}, u32[]{:S(2)}, u32[]{:S(2)}) collective-permute-start(bf16[512,1536]{1,0:T(8,128)(2,1)} %constant_dynamic-update-slice_fusion.refs_0_), channel_id=1, source_target_pairs={{0,48},{8,200},{16,0},{24,216},{32,16},{40,232},{48,32},{56,248},{... | collective-permute-start | bytes 4718600 | tf_op jit(solution)/shard_map/ppermute | solution.py:279
  31.2 21.1 %collective-permute-start.4 = (bf16[512,1536]{1,0:T(8,128)(2,1)}, bf16[512,1536]{1,0:T(8,128)(2,1)}, u32[]{:S(2)}, u32[]{:S(2)}) collective-permute-start(bf16[512,1536]{1,0:T(8,128)(2,1)} %constant_dynamic-update-slice_fusion.refs_0_), channel_id=1, source_target_pairs={{0,16},{8,72},{16,32},{24,88},{32,48},{40,104},{48,0},{56,120},{64... | collective-permute-start | bytes 4718600 | tf_op jit(solution)/shard_map/ppermute | solution.py:278
  32.1 1.2 copy-start.2
  48.9 1.1 copy-start.3
  52.3 2.6 %copy-start.4 = (bf16[512,1536]{1,0:T(8,128)(2,1)S(1)}, bf16[512,1536]{1,0:T(8,128)(2,1)}, u32[]{:S(2)}) copy-start(bf16[512,1536]{1,0:T(8,128)(2,1)} %copy-done.3) | copy-start | bytes 4718596
  52.3 5.2 %collective-permute-start.9 = (bf16[512,1536]{1,0:T(8,128)(2,1)}, bf16[512,1536]{1,0:T(8,128)(2,1)S(1)}, u32[]{:S(2)}, u32[]{:S(2)}) collective-permute-start(bf16[512,1536]{1,0:T(8,128)(2,1)} %collective-permute-done.4.refs_1_), channel_id=1, source_target_pairs={{0,8},{8,0},{16,24},{24,16},{32,40},{40,32},{48,56},{56,48},{64,72... | collective-permute-start | bytes 4718600 | tf_op jit(solution)/shard_map/ppermute | solution.py:291
  52.3 11.6 %collective-permute-start.10 = (bf16[512,1536]{1,0:T(8,128)(2,1)}, bf16[512,1536]{1,0:T(8,128)(2,1)S(1)}, u32[]{:S(2)}, u32[]{:S(2)}) collective-permute-start(bf16[512,1536]{1,0:T(8,128)(2,1)} %copy-done.3), channel_id=1, source_target_pairs={{0,8},{8,0},{16,24},{24,16},{32,40},{40,32},{48,56},{56,48},{64,72... | collective-permute-start | bytes 4718600 | tf_op jit(solution)/shard_map/ppermute | solution.py:291
  55.8 14.3 %collective-permute-start.8 = (bf16[256,1536]{1,0:T(8,128)(2,1)}, bf16[256,1536]{1,0:T(8,128)(2,1)S(1)}, u32[]{:S(2)}, u32[]{:S(2)}) collective-permute-start(bf16[256,1536]{1,0:T(8,128)(2,1)} %slice.97), channel_id=1, source_target_pairs={{0,48},{8,200},{16,0},{24,216},{32,16},{40,232},{48,32},{56,248},{... | collective-permute-start | bytes 2359304 | tf_op jit(solution)/shard_map/ppermute | solution.py:286
  57.4 12.7 %collective-permute-start.7 = (bf16[256,1536]{1,0:T(8,128)(2,1)}, bf16[256,1536]{1,0:T(8,128)(2,1)}, u32[]{:S(2)}, u32[]{:S(2)}) collective-permute-start(bf16[256,1536]{1,0:T(8,128)(2,1)} %slice.96), channel_id=1, source_target_pairs={{0,16},{8,72},{16,32},{24,88},{32,48},{40,104},{48,0},{56,120},{64... | collective-permute-start | bytes 2359304 | tf_op jit(solution)/shard_map/ppermute | solution.py:285
  57.5 1.2 copy-start
  63.9 1.1 copy-start.1
  70.1 3.7 %copy-start.10 = (bf16[256,1536]{1,0:T(8,128)(2,1)}, bf16[256,1536]{1,0:T(8,128)(2,1)S(1)}, u32[]{:S(2)}) copy-start(bf16[256,1536]{1,0:T(8,128)(2,1)S(1)} %collective-permute-done.8.refs_2_.refs_4_) | copy-start | bytes 2359300
  70.2 2.8 %collective-permute-start.11 = (bf16[256,1536]{1,0:T(8,128)(2,1)}, bf16[256,1536]{1,0:T(8,128)(2,1)S(1)}, u32[]{:S(2)}, u32[]{:S(2)}) collective-permute-start(bf16[256,1536]{1,0:T(8,128)(2,1)} %collective-permute-done.7.refs_1_.refs_3_), channel_id=1, source_target_pairs={{0,8},{8,0},{16,24},{24,16},{32,40},{40,32},{48,56},{56,48},{64,72... | collective-permute-start | bytes 2359304 | tf_op jit(solution)/shard_map/ppermute | solution.py:291
  70.8 3.0 %collective-permute-start.12 = (bf16[256,1536]{1,0:T(8,128)(2,1)S(1)}, bf16[256,1536]{1,0:T(8,128)(2,1)S(1)}, u32[]{:S(2)}, u32[]{:S(2)}) collective-permute-start(bf16[256,1536]{1,0:T(8,128)(2,1)S(1)} %collective-permute-done.8.refs_2_.refs_4_), channel_id=1, source_target_pairs={{0,8},{8,0},{16,24},{24,16},{32,40},{40,32},{48,56},{56,48},{64,72... | collective-permute-start | bytes 2359304 | tf_op jit(solution)/shard_map/ppermute | solution.py:291
  73.0 0.9 copy-start.5
  73.9 0.9 copy-start.6
  95.6 20.0 %collective-permute-start.14 = (bf16[12,128,512]{2,1,0:T(8,128)(2,1)}, bf16[12,128,512]{2,1,0:T(8,128)(2,1)S(1)}, u32[]{:S(2)}, u32[]{:S(2)}) collective-permute-start(bf16[12,128,512]{2,1,0:T(8,128)(2,1)} %get-tuple-element.26), channel_id=1, source_target_pairs={{0,192},{8,56},{16,208},{24,8},{32,224},{40,24},{48,240},{56,40},{... | collective-permute-start | bytes 4718600 | tf_op jit(solution)/shard_map/ppermute | solution.py:326
  97.9 28.1 %copy-start.9 = (bf16[8,128,512]{2,1,0:T(8,128)(2,1)S(1)}, bf16[8,128,512]{2,1,0:T(8,128)(2,1)}, u32[]{:S(2)}) copy-start(bf16[8,128,512]{2,1,0:T(8,128)(2,1)} %get-tuple-element.24) | copy-start | bytes 3145732
  97.9 21.2 %collective-permute-start.13 = (bf16[12,128,512]{2,1,0:T(8,128)(2,1)}, bf16[12,128,512]{2,1,0:T(8,128)(2,1)S(1)}, u32[]{:S(2)}, u32[]{:S(2)}) collective-permute-start(bf16[12,128,512]{2,1,0:T(8,128)(2,1)} %get-tuple-element.25), channel_id=1, source_target_pairs={{0,64},{8,24},{16,80},{24,40},{32,96},{40,56},{48,112},{56,8},{64,... | collective-permute-start | bytes 4718600 | tf_op jit(solution)/shard_map/ppermute | solution.py:325
  115.7 9.6 %collective-permute-start.17 = (bf16[4,128,512]{2,1,0:T(8,128)(2,1)S(1)}, bf16[4,128,512]{2,1,0:T(8,128)(2,1)S(1)}, u32[]{:S(2)}, u32[]{:S(2)}) collective-permute-start(bf16[4,128,512]{2,1,0:T(8,128)(2,1)S(1)} %slice.130), channel_id=1, source_target_pairs={{0,192},{8,56},{16,208},{24,8},{32,224},{40,24},{48,240},{56,40},{... | collective-permute-start | bytes 1572872 | tf_op jit(solution)/shard_map/ppermute | solution.py:333
  119.2 12.1 %collective-permute-start.15 = (bf16[4,128,512]{2,1,0:T(8,128)(2,1)S(1)}, bf16[4,128,512]{2,1,0:T(8,128)(2,1)S(1)}, u32[]{:S(2)}, u32[]{:S(2)}) collective-permute-start(bf16[4,128,512]{2,1,0:T(8,128)(2,1)S(1)} %slice.126), channel_id=1, source_target_pairs={{0,64},{8,24},{16,80},{24,40},{32,96},{40,56},{48,112},{56,8},{64,... | collective-permute-start | bytes 1572872 | tf_op jit(solution)/shard_map/ppermute | solution.py:332
  129.4 21.3 %collective-permute-start.18 = (bf16[12,128,512]{2,1,0:T(8,128)(2,1)}, bf16[12,128,512]{2,1,0:T(8,128)(2,1)S(1)}, u32[]{:S(2)}, u32[]{:S(2)}) collective-permute-start(bf16[12,128,512]{2,1,0:T(8,128)(2,1)} %slice_dynamic-update-slice_fusion.5), channel_id=1, source_target_pairs={{0,48},{8,200},{16,0},{24,216},{32,16},{40,232},{48,32},{56,248},{... | collective-permute-start | bytes 4718600 | tf_op jit(solution)/shard_map/ppermute | solution.py:326
  133.6 25.3 %collective-permute-start.16 = (bf16[12,128,512]{2,1,0:T(8,128)(2,1)}, bf16[12,128,512]{2,1,0:T(8,128)(2,1)}, u32[]{:S(2)}, u32[]{:S(2)}) collective-permute-start(bf16[12,128,512]{2,1,0:T(8,128)(2,1)} %slice_dynamic-update-slice_fusion.10), channel_id=1, source_target_pairs={{0,16},{8,72},{16,32},{24,88},{32,48},{40,104},{48,0},{56,120},{64... | collective-permute-start | bytes 4718600 | tf_op jit(solution)/shard_map/ppermute | solution.py:325
  138.5 24.1 %all-to-all-start = ((bf16[32,16,512]{2,1,0:T(8,128)(2,1)}), bf16[32,16,512]{2,1,0:T(8,128)(2,1)S(1)}, u32[]{:S(2)}, u32[]{:S(2)}) async-start(bf16[32,16,512]{2,1,0:T(8,128)(2,1)} %shard_map.82), calls=%async_computation.1 | async-start | bytes 1048576 | tf_op jit(solution)/shard_map/all_to_all | solution.py:413
  162.6 7.3 %copy-start.8 = (bf16[32,16,512]{2,1,0:T(8,128)(2,1)}, bf16[32,16,512]{2,1,0:T(8,128)(2,1)S(1)}, u32[]{:S(2)}) copy-start(bf16[32,16,512]{2,1,0:T(8,128)(2,1)S(1)} %all-to-all-done.summed_ref) | copy-start | bytes 1572868
  163.9 13.8 %collective-permute-start.20 = (bf16[4,128,512]{2,1,0:T(8,128)(2,1)S(1)}, bf16[4,128,512]{2,1,0:T(8,128)(2,1)S(1)}, u32[]{:S(2)}, u32[]{:S(2)}) collective-permute-start(bf16[4,128,512]{2,1,0:T(8,128)(2,1)S(1)} %slice.119), channel_id=1, source_target_pairs={{0,48},{8,200},{16,0},{24,216},{32,16},{40,232},{48,32},{56,248},{... | collective-permute-start | bytes 1572872 | tf_op jit(solution)/shard_map/ppermute | solution.py:333
  167.7 9.2 %collective-permute-start.19 = (bf16[4,128,512]{2,1,0:T(8,128)(2,1)S(1)}, bf16[4,128,512]{2,1,0:T(8,128)(2,1)S(1)}, u32[]{:S(2)}, u32[]{:S(2)}) collective-permute-start(bf16[4,128,512]{2,1,0:T(8,128)(2,1)S(1)} %slice.118), channel_id=1, source_target_pairs={{0,16},{8,72},{16,32},{24,88},{32,48},{40,104},{48,0},{56,120},{64... | collective-permute-start | bytes 1572872 | tf_op jit(solution)/shard_map/ppermute | solution.py:332
  183.3 28.8 %collective-permute-start.21 = (bf16[16,128,512]{2,1,0:T(8,128)(2,1)}, bf16[16,128,512]{2,1,0:T(8,128)(2,1)S(1)}, u32[]{:S(2)}, u32[]{:S(2)}) collective-permute-start(bf16[16,128,512]{2,1,0:T(8,128)(2,1)} %get-tuple-element.32), channel_id=1, source_target_pairs={{0,8},{8,0},{16,24},{24,16},{32,40},{40,32},{48,56},{56,48},{64,72... | collective-permute-start | bytes 6291464 | tf_op jit(solution)/shard_map/ppermute | solution.py:291
  186.0 26.1 %all-to-all-start.1 = ((bf16[8,16,2048]{2,1,0:T(8,128)(2,1)}), bf16[8,16,2048]{2,1,0:T(8,128)(2,1)S(1)}, u32[]{:S(2)}, u32[]{:S(2)}) async-start(bf16[8,16,2048]{2,1,0:T(8,128)(2,1)} %shard_map.83), calls=%async_computation.2 | async-start | bytes 1048576 | tf_op jit(solution)/shard_map/all_to_all | solution.py:417
  212.2 1.3 copy-start.7
Sparse Core Ops, SparseCore 0:
  9.8 58.6 all-gather.2
  80.1 56.5 reduce-scatter.1

commit v6 on v4

--- a/solution.py
+++ b/solution.py
@@ -124,9 +124,8 @@
                 )
 
 
-def quantize(rows, table, place, dp, width):
+def quantize(rows, table, place, dp, step, width):
     members, tokens, features = rows.shape
-    step = tokens // members
     count = 2 * step
     return pl.pallas_call(
         quantize_kernel,
@@ -216,15 +215,18 @@
     )(sources, rows)
 
 
-def gradient_kernel(sources, quantized_ref, *refs):
+def gradient_kernel(sources, early_ref, late_ref, *refs):
     out_ref = refs[-1]
     pieces = refs[:-1]
-    tokens = quantized_ref.shape[1]
+    tokens = early_ref.shape[1] + late_ref.shape[1]
     slot = 0
     for number, piece_ref in enumerate(pieces):
         count = piece_ref.shape[0] // tokens
         block = jnp.concatenate(
-            [quantized_ref[sources[slot + k]] for k in range(count)], axis=0
+            [
+                ref[sources[slot + k]] for k in range(count) for ref in (early_ref, late_ref)
+            ],
+            axis=0,
         )
         slot += count
         term = lax.dot_general(
@@ -233,13 +235,13 @@
         out_ref[...] = term if number == 0 else out_ref[...] + term
 
 
-def gradient(sources, quantized, pieces):
-    width, depth = quantized.shape[2], pieces[0].shape[1]
+def gradient(sources, early, late, pieces):
+    width, depth = early.shape[2], pieces[0].shape[1]
     rows = sum(piece.shape[0] for piece in pieces)
     return pl.pallas_call(
         gradient_kernel,
         in_specs=[pl.BlockSpec(memory_space=pltpu.SMEM)]
-        + [pl.BlockSpec(memory_space=pltpu.VMEM)] * (len(pieces) + 1),
+        + [pl.BlockSpec(memory_space=pltpu.VMEM)] * (len(pieces) + 2),
         out_specs=pl.BlockSpec(memory_space=pltpu.VMEM),
         out_shape=jax.ShapeDtypeStruct((width, depth), jnp.float32),
         compiler_params=pltpu.CompilerParams(vmem_limit_bytes=VMEM_BYTES),
@@ -248,7 +250,7 @@
             bytes_accessed=2 * rows * (depth + width) + 4 * width * depth,
             transcendentals=0,
         ),
-    )(sources, quantized, *pieces)
+    )(sources, early, late, *pieces)
 
 
 def chip_core(x, y, core):
@@ -349,7 +351,12 @@
     place = lax.axis_index("tensor").astype(jnp.int32).reshape(1)
     sources = jnp.asarray(sources_table())[lax.axis_index("dp")]
     table = hadamard_table(TABLE)
-    wide_rows = lax.all_gather(activations, "tensor", axis=0, tiled=False)
+    step, half = tokens // members, tokens // 2
+    early_rows, late_rows, grad_out = lax.optimization_barrier(
+        (activations[:half], activations[half:], grad_out)
+    )
+    wide_early = lax.all_gather(early_rows, "tensor", axis=0, tiled=False)
+    wide_late = lax.all_gather(late_rows, "tensor", axis=0, tiled=False)
     below, above = hops(grad_out, 0)
     near = jnp.concatenate([grad_out, below, above, *far_hops(below, above, 0)], axis=0)
     below, above = hops(near, 1)
@@ -359,21 +366,27 @@
     first, second = far_hops(below, above, 1)
     below_pair = [below, other_core(below)]
     above_pair = [above, other_core(above)]
+    early, early_slope = quantize(wide_early, table, place, dp, step, width)
+    q_early = lax.all_to_all(early, "dp", split_axis=0, concat_axis=0, tiled=True)
+    partial_rows, early_slope = lax.optimization_barrier((partial_rows, early_slope))
     partial_rows = product(partial_rows, below_pair, weight, 1, members)
     partial_rows = product(partial_rows, above_pair, weight, 2, members)
     first, second, partial_rows = lax.optimization_barrier((first, second, partial_rows))
     far_pair = [first, second, other_core(first), other_core(second)]
     partial_rows = product(partial_rows, far_pair, weight, 3, members)
-    partial_rows, wide_rows = lax.optimization_barrier((partial_rows, wide_rows))
+    partial_rows, wide_late = lax.optimization_barrier((partial_rows, wide_late))
     summed = lax.psum_scatter(partial_rows, "tensor", scatter_dimension=0, tiled=False)
-    quantized, slope = quantize(wide_rows, table, place, dp, width)
-    q_block = lax.all_to_all(quantized, "dp", split_axis=0, concat_axis=0, tiled=True)
-    summed, q_block = lax.optimization_barrier((summed, q_block))
-    ordered = order(summed.reshape(dp, tokens // members, width), sources)
+    late, late_slope = quantize(wide_late, table, place - members // 2, dp, step, width)
+    slope = jnp.where(place[0] < members // 2, early_slope, late_slope)
+    q_late = lax.all_to_all(late, "dp", split_axis=0, concat_axis=0, tiled=True)
+    summed, q_early, q_late = lax.optimization_barrier((summed, q_early, q_late))
+    ordered = order(summed.reshape(dp, step, width), sources)
     homed = lax.all_to_all(ordered, "dp", split_axis=0, concat_axis=0, tiled=True)
     mixed = finish(homed, slope, table, members)
     grad_input = lax.all_to_all(mixed, "tensor", split_axis=0, concat_axis=0, tiled=True)
-    weight_sum = gradient(sources, q_block, near_pair + below_pair + above_pair + far_pair)
+    weight_sum = gradient(
+        sources, q_early, q_late, near_pair + below_pair + above_pair + far_pair
+    )
     return (grad_input.reshape(tokens, features), weight_sum)
 
 

time: 206 us -> 220 us (1.068)
  blocking collectives: 18.8 us -> 0 us
  waiting for transfers between devices: 77.1 us -> 91.9 us
  starting transfers between devices: 32.8 us -> 43.6 us
  local copies, waits for them, and re-layouts: 9.83 us -> 13 us
  Pallas kernels: 53.3 us -> 55.6 us
    all_to_all x1 -> x0, blocking collectives: 18.8 us -> none  [shards(): lax.all_to_all(ordered, 'dp', split_axis=0, concat_axis=0, tiled=True)]
    all_to_all x1 -> x3, starting transfers between devices: 7.35 us -> 20.8 us  [the longest x1 11.2 us: shards(): lax.all_to_all(early, 'dp', split_axis=0, concat_axis=0, tiled=True)]
    all_gather x1 -> x2, waiting for transfers between devices: 0.01 us -> 7.47 us  [the longest x1 7.47 us: shards(): wide_late = lax.all_gather(late_rows, 'tensor', axis=0, tiled=False)]
    all_to_all x1 -> x3, waiting for transfers between devices: 51 us -> 58 us  [the longest x1 27 us: shards(): q_late = lax.all_to_all(late, 'dp', split_axis=0, concat_axis=0, tiled=True)]
    pallas_call x1 -> x2, Pallas kernels: 13.6 us -> 16.2 us  [quantize(): pl.pallas_call(quantize_kernel, grid_spec=pltpu.PrefetchScalarGridSpec(nu...]
    all_to_all x1, starting transfers between devices: 6.46 us -> 3.98 us  [shards(): lax.all_to_all(mixed, 'tensor', split_axis=0, concat_axis=0, tiled=True)]
    unnamed x15 -> x23, local copies, waits for them, and re-layouts: 5.89 us -> 7.01 us
  transfers between devices with their start and end apart: 17 -> 20, of which waited for: 8 -> 11; matrix products, arithmetic and copies ran while one was open for 4% -> 4% of each run, Pallas kernels for 24% -> 23%
where the time goes in v6:
time: 220 us; the launch traced here: 219 us
  waiting for transfers between devices  91.9 us (42%)
  Pallas kernels  55.6 us (25%)
  starting transfers between devices  43.6 us (20%)
  between operations  13.9 us (6%)
  local copies, waits for them, and re-layouts  13 us (6%)
    all_to_all x1, waiting for transfers between devices, shards(): q_late = lax.all_to_all(late, 'dp', split_axis=0, concat_axis=0, tiled=True)  27 us
    pallas_call x4, Pallas kernels, product(): pl.pallas_call(product_kernel, grid=(1,), in_specs=[pl.BlockSpec(memory_s...  20.7 us
    all_to_all x1, waiting for transfers between devices, shards(): lax.all_to_all(early, 'dp', split_axis=0, concat_axis=0, tiled=True)  20.5 us
    ppermute x2, waiting for transfers between devices, hops(): below = lax.ppermute(block, 'dp', route(turn, 1))  17.4 us
    pallas_call x2, Pallas kernels, quantize(): pl.pallas_call(quantize_kernel, grid_spec=pltpu.PrefetchScalarGridSpec(nu...  16.2 us
    pallas_call x1, Pallas kernels, gradient(): pl.pallas_call(gradient_kernel, in_specs=[pl.BlockSpec(memory_space=pltpu...  14.1 us
    all_to_all x1, starting transfers between devices, shards(): lax.all_to_all(early, 'dp', split_axis=0, concat_axis=0, tiled=True)  11.2 us
    all_to_all x1, waiting for transfers between devices, shards(): lax.all_to_all(ordered, 'dp', split_axis=0, concat_axis=0, tiled=True)  10.5 us
  transfers between devices with their start and end apart: 20, of which 11 were waited for; matrix products, arithmetic and copies ran while one was open for 4% of the time, Pallas kernels for 23%

profile of v6, /device:TPU:1, one launch (start us, length us, event | category | flops | bytes accessed | tf_op | source)
XLA Modules:
  0.0 219.2 jit_solution(9658611493663588614)
XLA Ops:
  7.2 1.9 fusion
  9.2 2.2 %collective-permute-start = (bf16[128,1536]{1,0:T(8,128)(2,1)}, bf16[128,1536]{1,0:T(8,128)(2,1)S(1)}, u32[]{:S(2)}, u32[]{:S(2)}) collective-permute-start(bf16[128,1536]{1,0:T(8,128)(2,1)} %param.7), channel_id=1, source_target_pairs={{0,64},{8,24},{16,80},{24,40},{32,96},{40,56},{48,112},{56,8},{64,... | collective-permute-start | bytes 1179656 | tf_op jit(solution)/shard_map/ppermute | solution.py:273
  11.4 1.5 collective-permute-start.1
  12.9 0.8 constant_dynamic-update-slice_fusion.4
  13.7 4.8 %collective-permute-done = bf16[128,1536]{1,0:T(8,128)(2,1)S(1)} collective-permute-done((bf16[128,1536]{1,0:T(8,128)(2,1)}, bf16[128,1536]{1,0:T(8,128)(2,1)S(1)}, u32[]{:S(2)}, u32[]{:S(2)}) %collective-permute-start) | collective-permute-done | bytes 393248 | tf_op jit(solution)/shard_map/ppermute | solution.py:273
  18.7 2.7 %collective-permute-start.3 = (bf16[64,1536]{1,0:T(8,128)(2,1)S(1)}, bf16[64,1536]{1,0:T(8,128)(2,1)S(1)}, u32[]{:S(2)}, u32[]{:S(2)}) collective-permute-start(bf16[64,1536]{1,0:T(8,128)(2,1)S(1)} %slice.25), channel_id=1, source_target_pairs={{0,192},{8,56},{16,208},{24,8},{32,224},{40,24},{48,240},{56,40},{... | collective-permute-start | bytes 589832 | tf_op jit(solution)/shard_map/ppermute | solution.py:281
  21.4 0.8 constant_dynamic-update-slice_fusion.3
  22.2 0.8 constant_dynamic-update-slice_fusion.2
  23.0 1.4 collective-permute-done.2
  24.3 0.7 constant_dynamic-update-slice_fusion.1
  25.0 0.7 constant_dynamic-update-slice_fusion.refs_0_
  25.7 4.3 %collective-permute-start.6 = (bf16[512,1536]{1,0:T(8,128)(2,1)}, bf16[512,1536]{1,0:T(8,128)(2,1)}, u32[]{:S(2)}, u32[]{:S(2)}) collective-permute-start(bf16[512,1536]{1,0:T(8,128)(2,1)} %constant_dynamic-update-slice_fusion.refs_0_), channel_id=1, source_target_pairs={{0,8},{8,0},{16,24},{24,16},{32,40},{40,32},{48,56},{56,48},{64,72... | collective-permute-start | bytes 4718600 | tf_op jit(solution)/shard_map/ppermute | solution.py:286
  30.1 2.7 %collective-permute-start.5 = (bf16[512,1536]{1,0:T(8,128)(2,1)}, bf16[512,1536]{1,0:T(8,128)(2,1)S(1)}, u32[]{:S(2)}, u32[]{:S(2)}) collective-permute-start(bf16[512,1536]{1,0:T(8,128)(2,1)} %constant_dynamic-update-slice_fusion.refs_0_), channel_id=1, source_target_pairs={{0,48},{8,200},{16,0},{24,216},{32,16},{40,232},{48,32},{56,248},{... | collective-permute-start | bytes 4718600 | tf_op jit(solution)/shard_map/ppermute | solution.py:274
  32.8 0.6 collective-permute-done.6.refs_1_
  33.5 5.2 %shard_map.68.refs_0_ = bf16[8,512,512]{2,1,0:T(8,128)(2,1)} custom-call(bf16[512,1536]{1,0:T(8,128)(2,1)} %constant_dynamic-update-slice_fusion.refs_0_, bf16[512,1536]{1,0:T(8,128)(2,1)} %collective-permute-done.6.refs_1_, bf16[512,1536]{1,0:T(8,128)(2,1)} %refs_5_.1), custom_call_target="tpu_custom_call" | custom-call | flops 1610612736 | bytes 4194304 | tf_op jit(solution)/shard_map/pallas_call | solution.py:184
  38.6 12.5 %collective-permute-done.4.refs_1_.refs_2_ = bf16[512,1536]{1,0:T(8,128)(2,1)S(1)} collective-permute-done((bf16[512,1536]{1,0:T(8,128)(2,1)}, bf16[512,1536]{1,0:T(8,128)(2,1)S(1)}, u32[]{:S(2)}, u32[]{:S(2)}) %collective-permute-start.4) | collective-permute-done | bytes 1572896 | tf_op jit(solution)/shard_map/ppermute | solution.py:273
  51.2 0.8 collective-permute-start.9
  52.0 0.1 collective-permute-start.10
  52.1 1.0 slice.22
  53.1 1.0 slice.23
  54.1 0.1 collective-permute-start.7
  54.2 2.5 %collective-permute-start.8 = (bf16[256,1536]{1,0:T(8,128)(2,1)}, bf16[256,1536]{1,0:T(8,128)(2,1)}, u32[]{:S(2)}, u32[]{:S(2)}) collective-permute-start(bf16[256,1536]{1,0:T(8,128)(2,1)} %slice.23), channel_id=1, source_target_pairs={{0,48},{8,200},{16,0},{24,216},{32,16},{40,232},{48,32},{56,248},{... | collective-permute-start | bytes 2359304 | tf_op jit(solution)/shard_map/ppermute | solution.py:281
  56.7 8.4 %shard_map.69 = (bf16[32,64,512]{2,1,0:T(8,128)(2,1)}, f32[32,16,512]{2,1,0:T(8,128)}) custom-call(s32[1]{0:T(128)} %bitcast.1.place, bf16[8,64,2048]{2,1,0:T(8,128)(2,1)} %bitcast.10, bf16[256,256]{1,0:T(8,128)(2,1)} %constant.23.clone.table_ref), custom_call_target="tpu_custom_call" | custom-call | flops 2147483648 | bytes 4194304 | tf_op jit(solution)/shard_map/pallas_call | solution.py:130
  65.1 5.1 %shard_map.70.refs_0_ = bf16[8,512,512]{2,1,0:T(8,128)(2,1)} custom-call(bf16[8,512,512]{2,1,0:T(8,128)(2,1)} %shard_map.68.refs_0_, bf16[512,1536]{1,0:T(8,128)(2,1)} %copy-done, bf16[512,1536]{1,0:T(8,128)(2,1)} %collective-permute-done.9.refs_2_.refs_3_, bf16[512,1536]{1,0:T(8,128)(2,1)} %refs_5_.1), custom_call_target="tpu_custom_call", output_to_operand_aliasing={{}: (0, {})} | custom-call | flops 1610612736 | bytes 4194304 | tf_op jit(solution)/shard_map/pallas_call | solution.py:184
  70.3 5.2 %shard_map.71.refs_0_ = bf16[8,512,512]{2,1,0:T(8,128)(2,1)} custom-call(bf16[8,512,512]{2,1,0:T(8,128)(2,1)} %shard_map.70.refs_0_, bf16[512,1536]{1,0:T(8,128)(2,1)} %copy-done.1, bf16[512,1536]{1,0:T(8,128)(2,1)} %collective-permute-done.10.refs_2_.refs_5_, bf16[512,1536]{1,0:T(8,128)(2,1)} %refs_5_.1), custom_call_target="tpu_custom_call", output_to_operand_aliasing={{}: (0, {})} | custom-call | flops 1610612736 | bytes 4194304 | tf_op jit(solution)/shard_map/pallas_call | solution.py:184
  75.4 1.4 collective-permute-start.11
  76.9 2.0 collective-permute-done.11.refs_3_.refs_8_
  78.9 1.1 collective-permute-done.12.refs_4_.refs_9_
  80.1 1.0 copy-done.7
  81.0 5.2 %shard_map.72 = bf16[8,512,512]{2,1,0:T(8,128)(2,1)} custom-call(bf16[8,512,512]{2,1,0:T(8,128)(2,1)} %shard_map.71.refs_0_, bf16[256,1536]{1,0:T(8,128)(2,1)} %collective-permute-done.7.refs_1_.refs_6_, bf16[256,1536]{1,0:T(8,128)(2,1)} %collective-permute-done.8.refs_2_.refs_7_, bf16[256,1536]{1,0:T(8,128)(2,1)} %copy-done.6, ...), custom_call_target="tpu_custom_call", output_to_operand_aliasing={{}: (0, {})} | custom-call | flops 1610612736 | bytes 4194304 | tf_op jit(solution)/shard_map/pallas_call | solution.py:184
  86.2 7.5 %all-gather.7.cloned.1.call-done = bf16[512,2048]{1,0:T(8,128)(2,1)} async-done(((bf16[64,2048]{1,0:T(8,128)(2,1)}), bf16[512,2048]{1,0:T(8,128)(2,1)}) %all-gather.7.cloned.1.call-update) | async-done | bytes 2097168 | tf_op jit(solution)/shard_map/all_gather | solution.py:359
  93.7 11.2 %all-to-all-start = ((bf16[32,64,512]{2,1,0:T(8,128)(2,1)}), bf16[32,64,512]{2,1,0:T(8,128)(2,1)S(1)}, u32[]{:S(2)}, u32[]{:S(2)}) async-start(bf16[32,64,512]{2,1,0:T(8,128)(2,1)} %get-tuple-element.34), calls=%async_computation.1 | async-start | bytes 4194304 | tf_op jit(solution)/shard_map/all_to_all | solution.py:370
  105.0 7.8 %shard_map.73 = (bf16[32,64,512]{2,1,0:T(8,128)(2,1)}, f32[32,16,512]{2,1,0:T(8,128)}) custom-call(s32[1]{0:T(128)S(6)} %sub.3.place, bf16[8,64,2048]{2,1,0:T(8,128)(2,1)} %bitcast.11, bf16[256,256]{1,0:T(8,128)(2,1)} %constant.23.clone.table_ref), custom_call_target="tpu_custom_call" | custom-call | flops 2147483648 | bytes 4194304 | tf_op jit(solution)/shard_map/pallas_call | solution.py:130
  112.8 20.5 %all-to-all-done.early_ref = bf16[32,64,512]{2,1,0:T(8,128)(2,1)S(1)} async-done(((bf16[32,64,512]{2,1,0:T(8,128)(2,1)}), bf16[32,64,512]{2,1,0:T(8,128)(2,1)S(1)}, u32[]{:S(2)}, u32[]{:S(2)}) %all-to-all-start) | async-done | bytes 2097184 | tf_op jit(solution)/shard_map/all_to_all | solution.py:370
  133.3 1.4 copy-done.3
  134.7 5.2 %all-to-all-start.1 = ((bf16[32,64,512]{2,1,0:T(8,128)(2,1)}), bf16[32,64,512]{2,1,0:T(8,128)(2,1)}, u32[]{:S(2)}, u32[]{:S(2)}) async-start(bf16[32,64,512]{2,1,0:T(8,128)(2,1)} %get-tuple-element.36), calls=%async_computation.2 | async-start | bytes 4194304 | tf_op jit(solution)/shard_map/all_to_all | solution.py:381
  139.9 1.4 dynamic-slice_bitcast_fusion.sources
  141.3 27.0 %all-to-all-done.1.late_ref = bf16[32,64,512]{2,1,0:T(8,128)(2,1)} async-done(((bf16[32,64,512]{2,1,0:T(8,128)(2,1)}), bf16[32,64,512]{2,1,0:T(8,128)(2,1)}, u32[]{:S(2)}, u32[]{:S(2)}) %all-to-all-start.1) | async-done | bytes 2097184 | tf_op jit(solution)/shard_map/all_to_all | solution.py:381
  168.3 1.9 shard_map.74
  170.2 4.4 %all-to-all-start.2 = ((bf16[32,16,512]{2,1,0:T(8,128)(2,1)}), bf16[32,16,512]{2,1,0:T(8,128)(2,1)S(1)}, u32[]{:S(2)}, u32[]{:S(2)}) async-start(bf16[32,16,512]{2,1,0:T(8,128)(2,1)} %shard_map.74), calls=%async_computation.3 | async-start | bytes 1048576 | tf_op jit(solution)/shard_map/all_to_all | solution.py:384
  174.6 1.2 broadcast_select_fusion.slope_ref
  175.8 10.5 %all-to-all-done.2.summed_ref = bf16[32,16,512]{2,1,0:T(8,128)(2,1)S(1)} async-done(((bf16[32,16,512]{2,1,0:T(8,128)(2,1)}), bf16[32,16,512]{2,1,0:T(8,128)(2,1)S(1)}, u32[]{:S(2)}, u32[]{:S(2)}) %all-to-all-start.2) | async-done | bytes 524320 | tf_op jit(solution)/shard_map/all_to_all | solution.py:384
  186.3 0.8 copy-done.2
  187.1 2.7 %shard_map.75 = bf16[8,16,2048]{2,1,0:T(8,128)(2,1)} custom-call(bf16[32,16,512]{2,1,0:T(8,128)(2,1)} %copy-done.2, f32[32,16,512]{2,1,0:T(8,128)} %broadcast_select_fusion.slope_ref, bf16[256,256]{1,0:T(8,128)(2,1)} %constant.23.clone.table_ref), custom_call_target="tpu_custom_call" | custom-call | flops 536870912 | bytes 2097152 | tf_op jit(solution)/shard_map/pallas_call | solution.py:335
  189.8 4.0 %all-to-all-start.3 = ((bf16[8,16,2048]{2,1,0:T(8,128)(2,1)}), bf16[8,16,2048]{2,1,0:T(8,128)(2,1)S(1)}, u32[]{:S(2)}, u32[]{:S(2)}) async-start(bf16[8,16,2048]{2,1,0:T(8,128)(2,1)} %shard_map.75), calls=%async_computation.4 | async-start | bytes 1048576 | tf_op jit(solution)/shard_map/all_to_all | solution.py:386
  193.8 14.1 %shard_map.76 = f32[512,1536]{1,0:T(8,128)} custom-call(s32[32]{0:T(128)} %dynamic-slice_bitcast_fusion.sources, bf16[32,64,512]{2,1,0:T(8,128)(2,1)} %copy-done.3, bf16[32,64,512]{2,1,0:T(8,128)(2,1)} %all-to-all-done.1.late_ref, bf16[512,1536]{1,0:T(8,128)(2,1)} %constant_dynamic-update-slice_fusion.refs_0_, ...), custom_call_target="tpu_custom_call" | custom-call | flops 6442450944 | bytes 19922944 | tf_op jit(solution)/shard_map/pallas_call | solution.py:241
  208.0 3.9 %all-to-all-done.3 = bf16[8,16,2048]{2,1,0:T(8,128)(2,1)S(1)} async-done(((bf16[8,16,2048]{2,1,0:T(8,128)(2,1)}), bf16[8,16,2048]{2,1,0:T(8,128)(2,1)S(1)}, u32[]{:S(2)}, u32[]{:S(2)}) %all-to-all-start.3) | async-done | bytes 524320 | tf_op jit(solution)/shard_map/all_to_all | solution.py:386
  211.9 0.8 copy.18
  (35 shorter events, 0.4 us)
Async XLA Ops:
  7.2 5.8 %copy-start.8 = (bf16[128,1536]{1,0:T(8,128)(2,1)S(1)}, bf16[128,1536]{1,0:T(8,128)(2,1)}, u32[]{:S(2)}) copy-start(bf16[128,1536]{1,0:T(8,128)(2,1)} %param.7) | copy-start | bytes 1179652
  7.2 49.6 %all-gather.5.cloned.1.call-start = ((), (), s32[]{:S(2)}) async-start(), calls=%async_computation.6 | async-start | bytes 2359296 | tf_op jit(solution)/shard_map/all_gather | solution.py:358
  9.2 84.6 %all-gather.7.cloned.1.call-start = ((), (), s32[]{:S(2)}) async-start(), calls=%async_computation.7 | async-start | bytes 2359296 | tf_op jit(solution)/shard_map/all_gather | solution.py:359
  9.2 9.3 %collective-permute-start = (bf16[128,1536]{1,0:T(8,128)(2,1)}, bf16[128,1536]{1,0:T(8,128)(2,1)S(1)}, u32[]{:S(2)}, u32[]{:S(2)}) collective-permute-start(bf16[128,1536]{1,0:T(8,128)(2,1)} %param.7), channel_id=1, source_target_pairs={{0,64},{8,24},{16,80},{24,40},{32,96},{40,56},{48,112},{56,8},{64,... | collective-permute-start | bytes 1179656 | tf_op jit(solution)/shard_map/ppermute | solution.py:273
  11.4 7.2 %collective-permute-start.1 = (bf16[128,1536]{1,0:T(8,128)(2,1)}, bf16[128,1536]{1,0:T(8,128)(2,1)S(1)}, u32[]{:S(2)}, u32[]{:S(2)}) collective-permute-start(bf16[128,1536]{1,0:T(8,128)(2,1)} %param.7), channel_id=1, source_target_pairs={{0,192},{8,56},{16,208},{24,8},{32,224},{40,24},{48,240},{56,40},{... | collective-permute-start | bytes 1179656 | tf_op jit(solution)/shard_map/ppermute | solution.py:274
  18.5 5.8 %collective-permute-start.2 = (bf16[64,1536]{1,0:T(8,128)(2,1)S(1)}, bf16[64,1536]{1,0:T(8,128)(2,1)S(1)}, u32[]{:S(2)}, u32[]{:S(2)}) collective-permute-start(bf16[64,1536]{1,0:T(8,128)(2,1)S(1)} %slice.24), channel_id=1, source_target_pairs={{0,64},{8,24},{16,80},{24,40},{32,96},{40,56},{48,112},{56,8},{64,... | collective-permute-start | bytes 589832 | tf_op jit(solution)/shard_map/ppermute | solution.py:280
  18.7 6.4 %collective-permute-start.3 = (bf16[64,1536]{1,0:T(8,128)(2,1)S(1)}, bf16[64,1536]{1,0:T(8,128)(2,1)S(1)}, u32[]{:S(2)}, u32[]{:S(2)}) collective-permute-start(bf16[64,1536]{1,0:T(8,128)(2,1)S(1)} %slice.25), channel_id=1, source_target_pairs={{0,192},{8,56},{16,208},{24,8},{32,224},{40,24},{48,240},{56,40},{... | collective-permute-start | bytes 589832 | tf_op jit(solution)/shard_map/ppermute | solution.py:281
  25.7 7.7 %collective-permute-start.6 = (bf16[512,1536]{1,0:T(8,128)(2,1)}, bf16[512,1536]{1,0:T(8,128)(2,1)}, u32[]{:S(2)}, u32[]{:S(2)}) collective-permute-start(bf16[512,1536]{1,0:T(8,128)(2,1)} %constant_dynamic-update-slice_fusion.refs_0_), channel_id=1, source_target_pairs={{0,8},{8,0},{16,24},{24,16},{32,40},{40,32},{48,56},{56,48},{64,72... | collective-permute-start | bytes 4718600 | tf_op jit(solution)/shard_map/ppermute | solution.py:286
  30.1 21.1 %collective-permute-start.4 = (bf16[512,1536]{1,0:T(8,128)(2,1)}, bf16[512,1536]{1,0:T(8,128)(2,1)S(1)}, u32[]{:S(2)}, u32[]{:S(2)}) collective-permute-start(bf16[512,1536]{1,0:T(8,128)(2,1)} %constant_dynamic-update-slice_fusion.refs_0_), channel_id=1, source_target_pairs={{0,16},{8,72},{16,32},{24,88},{32,48},{40,104},{48,0},{56,120},{64... | collective-permute-start | bytes 4718600 | tf_op jit(solution)/shard_map/ppermute | solution.py:273
  30.1 21.1 %collective-permute-start.5 = (bf16[512,1536]{1,0:T(8,128)(2,1)}, bf16[512,1536]{1,0:T(8,128)(2,1)S(1)}, u32[]{:S(2)}, u32[]{:S(2)}) collective-permute-start(bf16[512,1536]{1,0:T(8,128)(2,1)} %constant_dynamic-update-slice_fusion.refs_0_), channel_id=1, source_target_pairs={{0,48},{8,200},{16,0},{24,216},{32,16},{40,232},{48,32},{56,248},{... | collective-permute-start | bytes 4718600 | tf_op jit(solution)/shard_map/ppermute | solution.py:274
  32.8 135.5 %reduce-scatter.2.cloned.1.call-start = ((), (), s32[]{:S(2)}) async-start(), calls=%async_computation.5 | async-start | bytes 4718592 | tf_op jit(solution)/shard_map/reduce_scatter | solution.py:378
  51.2 2.9 %copy-start = (bf16[512,1536]{1,0:T(8,128)(2,1)}, bf16[512,1536]{1,0:T(8,128)(2,1)S(1)}, u32[]{:S(2)}) copy-start(bf16[512,1536]{1,0:T(8,128)(2,1)S(1)} %collective-permute-done.4.refs_1_.refs_2_) | copy-start | bytes 4718596
  51.2 2.9 %copy-start.1 = (bf16[512,1536]{1,0:T(8,128)(2,1)}, bf16[512,1536]{1,0:T(8,128)(2,1)S(1)}, u32[]{:S(2)}) copy-start(bf16[512,1536]{1,0:T(8,128)(2,1)S(1)} %collective-permute-done.5.refs_1_.refs_4_) | copy-start | bytes 4718596
  51.2 14.0 %collective-permute-start.9 = (bf16[512,1536]{1,0:T(8,128)(2,1)S(1)}, bf16[512,1536]{1,0:T(8,128)(2,1)}, u32[]{:S(2)}, u32[]{:S(2)}) collective-permute-start(bf16[512,1536]{1,0:T(8,128)(2,1)S(1)} %collective-permute-done.4.refs_1_.refs_2_), channel_id=1, source_target_pairs={{0,8},{8,0},{16,24},{24,16},{32,40},{40,32},{48,56},{56,48},{64,72... | collective-permute-start | bytes 4718600 | tf_op jit(solution)/shard_map/ppermute | solution.py:286
  52.0 18.3 %collective-permute-start.10 = (bf16[512,1536]{1,0:T(8,128)(2,1)S(1)}, bf16[512,1536]{1,0:T(8,128)(2,1)}, u32[]{:S(2)}, u32[]{:S(2)}) collective-permute-start(bf16[512,1536]{1,0:T(8,128)(2,1)S(1)} %collective-permute-done.5.refs_1_.refs_4_), channel_id=1, source_target_pairs={{0,8},{8,0},{16,24},{24,16},{32,40},{40,32},{48,56},{56,48},{64,72... | collective-permute-start | bytes 4718600 | tf_op jit(solution)/shard_map/ppermute | solution.py:286
  54.1 21.4 %collective-permute-start.7 = (bf16[256,1536]{1,0:T(8,128)(2,1)}, bf16[256,1536]{1,0:T(8,128)(2,1)}, u32[]{:S(2)}, u32[]{:S(2)}) collective-permute-start(bf16[256,1536]{1,0:T(8,128)(2,1)} %slice.22), channel_id=1, source_target_pairs={{0,16},{8,72},{16,32},{24,88},{32,48},{40,104},{48,0},{56,120},{64... | collective-permute-start | bytes 2359304 | tf_op jit(solution)/shard_map/ppermute | solution.py:280
  54.2 21.2 %collective-permute-start.8 = (bf16[256,1536]{1,0:T(8,128)(2,1)}, bf16[256,1536]{1,0:T(8,128)(2,1)}, u32[]{:S(2)}, u32[]{:S(2)}) collective-permute-start(bf16[256,1536]{1,0:T(8,128)(2,1)} %slice.23), channel_id=1, source_target_pairs={{0,48},{8,200},{16,0},{24,216},{32,16},{40,232},{48,32},{56,248},{... | collective-permute-start | bytes 2359304 | tf_op jit(solution)/shard_map/ppermute | solution.py:281
  75.4 3.5 %collective-permute-start.11 = (bf16[256,1536]{1,0:T(8,128)(2,1)}, bf16[256,1536]{1,0:T(8,128)(2,1)S(1)}, u32[]{:S(2)}, u32[]{:S(2)}) collective-permute-start(bf16[256,1536]{1,0:T(8,128)(2,1)} %collective-permute-done.7.refs_1_.refs_6_), channel_id=1, source_target_pairs={{0,8},{8,0},{16,24},{24,16},{32,40},{40,32},{48,56},{56,48},{64,72... | collective-permute-start | bytes 2359304 | tf_op jit(solution)/shard_map/ppermute | solution.py:286
  76.8 3.2 %collective-permute-start.12 = (bf16[256,1536]{1,0:T(8,128)(2,1)}, bf16[256,1536]{1,0:T(8,128)(2,1)S(1)}, u32[]{:S(2)}, u32[]{:S(2)}) collective-permute-start(bf16[256,1536]{1,0:T(8,128)(2,1)} %collective-permute-done.8.refs_2_.refs_7_), channel_id=1, source_target_pairs={{0,8},{8,0},{16,24},{24,16},{32,40},{40,32},{48,56},{56,48},{64,72... | collective-permute-start | bytes 2359304 | tf_op jit(solution)/shard_map/ppermute | solution.py:286
  78.9 1.1 copy-start.6
  80.1 1.0 copy-start.7
  93.7 39.5 %all-to-all-start = ((bf16[32,64,512]{2,1,0:T(8,128)(2,1)}), bf16[32,64,512]{2,1,0:T(8,128)(2,1)S(1)}, u32[]{:S(2)}, u32[]{:S(2)}) async-start(bf16[32,64,512]{2,1,0:T(8,128)(2,1)} %get-tuple-element.34), calls=%async_computation.1 | async-start | bytes 4194304 | tf_op jit(solution)/shard_map/all_to_all | solution.py:370
  133.3 1.4 copy-start.3
  134.7 33.6 %all-to-all-start.1 = ((bf16[32,64,512]{2,1,0:T(8,128)(2,1)}), bf16[32,64,512]{2,1,0:T(8,128)(2,1)}, u32[]{:S(2)}, u32[]{:S(2)}) async-start(bf16[32,64,512]{2,1,0:T(8,128)(2,1)} %get-tuple-element.36), calls=%async_computation.2 | async-start | bytes 4194304 | tf_op jit(solution)/shard_map/all_to_all | solution.py:381
  139.9 34.7 %copy-start.4 = (f32[32,16,512]{2,1,0:T(8,128)S(1)}, f32[32,16,512]{2,1,0:T(8,128)}, u32[]{:S(2)}) copy-start(f32[32,16,512]{2,1,0:T(8,128)} %get-tuple-element.38) | copy-start | bytes 3145732
  139.9 34.7 %copy-start.5 = (f32[32,16,512]{2,1,0:T(8,128)S(1)}, f32[32,16,512]{2,1,0:T(8,128)}, u32[]{:S(2)}) copy-start(f32[32,16,512]{2,1,0:T(8,128)} %get-tuple-element.39) | copy-start | bytes 3145732
  170.2 16.1 %all-to-all-start.2 = ((bf16[32,16,512]{2,1,0:T(8,128)(2,1)}), bf16[32,16,512]{2,1,0:T(8,128)(2,1)S(1)}, u32[]{:S(2)}, u32[]{:S(2)}) async-start(bf16[32,16,512]{2,1,0:T(8,128)(2,1)} %shard_map.74), calls=%async_computation.3 | async-start | bytes 1048576 | tf_op jit(solution)/shard_map/all_to_all | solution.py:384
  186.3 0.8 copy-start.2
  189.8 22.0 %all-to-all-start.3 = ((bf16[8,16,2048]{2,1,0:T(8,128)(2,1)}), bf16[8,16,2048]{2,1,0:T(8,128)(2,1)S(1)}, u32[]{:S(2)}, u32[]{:S(2)}) async-start(bf16[8,16,2048]{2,1,0:T(8,128)(2,1)} %shard_map.75), calls=%async_computation.4 | async-start | bytes 1048576 | tf_op jit(solution)/shard_map/all_to_all | solution.py:386
Sparse Core Ops, SparseCore 0:
  10.4 41.1 all-gather.4
  54.0 39.6 all-gather.6
  96.3 57.5 reduce-scatter.1

commit v7 on v4

--- a/solution.py
+++ b/solution.py
@@ -15,7 +15,7 @@
 VMEM_BYTES = 60 * 1024 * 1024
 NORM = 1.0 / math.sqrt(WIDTH)
 SIDE = 4
-PIECES = 4
+STEP = 16
 OFFSETS = (0, -1, 1, -2)
 
 levels = 127.0
@@ -160,7 +160,7 @@
 def product_kernel(*refs):
     weight_ref, out_ref = refs[-2:]
     pieces = [ref for ref in refs[:-2] if len(ref.shape) == 2]
-    members, step = out_ref.shape[0], out_ref.shape[1] // PIECES // 2
+    members, step = out_ref.shape[0], STEP
     done = 0
     for piece_ref in pieces:
         rows, depth = piece_ref.shape
@@ -177,7 +177,7 @@
             done += 1
 
 
-def product(held, pieces, weight, position, members):
+def product(held, pieces, weight, position, members, total):
     rows = sum(piece.shape[0] for piece in pieces)
     width, depth = weight.shape
     whole = [pl.BlockSpec(memory_space=pltpu.VMEM)] * (len(pieces) + 1)
@@ -187,7 +187,7 @@
         grid=(1,),
         in_specs=[pl.BlockSpec(memory_space=pl.ANY)] * len(earlier) + whole,
         out_specs=pl.BlockSpec((members, rows // members, width), lambda i: (0, position, 0)),
-        out_shape=jax.ShapeDtypeStruct((members, 4 * rows // members, width), jnp.bfloat16),
+        out_shape=jax.ShapeDtypeStruct((members, total // members, width), jnp.bfloat16),
         input_output_aliases={0: 0} if earlier else {},
         compiler_params=pltpu.CompilerParams(vmem_limit_bytes=VMEM_BYTES),
         cost_estimate=pl.CostEstimate(
@@ -267,17 +267,8 @@
     return pairs
 
 
-def hops(block, turn):
-    below = lax.ppermute(block, "dp", route(turn, 1))
-    above = lax.ppermute(block, "dp", route(turn, -1))
-    return below, above
-
-
-def far_hops(below, above, turn):
-    half = below.shape[0] // 2
-    first = lax.ppermute(below[:half], "dp", route(turn, 1))
-    second = lax.ppermute(above[half:], "dp", route(turn, -1))
-    return first, second
+def send(block, turn, sign):
+    return lax.ppermute(block, "dp", route(turn, sign))
 
 
 def other_core(block):
@@ -350,30 +341,47 @@
     sources = jnp.asarray(sources_table())[lax.axis_index("dp")]
     table = hadamard_table(TABLE)
     wide_rows = lax.all_gather(activations, "tensor", axis=0, tiled=False)
-    below, above = hops(grad_out, 0)
-    near = jnp.concatenate([grad_out, below, above, *far_hops(below, above, 0)], axis=0)
-    below, above = hops(near, 1)
-    near_pair = [near, other_core(near)]
-    partial_rows = product(None, near_pair, weight, 0, members)
-    below, above, partial_rows = lax.optimization_barrier((below, above, partial_rows))
-    first, second = far_hops(below, above, 1)
-    below_pair = [below, other_core(below)]
-    above_pair = [above, other_core(above)]
-    partial_rows = product(partial_rows, below_pair, weight, 1, members)
-    partial_rows = product(partial_rows, above_pair, weight, 2, members)
-    first, second, partial_rows = lax.optimization_barrier((first, second, partial_rows))
-    far_pair = [first, second, other_core(first), other_core(second)]
-    partial_rows = product(partial_rows, far_pair, weight, 3, members)
+    total = dp * tokens
+
+    def multiply(held, pieces, position):
+        return product(held, pieces, weight, position, members, total)
+
+    half = tokens // 2
+    below, above = send(grad_out, 0, 1), send(grad_out, 0, -1)
+    top = jnp.concatenate([grad_out, below], axis=0)
+    below_top, above_top = send(top, 1, 1), send(top, 1, -1)
+    far = [send(below[:half], 0, 1), send(above[half:], 0, -1)]
+    bottom = jnp.concatenate([above, *far], axis=0)
+    below_bottom, above_bottom = send(bottom, 1, 1), send(bottom, 1, -1)
+    far_top = send(below_top, 1, 1)
+    near = [top, bottom]
+    near_other = [other_core(block) for block in near]
+    held = multiply(None, near + near_other, 0)
+    below_bottom, above_bottom, held = lax.optimization_barrier(
+        (below_bottom, above_bottom, held)
+    )
+    far_bottom = send(above_bottom, 1, -1)
+    below, above = [below_top, below_bottom], [above_top, above_bottom]
+    below_other = [other_core(block) for block in below]
+    above_other = [other_core(block) for block in above]
+    held = multiply(held, below + below_other, 1)
+    held = multiply(held, above + above_other, 2)
+    far_top, far_bottom, held = lax.optimization_barrier((far_top, far_bottom, held))
+    far = [far_top, far_bottom]
+    far_other = [other_core(block) for block in far]
+    held = multiply(held, far, 6)
+    partial_rows = multiply(held, far_other, 7)
     partial_rows, wide_rows = lax.optimization_barrier((partial_rows, wide_rows))
     summed = lax.psum_scatter(partial_rows, "tensor", scatter_dimension=0, tiled=False)
     quantized, slope = quantize(wide_rows, table, place, dp, width)
     q_block = lax.all_to_all(quantized, "dp", split_axis=0, concat_axis=0, tiled=True)
-    summed, q_block = lax.optimization_barrier((summed, q_block))
     ordered = order(summed.reshape(dp, tokens // members, width), sources)
+    ordered, q_block = lax.optimization_barrier((ordered, q_block))
     homed = lax.all_to_all(ordered, "dp", split_axis=0, concat_axis=0, tiled=True)
     mixed = finish(homed, slope, table, members)
     grad_input = lax.all_to_all(mixed, "tensor", split_axis=0, concat_axis=0, tiled=True)
-    weight_sum = gradient(sources, q_block, near_pair + below_pair + above_pair + far_pair)
+    arrived = near + near_other + below + below_other + above + above_other + far + far_other
+    weight_sum = gradient(sources, q_block, arrived)
     return (grad_input.reshape(tokens, features), weight_sum)
 
 

time: 206 us -> 205 us (level)
  waiting for transfers between devices: 77.1 us -> 70.4 us
  starting transfers between devices: 32.8 us -> 37.9 us
  Pallas kernels: 53.3 us -> 55.4 us
  local copies, waits for them, and re-layouts: 9.83 us -> 7.73 us
    all_to_all x1, waiting for transfers between devices: 51 us -> 13.9 us  [shards(): lax.all_to_all(quantized, 'dp', split_axis=0, concat_axis=0, tiled=True)]
    reduce_scatter x1, waiting for transfers between devices: 0.01 us -> 35.3 us  [shards(): lax.psum_scatter(partial_rows, 'tensor', scatter_dimension=0, tiled=False)]
    ppermute x5 -> x8, starting transfers between devices: 6.97 us -> 11.2 us  [other_core(): lax.ppermute(block, 'dp', [(d, d ^ 1) for d in range(2 * SIDE * SIDE)])]
    ppermute x5 -> x8, waiting for transfers between devices: 3.85 us -> 0.02 us  [other_core(): lax.ppermute(block, 'dp', [(d, d ^ 1) for d in range(2 * SIDE * SIDE)])]
    all_to_all x1, starting transfers between devices: 7.35 us -> 5.01 us  [shards(): lax.all_to_all(quantized, 'dp', split_axis=0, concat_axis=0, tiled=True)]
    pallas_call x4 -> x5, Pallas kernels: 20.9 us -> 23.1 us  [product(): pl.pallas_call(product_kernel, grid=(1,), in_specs=[pl.BlockSpec(memory_s...]
    ppermute x8 -> x10, starting transfers between devices: 11.9 us -> 13.6 us  [send(): return lax.ppermute(block, 'dp', route(turn, sign))]
    ppermute x8 -> x10, waiting for transfers between devices: 17.6 us -> 16.7 us  [send(): return lax.ppermute(block, 'dp', route(turn, sign))]
  transfers between devices with their start and end apart: 17 -> 22, of which waited for: 8 -> 7; matrix products, arithmetic and copies ran while one was open for 4% -> 1% of each run, Pallas kernels for 24% -> 26%
where the time goes in v7:
time: 205 us; the launch traced here: 204 us
  waiting for transfers between devices  70.4 us (34%)
  Pallas kernels  55.4 us (27%)
  starting transfers between devices  37.9 us (18%)
  blocking collectives  18.8 us (9%)
  between operations  14.2 us (7%)
  local copies, waits for them, and re-layouts  7.73 us (4%)
    reduce_scatter x1, waiting for transfers between devices, shards(): lax.psum_scatter(partial_rows, 'tensor', scatter_dimension=0, tiled=False)  35.3 us
    pallas_call x5, Pallas kernels, product(): pl.pallas_call(product_kernel, grid=(1,), in_specs=[pl.BlockSpec(memory_s...  23.1 us
    all_to_all x1, blocking collectives, shards(): lax.all_to_all(ordered, 'dp', split_axis=0, concat_axis=0, tiled=True)  18.8 us
    ppermute x10, waiting for transfers between devices, send(): return lax.ppermute(block, 'dp', route(turn, sign))  16.7 us
    pallas_call x1, Pallas kernels, gradient(): pl.pallas_call(gradient_kernel, in_specs=[pl.BlockSpec(memory_space=pltpu...  14.2 us
    all_to_all x1, waiting for transfers between devices, shards(): lax.all_to_all(quantized, 'dp', split_axis=0, concat_axis=0, tiled=True)  13.9 us
    ppermute x10, starting transfers between devices, send(): return lax.ppermute(block, 'dp', route(turn, sign))  13.6 us
    pallas_call x1, Pallas kernels, quantize(): pl.pallas_call(quantize_kernel, grid_spec=pltpu.PrefetchScalarGridSpec(nu...  13.6 us
  transfers between devices with their start and end apart: 22, of which 7 were waited for; matrix products, arithmetic and copies ran while one was open for 1% of the time, Pallas kernels for 26%

profile of v7, /device:TPU:1, one launch (start us, length us, event | category | flops | bytes accessed | tf_op | source)
XLA Modules:
  0.0 204.4 jit_solution(984519211084370398)
XLA Ops:
  7.2 0.0 all-gather.3.cloned.1.call-start
  7.2 0.7 all-gather.3.cloned.1.call-update
  7.9 0.0 reduce-scatter.2.cloned.1.call-start
  7.9 2.2 %collective-permute-start = (bf16[128,1536]{1,0:T(8,128)(2,1)}, bf16[128,1536]{1,0:T(8,128)(2,1)S(1)}, u32[]{:S(2)}, u32[]{:S(2)}) collective-permute-start(bf16[128,1536]{1,0:T(8,128)(2,1)} %param.7), channel_id=1, source_target_pairs={{0,64},{8,24},{16,80},{24,40},{32,96},{40,56},{48,112},{56,8},{64,... | collective-permute-start | bytes 1179656 | tf_op jit(solution)/shard_map/ppermute | solution.py:271
  10.1 1.5 collective-permute-start.3
  11.7 1.1 constant_dynamic-update-slice_fusion.1
  12.7 4.5 %collective-permute-done = bf16[128,1536]{1,0:T(8,128)(2,1)S(1)} collective-permute-done((bf16[128,1536]{1,0:T(8,128)(2,1)}, bf16[128,1536]{1,0:T(8,128)(2,1)S(1)}, u32[]{:S(2)}, u32[]{:S(2)}) %collective-permute-start) | collective-permute-done | bytes 393248 | tf_op jit(solution)/shard_map/ppermute | solution.py:271
  17.3 1.0 collective-permute-start.1
  18.3 2.4 %collective-permute-start.8 = (bf16[256,1536]{1,0:T(8,128)(2,1)S(1)}, bf16[256,1536]{1,0:T(8,128)(2,1)S(1)}, u32[]{:S(2)}, u32[]{:S(2)}) collective-permute-start(bf16[256,1536]{1,0:T(8,128)(2,1)S(1)} %constant_dynamic-update-slice_fusion.refs_0_), channel_id=1, source_target_pairs={{0,8},{8,0},{16,24},{24,16},{32,40},{40,32},{48,56},{56,48},{64,72... | collective-permute-start | bytes 2359304 | tf_op jit(solution)/shard_map/ppermute | solution.py:275
  20.7 1.1 collective-permute-start.4
  21.8 1.9 collective-permute-start.5
  23.8 5.2 %collective-permute-done.4 = bf16[64,1536]{1,0:T(8,128)(2,1)S(1)} collective-permute-done((bf16[64,1536]{1,0:T(8,128)(2,1)S(1)}, bf16[64,1536]{1,0:T(8,128)(2,1)S(1)}, u32[]{:S(2)}, u32[]{:S(2)}) %collective-permute-start.4) | collective-permute-done | bytes 196640 | tf_op jit(solution)/shard_map/ppermute | solution.py:271
  29.1 0.9 collective-permute-start.9
  30.0 2.7 %collective-permute-start.7 = (bf16[256,1536]{1,0:T(8,128)(2,1)S(1)}, bf16[256,1536]{1,0:T(8,128)(2,1)}, u32[]{:S(2)}, u32[]{:S(2)}) collective-permute-start(bf16[256,1536]{1,0:T(8,128)(2,1)S(1)} %constant_dynamic-update-slice_fusion.2.refs_1_), channel_id=1, source_target_pairs={{0,48},{8,200},{16,0},{24,216},{32,16},{40,232},{48,32},{56,248},{... | collective-permute-start | bytes 2359304 | tf_op jit(solution)/shard_map/ppermute | solution.py:271
  32.7 0.0 collective-permute-done.1.refs_1_.refs_4_
  32.7 0.5 collective-permute-start.13
  33.2 0.0 collective-permute-done.8.refs_2_
  33.2 2.8 %collective-permute-start.11 = (bf16[256,1536]{1,0:T(8,128)(2,1)S(1)}, bf16[256,1536]{1,0:T(8,128)(2,1)}, u32[]{:S(2)}, u32[]{:S(2)}) collective-permute-start(bf16[256,1536]{1,0:T(8,128)(2,1)S(1)} %collective-permute-done.1.refs_1_.refs_4_), channel_id=1, source_target_pairs={{0,8},{8,0},{16,24},{24,16},{32,40},{40,32},{48,56},{56,48},{64,72... | collective-permute-start | bytes 2359304 | tf_op jit(solution)/shard_map/ppermute | solution.py:275
  36.0 5.2 %shard_map.68.refs_0_ = bf16[8,512,512]{2,1,0:T(8,128)(2,1)} custom-call(bf16[256,1536]{1,0:T(8,128)(2,1)} %copy-done.1, bf16[256,1536]{1,0:T(8,128)(2,1)} %copy-done, bf16[256,1536]{1,0:T(8,128)(2,1)} %copy-done.3, bf16[256,1536]{1,0:T(8,128)(2,1)} %collective-permute-done.9.refs_3_, bf16[512,1536]{1,0:T(8,128)(2,1)} %refs_3_.3), custom_call_target="tpu_custom_call" | custom-call | flops 1610612736 | bytes 4194304 | tf_op jit(solution)/shard_map/pallas_call | solution.py:185
  41.2 1.3 collective-permute-done.6.refs_2_.refs_5_
  42.4 1.9 collective-permute-start.12
  44.3 5.7 %collective-permute-done.13.refs_1_.refs_8_ = bf16[256,1536]{1,0:T(8,128)(2,1)} collective-permute-done((bf16[256,1536]{1,0:T(8,128)(2,1)S(1)}, bf16[256,1536]{1,0:T(8,128)(2,1)}, u32[]{:S(2)}, u32[]{:S(2)}) %collective-permute-start.13) | collective-permute-done | bytes 786464 | tf_op jit(solution)/shard_map/ppermute | solution.py:271
  50.0 1.9 collective-permute-start.14
  51.9 2.7 %collective-permute-start.10 = (bf16[256,1536]{1,0:T(8,128)(2,1)}, bf16[256,1536]{1,0:T(8,128)(2,1)}, u32[]{:S(2)}, u32[]{:S(2)}) collective-permute-start(bf16[256,1536]{1,0:T(8,128)(2,1)} %collective-permute-done.7.refs_2_.refs_9_), channel_id=1, source_target_pairs={{0,48},{8,200},{16,0},{24,216},{32,16},{40,232},{48,32},{56,248},{... | collective-permute-start | bytes 2359304 | tf_op jit(solution)/shard_map/ppermute | solution.py:271
  54.6 0.9 copy-done.4
  55.5 5.2 %shard_map.69.refs_0_ = bf16[8,512,512]{2,1,0:T(8,128)(2,1)} custom-call(bf16[8,512,512]{2,1,0:T(8,128)(2,1)} %shard_map.68.refs_0_, bf16[256,1536]{1,0:T(8,128)(2,1)} %copy-done.2, bf16[256,1536]{1,0:T(8,128)(2,1)} %collective-permute-done.6.refs_2_.refs_5_, ...), custom_call_target="tpu_custom_call", output_to_operand_aliasing={{}: (0, {})} | custom-call | flops 1610612736 | bytes 4194304 | tf_op jit(solution)/shard_map/pallas_call | solution.py:185
  60.8 0.9 copy-done.5
  61.6 0.9 copy-done.6
  62.6 5.2 %shard_map.70.refs_0_ = bf16[8,512,512]{2,1,0:T(8,128)(2,1)} custom-call(bf16[8,512,512]{2,1,0:T(8,128)(2,1)} %shard_map.69.refs_0_, bf16[256,1536]{1,0:T(8,128)(2,1)} %collective-permute-done.13.refs_1_.refs_8_, bf16[256,1536]{1,0:T(8,128)(2,1)} %collective-permute-done.7.refs_2_.refs_9_, ...), custom_call_target="tpu_custom_call", output_to_operand_aliasing={{}: (0, {})} | custom-call | flops 1610612736 | bytes 4194304 | tf_op jit(solution)/shard_map/pallas_call | solution.py:185
  67.8 1.3 collective-permute-start.16
  69.1 0.1 collective-permute-start.17
  69.2 3.7 %shard_map.71.refs_0_ = bf16[8,512,512]{2,1,0:T(8,128)(2,1)} custom-call(bf16[8,512,512]{2,1,0:T(8,128)(2,1)} %shard_map.70.refs_0_, bf16[256,1536]{1,0:T(8,128)(2,1)} %collective-permute-done.2.refs_1_.refs_12_, bf16[256,1536]{1,0:T(8,128)(2,1)} %collective-permute-done.10.refs_2_.refs_13_, bf16[512,1536]{1,0:T(8,128)(2,1)} %refs_3_.3), custom_call_target="tpu_custom_call", output_to_operand_aliasing={{}: (0, {})} | custom-call | flops 805306368 | bytes 2097152 | tf_op jit(solution)/shard_map/pallas_call | solution.py:185
  72.9 0.9 copy-done.7
  73.8 0.9 copy-done.8
  74.7 3.7 %shard_map.72 = bf16[8,512,512]{2,1,0:T(8,128)(2,1)} custom-call(bf16[8,512,512]{2,1,0:T(8,128)(2,1)} %shard_map.71.refs_0_, bf16[256,1536]{1,0:T(8,128)(2,1)} %copy-done.7, bf16[256,1536]{1,0:T(8,128)(2,1)} %copy-done.8, bf16[512,1536]{1,0:T(8,128)(2,1)} %refs_3_.3), custom_call_target="tpu_custom_call", output_to_operand_aliasing={{}: (0, {})} | custom-call | flops 805306368 | bytes 2097152 | tf_op jit(solution)/shard_map/pallas_call | solution.py:185
  78.4 0.0 reduce-scatter.2.cloned.1.call-update
  78.5 13.6 %shard_map.74 = (bf16[32,128,512]{2,1,0:T(8,128)(2,1)}, f32[32,16,512]{2,1,0:T(8,128)}) custom-call(s32[1]{0:T(128)} %bitcast.3.place, bf16[8,128,2048]{2,1,0:T(8,128)(2,1)} %bitcast.8, bf16[256,256]{1,0:T(8,128)(2,1)} %constant.18.clone.table_ref), custom_call_target="tpu_custom_call" | custom-call | flops 4294967296 | bytes 8388608 | tf_op jit(solution)/shard_map/pallas_call | solution.py:131
  92.1 5.0 %all-to-all-start = ((bf16[32,128,512]{2,1,0:T(8,128)(2,1)}), bf16[32,128,512]{2,1,0:T(8,128)(2,1)}, u32[]{:S(2)}, u32[]{:S(2)}) async-start(bf16[32,128,512]{2,1,0:T(8,128)(2,1)} %get-tuple-element.22), calls=%async_computation.1 | async-start | bytes 8388608 | tf_op jit(solution)/shard_map/all_to_all | solution.py:377
  97.1 1.2 dynamic-slice_bitcast_fusion.sources
  98.3 35.3 %reduce-scatter.2.cloned.1.call-done = bf16[1,512,512]{2,1,0:T(8,128)(2,1)} async-done(((bf16[8,512,512]{2,1,0:T(8,128)(2,1)}), bf16[1,512,512]{2,1,0:T(8,128)(2,1)}) %reduce-scatter.2.cloned.1.call-update) | async-done | bytes 524304 | tf_op jit(solution)/shard_map/reduce_scatter | solution.py:375
  133.6 1.9 shard_map.73
  135.5 13.9 %all-to-all-done.quantized_ref = bf16[32,128,512]{2,1,0:T(8,128)(2,1)} async-done(((bf16[32,128,512]{2,1,0:T(8,128)(2,1)}), bf16[32,128,512]{2,1,0:T(8,128)(2,1)}, u32[]{:S(2)}, u32[]{:S(2)}) %all-to-all-start) | async-done | bytes 4194336 | tf_op jit(solution)/shard_map/all_to_all | solution.py:377
  149.3 18.8 %all_to_all.15.summed_ref = bf16[32,16,512]{2,1,0:T(8,128)(2,1)} all-to-all(bf16[32,16,512]{2,1,0:T(8,128)(2,1)} %shard_map.73), channel_id=1, replica_groups=mesh['dp'=32,'tensor'=8] {'dp'}, dimensions={0} | all-to-all | bytes 1048576 | tf_op jit(solution)/shard_map/all_to_all | solution.py:380
  168.2 2.7 %shard_map.75 = bf16[8,16,2048]{2,1,0:T(8,128)(2,1)} custom-call(bf16[32,16,512]{2,1,0:T(8,128)(2,1)} %all_to_all.15.summed_ref, f32[32,16,512]{2,1,0:T(8,128)} %get-tuple-element.24.slope_ref, bf16[256,256]{1,0:T(8,128)(2,1)} %constant.18.clone.table_ref), custom_call_target="tpu_custom_call" | custom-call | flops 536870912 | bytes 2097152 | tf_op jit(solution)/shard_map/pallas_call | solution.py:324
  170.8 7.9 %all-to-all-start.2 = ((bf16[8,16,2048]{2,1,0:T(8,128)(2,1)}), bf16[8,16,2048]{2,1,0:T(8,128)(2,1)S(1)}, u32[]{:S(2)}, u32[]{:S(2)}) async-start(bf16[8,16,2048]{2,1,0:T(8,128)(2,1)} %shard_map.75), calls=%async_computation.3 | async-start | bytes 1048576 | tf_op jit(solution)/shard_map/all_to_all | solution.py:382
  178.7 14.2 %shard_map.76 = f32[512,1536]{1,0:T(8,128)} custom-call(s32[32]{0:T(128)} %dynamic-slice_bitcast_fusion.sources, bf16[32,128,512]{2,1,0:T(8,128)(2,1)} %all-to-all-done.quantized_ref, bf16[256,1536]{1,0:T(8,128)(2,1)} %copy-done.1, bf16[256,1536]{1,0:T(8,128)(2,1)} %copy-done, bf16[256,1536]{1,0:T(8,128)(2,1)} %copy-done.3, ...), custom_call_target="tpu_custom_call" | custom-call | flops 6442450944 | bytes 19922944 | tf_op jit(solution)/shard_map/pallas_call | solution.py:239
  192.9 3.9 %all-to-all-done.2 = bf16[8,16,2048]{2,1,0:T(8,128)(2,1)S(1)} async-done(((bf16[8,16,2048]{2,1,0:T(8,128)(2,1)}), bf16[8,16,2048]{2,1,0:T(8,128)(2,1)S(1)}, u32[]{:S(2)}, u32[]{:S(2)}) %all-to-all-start.2) | async-done | bytes 524320 | tf_op jit(solution)/shard_map/all_to_all | solution.py:382
  196.8 0.8 copy.19
  (35 shorter events, 0.2 us)
Async XLA Ops:
  7.2 71.3 %all-gather.3.cloned.1.call-start = ((), (), s32[]{:S(2)}) async-start(), calls=%async_computation.5 | async-start | bytes 4718592 | tf_op jit(solution)/shard_map/all_gather | solution.py:343
  7.9 125.7 %reduce-scatter.2.cloned.1.call-start = ((), (), s32[]{:S(2)}) async-start(), calls=%async_computation.4 | async-start | bytes 4718592 | tf_op jit(solution)/shard_map/reduce_scatter | solution.py:375
  7.9 9.3 %collective-permute-start = (bf16[128,1536]{1,0:T(8,128)(2,1)}, bf16[128,1536]{1,0:T(8,128)(2,1)S(1)}, u32[]{:S(2)}, u32[]{:S(2)}) collective-permute-start(bf16[128,1536]{1,0:T(8,128)(2,1)} %param.7), channel_id=1, source_target_pairs={{0,64},{8,24},{16,80},{24,40},{32,96},{40,56},{48,112},{56,8},{64,... | collective-permute-start | bytes 1179656 | tf_op jit(solution)/shard_map/ppermute | solution.py:271
  10.1 11.7 %collective-permute-start.3 = (bf16[128,1536]{1,0:T(8,128)(2,1)}, bf16[128,1536]{1,0:T(8,128)(2,1)S(1)}, u32[]{:S(2)}, u32[]{:S(2)}) collective-permute-start(bf16[128,1536]{1,0:T(8,128)(2,1)} %param.7), channel_id=1, source_target_pairs={{0,192},{8,56},{16,208},{24,8},{32,224},{40,24},{48,240},{56,40},{... | collective-permute-start | bytes 1179656 | tf_op jit(solution)/shard_map/ppermute | solution.py:271
  17.3 18.7 %copy-start.1 = (bf16[256,1536]{1,0:T(8,128)(2,1)}, bf16[256,1536]{1,0:T(8,128)(2,1)S(1)}, u32[]{:S(2)}) copy-start(bf16[256,1536]{1,0:T(8,128)(2,1)S(1)} %constant_dynamic-update-slice_fusion.refs_0_) | copy-start | bytes 2359300
  17.3 15.4 %collective-permute-start.1 = (bf16[256,1536]{1,0:T(8,128)(2,1)S(1)}, bf16[256,1536]{1,0:T(8,128)(2,1)S(1)}, u32[]{:S(2)}, u32[]{:S(2)}) collective-permute-start(bf16[256,1536]{1,0:T(8,128)(2,1)S(1)} %constant_dynamic-update-slice_fusion.refs_0_), channel_id=1, source_target_pairs={{0,16},{8,72},{16,32},{24,88},{32,48},{40,104},{48,0},{56,120},{64... | collective-permute-start | bytes 2359304 | tf_op jit(solution)/shard_map/ppermute | solution.py:271
  18.3 14.9 %collective-permute-start.8 = (bf16[256,1536]{1,0:T(8,128)(2,1)S(1)}, bf16[256,1536]{1,0:T(8,128)(2,1)S(1)}, u32[]{:S(2)}, u32[]{:S(2)}) collective-permute-start(bf16[256,1536]{1,0:T(8,128)(2,1)S(1)} %constant_dynamic-update-slice_fusion.refs_0_), channel_id=1, source_target_pairs={{0,8},{8,0},{16,24},{24,16},{32,40},{40,32},{48,56},{56,48},{64,72... | collective-permute-start | bytes 2359304 | tf_op jit(solution)/shard_map/ppermute | solution.py:275
  20.7 8.3 %collective-permute-start.4 = (bf16[64,1536]{1,0:T(8,128)(2,1)S(1)}, bf16[64,1536]{1,0:T(8,128)(2,1)S(1)}, u32[]{:S(2)}, u32[]{:S(2)}) collective-permute-start(bf16[64,1536]{1,0:T(8,128)(2,1)S(1)} %slice.8), channel_id=1, source_target_pairs={{0,64},{8,24},{16,80},{24,40},{32,96},{40,56},{48,112},{56,8},{64,... | collective-permute-start | bytes 589832 | tf_op jit(solution)/shard_map/ppermute | solution.py:271
  21.8 7.2 %collective-permute-start.5 = (bf16[64,1536]{1,0:T(8,128)(2,1)S(1)}, bf16[64,1536]{1,0:T(8,128)(2,1)S(1)}, u32[]{:S(2)}, u32[]{:S(2)}) collective-permute-start(bf16[64,1536]{1,0:T(8,128)(2,1)S(1)} %slice.9), channel_id=1, source_target_pairs={{0,192},{8,56},{16,208},{24,8},{32,224},{40,24},{48,240},{56,40},{... | collective-permute-start | bytes 589832 | tf_op jit(solution)/shard_map/ppermute | solution.py:271
  29.1 6.9 %copy-start = (bf16[256,1536]{1,0:T(8,128)(2,1)}, bf16[256,1536]{1,0:T(8,128)(2,1)S(1)}, u32[]{:S(2)}) copy-start(bf16[256,1536]{1,0:T(8,128)(2,1)S(1)} %constant_dynamic-update-slice_fusion.2.refs_1_) | copy-start | bytes 2359300
  29.1 6.9 %collective-permute-start.9 = (bf16[256,1536]{1,0:T(8,128)(2,1)S(1)}, bf16[256,1536]{1,0:T(8,128)(2,1)}, u32[]{:S(2)}, u32[]{:S(2)}) collective-permute-start(bf16[256,1536]{1,0:T(8,128)(2,1)S(1)} %constant_dynamic-update-slice_fusion.2.refs_1_), channel_id=1, source_target_pairs={{0,8},{8,0},{16,24},{24,16},{32,40},{40,32},{48,56},{56,48},{64,72... | collective-permute-start | bytes 2359304 | tf_op jit(solution)/shard_map/ppermute | solution.py:275
  30.0 12.5 %collective-permute-start.6 = (bf16[256,1536]{1,0:T(8,128)(2,1)S(1)}, bf16[256,1536]{1,0:T(8,128)(2,1)}, u32[]{:S(2)}, u32[]{:S(2)}) collective-permute-start(bf16[256,1536]{1,0:T(8,128)(2,1)S(1)} %constant_dynamic-update-slice_fusion.2.refs_1_), channel_id=1, source_target_pairs={{0,16},{8,72},{16,32},{24,88},{32,48},{40,104},{48,0},{56,120},{64... | collective-permute-start | bytes 2359304 | tf_op jit(solution)/shard_map/ppermute | solution.py:271
  30.0 12.5 %collective-permute-start.7 = (bf16[256,1536]{1,0:T(8,128)(2,1)S(1)}, bf16[256,1536]{1,0:T(8,128)(2,1)}, u32[]{:S(2)}, u32[]{:S(2)}) collective-permute-start(bf16[256,1536]{1,0:T(8,128)(2,1)S(1)} %constant_dynamic-update-slice_fusion.2.refs_1_), channel_id=1, source_target_pairs={{0,48},{8,200},{16,0},{24,216},{32,16},{40,232},{48,32},{56,248},{... | collective-permute-start | bytes 2359304 | tf_op jit(solution)/shard_map/ppermute | solution.py:271
  32.7 19.2 %copy-start.2 = (bf16[256,1536]{1,0:T(8,128)(2,1)}, bf16[256,1536]{1,0:T(8,128)(2,1)S(1)}, u32[]{:S(2)}) copy-start(bf16[256,1536]{1,0:T(8,128)(2,1)S(1)} %collective-permute-done.1.refs_1_.refs_4_) | copy-start | bytes 2359300
  32.7 17.4 %collective-permute-start.13 = (bf16[256,1536]{1,0:T(8,128)(2,1)S(1)}, bf16[256,1536]{1,0:T(8,128)(2,1)}, u32[]{:S(2)}, u32[]{:S(2)}) collective-permute-start(bf16[256,1536]{1,0:T(8,128)(2,1)S(1)} %constant_dynamic-update-slice_fusion.refs_0_), channel_id=1, source_target_pairs={{0,48},{8,200},{16,0},{24,216},{32,16},{40,232},{48,32},{56,248},{... | collective-permute-start | bytes 2359304 | tf_op jit(solution)/shard_map/ppermute | solution.py:271
  33.2 2.8 %copy-start.3 = (bf16[256,1536]{1,0:T(8,128)(2,1)}, bf16[256,1536]{1,0:T(8,128)(2,1)S(1)}, u32[]{:S(2)}) copy-start(bf16[256,1536]{1,0:T(8,128)(2,1)S(1)} %collective-permute-done.8.refs_2_) | copy-start | bytes 2359300
  33.2 18.7 %collective-permute-start.11 = (bf16[256,1536]{1,0:T(8,128)(2,1)S(1)}, bf16[256,1536]{1,0:T(8,128)(2,1)}, u32[]{:S(2)}, u32[]{:S(2)}) collective-permute-start(bf16[256,1536]{1,0:T(8,128)(2,1)S(1)} %collective-permute-done.1.refs_1_.refs_4_), channel_id=1, source_target_pairs={{0,8},{8,0},{16,24},{24,16},{32,40},{40,32},{48,56},{56,48},{64,72... | collective-permute-start | bytes 2359304 | tf_op jit(solution)/shard_map/ppermute | solution.py:275
  42.4 12.2 %collective-permute-start.12 = (bf16[256,1536]{1,0:T(8,128)(2,1)}, bf16[256,1536]{1,0:T(8,128)(2,1)S(1)}, u32[]{:S(2)}, u32[]{:S(2)}) collective-permute-start(bf16[256,1536]{1,0:T(8,128)(2,1)} %collective-permute-done.6.refs_2_.refs_5_), channel_id=1, source_target_pairs={{0,8},{8,0},{16,24},{24,16},{32,40},{40,32},{48,56},{56,48},{64,72... | collective-permute-start | bytes 2359304 | tf_op jit(solution)/shard_map/ppermute | solution.py:275
  50.0 10.7 %collective-permute-start.14 = (bf16[256,1536]{1,0:T(8,128)(2,1)}, bf16[256,1536]{1,0:T(8,128)(2,1)S(1)}, u32[]{:S(2)}, u32[]{:S(2)}) collective-permute-start(bf16[256,1536]{1,0:T(8,128)(2,1)} %collective-permute-done.13.refs_1_.refs_8_), channel_id=1, source_target_pairs={{0,8},{8,0},{16,24},{24,16},{32,40},{40,32},{48,56},{56,48},{64,72... | collective-permute-start | bytes 2359304 | tf_op jit(solution)/shard_map/ppermute | solution.py:275
  51.9 8.8 %collective-permute-start.15 = (bf16[256,1536]{1,0:T(8,128)(2,1)}, bf16[256,1536]{1,0:T(8,128)(2,1)S(1)}, u32[]{:S(2)}, u32[]{:S(2)}) collective-permute-start(bf16[256,1536]{1,0:T(8,128)(2,1)} %collective-permute-done.7.refs_2_.refs_9_), channel_id=1, source_target_pairs={{0,8},{8,0},{16,24},{24,16},{32,40},{40,32},{48,56},{56,48},{64,72... | collective-permute-start | bytes 2359304 | tf_op jit(solution)/shard_map/ppermute | solution.py:275
  51.9 15.8 %collective-permute-start.2 = (bf16[256,1536]{1,0:T(8,128)(2,1)S(1)}, bf16[256,1536]{1,0:T(8,128)(2,1)}, u32[]{:S(2)}, u32[]{:S(2)}) collective-permute-start(bf16[256,1536]{1,0:T(8,128)(2,1)S(1)} %collective-permute-done.1.refs_1_.refs_4_), channel_id=1, source_target_pairs={{0,16},{8,72},{16,32},{24,88},{32,48},{40,104},{48,0},{56,120},{64... | collective-permute-start | bytes 2359304 | tf_op jit(solution)/shard_map/ppermute | solution.py:271
  51.9 15.8 %collective-permute-start.10 = (bf16[256,1536]{1,0:T(8,128)(2,1)}, bf16[256,1536]{1,0:T(8,128)(2,1)}, u32[]{:S(2)}, u32[]{:S(2)}) collective-permute-start(bf16[256,1536]{1,0:T(8,128)(2,1)} %collective-permute-done.7.refs_2_.refs_9_), channel_id=1, source_target_pairs={{0,48},{8,200},{16,0},{24,216},{32,16},{40,232},{48,32},{56,248},{... | collective-permute-start | bytes 2359304 | tf_op jit(solution)/shard_map/ppermute | solution.py:271
  54.6 0.9 copy-start.4
  60.7 0.9 copy-start.5
  61.6 0.9 copy-start.6
  67.8 5.1 %collective-permute-start.16 = (bf16[256,1536]{1,0:T(8,128)(2,1)}, bf16[256,1536]{1,0:T(8,128)(2,1)S(1)}, u32[]{:S(2)}, u32[]{:S(2)}) collective-permute-start(bf16[256,1536]{1,0:T(8,128)(2,1)} %collective-permute-done.2.refs_1_.refs_12_), channel_id=1, source_target_pairs={{0,8},{8,0},{16,24},{24,16},{32,40},{40,32},{48,56},{56,48},{64,72... | collective-permute-start | bytes 2359304 | tf_op jit(solution)/shard_map/ppermute | solution.py:275
  69.1 3.8 %collective-permute-start.17 = (bf16[256,1536]{1,0:T(8,128)(2,1)}, bf16[256,1536]{1,0:T(8,128)(2,1)S(1)}, u32[]{:S(2)}, u32[]{:S(2)}) collective-permute-start(bf16[256,1536]{1,0:T(8,128)(2,1)} %collective-permute-done.10.refs_2_.refs_13_), channel_id=1, source_target_pairs={{0,8},{8,0},{16,24},{24,16},{32,40},{40,32},{48,56},{56,48},{64,72... | collective-permute-start | bytes 2359304 | tf_op jit(solution)/shard_map/ppermute | solution.py:275
  72.9 0.9 copy-start.7
  73.8 0.9 copy-start.8
  92.1 57.2 %all-to-all-start = ((bf16[32,128,512]{2,1,0:T(8,128)(2,1)}), bf16[32,128,512]{2,1,0:T(8,128)(2,1)}, u32[]{:S(2)}, u32[]{:S(2)}) async-start(bf16[32,128,512]{2,1,0:T(8,128)(2,1)} %get-tuple-element.22), calls=%async_computation.1 | async-start | bytes 8388608 | tf_op jit(solution)/shard_map/all_to_all | solution.py:377
  170.8 26.0 %all-to-all-start.2 = ((bf16[8,16,2048]{2,1,0:T(8,128)(2,1)}), bf16[8,16,2048]{2,1,0:T(8,128)(2,1)S(1)}, u32[]{:S(2)}, u32[]{:S(2)}) async-start(bf16[8,16,2048]{2,1,0:T(8,128)(2,1)} %shard_map.75), calls=%async_computation.3 | async-start | bytes 1048576 | tf_op jit(solution)/shard_map/all_to_all | solution.py:382
Sparse Core Ops, SparseCore 0:
  9.8 58.6 all-gather.2
  78.6 54.9 reduce-scatter.1

commit v8 on v7

v8 whole, which is shorter than its diff:
```python
import functools
import math

import jax
import jax.numpy as jnp
import numpy as np
from jax import lax
from jax.experimental import pallas as pl
from jax.experimental.pallas import tpu as pltpu
from jax.sharding import PartitionSpec as P

BLOCK = 1024
WIDTH = 16384
TABLE = 256
LANES = 128
VMEM_BYTES = 60 * 1024 * 1024
NORM = 1.0 / math.sqrt(WIDTH)
SIDE = 4
STEP = 16
OFFSETS = (0, -1, 1, -2)

levels = 127.0
ripple = 0.5
epsilon = 1e-06


def hadamard_table(length):
    table = np.ones((1, 1), np.float32)
    while table.shape[0] < length:
        table = np.block([[table, table], [table, -table]])
    return jnp.asarray(table, jnp.bfloat16)


def fit(odd, terms):
    nodes = 0.5 * np.cos(np.pi * (np.arange(400) + 0.5) / 800.0)
    squares = nodes * nodes
    values = np.sin(2.0 * np.pi * nodes) / nodes if odd else np.cos(2.0 * np.pi * nodes)
    scaled = np.polynomial.chebyshev.Chebyshev.fit(squares, values, terms - 1, domain=[0.0, 0.25])
    return [float(c) for c in scaled.convert(kind=np.polynomial.Polynomial).coef]


SINE = fit(True, 6)
COSINE = fit(False, 7)


def horner(coefficients, square):
    total = jnp.full_like(square, coefficients[-1])
    for coefficient in coefficients[-2::-1]:
        total = total * square + coefficient
    return total


def butterfly(parts):
    distance = 1
    while distance < len(parts):
        mixed = list(parts)
        for low in range(len(parts)):
            if not low & distance:
                mixed[low] = parts[low] + parts[low | distance]
                mixed[low | distance] = parts[low] - parts[low | distance]
        parts = mixed
        distance *= 2
    return parts


def levels_of(largest):
    rows = largest.shape[0]
    peak = jnp.max(largest, axis=1, keepdims=True) * NORM
    scale = (peak + epsilon) / levels
    inverse = jnp.broadcast_to(NORM / scale, (rows, LANES))
    depth = jnp.broadcast_to((ripple / (2.0 * math.pi)) * scale, (rows, LANES))
    return inverse, depth


def remainder(value, inverse):
    turns = value * inverse
    return turns - jnp.round(turns)


def quantized_of(value, inverse, depth):
    rest = remainder(value, inverse)
    return value * NORM - depth * (rest * horner(SINE, rest * rest))


def slope_of(value, inverse):
    rest = remainder(value, inverse)
    return 1.0 - ripple * horner(COSINE, rest * rest)


def quantize_kernel(place, rows_ref, table_ref, quantized_ref, slope_ref, inner, mixed):
    members, count, features = rows_ref.shape
    own, width = slope_ref.shape[1:]
    chunks, per_shard, per_width = features // TABLE, features // width, width // TABLE
    rows = rows_ref[...].reshape(members * count, features)
    for c in range(chunks):
        inner[c] = jnp.dot(
            rows[:, c * TABLE : (c + 1) * TABLE],
            table_ref[...],
            preferred_element_type=jnp.float32,
        )
    halves = [slice(l * LANES, (l + 1) * LANES) for l in range(TABLE // LANES)]
    for group in range(count // STEP):
        spans = [
            slice(t * count + group * STEP, t * count + (group + 1) * STEP)
            for t in range(members)
        ]
        here = slice(group * STEP, (group + 1) * STEP)
        for span in spans:
            for lanes in halves:
                parts = butterfly([inner[c, span, lanes] for c in range(chunks)])
                for c in range(chunks):
                    inner[c, span, lanes] = parts[c]
        largest = jnp.zeros((STEP, LANES), jnp.float32)
        for c in range(chunks):
            for lanes in halves:
                parts = butterfly([inner[c, span, lanes] for span in spans])
                for span, part in zip(spans, parts):
                    mixed[c, span, lanes] = part
                    largest = jnp.maximum(largest, jnp.abs(part))
        inverse, depth = levels_of(largest)

        def places():
            for t, span in enumerate(spans):
                for c in range(chunks):
                    for l, lanes in enumerate(halves):
                        start = (c % per_width) * TABLE + l * LANES
                        yield t * per_shard + c // per_width, start, (c, span, lanes)

        for block, start, index in places():
            quantized_ref[block, here, start : start + LANES] = quantized_of(
                mixed[index], inverse, depth
            ).astype(jnp.bfloat16)

        for part in range(STEP // own):
            mine = slice(part * own, (part + 1) * own)
            number = (pl.program_id(0) * (count // STEP) + group) * (STEP // own) + part

            @pl.when(number == place[0])
            def _():
                for block, start, (c, span, lanes) in places():
                    slope_ref[block, :, start : start + LANES] = slope_of(
                        mixed[c, span.start + mine.start : span.start + mine.stop, lanes],
                        inverse[mine],
                    )


def quantize(rows, table, place, dp, width):
    members, tokens, features = rows.shape
    own = tokens // members
    count = 2 * STEP
    return pl.pallas_call(
        quantize_kernel,
        grid_spec=pltpu.PrefetchScalarGridSpec(
            num_scalar_prefetch=1,
            grid=(tokens // count,),
            in_specs=[
                pl.BlockSpec((members, count, features), lambda i, place: (0, i, 0)),
                pl.BlockSpec((TABLE, TABLE), lambda i, place: (0, 0)),
            ],
            out_specs=[
                pl.BlockSpec((dp, count, width), lambda i, place: (0, i, 0)),
                pl.BlockSpec((dp, own, width), lambda i, place: (0, 0, 0)),
            ],
            scratch_shapes=[
                pltpu.VMEM((features // TABLE, members * count, TABLE), jnp.float32),
                pltpu.VMEM((features // TABLE, members * count, TABLE), jnp.float32),
            ],
        ),
        out_shape=[
            jax.ShapeDtypeStruct((dp, tokens, width), jnp.bfloat16),
            jax.ShapeDtypeStruct((dp, own, width), jnp.float32),
        ],
        compiler_params=pltpu.CompilerParams(vmem_limit_bytes=VMEM_BYTES),
        cost_estimate=pl.CostEstimate(
            flops=2 * tokens * WIDTH * BLOCK, bytes_accessed=4 * tokens * WIDTH, transcendentals=0
        ),
    )(place, rows, table)


def quantize_own_kernel(rows_ref, table_ref, quantized_ref, slope_ref, inner):
    devices, own, width = slope_ref.shape
    features = rows_ref.shape[1]
    members = rows_ref.shape[0] // own
    chunks, per_width = features // TABLE, width // TABLE
    for c in range(chunks):
        inner[c] = jnp.dot(
            rows_ref[:, c * TABLE : (c + 1) * TABLE],
            table_ref[...],
            preferred_element_type=jnp.float32,
        )
    halves = [slice(l * LANES, (l + 1) * LANES) for l in range(TABLE // LANES)]
    spans = [slice(t * own, (t + 1) * own) for t in range(members)]
    for span in spans:
        for lanes in halves:
            parts = butterfly([inner[c, span, lanes] for c in range(chunks)])
            for c in range(chunks):
                inner[c, span, lanes] = parts[c]
    largest = jnp.zeros((own, LANES), jnp.float32)
    for c in range(chunks):
        for lanes in halves:
            parts = butterfly([inner[c, span, lanes] for span in spans])
            for span, part in zip(spans, parts):
                inner[c, span, lanes] = part
                largest = jnp.maximum(largest, jnp.abs(part))
    inverse, depth = levels_of(largest)
    per_shard = devices // members
    for pair in range(devices // 2):
        for k in range(per_width):
            for l, lanes in enumerate(halves):
                columns = slice(k * TABLE + l * LANES, k * TABLE + (l + 1) * LANES)
                found = []
                for block in (2 * pair, 2 * pair + 1):
                    t, c = block // per_shard, block % per_shard * per_width + k
                    value = inner[c, spans[t], lanes]
                    found.append(quantized_of(value, inverse, depth))
                    slope_ref[block, :, columns] = slope_of(value, inverse)
                quantized_ref[pair * 2 * own : (pair + 1) * 2 * own, columns] = jnp.concatenate(
                    found, axis=0
                ).astype(jnp.bfloat16)


def quantize_own(rows, table, dp, width):
    members, own, features = rows.shape
    return pl.pallas_call(
        quantize_own_kernel,
        out_shape=[
            jax.ShapeDtypeStruct((dp * own, width), jnp.bfloat16),
            jax.ShapeDtypeStruct((dp, own, width), jnp.float32),
        ],
        scratch_shapes=[pltpu.VMEM((features // TABLE, members * own, TABLE), jnp.float32)],
        compiler_params=pltpu.CompilerParams(vmem_limit_bytes=VMEM_BYTES),
        cost_estimate=pl.CostEstimate(
            flops=2 * own * WIDTH * BLOCK, bytes_accessed=8 * own * WIDTH, transcendentals=0
        ),
    )(rows.reshape(members * own, features), table)


def product_kernel(count, slots, sources, *refs):
    pieces, weight_ref = refs[:count], refs[count]
    out_ref, weight, rows, results, weight_sem, in_sems, out_sems = refs[-7:]
    members = out_ref.shape[0]
    load_weight = pltpu.make_async_copy(weight_ref, weight, weight_sem)
    load_weight.start()
    loads = [pltpu.make_async_copy(pieces[n], rows.at[n], in_sems.at[n]) for n in range(count)]
    for load in loads:
        load.start()
    load_weight.wait()
    stores = []
    for n in range(count):
        loads[n].wait()
        product = lax.dot_general(
            rows[n], weight[...], (((1,), (1,)), ((), ())), preferred_element_type=jnp.float32
        )
        for k in range(2):
            for t in range(members):
                starts = [k * 16 * members + half * 8 * members + t * 8 for half in range(2)]
                results[n, k, t] = jnp.concatenate(
                    [product[start : start + 8] for start in starts], axis=0
                ).astype(results.dtype)
            place = pl.multiple_of(sources[slots[n] + k] * STEP, STEP)
            store = pltpu.make_async_copy(
                results.at[n, k], out_ref.at[:, pl.ds(place, STEP), :], out_sems.at[n, k]
            )
            store.start()
            stores.append(store)
    for store in stores:
        store.wait()


def product(held, pieces, slots, weight, sources, members, total):
    count, rows = len(pieces), pieces[0].shape[0]
    width, depth = weight.shape
    earlier = [] if held is None else [held]
    return pl.pallas_call(
        functools.partial(product_kernel, count, slots),
        in_specs=[pl.BlockSpec(memory_space=pltpu.SMEM)]
        + [pl.BlockSpec(memory_space=pl.ANY)] * (count + 1 + len(earlier)),
        out_specs=pl.BlockSpec(memory_space=pl.ANY),
        out_shape=jax.ShapeDtypeStruct((members, total // members, width), jnp.bfloat16),
        scratch_shapes=[
            pltpu.VMEM((width, depth), jnp.bfloat16),
            pltpu.VMEM((count, rows, depth), jnp.bfloat16),
            pltpu.VMEM((count, 2, members, STEP, width), jnp.bfloat16),
            pltpu.SemaphoreType.DMA,
            pltpu.SemaphoreType.DMA((count,)),
            pltpu.SemaphoreType.DMA((count, 2)),
        ],
        input_output_aliases={count + 2: 0} if earlier else {},
        compiler_params=pltpu.CompilerParams(vmem_limit_bytes=VMEM_BYTES),
        cost_estimate=pl.CostEstimate(
            flops=2 * count * rows * depth * width,
            bytes_accessed=2 * count * rows * (depth + width),
            transcendentals=0,
        ),
    )(sources, *pieces, weight, *earlier)


def gradient_kernel(half, held, sources, quantized_ref, *refs):
    out_ref = refs[-1]
    pieces = refs[1:-1] if held else refs[:-1]
    tokens = quantized_ref.shape[1]
    total = refs[0][...] if held else None
    slot = 0
    for first in range(0, len(pieces), 2):
        pair = pieces[first : first + 2]
        rows, block = [], []
        for piece_ref in pair:
            for k in range(piece_ref.shape[0] // (2 * tokens)):
                start = (2 * k + half) * tokens
                rows.append(piece_ref[start : start + tokens, :])
                block.append(quantized_ref[sources[slot]])
                slot += 1
        term = lax.dot_general(
            jnp.concatenate(block, axis=0),
            jnp.concatenate(rows, axis=0),
            (((0,), (0,)), ((), ())),
            preferred_element_type=jnp.float32,
        )
        total = term if total is None else total + term
    out_ref[...] = total


def gradient(held, half, sources, quantized, pieces):
    width, depth = quantized.shape[2], pieces[0].shape[1]
    rows = sum(piece.shape[0] for piece in pieces) // 2
    earlier = [] if held is None else [held]
    return pl.pallas_call(
        functools.partial(gradient_kernel, half, bool(earlier)),
        in_specs=[pl.BlockSpec(memory_space=pltpu.SMEM)]
        + [pl.BlockSpec(memory_space=pltpu.VMEM)] * (len(pieces) + 1 + len(earlier)),
        out_specs=pl.BlockSpec(memory_space=pltpu.VMEM),
        out_shape=jax.ShapeDtypeStruct((width, depth), jnp.float32),
        compiler_params=pltpu.CompilerParams(vmem_limit_bytes=VMEM_BYTES),
        cost_estimate=pl.CostEstimate(
            flops=2 * rows * depth * width,
            bytes_accessed=2 * rows * (depth + width) + 4 * width * depth,
            transcendentals=0,
        ),
    )(sources, quantized, *earlier, *pieces)


def chip_core(x, y, core):
    return (x % SIDE * SIDE + y % SIDE) * 2 + core


def route(turn, sign):
    pairs = []
    for x in range(SIDE):
        for y in range(SIDE):
            for core in range(2):
                along = (sign, 0) if core == turn else (0, sign)
                pairs.append(
                    (chip_core(x, y, core), chip_core(x + along[0], y + along[1], core))
                )
    return pairs


def send(block, turn, sign):
    return lax.ppermute(block, "dp", route(turn, sign))


def other_core(block):
    return lax.ppermute(block, "dp", [(d, d ^ 1) for d in range(2 * SIDE * SIDE)])


def sources_table():
    table = []
    for x in range(SIDE):
        for y in range(SIDE):
            for core in range(2):
                found = []
                for outer in OFFSETS:
                    for sender in (core, 1 - core):
                        for inner in OFFSETS:
                            along = (inner, outer) if sender == 0 else (outer, inner)
                            found.append(chip_core(x + along[0], y + along[1], sender))
                table.append(found)
    return np.asarray(table, np.int32)


def finish_kernel(summed_ref, early_ref, late_ref, table_ref, out_ref, inner):
    devices, step, width = summed_ref.shape
    members, per_width = out_ref.shape[0], width // TABLE
    per_shard = devices // members
    slope = jnp.concatenate([early_ref[...], late_ref[...]], axis=1)
    upstream = (summed_ref[...].astype(jnp.float32) * slope).astype(jnp.bfloat16)
    upstream = upstream.reshape(devices * step, width)
    for c in range(per_width):
        inner[c] = jnp.dot(
            upstream[:, c * TABLE : (c + 1) * TABLE],
            table_ref[...],
            preferred_element_type=jnp.float32,
        )
    span = lambda d: slice(d * step, (d + 1) * step)
    for l in range(TABLE // LANES):
        lanes = slice(l * LANES, (l + 1) * LANES)
        for t in range(members):
            near = [(c, span(t * per_shard + k)) for k in range(per_shard) for c in range(per_width)]
            parts = butterfly([inner[c, rows, lanes] for c, rows in near])
            for (c, rows), part in zip(near, parts):
                inner[c, rows, lanes] = part
        for k in range(per_shard):
            for c in range(per_width):
                far = [span(t * per_shard + k) for t in range(members)]
                parts = butterfly([inner[c, rows, lanes] for rows in far])
                start = (k * per_width + c) * TABLE + l * LANES
                for t in range(members):
                    out_ref[t, :, start : start + LANES] = (parts[t] * NORM).astype(out_ref.dtype)


def finish(summed, slopes, table, members):
    devices, step, width = summed.shape
    return pl.pallas_call(
        finish_kernel,
        out_shape=jax.ShapeDtypeStruct((members, step, WIDTH // members), jnp.bfloat16),
        scratch_shapes=[pltpu.VMEM((width // TABLE, devices * step, TABLE), jnp.float32)],
        compiler_params=pltpu.CompilerParams(vmem_limit_bytes=VMEM_BYTES),
        cost_estimate=pl.CostEstimate(
            flops=2 * step * WIDTH * BLOCK, bytes_accessed=8 * step * WIDTH, transcendentals=0
        ),
    )(summed, *slopes, table)


def shards(activations, weight, grad_out):
    dp = lax.axis_size("dp")
    members = lax.axis_size("tensor")
    tokens, features = activations.shape
    width = weight.shape[0]
    place = lax.axis_index("tensor").astype(jnp.int32).reshape(1)
    sources = jnp.asarray(sources_table())[lax.axis_index("dp")]
    table = hadamard_table(TABLE)
    total = dp * tokens
    own, half = STEP // 2, tokens // 2
    early_rows, late_rows = jnp.moveaxis(activations.reshape(members, 2, own, features), 1, 0)
    grad_out = jnp.moveaxis(grad_out.reshape(members, 2, own, -1), 1, 0).reshape(tokens, -1)
    early_rows, late_rows, grad_out = lax.optimization_barrier((early_rows, late_rows, grad_out))
    wide_rows = lax.all_gather(early_rows.reshape(half, features), "tensor", axis=0, tiled=False)
    late_rows = lax.all_to_all(late_rows, "tensor", split_axis=0, concat_axis=0, tiled=True)

    def multiply(held, pieces, slot):
        slots = [slot + 2 * n for n in range(len(pieces))]
        return product(held, pieces, slots, weight, sources, members, total)

    below, above = send(grad_out, 0, 1), send(grad_out, 0, -1)
    top = jnp.concatenate([grad_out, below], axis=0)
    below_top, above_top = send(top, 1, 1), send(top, 1, -1)
    far = [send(below[:half], 0, 1), send(above[half:], 0, -1)]
    bottom = jnp.concatenate([above, *far], axis=0)
    below_bottom, above_bottom = send(bottom, 1, 1), send(bottom, 1, -1)
    far_top = send(below_top, 1, 1)
    near = [top, bottom]
    near_other = [other_core(block) for block in near]
    held = multiply(None, near + near_other, 0)
    below_bottom, above_bottom, held = lax.optimization_barrier(
        (below_bottom, above_bottom, held)
    )
    far_bottom = send(above_bottom, 1, -1)
    below, above = [below_top, below_bottom], [above_top, above_bottom]
    below_other = [other_core(block) for block in below]
    above_other = [other_core(block) for block in above]
    held = multiply(held, below + below_other, 8)
    held = multiply(held, above + above_other, 16)
    late, late_slope = quantize_own(late_rows, table, dp, width)
    far_top, far_bottom, held, late = lax.optimization_barrier(
        (far_top, far_bottom, held, late)
    )
    far = [far_top, far_bottom]
    far_other = [other_core(block) for block in far]
    held = multiply(held, far, 24)
    partial_rows = multiply(held, far_other, 28)
    q_own = lax.all_to_all(
        late.reshape(dp, own, width), "dp", split_axis=0, concat_axis=0, tiled=True
    )
    partial_rows, wide_rows = lax.optimization_barrier((partial_rows, wide_rows))
    summed = lax.psum_scatter(partial_rows, "tensor", scatter_dimension=0, tiled=False)
    early, early_slope = quantize(wide_rows, table, place, dp, width)
    q_early = lax.all_to_all(early, "dp", split_axis=0, concat_axis=0, tiled=True)
    summed, q_early, q_own = lax.optimization_barrier((summed, q_early, q_own))
    homed = lax.all_to_all(
        summed.reshape(dp, STEP, width), "dp", split_axis=0, concat_axis=0, tiled=True
    )
    q_late = lax.all_gather(q_own, "tensor", axis=1, tiled=True)
    mixed = finish(homed, (early_slope, late_slope), table, members)
    grad_input = lax.all_to_all(mixed, "tensor", split_axis=0, concat_axis=0, tiled=True)
    arrived = near + near_other + below + below_other + above + above_other + far + far_other
    weight_sum = gradient(None, 0, sources, q_early, arrived)
    weight_sum = gradient(weight_sum, 1, sources, q_late, arrived)
    return (grad_input.reshape(tokens, features), weight_sum)


def solution(mesh):
    return jax.shard_map(
        shards,
        mesh=mesh,
        in_specs=(P("dp", "tensor"), P("dp", "tensor"), P("dp", "tensor")),
        out_specs=(P("dp", "tensor"), P("dp", "tensor")),
        check_vma=False,
    )
```

time: 205 us -> 226 us (1.10)
  blocking collectives: 18.8 us -> 72.3 us
  waiting for transfers between devices: 70.4 us -> 29.5 us
  Pallas kernels: 55.4 us -> 62 us
  local copies, waits for them, and re-layouts: 7.73 us -> 12.9 us
  starting transfers between devices: 37.9 us -> 33.4 us
    all_to_all x1 -> x3, blocking collectives: 18.8 us -> 72.3 us  [the longest x1 34.9 us: shards(): lax.all_to_all(early, 'dp', split_axis=0, concat_axis=0, tiled=True)]
    reduce_scatter x1, waiting for transfers between devices: 35.3 us -> 0.16 us  [shards(): lax.psum_scatter(partial_rows, 'tensor', scatter_dimension=0, tiled=False)]
    all_to_all x1, waiting for transfers between devices: 13.9 us -> 0.96 us  [shards(): lax.all_to_all(late.reshape(dp, own, width), 'dp', split_axis=0, concat_a...]
    pallas_call x7 -> x8, Pallas kernels: 39.1 us -> 51.3 us  [the longest x5 26.7 us: product(): pl.pallas_call(functools.partial(product_kernel, count, slots), in_specs=...]
    all_to_all x1, waiting for transfers between devices: 3.88 us -> 12.6 us  [shards(): lax.all_to_all(mixed, 'tensor', split_axis=0, concat_axis=0, tiled=True)]
    pallas_call x1, Pallas kernels: 13.6 us -> 7.97 us  [quantize(): pl.pallas_call(quantize_kernel, grid_spec=pltpu.PrefetchScalarGridSpec(nu...]
    all_to_all x1, starting transfers between devices: 7.91 us -> 4.06 us  [shards(): lax.all_to_all(mixed, 'tensor', split_axis=0, concat_axis=0, tiled=True)]
    unnamed x22 -> x28, local copies, waits for them, and re-layouts: 6.44 us -> 7.76 us
  transfers between devices with their start and end apart: 22 -> 23, of which waited for: 7 -> 6; matrix products, arithmetic and copies ran while one was open for 1% -> 1% of each run, Pallas kernels for 26% -> 23%
where the time goes in v8:
time: 226 us; the launch traced here: 224 us
  blocking collectives  72.3 us (32%)
  Pallas kernels  62 us (27%)
  starting transfers between devices  33.4 us (15%)
  waiting for transfers between devices  29.5 us (13%)
  between operations  14 us (6%)
  local copies, waits for them, and re-layouts  12.9 us (6%)
    all_to_all x1, blocking collectives, shards(): lax.all_to_all(early, 'dp', split_axis=0, concat_axis=0, tiled=True)  34.9 us
    pallas_call x5, Pallas kernels, product(): pl.pallas_call(functools.partial(product_kernel, count, slots), in_specs=...  26.7 us
    pallas_call x2, Pallas kernels, gradient(): pl.pallas_call(functools.partial(gradient_kernel, half, bool(earlier)), i...  21.6 us
    all_to_all x1, blocking collectives, shards(): lax.all_to_all(summed.reshape(dp, STEP, width), 'dp', split_axis=0, conca...  19.2 us
    all_to_all x1, blocking collectives, shards(): lax.all_to_all(late_rows, 'tensor', split_axis=0, concat_axis=0, tiled=True)  18.2 us
    ppermute x10, waiting for transfers between devices, send(): return lax.ppermute(block, 'dp', route(turn, sign))  15.6 us
    ppermute x10, starting transfers between devices, send(): return lax.ppermute(block, 'dp', route(turn, sign))  13.3 us
    all_to_all x1, waiting for transfers between devices, shards(): lax.all_to_all(mixed, 'tensor', split_axis=0, concat_axis=0, tiled=True)  12.6 us
  transfers between devices with their start and end apart: 23, of which 6 were waited for; matrix products, arithmetic and copies ran while one was open for 1% of the time, Pallas kernels for 23%

profile of v8, /device:TPU:1, one launch (start us, length us, event | category | flops | bytes accessed | tf_op | source)
XLA Modules:
  0.0 224.0 jit_solution(11557508371589712509)
XLA Ops:
  7.2 1.1 copy.16
  8.3 0.7 slice_bitcast_fusion
  9.0 1.0 copy.14
  10.1 2.2 collective-permute-start
  12.3 1.5 collective-permute-start.3
  13.9 5.3 %collective-permute-done = bf16[128,1536]{1,0:T(8,128)(2,1)S(1)} collective-permute-done((bf16[128,1536]{1,0:T(8,128)(2,1)S(1)}, bf16[128,1536]{1,0:T(8,128)(2,1)S(1)}, u32[]{:S(2)}, u32[]{:S(2)}) %collective-permute-start) | collective-permute-done | bytes 393248 | tf_op jit(solution)/shard_map/ppermute | solution.py:359
  19.2 0.7 copy-done.11
  19.9 1.0 collective-permute-start.1
  20.9 2.4 %collective-permute-start.8 = (bf16[256,1536]{1,0:T(8,128)(2,1)S(1)}, bf16[256,1536]{1,0:T(8,128)(2,1)S(1)}, u32[]{:S(2)}, u32[]{:S(2)}) collective-permute-start(bf16[256,1536]{1,0:T(8,128)(2,1)S(1)} %constant_dynamic-update-slice_fusion.refs_0_.refs_1_), channel_id=1, source_target_pairs={{0,8},{8,0},{16,24},{24,16},{32,40},{40,32},{48,56},{56,48},{64,72... | collective-permute-start | bytes 2359304 | tf_op jit(solution)/shard_map/ppermute | solution.py:363
  23.3 0.9 slice.8
  24.3 1.1 collective-permute-start.4
  25.4 0.7 copy-done.10
  26.1 1.8 collective-permute-start.5
  28.0 1.0 constant_dynamic-update-slice_fusion.4
  29.0 3.7 %collective-permute-done.4 = bf16[64,1536]{1,0:T(8,128)(2,1)S(1)} collective-permute-done((bf16[64,1536]{1,0:T(8,128)(2,1)S(1)}, bf16[64,1536]{1,0:T(8,128)(2,1)S(1)}, u32[]{:S(2)}, u32[]{:S(2)}) %collective-permute-start.4) | collective-permute-done | bytes 196640 | tf_op jit(solution)/shard_map/ppermute | solution.py:359
  32.8 0.8 collective-permute-start.9
  33.7 2.7 %collective-permute-start.7 = (bf16[256,1536]{1,0:T(8,128)(2,1)S(1)}, bf16[256,1536]{1,0:T(8,128)(2,1)}, u32[]{:S(2)}, u32[]{:S(2)}) collective-permute-start(bf16[256,1536]{1,0:T(8,128)(2,1)S(1)} %constant_dynamic-update-slice_fusion.2.refs_1_.refs_2_), channel_id=1, source_target_pairs={{0,48},{8,200},{16,0},{24,216},{32,16},{40,232},{48,32},{56,248},{... | collective-permute-start | bytes 2359304 | tf_op jit(solution)/shard_map/ppermute | solution.py:359
  36.3 0.3 collective-permute-start.11
  36.6 2.2 collective-permute-start.14
  38.8 1.3 dynamic-slice_bitcast_fusion.sources
  40.1 6.1 %shard_map.68.refs_5_ = bf16[8,512,512]{2,1,0:T(8,128)(2,1)} custom-call(s32[32]{0:T(128)} %dynamic-slice_bitcast_fusion.sources, bf16[256,1536]{1,0:T(8,128)(2,1)} %copy-done.1, bf16[256,1536]{1,0:T(8,128)(2,1)} %copy-done, bf16[256,1536]{1,0:T(8,128)(2,1)} %copy-done.3, bf16[256,1536]{1,0:T(8,128)(2,1)} %collective-permute-done.9.refs_3_.refs_4_, ...), custom_call_target="tpu_custom_call" | custom-call | flops 1610612736 | bytes 4194304 | tf_op jit(solution)/shard_map/pallas_call | solution.py:274
  46.2 0.9 collective-permute-start.15
  47.1 6.6 %collective-permute-done.11.refs_0_.refs_8_.refs_9_ = bf16[256,1536]{1,0:T(8,128)(2,1)} collective-permute-done((bf16[256,1536]{1,0:T(8,128)(2,1)S(1)}, bf16[256,1536]{1,0:T(8,128)(2,1)}, u32[]{:S(2)}, u32[]{:S(2)}) %collective-permute-start.11) | collective-permute-done | bytes 786464 | tf_op jit(solution)/shard_map/ppermute | solution.py:359
  53.7 1.8 collective-permute-start.12
  55.5 2.7 %collective-permute-start.10 = (bf16[256,1536]{1,0:T(8,128)(2,1)}, bf16[256,1536]{1,0:T(8,128)(2,1)}, u32[]{:S(2)}, u32[]{:S(2)}) collective-permute-start(bf16[256,1536]{1,0:T(8,128)(2,1)} %collective-permute-done.7.refs_1_.refs_9_.refs_10_), channel_id=1, source_target_pairs={{0,48},{8,200},{16,0},{24,216},{32,16},{40,232},{48,32},{56,248},{... | collective-permute-start | bytes 2359304 | tf_op jit(solution)/shard_map/ppermute | solution.py:359
  58.2 18.2 %all_to_all.25 = bf16[8,8,2048]{2,1,0:T(8,128)(2,1)} all-to-all(bf16[8,8,2048]{2,1,0:T(8,128)(2,1)S(1)} %get-tuple-element.25), channel_id=1, replica_groups=mesh['dp'=32,'tensor'=8] {'tensor'}, dimensions={0} | all-to-all | bytes 524288 | tf_op jit(solution)/shard_map/all_to_all | solution.py:438
  76.3 3.0 %shard_map.71 = (bf16[256,512]{1,0:T(8,128)(2,1)}, f32[32,8,512]{2,1,0:T(8,128)}) custom-call(bf16[64,2048]{1,0:T(8,128)(2,1)} %bitcast.30, bf16[256,256]{1,0:T(8,128)(2,1)} %constant.18.clone.table_ref), custom_call_target="tpu_custom_call" | custom-call | flops 268435456 | bytes 1048576 | tf_op jit(solution)/shard_map/pallas_call | solution.py:224
  79.3 0.9 copy-done.4
  80.2 6.0 %shard_map.69.refs_5_ = bf16[8,512,512]{2,1,0:T(8,128)(2,1)} custom-call(s32[32]{0:T(128)} %dynamic-slice_bitcast_fusion.sources, bf16[256,1536]{1,0:T(8,128)(2,1)} %copy-done.2, bf16[256,1536]{1,0:T(8,128)(2,1)} %collective-permute-done.6.refs_1_.refs_5_.refs_6_, ...), custom_call_target="tpu_custom_call", output_to_operand_aliasing={{}: (6, {})} | custom-call | flops 1610612736 | bytes 4194304 | tf_op jit(solution)/shard_map/pallas_call | solution.py:274
  86.3 0.9 copy-done.5
  87.2 0.9 copy-done.6
  88.1 6.0 %shard_map.70.refs_3_ = bf16[8,512,512]{2,1,0:T(8,128)(2,1)} custom-call(s32[32]{0:T(128)} %dynamic-slice_bitcast_fusion.sources, bf16[256,1536]{1,0:T(8,128)(2,1)} %collective-permute-done.11.refs_0_.refs_8_.refs_9_, bf16[256,1536]{1,0:T(8,128)(2,1)} %collective-permute-done.7.refs_1_.refs_9_.refs_10_, ...), custom_call_target="tpu_custom_call", output_to_operand_aliasing={{}: (6, {})} | custom-call | flops 1610612736 | bytes 4194304 | tf_op jit(solution)/shard_map/pallas_call | solution.py:274
  94.1 2.8 %collective-permute-start.16 = (bf16[256,1536]{1,0:T(8,128)(2,1)}, bf16[256,1536]{1,0:T(8,128)(2,1)S(1)}, u32[]{:S(2)}, u32[]{:S(2)}) collective-permute-start(bf16[256,1536]{1,0:T(8,128)(2,1)} %collective-permute-done.2.refs_0_.refs_12_.refs_13_), channel_id=1, source_target_pairs={{0,8},{8,0},{16,24},{24,16},{32,40},{40,32},{48,56},{56,48},{64,72... | collective-permute-start | bytes 2359304 | tf_op jit(solution)/shard_map/ppermute | solution.py:363
  97.0 4.3 %shard_map.72.refs_3_ = bf16[8,512,512]{2,1,0:T(8,128)(2,1)} custom-call(s32[32]{0:T(128)} %dynamic-slice_bitcast_fusion.sources, bf16[256,1536]{1,0:T(8,128)(2,1)} %collective-permute-done.2.refs_0_.refs_12_.refs_13_, bf16[256,1536]{1,0:T(8,128)(2,1)} %collective-permute-done.10.refs_1_.refs_13_.refs_14_, ...), custom_call_target="tpu_custom_call", output_to_operand_aliasing={{}: (4, {})} | custom-call | flops 805306368 | bytes 2097152 | tf_op jit(solution)/shard_map/pallas_call | solution.py:274
  101.3 0.9 copy-done.7
  102.2 0.9 copy-done.8
  103.1 4.3 %shard_map.73 = bf16[8,512,512]{2,1,0:T(8,128)(2,1)} custom-call(s32[32]{0:T(128)} %dynamic-slice_bitcast_fusion.sources, bf16[256,1536]{1,0:T(8,128)(2,1)} %copy-done.7, bf16[256,1536]{1,0:T(8,128)(2,1)} %copy-done.8, bf16[512,1536]{1,0:T(8,128)(2,1)} %refs_2_.3, bf16[8,512,512]{2,1,0:T(8,128)(2,1)} %shard_map.72.refs_3_), custom_call_target="tpu_custom_call", output_to_operand_aliasing={{}: (4, {})} | custom-call | flops 805306368 | bytes 2097152 | tf_op jit(solution)/shard_map/pallas_call | solution.py:274
  107.4 4.9 %all-to-all-start.2 = ((bf16[32,8,512]{2,1,0:T(8,128)(2,1)}), bf16[32,8,512]{2,1,0:T(8,128)(2,1)S(1)}, u32[]{:S(2)}, u32[]{:S(2)}) async-start(bf16[32,8,512]{2,1,0:T(8,128)(2,1)} %bitcast.12), calls=%async_computation.3 | async-start | bytes 524288 | tf_op jit(solution)/shard_map/all_to_all | solution.py:471
  112.4 8.0 %shard_map.74 = (bf16[32,64,512]{2,1,0:T(8,128)(2,1)}, f32[32,8,512]{2,1,0:T(8,128)}) custom-call(s32[1]{0:T(128)} %bitcast.11.place, bf16[8,64,2048]{2,1,0:T(8,128)(2,1)} %all-gather.3.cloned.1.call-done.rows_ref, bf16[256,256]{1,0:T(8,128)(2,1)} %constant.18.clone.table_ref), custom_call_target="tpu_custom_call" | custom-call | flops 2147483648 | bytes 4194304 | tf_op jit(solution)/shard_map/pallas_call | solution.py:151
  120.4 1.0 all-to-all-done.2
  121.3 34.9 %all_to_all.26.quantized_ref = bf16[32,64,512]{2,1,0:T(8,128)(2,1)} all-to-all(bf16[32,64,512]{2,1,0:T(8,128)(2,1)} %get-tuple-element.33), channel_id=1, replica_groups=mesh['dp'=32,'tensor'=8] {'dp'}, dimensions={0} | all-to-all | bytes 4194304 | tf_op jit(solution)/shard_map/all_to_all | solution.py:477
  156.4 19.2 %all_to_all.27.summed_ref = bf16[32,16,512]{2,1,0:T(8,128)(2,1)} all-to-all(bf16[32,16,512]{2,1,0:T(8,128)(2,1)} %bitcast.28), channel_id=1, replica_groups=mesh['dp'=32,'tensor'=8] {'dp'}, dimensions={0} | all-to-all | bytes 1048576 | tf_op jit(solution)/shard_map/all_to_all | solution.py:479
  175.7 2.7 %shard_map.75 = bf16[8,16,2048]{2,1,0:T(8,128)(2,1)} custom-call(bf16[32,16,512]{2,1,0:T(8,128)(2,1)} %all_to_all.27.summed_ref, f32[32,8,512]{2,1,0:T(8,128)} %get-tuple-element.36.early_ref, f32[32,8,512]{2,1,0:T(8,128)} %get-tuple-element.37.late_ref, bf16[256,256]{1,0:T(8,128)(2,1)} %constant.18.clone.table_ref), custom_call_target="tpu_custom_call" | custom-call | flops 536870912 | bytes 2097152 | tf_op jit(solution)/shard_map/pallas_call | solution.py:413
  178.3 4.1 %all-to-all-start.4 = ((bf16[8,16,2048]{2,1,0:T(8,128)(2,1)}), bf16[8,16,2048]{2,1,0:T(8,128)(2,1)S(1)}, u32[]{:S(2)}, u32[]{:S(2)}) async-start(bf16[8,16,2048]{2,1,0:T(8,128)(2,1)} %shard_map.75), calls=%async_computation.5 | async-start | bytes 1048576 | tf_op jit(solution)/shard_map/all_to_all | solution.py:484
  182.4 10.4 %shard_map.76.refs_0_ = f32[512,1536]{1,0:T(8,128)} custom-call(s32[32]{0:T(128)} %dynamic-slice_bitcast_fusion.sources, bf16[32,64,512]{2,1,0:T(8,128)(2,1)} %all_to_all.26.quantized_ref, bf16[256,1536]{1,0:T(8,128)(2,1)} %copy-done.1, bf16[256,1536]{1,0:T(8,128)(2,1)} %copy-done, bf16[256,1536]{1,0:T(8,128)(2,1)} %copy-done.3, ...), custom_call_target="tpu_custom_call" | custom-call | flops 3221225472 | bytes 11534336 | tf_op jit(solution)/shard_map/pallas_call | solution.py:327
  192.8 12.6 %all-to-all-done.4 = bf16[8,16,2048]{2,1,0:T(8,128)(2,1)S(1)} async-done(((bf16[8,16,2048]{2,1,0:T(8,128)(2,1)}), bf16[8,16,2048]{2,1,0:T(8,128)(2,1)S(1)}, u32[]{:S(2)}, u32[]{:S(2)}) %all-to-all-start.4) | async-done | bytes 524320 | tf_op jit(solution)/shard_map/all_to_all | solution.py:484
  205.4 11.2 %shard_map.77 = f32[512,1536]{1,0:T(8,128)} custom-call(s32[32]{0:T(128)} %dynamic-slice_bitcast_fusion.sources, bf16[32,64,512]{2,1,0:T(8,128)(2,1)} %all-gather.5.cloned.1.call-done.quantized_ref, f32[512,1536]{1,0:T(8,128)} %shard_map.76.refs_0_, bf16[256,1536]{1,0:T(8,128)(2,1)} %copy-done.1, bf16[256,1536]{1,0:T(8,128)(2,1)} %copy-done, ...), custom_call_target="tpu_custom_call" | custom-call | flops 3221225472 | bytes 11534336 | tf_op jit(solution)/shard_map/pallas_call | solution.py:327
  216.7 0.8 copy.25
  (50 shorter events, 0.6 us)
Async XLA Ops:
  7.2 100.3 %all-gather.3.cloned.1.call-start = ((), (), s32[]{:S(2)}) async-start(), calls=%async_computation.6 | async-start | bytes 2359296 | tf_op jit(solution)/shard_map/all_gather | solution.py:437
  10.1 9.1 %collective-permute-start = (bf16[128,1536]{1,0:T(8,128)(2,1)S(1)}, bf16[128,1536]{1,0:T(8,128)(2,1)S(1)}, u32[]{:S(2)}, u32[]{:S(2)}) collective-permute-start(bf16[128,1536]{1,0:T(8,128)(2,1)S(1)} %bitcast.23), channel_id=1, source_target_pairs={{0,64},{8,24},{16,80},{24,40},{32,96},{40,56},{48,112},{56,8},{64,... | collective-permute-start | bytes 1179656 | tf_op jit(solution)/shard_map/ppermute | solution.py:359
  12.3 13.1 %collective-permute-start.3 = (bf16[128,1536]{1,0:T(8,128)(2,1)S(1)}, bf16[128,1536]{1,0:T(8,128)(2,1)S(1)}, u32[]{:S(2)}, u32[]{:S(2)}) collective-permute-start(bf16[128,1536]{1,0:T(8,128)(2,1)S(1)} %bitcast.24), channel_id=1, source_target_pairs={{0,192},{8,56},{16,208},{24,8},{32,224},{40,24},{48,240},{56,40},{... | collective-permute-start | bytes 1179656 | tf_op jit(solution)/shard_map/ppermute | solution.py:359
  13.8 142.6 %reduce-scatter.2.cloned.1.call-start = ((), (), s32[]{:S(2)}) async-start(), calls=%async_computation.7 | async-start | bytes 4718592 | tf_op jit(solution)/shard_map/reduce_scatter | solution.py:475
  19.2 0.7 copy-start.11
  19.9 20.1 %copy-start.1 = (bf16[256,1536]{1,0:T(8,128)(2,1)}, bf16[256,1536]{1,0:T(8,128)(2,1)S(1)}, u32[]{:S(2)}) copy-start(bf16[256,1536]{1,0:T(8,128)(2,1)S(1)} %constant_dynamic-update-slice_fusion.refs_0_.refs_1_) | copy-start | bytes 2359300
  19.9 16.4 %collective-permute-start.1 = (bf16[256,1536]{1,0:T(8,128)(2,1)S(1)}, bf16[256,1536]{1,0:T(8,128)(2,1)S(1)}, u32[]{:S(2)}, u32[]{:S(2)}) collective-permute-start(bf16[256,1536]{1,0:T(8,128)(2,1)S(1)} %constant_dynamic-update-slice_fusion.refs_0_.refs_1_), channel_id=1, source_target_pairs={{0,16},{8,72},{16,32},{24,88},{32,48},{40,104},{48,0},{56,120},{64... | collective-permute-start | bytes 2359304 | tf_op jit(solution)/shard_map/ppermute | solution.py:359
  20.9 15.7 %collective-permute-start.8 = (bf16[256,1536]{1,0:T(8,128)(2,1)S(1)}, bf16[256,1536]{1,0:T(8,128)(2,1)S(1)}, u32[]{:S(2)}, u32[]{:S(2)}) collective-permute-start(bf16[256,1536]{1,0:T(8,128)(2,1)S(1)} %constant_dynamic-update-slice_fusion.refs_0_.refs_1_), channel_id=1, source_target_pairs={{0,8},{8,0},{16,24},{24,16},{32,40},{40,32},{48,56},{56,48},{64,72... | collective-permute-start | bytes 2359304 | tf_op jit(solution)/shard_map/ppermute | solution.py:363
  24.3 8.5 %collective-permute-start.4 = (bf16[64,1536]{1,0:T(8,128)(2,1)S(1)}, bf16[64,1536]{1,0:T(8,128)(2,1)S(1)}, u32[]{:S(2)}, u32[]{:S(2)}) collective-permute-start(bf16[64,1536]{1,0:T(8,128)(2,1)S(1)} %slice.8), channel_id=1, source_target_pairs={{0,64},{8,24},{16,80},{24,40},{32,96},{40,56},{48,112},{56,8},{64,... | collective-permute-start | bytes 589832 | tf_op jit(solution)/shard_map/ppermute | solution.py:359
  25.4 0.7 copy-start.10
  26.1 6.6 %collective-permute-start.5 = (bf16[64,1536]{1,0:T(8,128)(2,1)S(1)}, bf16[64,1536]{1,0:T(8,128)(2,1)S(1)}, u32[]{:S(2)}, u32[]{:S(2)}) collective-permute-start(bf16[64,1536]{1,0:T(8,128)(2,1)S(1)} %slice.9), channel_id=1, source_target_pairs={{0,192},{8,56},{16,208},{24,8},{32,224},{40,24},{48,240},{56,40},{... | collective-permute-start | bytes 589832 | tf_op jit(solution)/shard_map/ppermute | solution.py:359
  32.8 7.3 %copy-start = (bf16[256,1536]{1,0:T(8,128)(2,1)}, bf16[256,1536]{1,0:T(8,128)(2,1)S(1)}, u32[]{:S(2)}) copy-start(bf16[256,1536]{1,0:T(8,128)(2,1)S(1)} %constant_dynamic-update-slice_fusion.2.refs_1_.refs_2_) | copy-start | bytes 2359300
  32.8 7.3 %collective-permute-start.9 = (bf16[256,1536]{1,0:T(8,128)(2,1)S(1)}, bf16[256,1536]{1,0:T(8,128)(2,1)}, u32[]{:S(2)}, u32[]{:S(2)}) collective-permute-start(bf16[256,1536]{1,0:T(8,128)(2,1)S(1)} %constant_dynamic-update-slice_fusion.2.refs_1_.refs_2_), channel_id=1, source_target_pairs={{0,8},{8,0},{16,24},{24,16},{32,40},{40,32},{48,56},{56,48},{64,72... | collective-permute-start | bytes 2359304 | tf_op jit(solution)/shard_map/ppermute | solution.py:363
  33.6 12.5 %collective-permute-start.6 = (bf16[256,1536]{1,0:T(8,128)(2,1)S(1)}, bf16[256,1536]{1,0:T(8,128)(2,1)}, u32[]{:S(2)}, u32[]{:S(2)}) collective-permute-start(bf16[256,1536]{1,0:T(8,128)(2,1)S(1)} %constant_dynamic-update-slice_fusion.2.refs_1_.refs_2_), channel_id=1, source_target_pairs={{0,16},{8,72},{16,32},{24,88},{32,48},{40,104},{48,0},{56,120},{64... | collective-permute-start | bytes 2359304 | tf_op jit(solution)/shard_map/ppermute | solution.py:359
  33.7 12.5 %collective-permute-start.7 = (bf16[256,1536]{1,0:T(8,128)(2,1)S(1)}, bf16[256,1536]{1,0:T(8,128)(2,1)}, u32[]{:S(2)}, u32[]{:S(2)}) collective-permute-start(bf16[256,1536]{1,0:T(8,128)(2,1)S(1)} %constant_dynamic-update-slice_fusion.2.refs_1_.refs_2_), channel_id=1, source_target_pairs={{0,48},{8,200},{16,0},{24,216},{32,16},{40,232},{48,32},{56,248},{... | collective-permute-start | bytes 2359304 | tf_op jit(solution)/shard_map/ppermute | solution.py:359
  36.3 19.2 %copy-start.2 = (bf16[256,1536]{1,0:T(8,128)(2,1)}, bf16[256,1536]{1,0:T(8,128)(2,1)S(1)}, u32[]{:S(2)}) copy-start(bf16[256,1536]{1,0:T(8,128)(2,1)S(1)} %collective-permute-done.1.refs_0_.refs_4_.refs_5_) | copy-start | bytes 2359300
  36.3 17.4 %collective-permute-start.11 = (bf16[256,1536]{1,0:T(8,128)(2,1)S(1)}, bf16[256,1536]{1,0:T(8,128)(2,1)}, u32[]{:S(2)}, u32[]{:S(2)}) collective-permute-start(bf16[256,1536]{1,0:T(8,128)(2,1)S(1)} %constant_dynamic-update-slice_fusion.refs_0_.refs_1_), channel_id=1, source_target_pairs={{0,48},{8,200},{16,0},{24,216},{32,16},{40,232},{48,32},{56,248},{... | collective-permute-start | bytes 2359304 | tf_op jit(solution)/shard_map/ppermute | solution.py:359
  36.6 3.5 %copy-start.3 = (bf16[256,1536]{1,0:T(8,128)(2,1)}, bf16[256,1536]{1,0:T(8,128)(2,1)S(1)}, u32[]{:S(2)}) copy-start(bf16[256,1536]{1,0:T(8,128)(2,1)S(1)} %collective-permute-done.8.refs_2_.refs_3_) | copy-start | bytes 2359300
  36.6 18.9 %collective-permute-start.14 = (bf16[256,1536]{1,0:T(8,128)(2,1)S(1)}, bf16[256,1536]{1,0:T(8,128)(2,1)}, u32[]{:S(2)}, u32[]{:S(2)}) collective-permute-start(bf16[256,1536]{1,0:T(8,128)(2,1)S(1)} %collective-permute-done.1.refs_0_.refs_4_.refs_5_), channel_id=1, source_target_pairs={{0,8},{8,0},{16,24},{24,16},{32,40},{40,32},{48,56},{56,48},{64,72... | collective-permute-start | bytes 2359304 | tf_op jit(solution)/shard_map/ppermute | solution.py:363
  46.2 33.1 %collective-permute-start.15 = (bf16[256,1536]{1,0:T(8,128)(2,1)}, bf16[256,1536]{1,0:T(8,128)(2,1)S(1)}, u32[]{:S(2)}, u32[]{:S(2)}) collective-permute-start(bf16[256,1536]{1,0:T(8,128)(2,1)} %collective-permute-done.6.refs_1_.refs_5_.refs_6_), channel_id=1, source_target_pairs={{0,8},{8,0},{16,24},{24,16},{32,40},{40,32},{48,56},{56,48},{64,72... | collective-permute-start | bytes 2359304 | tf_op jit(solution)/shard_map/ppermute | solution.py:363
  53.7 32.6 %collective-permute-start.12 = (bf16[256,1536]{1,0:T(8,128)(2,1)}, bf16[256,1536]{1,0:T(8,128)(2,1)S(1)}, u32[]{:S(2)}, u32[]{:S(2)}) collective-permute-start(bf16[256,1536]{1,0:T(8,128)(2,1)} %collective-permute-done.11.refs_0_.refs_8_.refs_9_), channel_id=1, source_target_pairs={{0,8},{8,0},{16,24},{24,16},{32,40},{40,32},{48,56},{56,48},{64,72... | collective-permute-start | bytes 2359304 | tf_op jit(solution)/shard_map/ppermute | solution.py:363
  55.5 30.8 %collective-permute-start.13 = (bf16[256,1536]{1,0:T(8,128)(2,1)}, bf16[256,1536]{1,0:T(8,128)(2,1)S(1)}, u32[]{:S(2)}, u32[]{:S(2)}) collective-permute-start(bf16[256,1536]{1,0:T(8,128)(2,1)} %collective-permute-done.7.refs_1_.refs_9_.refs_10_), channel_id=1, source_target_pairs={{0,8},{8,0},{16,24},{24,16},{32,40},{40,32},{48,56},{56,48},{64,72... | collective-permute-start | bytes 2359304 | tf_op jit(solution)/shard_map/ppermute | solution.py:363
  55.5 38.6 %collective-permute-start.2 = (bf16[256,1536]{1,0:T(8,128)(2,1)S(1)}, bf16[256,1536]{1,0:T(8,128)(2,1)}, u32[]{:S(2)}, u32[]{:S(2)}) collective-permute-start(bf16[256,1536]{1,0:T(8,128)(2,1)S(1)} %collective-permute-done.1.refs_0_.refs_4_.refs_5_), channel_id=1, source_target_pairs={{0,16},{8,72},{16,32},{24,88},{32,48},{40,104},{48,0},{56,120},{64... | collective-permute-start | bytes 2359304 | tf_op jit(solution)/shard_map/ppermute | solution.py:359
  55.5 38.6 %collective-permute-start.10 = (bf16[256,1536]{1,0:T(8,128)(2,1)}, bf16[256,1536]{1,0:T(8,128)(2,1)}, u32[]{:S(2)}, u32[]{:S(2)}) collective-permute-start(bf16[256,1536]{1,0:T(8,128)(2,1)} %collective-permute-done.7.refs_1_.refs_9_.refs_10_), channel_id=1, source_target_pairs={{0,48},{8,200},{16,0},{24,216},{32,16},{40,232},{48,32},{56,248},{... | collective-permute-start | bytes 2359304 | tf_op jit(solution)/shard_map/ppermute | solution.py:359
  79.3 0.9 copy-start.4
  86.3 0.9 copy-start.5
  87.2 0.9 copy-start.6
  94.1 7.2 %collective-permute-start.16 = (bf16[256,1536]{1,0:T(8,128)(2,1)}, bf16[256,1536]{1,0:T(8,128)(2,1)S(1)}, u32[]{:S(2)}, u32[]{:S(2)}) collective-permute-start(bf16[256,1536]{1,0:T(8,128)(2,1)} %collective-permute-done.2.refs_0_.refs_12_.refs_13_), channel_id=1, source_target_pairs={{0,8},{8,0},{16,24},{24,16},{32,40},{40,32},{48,56},{56,48},{64,72... | collective-permute-start | bytes 2359304 | tf_op jit(solution)/shard_map/ppermute | solution.py:363
  96.9 4.4 %collective-permute-start.17 = (bf16[256,1536]{1,0:T(8,128)(2,1)}, bf16[256,1536]{1,0:T(8,128)(2,1)S(1)}, u32[]{:S(2)}, u32[]{:S(2)}) collective-permute-start(bf16[256,1536]{1,0:T(8,128)(2,1)} %collective-permute-done.10.refs_1_.refs_13_.refs_14_), channel_id=1, source_target_pairs={{0,8},{8,0},{16,24},{24,16},{32,40},{40,32},{48,56},{56,48},{64,72... | collective-permute-start | bytes 2359304 | tf_op jit(solution)/shard_map/ppermute | solution.py:363
  101.3 0.9 copy-start.7
  102.2 0.9 copy-start.8
  107.4 13.9 %all-to-all-start.2 = ((bf16[32,8,512]{2,1,0:T(8,128)(2,1)}), bf16[32,8,512]{2,1,0:T(8,128)(2,1)S(1)}, u32[]{:S(2)}, u32[]{:S(2)}) async-start(bf16[32,8,512]{2,1,0:T(8,128)(2,1)} %bitcast.12), calls=%async_computation.3 | async-start | bytes 524288 | tf_op jit(solution)/shard_map/all_to_all | solution.py:471
  112.3 93.1 %all-gather.5.cloned.1.call-start = ((), (), s32[]{:S(2)}) async-start(), calls=%async_computation.8 | async-start | bytes 2359296 | tf_op jit(solution)/shard_map/all_gather | solution.py:482
  121.3 35.1 %copy-start.9 = (bf16[32,8,512]{2,1,0:T(8,128)(2,1)}, bf16[32,8,512]{2,1,0:T(8,128)(2,1)S(1)}, u32[]{:S(2)}) copy-start(bf16[32,8,512]{2,1,0:T(8,128)(2,1)S(1)} %all-to-all-done.2) | copy-start | bytes 786436
  178.3 27.1 %all-to-all-start.4 = ((bf16[8,16,2048]{2,1,0:T(8,128)(2,1)}), bf16[8,16,2048]{2,1,0:T(8,128)(2,1)S(1)}, u32[]{:S(2)}, u32[]{:S(2)}) async-start(bf16[8,16,2048]{2,1,0:T(8,128)(2,1)} %shard_map.75), calls=%async_computation.5 | async-start | bytes 1048576 | tf_op jit(solution)/shard_map/all_to_all | solution.py:484
Sparse Core Ops, SparseCore 0:
  13.9 39.5 all-gather.2
  107.6 48.7 reduce-scatter.1
  158.2 46.4 all-gather.4

commit v9 on v8

--- a/solution.py
+++ b/solution.py
@@ -13,7 +13,8 @@
 WIDTH = 16384
 TABLE = 256
 LANES = 128
-VMEM_BYTES = 60 * 1024 * 1024
+VMEM_BYTES = 16 * 1024 * 1024
+HELD = pltpu.HBM
 NORM = 1.0 / math.sqrt(WIDTH)
 SIDE = 4
 STEP = 16
@@ -146,8 +147,7 @@
 
 def quantize(rows, table, place, dp, width):
     members, tokens, features = rows.shape
-    own = tokens // members
-    count = 2 * STEP
+    tokens, own, count = tokens // 2, STEP // 2, 2 * STEP
     return pl.pallas_call(
         quantize_kernel,
         grid_spec=pltpu.PrefetchScalarGridSpec(
@@ -177,19 +177,20 @@
     )(place, rows, table)
 
 
-def quantize_own_kernel(rows_ref, table_ref, quantized_ref, slope_ref, inner):
+def quantize_own_kernel(place, rows_ref, table_ref, quantized_ref, slope_ref, inner):
     devices, own, width = slope_ref.shape
-    features = rows_ref.shape[1]
-    members = rows_ref.shape[0] // own
+    members, _, features = rows_ref.shape
+    rows = rows_ref[...].reshape(members * STEP, features)
+    shift = pl.multiple_of(place[0] % 2 * own, own)
     chunks, per_width = features // TABLE, width // TABLE
     for c in range(chunks):
         inner[c] = jnp.dot(
-            rows_ref[:, c * TABLE : (c + 1) * TABLE],
+            rows[:, c * TABLE : (c + 1) * TABLE],
             table_ref[...],
             preferred_element_type=jnp.float32,
         )
     halves = [slice(l * LANES, (l + 1) * LANES) for l in range(TABLE // LANES)]
-    spans = [slice(t * own, (t + 1) * own) for t in range(members)]
+    spans = [pl.ds(pl.multiple_of(t * STEP + shift, own), own) for t in range(members)]
     for span in spans:
         for lanes in halves:
             parts = butterfly([inner[c, span, lanes] for c in range(chunks)])
@@ -219,37 +220,47 @@
                 ).astype(jnp.bfloat16)
 
 
-def quantize_own(rows, table, dp, width):
-    members, own, features = rows.shape
+def quantize_own(rows, table, place, dp, width):
+    members, tokens, features = rows.shape
+    own = STEP // 2
+    first = tokens // 2 // STEP
     return pl.pallas_call(
         quantize_own_kernel,
+        grid_spec=pltpu.PrefetchScalarGridSpec(
+            num_scalar_prefetch=1,
+            grid=(1,),
+            in_specs=[
+                pl.BlockSpec((members, STEP, features), lambda i, place: (0, first + place[0] // 2, 0)),
+                pl.BlockSpec((TABLE, TABLE), lambda i, place: (0, 0)),
+            ],
+            out_specs=[
+                pl.BlockSpec((dp * own, width), lambda i, place: (0, 0)),
+                pl.BlockSpec((dp, own, width), lambda i, place: (0, 0, 0)),
+            ],
+            scratch_shapes=[pltpu.VMEM((features // TABLE, members * STEP, TABLE), jnp.float32)],
+        ),
         out_shape=[
             jax.ShapeDtypeStruct((dp * own, width), jnp.bfloat16),
             jax.ShapeDtypeStruct((dp, own, width), jnp.float32),
         ],
-        scratch_shapes=[pltpu.VMEM((features // TABLE, members * own, TABLE), jnp.float32)],
         compiler_params=pltpu.CompilerParams(vmem_limit_bytes=VMEM_BYTES),
         cost_estimate=pl.CostEstimate(
             flops=2 * own * WIDTH * BLOCK, bytes_accessed=8 * own * WIDTH, transcendentals=0
         ),
-    )(rows.reshape(members * own, features), table)
+    )(place, rows, table)
 
 
 def product_kernel(count, slots, sources, *refs):
     pieces, weight_ref = refs[:count], refs[count]
-    out_ref, weight, rows, results, weight_sem, in_sems, out_sems = refs[-7:]
+    out_ref, results, out_sems = refs[-3:]
     members = out_ref.shape[0]
-    load_weight = pltpu.make_async_copy(weight_ref, weight, weight_sem)
-    load_weight.start()
-    loads = [pltpu.make_async_copy(pieces[n], rows.at[n], in_sems.at[n]) for n in range(count)]
-    for load in loads:
-        load.start()
-    load_weight.wait()
     stores = []
     for n in range(count):
-        loads[n].wait()
         product = lax.dot_general(
-            rows[n], weight[...], (((1,), (1,)), ((), ())), preferred_element_type=jnp.float32
+            pieces[n][...],
+            weight_ref[...],
+            (((1,), (1,)), ((), ())),
+            preferred_element_type=jnp.float32,
         )
         for k in range(2):
             for t in range(members):
@@ -274,15 +285,12 @@
     return pl.pallas_call(
         functools.partial(product_kernel, count, slots),
         in_specs=[pl.BlockSpec(memory_space=pltpu.SMEM)]
-        + [pl.BlockSpec(memory_space=pl.ANY)] * (count + 1 + len(earlier)),
-        out_specs=pl.BlockSpec(memory_space=pl.ANY),
+        + [pl.BlockSpec(memory_space=pltpu.VMEM)] * (count + 1)
+        + [pl.BlockSpec(memory_space=HELD)] * len(earlier),
+        out_specs=pl.BlockSpec(memory_space=HELD),
         out_shape=jax.ShapeDtypeStruct((members, total // members, width), jnp.bfloat16),
         scratch_shapes=[
-            pltpu.VMEM((width, depth), jnp.bfloat16),
-            pltpu.VMEM((count, rows, depth), jnp.bfloat16),
             pltpu.VMEM((count, 2, members, STEP, width), jnp.bfloat16),
-            pltpu.SemaphoreType.DMA,
-            pltpu.SemaphoreType.DMA((count,)),
             pltpu.SemaphoreType.DMA((count, 2)),
         ],
         input_output_aliases={count + 2: 0} if earlier else {},
@@ -330,7 +338,7 @@
         + [pl.BlockSpec(memory_space=pltpu.VMEM)] * (len(pieces) + 1 + len(earlier)),
         out_specs=pl.BlockSpec(memory_space=pltpu.VMEM),
         out_shape=jax.ShapeDtypeStruct((width, depth), jnp.float32),
-        compiler_params=pltpu.CompilerParams(vmem_limit_bytes=VMEM_BYTES),
+        compiler_params=pltpu.CompilerParams(vmem_limit_bytes=2 * VMEM_BYTES),
         cost_estimate=pl.CostEstimate(
             flops=2 * rows * depth * width,
             bytes_accessed=2 * rows * (depth + width) + 4 * width * depth,
@@ -431,11 +439,12 @@
     table = hadamard_table(TABLE)
     total = dp * tokens
     own, half = STEP // 2, tokens // 2
-    early_rows, late_rows = jnp.moveaxis(activations.reshape(members, 2, own, features), 1, 0)
+    activations = jnp.moveaxis(activations.reshape(members, 2, own, features), 1, 0)
     grad_out = jnp.moveaxis(grad_out.reshape(members, 2, own, -1), 1, 0).reshape(tokens, -1)
-    early_rows, late_rows, grad_out = lax.optimization_barrier((early_rows, late_rows, grad_out))
-    wide_rows = lax.all_gather(early_rows.reshape(half, features), "tensor", axis=0, tiled=False)
-    late_rows = lax.all_to_all(late_rows, "tensor", split_axis=0, concat_axis=0, tiled=True)
+    activations, grad_out = lax.optimization_barrier((activations, grad_out))
+    wide_rows = lax.all_gather(
+        activations.reshape(tokens, features), "tensor", axis=0, tiled=False
+    )
 
     def multiply(held, pieces, slot):
         slots = [slot + 2 * n for n in range(len(pieces))]
@@ -460,19 +469,17 @@
     above_other = [other_core(block) for block in above]
     held = multiply(held, below + below_other, 8)
     held = multiply(held, above + above_other, 16)
-    late, late_slope = quantize_own(late_rows, table, dp, width)
-    far_top, far_bottom, held, late = lax.optimization_barrier(
-        (far_top, far_bottom, held, late)
-    )
+    far_top, far_bottom, held = lax.optimization_barrier((far_top, far_bottom, held))
     far = [far_top, far_bottom]
     far_other = [other_core(block) for block in far]
     held = multiply(held, far, 24)
     partial_rows = multiply(held, far_other, 28)
+    partial_rows, wide_rows = lax.optimization_barrier((partial_rows, wide_rows))
+    summed = lax.psum_scatter(partial_rows, "tensor", scatter_dimension=0, tiled=False)
+    late, late_slope = quantize_own(wide_rows, table, place, dp, width)
     q_own = lax.all_to_all(
         late.reshape(dp, own, width), "dp", split_axis=0, concat_axis=0, tiled=True
     )
-    partial_rows, wide_rows = lax.optimization_barrier((partial_rows, wide_rows))
-    summed = lax.psum_scatter(partial_rows, "tensor", scatter_dimension=0, tiled=False)
     early, early_slope = quantize(wide_rows, table, place, dp, width)
     q_early = lax.all_to_all(early, "dp", split_axis=0, concat_axis=0, tiled=True)
     summed, q_early, q_own = lax.optimization_barrier((summed, q_early, q_own))

time: 226 us -> 214 us (0.947)
  local copies, waits for them, and re-layouts: 12.9 us -> 43.1 us
  Pallas kernels: 62 us -> 39.4 us
  blocking collectives: 72.3 us -> 54.3 us
  waiting for transfers between devices: 29.5 us -> 24.3 us
    unnamed x28 -> x82, local copies, waits for them, and re-layouts: 7.76 us -> 39.3 us
    all_to_all x1 -> x0, blocking collectives: 18.2 us -> none  [shards(): lax.all_to_all(late_rows, 'tensor', split_axis=0, concat_axis=0, tiled=True)]
    pallas_call x5, Pallas kernels: 26.7 us -> 17 us  [product(): pl.pallas_call(functools.partial(product_kernel, count, slots), in_specs=...]
    pallas_call x2, Pallas kernels: 21.6 us -> 13.2 us  [gradient(): pl.pallas_call(functools.partial(gradient_kernel, half, bool(earlier)), i...]
    all_to_all x1, waiting for transfers between devices: 12.6 us -> 4.82 us  [shards(): lax.all_to_all(mixed, 'tensor', split_axis=0, concat_axis=0, tiled=True)]
  transfers between devices with their start and end apart: 23 -> 23, of which waited for: 6 -> 9; matrix products, arithmetic and copies ran while one was open for 1% -> 0% of each run, Pallas kernels for 23% -> 15%
where the time goes in v9:
time: 214 us; the launch traced here: 211 us
  blocking collectives  54.3 us (25%)
  local copies, waits for them, and re-layouts  43.1 us (20%)
  Pallas kernels  39.4 us (18%)
  starting transfers between devices  35.6 us (17%)
  waiting for transfers between devices  24.3 us (11%)
  between operations  14.1 us (7%)
    unnamed x82, local copies, waits for them, and re-layouts  39.3 us
    all_to_all x1, blocking collectives, shards(): lax.all_to_all(early, 'dp', split_axis=0, concat_axis=0, tiled=True)  35.2 us
    all_to_all x1, blocking collectives, shards(): lax.all_to_all(summed.reshape(dp, STEP, width), 'dp', split_axis=0, conca...  19.1 us
    pallas_call x5, Pallas kernels, product(): pl.pallas_call(functools.partial(product_kernel, count, slots), in_specs=...  17 us
    ppermute x10, waiting for transfers between devices, send(): return lax.ppermute(block, 'dp', route(turn, sign))  17 us
    ppermute x10, starting transfers between devices, send(): return lax.ppermute(block, 'dp', route(turn, sign))  13.6 us
    pallas_call x2, Pallas kernels, gradient(): pl.pallas_call(functools.partial(gradient_kernel, half, bool(earlier)), i...  13.2 us
    ppermute x8, starting transfers between devices, other_core(): lax.ppermute(block, 'dp', [(d, d ^ 1) for d in range(2 * SIDE * SIDE)])  11 us
  transfers between devices with their start and end apart: 23, of which 9 were waited for; matrix products, arithmetic and copies ran while one was open for 0% of the time, Pallas kernels for 15%

profile of v9, /device:TPU:1, one launch (start us, length us, event | category | flops | bytes accessed | tf_op | source)
XLA Modules:
  0.0 210.6 jit_solution(1845569653448445650)
XLA Ops:
  7.2 2.0 copy.16
  10.3 2.2 %collective-permute-start = (bf16[128,1536]{1,0:T(8,128)(2,1)S(1)}, bf16[128,1536]{1,0:T(8,128)(2,1)S(1)}, u32[]{:S(2)}, u32[]{:S(2)}) collective-permute-start(bf16[128,1536]{1,0:T(8,128)(2,1)S(1)} %bitcast.17), channel_id=1, source_target_pairs={{0,64},{8,24},{16,80},{24,40},{32,96},{40,56},{48,112},{56,8},{64,... | collective-permute-start | bytes 1179656 | tf_op jit(solution)/shard_map/ppermute | solution.py:367
  12.5 1.5 collective-permute-start.3
  14.1 5.3 %collective-permute-done = bf16[128,1536]{1,0:T(8,128)(2,1)S(1)} collective-permute-done((bf16[128,1536]{1,0:T(8,128)(2,1)S(1)}, bf16[128,1536]{1,0:T(8,128)(2,1)S(1)}, u32[]{:S(2)}, u32[]{:S(2)}) %collective-permute-start) | collective-permute-done | bytes 393248 | tf_op jit(solution)/shard_map/ppermute | solution.py:367
  20.4 2.4 %collective-permute-start.8 = (bf16[256,1536]{1,0:T(8,128)(2,1)S(1)}, bf16[256,1536]{1,0:T(8,128)(2,1)S(1)}, u32[]{:S(2)}, u32[]{:S(2)}) collective-permute-start(bf16[256,1536]{1,0:T(8,128)(2,1)S(1)} %constant_dynamic-update-slice_fusion.refs_0_.refs_1_), channel_id=1, source_target_pairs={{0,8},{8,0},{16,24},{24,16},{32,40},{40,32},{48,56},{56,48},{64,72... | collective-permute-start | bytes 2359304 | tf_op jit(solution)/shard_map/ppermute | solution.py:371
  24.0 1.9 collective-permute-start.5
  25.9 5.3 %collective-permute-done.4 = bf16[64,1536]{1,0:T(8,128)(2,1)S(1)} collective-permute-done((bf16[64,1536]{1,0:T(8,128)(2,1)S(1)}, bf16[64,1536]{1,0:T(8,128)(2,1)S(1)}, u32[]{:S(2)}, u32[]{:S(2)}) %collective-permute-start.4) | collective-permute-done | bytes 196640 | tf_op jit(solution)/shard_map/ppermute | solution.py:367
  32.1 2.7 %collective-permute-start.7 = (bf16[256,1536]{1,0:T(8,128)(2,1)S(1)}, bf16[256,1536]{1,0:T(8,128)(2,1)}, u32[]{:S(2)}, u32[]{:S(2)}) collective-permute-start(bf16[256,1536]{1,0:T(8,128)(2,1)S(1)} %constant_dynamic-update-slice_fusion.2.refs_1_.refs_2_), channel_id=1, source_target_pairs={{0,48},{8,200},{16,0},{24,216},{32,16},{40,232},{48,32},{56,248},{... | collective-permute-start | bytes 2359304 | tf_op jit(solution)/shard_map/ppermute | solution.py:367
  36.2 2.9 %collective-permute-start.14 = (bf16[256,1536]{1,0:T(8,128)(2,1)}, bf16[256,1536]{1,0:T(8,128)(2,1)}, u32[]{:S(2)}, u32[]{:S(2)}) collective-permute-start(bf16[256,1536]{1,0:T(8,128)(2,1)} %collective-permute-done.1.refs_0_.refs_4_.refs_5_), channel_id=1, source_target_pairs={{0,8},{8,0},{16,24},{24,16},{32,40},{40,32},{48,56},{56,48},{64,72... | collective-permute-start | bytes 2359304 | tf_op jit(solution)/shard_map/ppermute | solution.py:371
  39.8 1.1 copy-done.10
  40.9 3.9 %shard_map.68.refs_5_ = bf16[8,512,512]{2,1,0:T(8,128)(2,1)S(1)} custom-call(s32[32]{0:T(128)S(1)} %dynamic-slice_bitcast_fusion.sources, bf16[256,1536]{1,0:T(8,128)(2,1)S(1)} %constant_dynamic-update-slice_fusion.refs_0_.refs_1_, bf16[256,1536]{1,0:T(8,128)(2,1)S(1)} %constant_dynamic-update-slice_fusion.2.refs_1_.refs_2_, ...), custom_call_target="tpu_custom_call" | custom-call | flops 1610612736 | bytes 4194304 | tf_op jit(solution)/shard_map/pallas_call | solution.py:285
  44.9 1.6 collective-permute-start.15
  46.5 5.7 %collective-permute-done.11.refs_0_.refs_8_.refs_9_ = bf16[256,1536]{1,0:T(8,128)(2,1)} collective-permute-done((bf16[256,1536]{1,0:T(8,128)(2,1)S(1)}, bf16[256,1536]{1,0:T(8,128)(2,1)}, u32[]{:S(2)}, u32[]{:S(2)}) %collective-permute-start.11) | collective-permute-done | bytes 786464 | tf_op jit(solution)/shard_map/ppermute | solution.py:367
  52.2 1.9 collective-permute-start.12
  54.1 2.7 %collective-permute-start.10 = (bf16[256,1536]{1,0:T(8,128)(2,1)}, bf16[256,1536]{1,0:T(8,128)(2,1)S(1)}, u32[]{:S(2)}, u32[]{:S(2)}) collective-permute-start(bf16[256,1536]{1,0:T(8,128)(2,1)} %collective-permute-done.7.refs_1_.refs_9_.refs_10_), channel_id=1, source_target_pairs={{0,48},{8,200},{16,0},{24,216},{32,16},{40,232},{48,32},{56,248},{... | collective-permute-start | bytes 2359304 | tf_op jit(solution)/shard_map/ppermute | solution.py:367
  56.7 4.6 %shard_map.69.refs_5_ = bf16[8,512,512]{2,1,0:T(8,128)(2,1)S(1)} custom-call(s32[32]{0:T(128)S(1)} %dynamic-slice_bitcast_fusion.sources, bf16[256,1536]{1,0:T(8,128)(2,1)} %collective-permute-done.1.refs_0_.refs_4_.refs_5_, bf16[256,1536]{1,0:T(8,128)(2,1)} %collective-permute-done.6.refs_1_.refs_5_.refs_6_, ...), custom_call_target="tpu_custom_call", output_to_operand_aliasing={{}: (6, {})} | custom-call | flops 1610612736 | bytes 4194304 | tf_op jit(solution)/shard_map/pallas_call | solution.py:285
  61.4 4.7 %shard_map.70.refs_3_ = bf16[8,512,512]{2,1,0:T(8,128)(2,1)S(1)} custom-call(s32[32]{0:T(128)S(1)} %dynamic-slice_bitcast_fusion.sources, bf16[256,1536]{1,0:T(8,128)(2,1)} %collective-permute-done.11.refs_0_.refs_8_.refs_9_, bf16[256,1536]{1,0:T(8,128)(2,1)} %collective-permute-done.7.refs_1_.refs_9_.refs_10_, ...), custom_call_target="tpu_custom_call", output_to_operand_aliasing={{}: (6, {})} | custom-call | flops 1610612736 | bytes 4194304 | tf_op jit(solution)/shard_map/pallas_call | solution.py:285
  66.7 1.3 collective-permute-start.16
  68.2 1.9 shard_map.71.refs_3_
  71.1 1.9 shard_map.72
  73.0 2.0 copy-done
  77.7 2.2 %copy-done.34 = bf16[8,128,2048]{2,1,0:T(8,128)(2,1)S(1)} copy-done((bf16[8,128,2048]{2,1,0:T(8,128)(2,1)S(1)}, bf16[8,128,2048]{2,1,0:T(8,128)(2,1)}, u32[]{:S(2)}) %copy-start.34) | copy-done | bytes 4194328
  79.9 2.0 shard_map.74
  81.9 6.5 %all-to-all-start.1 = ((bf16[32,8,512]{2,1,0:T(8,128)(2,1)}), bf16[32,8,512]{2,1,0:T(8,128)(2,1)S(1)}, u32[]{:S(2)}, u32[]{:S(2)}) async-start(bf16[32,8,512]{2,1,0:T(8,128)(2,1)} %bitcast.9), calls=%async_computation.2 | async-start | bytes 524288 | tf_op jit(solution)/shard_map/all_to_all | solution.py:480
  88.6 2.6 %copy-done.35 = bf16[8,128,2048]{2,1,0:T(8,128)(2,1)S(1)} copy-done((bf16[8,128,2048]{2,1,0:T(8,128)(2,1)S(1)}, bf16[8,128,2048]{2,1,0:T(8,128)(2,1)}, u32[]{:S(2)}) %copy-start.35) | copy-done | bytes 4194328
  91.2 5.8 %shard_map.73 = (bf16[32,64,512]{2,1,0:T(8,128)(2,1)S(1)}, f32[32,8,512]{2,1,0:T(8,128)S(1)}) custom-call(s32[1]{0:T(128)} %bitcast.8.place, bf16[8,128,2048]{2,1,0:T(8,128)(2,1)S(1)} %copy-done.35, bf16[256,256]{1,0:T(8,128)(2,1)S(1)} %copy-done.37), custom_call_target="tpu_custom_call" | custom-call | flops 2147483648 | bytes 4194304 | tf_op jit(solution)/shard_map/pallas_call | solution.py:151
  97.3 35.2 %all_to_all.20.quantized_ref = bf16[32,64,512]{2,1,0:T(8,128)(2,1)} all-to-all(bf16[32,64,512]{2,1,0:T(8,128)(2,1)S(1)} %get-tuple-element.29), channel_id=1, replica_groups=mesh['dp'=32,'tensor'=8] {'dp'}, dimensions={0} | all-to-all | bytes 4194304 | tf_op jit(solution)/shard_map/all_to_all | solution.py:484
  133.6 19.1 %all_to_all.21.summed_ref = bf16[32,16,512]{2,1,0:T(8,128)(2,1)S(1)} all-to-all(bf16[32,16,512]{2,1,0:T(8,128)(2,1)} %bitcast.21), channel_id=1, replica_groups=mesh['dp'=32,'tensor'=8] {'dp'}, dimensions={0} | all-to-all | bytes 1048576 | tf_op jit(solution)/shard_map/all_to_all | solution.py:486
  152.7 1.3 shard_map.75
  154.0 4.1 %all-to-all-start.3 = ((bf16[8,16,2048]{2,1,0:T(8,128)(2,1)}), bf16[8,16,2048]{2,1,0:T(8,128)(2,1)}, u32[]{:S(2)}, u32[]{:S(2)}) async-start(bf16[8,16,2048]{2,1,0:T(8,128)(2,1)} %shard_map.75), calls=%async_computation.4 | async-start | bytes 1048576 | tf_op jit(solution)/shard_map/all_to_all | solution.py:491
  158.1 1.1 copy-done.3
  160.4 1.6 copy-done.8
  162.0 1.1 copy-done.11
  163.2 1.1 copy-done.14
  164.3 1.1 copy-done.17
  165.4 1.1 copy-done.20
  168.8 1.1 copy-done.29
  170.0 1.1 copy-done.32
  171.1 5.8 %shard_map.76.refs_0_ = f32[512,1536]{1,0:T(8,128)S(1)} custom-call(s32[32]{0:T(128)S(1)} %dynamic-slice_bitcast_fusion.sources, bf16[32,64,512]{2,1,0:T(8,128)(2,1)S(1)} %copy-done.8, bf16[256,1536]{1,0:T(8,128)(2,1)S(1)} %copy-done.6, bf16[256,1536]{1,0:T(8,128)(2,1)S(1)} %copy-done.3, bf16[256,1536]{1,0:T(8,128)(2,1)S(1)} %copy-done.11, ...), custom_call_target="tpu_custom_call" | custom-call | flops 3221225472 | bytes 11534336 | tf_op jit(solution)/shard_map/pallas_call | solution.py:335
  176.9 4.8 %all-to-all-done.3 = bf16[8,16,2048]{2,1,0:T(8,128)(2,1)} async-done(((bf16[8,16,2048]{2,1,0:T(8,128)(2,1)}), bf16[8,16,2048]{2,1,0:T(8,128)(2,1)}, u32[]{:S(2)}, u32[]{:S(2)}) %all-to-all-start.3) | async-done | bytes 524320 | tf_op jit(solution)/shard_map/all_to_all | solution.py:491
  181.8 1.1 copy-done.4
  182.9 1.1 copy-done.7
  186.3 1.1 copy-done.18
  187.5 1.1 copy-done.21
  188.6 1.1 copy-done.24
  193.1 1.6 copy-done.36
  194.7 7.5 %shard_map.77 = f32[512,1536]{1,0:T(8,128)} custom-call(s32[32]{0:T(128)S(1)} %dynamic-slice_bitcast_fusion.sources, bf16[32,64,512]{2,1,0:T(8,128)(2,1)S(1)} %copy-done.36, f32[512,1536]{1,0:T(8,128)S(1)} %shard_map.76.refs_0_, bf16[256,1536]{1,0:T(8,128)(2,1)S(1)} %copy-done.7, bf16[256,1536]{1,0:T(8,128)(2,1)S(1)} %copy-done.4, ...), custom_call_target="tpu_custom_call" | custom-call | flops 3221225472 | bytes 11534336 | tf_op jit(solution)/shard_map/pallas_call | solution.py:335
  202.2 1.9 copy.25
  (102 shorter events, 21.5 us)
Async XLA Ops:
  7.2 32.6 %copy-start.1 = (bf16[512,1536]{1,0:T(8,128)(2,1)S(1)}, bf16[512,1536]{1,0:T(8,128)(2,1)}, u32[]{:S(2)}) copy-start(bf16[512,1536]{1,0:T(8,128)(2,1)} %refs_2_.3) | copy-start | bytes 4718596
  7.2 69.6 %all-gather.3.cloned.1.call-start = ((), (), s32[]{:S(2)}) async-start(), calls=%async_computation.5 | async-start | bytes 4718592 | tf_op jit(solution)/shard_map/all_gather | solution.py:445
  10.3 123.3 %reduce-scatter.2.cloned.1.call-start = ((), (), s32[]{:S(2)}) async-start(), calls=%async_computation.6 | async-start | bytes 4718592 | tf_op jit(solution)/shard_map/reduce_scatter | solution.py:478
  10.3 9.1 %collective-permute-start = (bf16[128,1536]{1,0:T(8,128)(2,1)S(1)}, bf16[128,1536]{1,0:T(8,128)(2,1)S(1)}, u32[]{:S(2)}, u32[]{:S(2)}) collective-permute-start(bf16[128,1536]{1,0:T(8,128)(2,1)S(1)} %bitcast.17), channel_id=1, source_target_pairs={{0,64},{8,24},{16,80},{24,40},{32,96},{40,56},{48,112},{56,8},{64,... | collective-permute-start | bytes 1179656 | tf_op jit(solution)/shard_map/ppermute | solution.py:367
  12.5 11.5 %collective-permute-start.3 = (bf16[128,1536]{1,0:T(8,128)(2,1)S(1)}, bf16[128,1536]{1,0:T(8,128)(2,1)S(1)}, u32[]{:S(2)}, u32[]{:S(2)}) collective-permute-start(bf16[128,1536]{1,0:T(8,128)(2,1)S(1)} %bitcast.18), channel_id=1, source_target_pairs={{0,192},{8,56},{16,208},{24,8},{32,224},{40,24},{48,240},{56,40},{... | collective-permute-start | bytes 1179656 | tf_op jit(solution)/shard_map/ppermute | solution.py:367
  19.4 25.4 %copy-start.5 = (bf16[256,1536]{1,0:T(8,128)(2,1)}, bf16[256,1536]{1,0:T(8,128)(2,1)S(1)}, u32[]{:S(2)}) copy-start(bf16[256,1536]{1,0:T(8,128)(2,1)S(1)} %constant_dynamic-update-slice_fusion.refs_0_.refs_1_) | copy-start | bytes 2359300
  19.5 15.4 %collective-permute-start.1 = (bf16[256,1536]{1,0:T(8,128)(2,1)S(1)}, bf16[256,1536]{1,0:T(8,128)(2,1)}, u32[]{:S(2)}, u32[]{:S(2)}) collective-permute-start(bf16[256,1536]{1,0:T(8,128)(2,1)S(1)} %constant_dynamic-update-slice_fusion.refs_0_.refs_1_), channel_id=1, source_target_pairs={{0,16},{8,72},{16,32},{24,88},{32,48},{40,104},{48,0},{56,120},{64... | collective-permute-start | bytes 2359304 | tf_op jit(solution)/shard_map/ppermute | solution.py:367
  20.4 14.9 %collective-permute-start.8 = (bf16[256,1536]{1,0:T(8,128)(2,1)S(1)}, bf16[256,1536]{1,0:T(8,128)(2,1)S(1)}, u32[]{:S(2)}, u32[]{:S(2)}) collective-permute-start(bf16[256,1536]{1,0:T(8,128)(2,1)S(1)} %constant_dynamic-update-slice_fusion.refs_0_.refs_1_), channel_id=1, source_target_pairs={{0,8},{8,0},{16,24},{24,16},{32,40},{40,32},{48,56},{56,48},{64,72... | collective-permute-start | bytes 2359304 | tf_op jit(solution)/shard_map/ppermute | solution.py:371
  22.9 8.4 %collective-permute-start.4 = (bf16[64,1536]{1,0:T(8,128)(2,1)S(1)}, bf16[64,1536]{1,0:T(8,128)(2,1)S(1)}, u32[]{:S(2)}, u32[]{:S(2)}) collective-permute-start(bf16[64,1536]{1,0:T(8,128)(2,1)S(1)} %slice.8), channel_id=1, source_target_pairs={{0,64},{8,24},{16,80},{24,40},{32,96},{40,56},{48,112},{56,8},{64,... | collective-permute-start | bytes 589832 | tf_op jit(solution)/shard_map/ppermute | solution.py:367
  24.0 7.3 %collective-permute-start.5 = (bf16[64,1536]{1,0:T(8,128)(2,1)S(1)}, bf16[64,1536]{1,0:T(8,128)(2,1)S(1)}, u32[]{:S(2)}, u32[]{:S(2)}) collective-permute-start(bf16[64,1536]{1,0:T(8,128)(2,1)S(1)} %slice.9), channel_id=1, source_target_pairs={{0,192},{8,56},{16,208},{24,8},{32,224},{40,24},{48,240},{56,40},{... | collective-permute-start | bytes 589832 | tf_op jit(solution)/shard_map/ppermute | solution.py:367
  31.3 13.5 %copy-start.2 = (bf16[256,1536]{1,0:T(8,128)(2,1)}, bf16[256,1536]{1,0:T(8,128)(2,1)S(1)}, u32[]{:S(2)}) copy-start(bf16[256,1536]{1,0:T(8,128)(2,1)S(1)} %constant_dynamic-update-slice_fusion.2.refs_1_.refs_2_) | copy-start | bytes 2359300
  31.3 8.5 %collective-permute-start.9 = (bf16[256,1536]{1,0:T(8,128)(2,1)S(1)}, bf16[256,1536]{1,0:T(8,128)(2,1)}, u32[]{:S(2)}, u32[]{:S(2)}) collective-permute-start(bf16[256,1536]{1,0:T(8,128)(2,1)S(1)} %constant_dynamic-update-slice_fusion.2.refs_1_.refs_2_), channel_id=1, source_target_pairs={{0,8},{8,0},{16,24},{24,16},{32,40},{40,32},{48,56},{56,48},{64,72... | collective-permute-start | bytes 2359304 | tf_op jit(solution)/shard_map/ppermute | solution.py:371
  32.1 12.7 %collective-permute-start.6 = (bf16[256,1536]{1,0:T(8,128)(2,1)S(1)}, bf16[256,1536]{1,0:T(8,128)(2,1)}, u32[]{:S(2)}, u32[]{:S(2)}) collective-permute-start(bf16[256,1536]{1,0:T(8,128)(2,1)S(1)} %constant_dynamic-update-slice_fusion.2.refs_1_.refs_2_), channel_id=1, source_target_pairs={{0,16},{8,72},{16,32},{24,88},{32,48},{40,104},{48,0},{56,120},{64... | collective-permute-start | bytes 2359304 | tf_op jit(solution)/shard_map/ppermute | solution.py:367
  32.1 12.7 %collective-permute-start.7 = (bf16[256,1536]{1,0:T(8,128)(2,1)S(1)}, bf16[256,1536]{1,0:T(8,128)(2,1)}, u32[]{:S(2)}, u32[]{:S(2)}) collective-permute-start(bf16[256,1536]{1,0:T(8,128)(2,1)S(1)} %constant_dynamic-update-slice_fusion.2.refs_1_.refs_2_), channel_id=1, source_target_pairs={{0,48},{8,200},{16,0},{24,216},{32,16},{40,232},{48,32},{56,248},{... | collective-permute-start | bytes 2359304 | tf_op jit(solution)/shard_map/ppermute | solution.py:367
  34.8 17.4 %collective-permute-start.11 = (bf16[256,1536]{1,0:T(8,128)(2,1)S(1)}, bf16[256,1536]{1,0:T(8,128)(2,1)}, u32[]{:S(2)}, u32[]{:S(2)}) collective-permute-start(bf16[256,1536]{1,0:T(8,128)(2,1)S(1)} %constant_dynamic-update-slice_fusion.refs_0_.refs_1_), channel_id=1, source_target_pairs={{0,48},{8,200},{16,0},{24,216},{32,16},{40,232},{48,32},{56,248},{... | collective-permute-start | bytes 2359304 | tf_op jit(solution)/shard_map/ppermute | solution.py:367
  36.2 17.8 %collective-permute-start.14 = (bf16[256,1536]{1,0:T(8,128)(2,1)}, bf16[256,1536]{1,0:T(8,128)(2,1)}, u32[]{:S(2)}, u32[]{:S(2)}) collective-permute-start(bf16[256,1536]{1,0:T(8,128)(2,1)} %collective-permute-done.1.refs_0_.refs_4_.refs_5_), channel_id=1, source_target_pairs={{0,8},{8,0},{16,24},{24,16},{32,40},{40,32},{48,56},{56,48},{64,72... | collective-permute-start | bytes 2359304 | tf_op jit(solution)/shard_map/ppermute | solution.py:371
  39.8 1.2 copy-start.10
  44.9 11.9 %collective-permute-start.15 = (bf16[256,1536]{1,0:T(8,128)(2,1)}, bf16[256,1536]{1,0:T(8,128)(2,1)S(1)}, u32[]{:S(2)}, u32[]{:S(2)}) collective-permute-start(bf16[256,1536]{1,0:T(8,128)(2,1)} %collective-permute-done.6.refs_1_.refs_5_.refs_6_), channel_id=1, source_target_pairs={{0,8},{8,0},{16,24},{24,16},{32,40},{40,32},{48,56},{56,48},{64,72... | collective-permute-start | bytes 2359304 | tf_op jit(solution)/shard_map/ppermute | solution.py:371
  52.2 9.2 %collective-permute-start.12 = (bf16[256,1536]{1,0:T(8,128)(2,1)}, bf16[256,1536]{1,0:T(8,128)(2,1)S(1)}, u32[]{:S(2)}, u32[]{:S(2)}) collective-permute-start(bf16[256,1536]{1,0:T(8,128)(2,1)} %collective-permute-done.11.refs_0_.refs_8_.refs_9_), channel_id=1, source_target_pairs={{0,8},{8,0},{16,24},{24,16},{32,40},{40,32},{48,56},{56,48},{64,72... | collective-permute-start | bytes 2359304 | tf_op jit(solution)/shard_map/ppermute | solution.py:371
  54.1 7.4 %collective-permute-start.13 = (bf16[256,1536]{1,0:T(8,128)(2,1)}, bf16[256,1536]{1,0:T(8,128)(2,1)S(1)}, u32[]{:S(2)}, u32[]{:S(2)}) collective-permute-start(bf16[256,1536]{1,0:T(8,128)(2,1)} %collective-permute-done.7.refs_1_.refs_9_.refs_10_), channel_id=1, source_target_pairs={{0,8},{8,0},{16,24},{24,16},{32,40},{40,32},{48,56},{56,48},{64,72... | collective-permute-start | bytes 2359304 | tf_op jit(solution)/shard_map/ppermute | solution.py:371
  54.1 12.7 %collective-permute-start.2 = (bf16[256,1536]{1,0:T(8,128)(2,1)}, bf16[256,1536]{1,0:T(8,128)(2,1)S(1)}, u32[]{:S(2)}, u32[]{:S(2)}) collective-permute-start(bf16[256,1536]{1,0:T(8,128)(2,1)} %collective-permute-done.1.refs_0_.refs_4_.refs_5_), channel_id=1, source_target_pairs={{0,16},{8,72},{16,32},{24,88},{32,48},{40,104},{48,0},{56,120},{64... | collective-permute-start | bytes 2359304 | tf_op jit(solution)/shard_map/ppermute | solution.py:367
  54.1 12.7 %collective-permute-start.10 = (bf16[256,1536]{1,0:T(8,128)(2,1)}, bf16[256,1536]{1,0:T(8,128)(2,1)S(1)}, u32[]{:S(2)}, u32[]{:S(2)}) collective-permute-start(bf16[256,1536]{1,0:T(8,128)(2,1)} %collective-permute-done.7.refs_1_.refs_9_.refs_10_), channel_id=1, source_target_pairs={{0,48},{8,200},{16,0},{24,216},{32,16},{40,232},{48,32},{56,248},{... | collective-permute-start | bytes 2359304 | tf_op jit(solution)/shard_map/ppermute | solution.py:367
  56.7 4.6 %copy-start.13 = (bf16[256,1536]{1,0:T(8,128)(2,1)}, bf16[256,1536]{1,0:T(8,128)(2,1)S(1)}, u32[]{:S(2)}) copy-start(bf16[256,1536]{1,0:T(8,128)(2,1)S(1)} %collective-permute-done.15.refs_3_.refs_7_.refs_8_) | copy-start | bytes 2359300
  61.4 4.7 %copy-start.16 = (bf16[256,1536]{1,0:T(8,128)(2,1)}, bf16[256,1536]{1,0:T(8,128)(2,1)S(1)}, u32[]{:S(2)}) copy-start(bf16[256,1536]{1,0:T(8,128)(2,1)S(1)} %collective-permute-done.12.refs_2_.refs_10_.refs_11_) | copy-start | bytes 2359300
  61.4 4.7 %copy-start.19 = (bf16[256,1536]{1,0:T(8,128)(2,1)}, bf16[256,1536]{1,0:T(8,128)(2,1)S(1)}, u32[]{:S(2)}) copy-start(bf16[256,1536]{1,0:T(8,128)(2,1)S(1)} %collective-permute-done.13.refs_3_.refs_11_.refs_12_) | copy-start | bytes 2359300
  66.7 3.4 %copy-start.22 = (bf16[256,1536]{1,0:T(8,128)(2,1)}, bf16[256,1536]{1,0:T(8,128)(2,1)S(1)}, u32[]{:S(2)}) copy-start(bf16[256,1536]{1,0:T(8,128)(2,1)S(1)} %collective-permute-done.2.refs_0_.refs_12_.refs_13_) | copy-start | bytes 2359300
  66.7 3.4 %copy-start.25 = (bf16[256,1536]{1,0:T(8,128)(2,1)}, bf16[256,1536]{1,0:T(8,128)(2,1)S(1)}, u32[]{:S(2)}) copy-start(bf16[256,1536]{1,0:T(8,128)(2,1)S(1)} %collective-permute-done.10.refs_1_.refs_13_.refs_14_) | copy-start | bytes 2359300
  66.7 3.4 %collective-permute-start.16 = (bf16[256,1536]{1,0:T(8,128)(2,1)S(1)}, bf16[256,1536]{1,0:T(8,128)(2,1)S(1)}, u32[]{:S(2)}, u32[]{:S(2)}) collective-permute-start(bf16[256,1536]{1,0:T(8,128)(2,1)S(1)} %collective-permute-done.2.refs_0_.refs_12_.refs_13_), channel_id=1, source_target_pairs={{0,8},{8,0},{16,24},{24,16},{32,40},{40,32},{48,56},{56,48},{64,72... | collective-permute-start | bytes 2359304 | tf_op jit(solution)/shard_map/ppermute | solution.py:371
  68.1 3.0 %collective-permute-start.17 = (bf16[256,1536]{1,0:T(8,128)(2,1)S(1)}, bf16[256,1536]{1,0:T(8,128)(2,1)S(1)}, u32[]{:S(2)}, u32[]{:S(2)}) collective-permute-start(bf16[256,1536]{1,0:T(8,128)(2,1)S(1)} %collective-permute-done.10.refs_1_.refs_13_.refs_14_), channel_id=1, source_target_pairs={{0,8},{8,0},{16,24},{24,16},{32,40},{40,32},{48,56},{56,48},{64,72... | collective-permute-start | bytes 2359304 | tf_op jit(solution)/shard_map/ppermute | solution.py:371
  73.0 2.0 copy-start
  77.7 2.2 %copy-start.34 = (bf16[8,128,2048]{2,1,0:T(8,128)(2,1)S(1)}, bf16[8,128,2048]{2,1,0:T(8,128)(2,1)}, u32[]{:S(2)}) copy-start(bf16[8,128,2048]{2,1,0:T(8,128)(2,1)} %all-gather.3.cloned.1.call-done.rows_ref) | copy-start | bytes 12582916
  81.9 15.4 %all-to-all-start.1 = ((bf16[32,8,512]{2,1,0:T(8,128)(2,1)}), bf16[32,8,512]{2,1,0:T(8,128)(2,1)S(1)}, u32[]{:S(2)}, u32[]{:S(2)}) async-start(bf16[32,8,512]{2,1,0:T(8,128)(2,1)} %bitcast.9), calls=%async_computation.2 | async-start | bytes 524288 | tf_op jit(solution)/shard_map/all_to_all | solution.py:480
  88.3 93.5 %all-gather.5.cloned.1.call-start = ((), (), s32[]{:S(2)}) async-start(), calls=%async_computation.7 | async-start | bytes 2359296 | tf_op jit(solution)/shard_map/all_gather | solution.py:489
  88.6 2.6 %copy-start.35 = (bf16[8,128,2048]{2,1,0:T(8,128)(2,1)S(1)}, bf16[8,128,2048]{2,1,0:T(8,128)(2,1)}, u32[]{:S(2)}) copy-start(bf16[8,128,2048]{2,1,0:T(8,128)(2,1)} %all-gather.3.cloned.1.call-done.rows_ref) | copy-start | bytes 12582916
  97.3 36.3 %copy-start.38 = (bf16[32,8,512]{2,1,0:T(8,128)(2,1)}, bf16[32,8,512]{2,1,0:T(8,128)(2,1)S(1)}, u32[]{:S(2)}) copy-start(bf16[32,8,512]{2,1,0:T(8,128)(2,1)S(1)} %all-to-all-done.1) | copy-start | bytes 786436
  154.0 27.8 %all-to-all-start.3 = ((bf16[8,16,2048]{2,1,0:T(8,128)(2,1)}), bf16[8,16,2048]{2,1,0:T(8,128)(2,1)}, u32[]{:S(2)}, u32[]{:S(2)}) async-start(bf16[8,16,2048]{2,1,0:T(8,128)(2,1)} %shard_map.75), calls=%async_computation.4 | async-start | bytes 1048576 | tf_op jit(solution)/shard_map/all_to_all | solution.py:491
  158.1 1.1 copy-start.3
  159.3 1.1 copy-start.6
  160.4 1.6 copy-start.8
  162.0 1.1 copy-start.11
  163.2 1.1 copy-start.14
  164.3 1.1 copy-start.17
  165.4 1.1 copy-start.20
  166.6 1.1 copy-start.23
  168.8 1.1 copy-start.29
  170.0 1.1 copy-start.32
  181.8 1.1 copy-start.4
  193.1 1.6 copy-start.36
  (14 other events, 14.9 us)
Sparse Core Ops, SparseCore 0:
  10.4 58.6 all-gather.2
  76.9 56.5 reduce-scatter.1
  135.4 46.3 all-gather.4

commit v10 on v9

v10 whole, which is shorter than its diff:
```python
import functools
import math

import jax
import jax.numpy as jnp
import numpy as np
from jax import lax
from jax.experimental import pallas as pl
from jax.experimental.pallas import tpu as pltpu
from jax.sharding import PartitionSpec as P

BLOCK = 1024
WIDTH = 16384
TABLE = 256
LANES = 128
VMEM_BYTES = 16 * 1024 * 1024
HALVES = [slice(start, start + LANES) for start in range(0, TABLE, LANES)]
NORM = 1.0 / math.sqrt(WIDTH)
SIDE = 4
STEP = 16
OFFSETS = (0, -1, 1, -2)

levels = 127.0
ripple = 0.5
epsilon = 1e-06


def hadamard_table(length):
    table = np.ones((1, 1), np.float32)
    while table.shape[0] < length:
        table = np.block([[table, table], [table, -table]])
    return jnp.asarray(table, jnp.bfloat16)


def fit(odd, terms):
    nodes = 0.5 * np.cos(np.pi * (np.arange(400) + 0.5) / 800.0)
    squares = nodes * nodes
    values = np.sin(2.0 * np.pi * nodes) / nodes if odd else np.cos(2.0 * np.pi * nodes)
    scaled = np.polynomial.chebyshev.Chebyshev.fit(squares, values, terms - 1, domain=[0.0, 0.25])
    return [float(c) for c in scaled.convert(kind=np.polynomial.Polynomial).coef]


SINE = fit(True, 6)
COSINE = fit(False, 7)


def horner(coefficients, square):
    total = jnp.full_like(square, coefficients[-1])
    for coefficient in coefficients[-2::-1]:
        total = total * square + coefficient
    return total


def butterfly(parts):
    distance = 1
    while distance < len(parts):
        mixed = list(parts)
        for low in range(len(parts)):
            if not low & distance:
                mixed[low] = parts[low] + parts[low | distance]
                mixed[low | distance] = parts[low] - parts[low | distance]
        parts = mixed
        distance *= 2
    return parts


def levels_of(largest):
    rows = largest.shape[0]
    peak = jnp.max(largest, axis=1, keepdims=True) * NORM
    scale = (peak + epsilon) / levels
    inverse = jnp.broadcast_to(NORM / scale, (rows, LANES))
    depth = jnp.broadcast_to((ripple / (2.0 * math.pi)) * scale, (rows, LANES))
    return inverse, depth


def remainder(value, inverse):
    turns = value * inverse
    return turns - jnp.round(turns)


def quantized_of(value, inverse, depth):
    rest = remainder(value, inverse)
    return value * NORM - depth * (rest * horner(SINE, rest * rest))


def slope_of(value, inverse):
    rest = remainder(value, inverse)
    return 1.0 - ripple * horner(COSINE, rest * rest)


def mix(rows, table, inner, spans):
    chunks = inner.shape[0]
    for c in range(chunks):
        inner[c] = jnp.dot(
            rows[:, c * TABLE : (c + 1) * TABLE], table, preferred_element_type=jnp.float32
        )
    return [mix_group(inner, group) for group in spans]


def mix_group(inner, spans):
    chunks = inner.shape[0]
    rows = spans[0].stop - spans[0].start
    for span in spans:
        for lanes in HALVES:
            parts = butterfly([inner[c, span, lanes] for c in range(chunks)])
            for c in range(chunks):
                inner[c, span, lanes] = parts[c]
    largest = jnp.zeros((rows, LANES), jnp.float32)
    for c in range(chunks):
        for lanes in HALVES:
            parts = butterfly([inner[c, span, lanes] for span in spans])
            for span, part in zip(spans, parts):
                inner[c, span, lanes] = part
                largest = jnp.maximum(largest, jnp.abs(part))
    return largest


def quantize_kernel(rows_ref, table_ref, quantized_ref, inner):
    members, count, features = rows_ref.shape
    width = quantized_ref.shape[2]
    chunks, per_shard, per_width = features // TABLE, features // width, width // TABLE
    groups = [
        [slice(t * count + g, t * count + g + STEP) for t in range(members)]
        for g in range(0, count, STEP)
    ]
    rows = rows_ref[...].reshape(members * count, features)
    found = mix(rows, table_ref[...], inner, groups)
    for g, (spans, largest) in enumerate(zip(groups, found)):
        inverse, depth = levels_of(largest)
        here = slice(g * STEP, (g + 1) * STEP)
        for t, span in enumerate(spans):
            for c in range(chunks):
                for l, lanes in enumerate(HALVES):
                    start = (c % per_width) * TABLE + l * LANES
                    block = t * per_shard + c // per_width
                    quantized_ref[block, here, start : start + LANES] = quantized_of(
                        inner[c, span, lanes], inverse, depth
                    ).astype(jnp.bfloat16)


def quantize(rows, table, dp, width):
    members, tokens, features = rows.shape
    tokens, count = tokens // 2, 2 * STEP
    return pl.pallas_call(
        quantize_kernel,
        grid=(tokens // count,),
        in_specs=[
            pl.BlockSpec((members, count, features), lambda i: (0, i, 0)),
            pl.BlockSpec((TABLE, TABLE), lambda i: (0, 0)),
        ],
        out_specs=pl.BlockSpec((dp, count, width), lambda i: (0, i, 0)),
        scratch_shapes=[pltpu.VMEM((features // TABLE, members * count, TABLE), jnp.float32)],
        out_shape=jax.ShapeDtypeStruct((dp, tokens, width), jnp.bfloat16),
        compiler_params=pltpu.CompilerParams(vmem_limit_bytes=VMEM_BYTES),
        cost_estimate=pl.CostEstimate(
            flops=2 * tokens * WIDTH * BLOCK, bytes_accessed=4 * tokens * WIDTH, transcendentals=0
        ),
    )(rows, table)


def quantize_own_kernel(place, mine_ref, spread_ref, table_ref, quantized_ref, slope_ref, inner):
    devices, _, width = slope_ref.shape
    own = quantized_ref.shape[0] // devices
    members, _, features = mine_ref.shape
    per_shard, per_width = devices // members, width // TABLE
    spans = [slice(t * STEP, (t + 1) * STEP) for t in range(members)]

    def blocks():
        for block in range(devices):
            for k in range(per_width):
                for l, lanes in enumerate(HALVES):
                    t, c = block // per_shard, block % per_shard * per_width + k
                    start = k * TABLE + l * LANES
                    yield block, t, c, lanes, slice(start, start + LANES)

    flat = lambda ref: ref[...].reshape(members * STEP, features)
    (largest,) = mix(flat(mine_ref), table_ref[...], inner, [spans])
    inverse, _ = levels_of(largest)
    for block, t, c, lanes, columns in blocks():
        slope_ref[block, :, columns] = slope_of(inner[c, spans[t], lanes], inverse)
    (largest,) = mix(flat(spread_ref), table_ref[...], inner, [spans])
    upper = place[0] % 2 == 1
    inverse, depth = levels_of(jnp.where(upper, largest[own:], largest[:own]))
    shift = pl.multiple_of(place[0] % 2 * own, own)
    held = {}
    for block, t, c, lanes, columns in blocks():
        rows = pl.ds(pl.multiple_of(t * STEP + shift, own), own)
        value = quantized_of(inner[c, rows, lanes], inverse, depth)
        if block % 2 == 0:
            held[columns.start] = value
        else:
            quantized_ref[(block - 1) * own : (block + 1) * own, columns] = jnp.concatenate(
                [held[columns.start], value], axis=0
            ).astype(jnp.bfloat16)


def quantize_own(rows, table, place, dp, width):
    members, tokens, features = rows.shape
    own, half = STEP // 2, tokens // 2 // STEP
    shape = (members, STEP, features)
    return pl.pallas_call(
        quantize_own_kernel,
        grid_spec=pltpu.PrefetchScalarGridSpec(
            num_scalar_prefetch=1,
            grid=(1,),
            in_specs=[
                pl.BlockSpec(shape, lambda i, place: (0, place[0], 0)),
                pl.BlockSpec(shape, lambda i, place: (0, half + place[0] // 2, 0)),
                pl.BlockSpec((TABLE, TABLE), lambda i, place: (0, 0)),
            ],
            out_specs=[
                pl.BlockSpec((dp * own, width), lambda i, place: (0, 0)),
                pl.BlockSpec((dp, STEP, width), lambda i, place: (0, 0, 0)),
            ],
            scratch_shapes=[pltpu.VMEM((features // TABLE, members * STEP, TABLE), jnp.float32)],
        ),
        out_shape=[
            jax.ShapeDtypeStruct((dp * own, width), jnp.bfloat16),
            jax.ShapeDtypeStruct((dp, STEP, width), jnp.float32),
        ],
        compiler_params=pltpu.CompilerParams(vmem_limit_bytes=VMEM_BYTES),
        cost_estimate=pl.CostEstimate(
            flops=2 * STEP * WIDTH * BLOCK, bytes_accessed=8 * STEP * WIDTH, transcendentals=0
        ),
    )(place, rows, rows, table)


def product_kernel(count, slots, sources, *refs):
    pieces, weight_ref = refs[: 2 * count], refs[2 * count]
    out_ref, early_ref, late_ref, results, out_sems, row_sems = refs[-6:]
    members, tokens = out_ref.shape[0], out_ref.shape[0] * STEP
    half = early_ref.shape[1]
    stores = []
    for n in range(count):
        for k in range(4):
            piece, first = pieces[2 * n + k // 2], k % 2 * tokens
            source = sources[slots[n] + k]
            for h, ref in enumerate((early_ref, late_ref)):
                stores.append(
                    pltpu.make_async_copy(
                        piece.at[pl.ds(first + h * half, half), :],
                        ref.at[source],
                        row_sems.at[n, k, h],
                    )
                )
                stores[-1].start()
    for n in range(count):
        result = lax.dot_general(
            jnp.concatenate([pieces[2 * n][...], pieces[2 * n + 1][...]], axis=0),
            weight_ref[...],
            (((1,), (1,)), ((), ())),
            preferred_element_type=jnp.float32,
        ).astype(results.dtype)
        for k in range(4):
            for t in range(members):
                start = k * tokens + t * STEP
                results[n, k, t] = result[start : start + STEP]
            place = pl.multiple_of(sources[slots[n] + k] * STEP, STEP)
            stores.append(
                pltpu.make_async_copy(
                    results.at[n, k], out_ref.at[:, pl.ds(place, STEP), :], out_sems.at[n, k]
                )
            )
            stores[-1].start()
    for store in stores:
        store.wait()


def product(held, pieces, slots, weight, sources, members, dp):
    count, rows = len(pieces) // 2, pieces[0].shape[0]
    width, depth = weight.shape
    half = members * STEP // 2
    shapes = [(members, dp * STEP, width), (dp, half, depth), (dp, half, depth)]
    earlier = [] if held is None else list(held)
    return pl.pallas_call(
        functools.partial(product_kernel, count, slots),
        in_specs=[pl.BlockSpec(memory_space=pltpu.SMEM)]
        + [pl.BlockSpec(memory_space=pltpu.VMEM)] * (2 * count + 1)
        + [pl.BlockSpec(memory_space=pltpu.HBM)] * len(earlier),
        out_specs=[pl.BlockSpec(memory_space=pltpu.HBM)] * 3,
        out_shape=[jax.ShapeDtypeStruct(shape, jnp.bfloat16) for shape in shapes],
        scratch_shapes=[
            pltpu.VMEM((count, 4, members, STEP, width), jnp.bfloat16),
            pltpu.SemaphoreType.DMA((count, 4)),
            pltpu.SemaphoreType.DMA((count, 4, 2)),
        ],
        input_output_aliases={2 * count + 2 + n: n for n in range(len(earlier))},
        compiler_params=pltpu.CompilerParams(vmem_limit_bytes=VMEM_BYTES),
        cost_estimate=pl.CostEstimate(
            flops=4 * count * rows * depth * width,
            bytes_accessed=4 * count * rows * (depth + width),
            transcendentals=0,
        ),
    )(sources, *pieces, weight, *earlier)


def gradient(quantized, rows):
    return lax.dot_general(
        quantized.reshape(-1, quantized.shape[2]),
        rows.reshape(-1, rows.shape[2]),
        (((0,), (0,)), ((), ())),
        preferred_element_type=jnp.float32,
    )


def chip_core(x, y, core):
    return (x % SIDE * SIDE + y % SIDE) * 2 + core


def route(turn, sign):
    pairs = []
    for x in range(SIDE):
        for y in range(SIDE):
            for core in range(2):
                along = (sign, 0) if core == turn else (0, sign)
                pairs.append(
                    (chip_core(x, y, core), chip_core(x + along[0], y + along[1], core))
                )
    return pairs


def send(block, turn, sign):
    return lax.ppermute(block, "dp", route(turn, sign))


def other_core(block):
    return lax.ppermute(block, "dp", [(d, d ^ 1) for d in range(2 * SIDE * SIDE)])


def sources_table():
    table = []
    for x in range(SIDE):
        for y in range(SIDE):
            for core in range(2):
                found = []
                for outer in OFFSETS:
                    for sender in (core, 1 - core):
                        for inner in OFFSETS:
                            along = (inner, outer) if sender == 0 else (outer, inner)
                            found.append(chip_core(x + along[0], y + along[1], sender))
                table.append(found)
    return np.asarray(table, np.int32)


def finish_kernel(summed_ref, slope_ref, table_ref, out_ref, inner):
    devices, step, width = summed_ref.shape
    members, per_width = out_ref.shape[0], width // TABLE
    per_shard = devices // members
    upstream = (summed_ref[...].astype(jnp.float32) * slope_ref[...]).astype(jnp.bfloat16)
    upstream = upstream.reshape(devices * step, width)
    for c in range(per_width):
        inner[c] = jnp.dot(
            upstream[:, c * TABLE : (c + 1) * TABLE],
            table_ref[...],
            preferred_element_type=jnp.float32,
        )
    span = lambda d: slice(d * step, (d + 1) * step)
    for l in range(TABLE // LANES):
        lanes = slice(l * LANES, (l + 1) * LANES)
        for t in range(members):
            near = [(c, span(t * per_shard + k)) for k in range(per_shard) for c in range(per_width)]
            parts = butterfly([inner[c, rows, lanes] for c, rows in near])
            for (c, rows), part in zip(near, parts):
                inner[c, rows, lanes] = part
        for k in range(per_shard):
            for c in range(per_width):
                far = [span(t * per_shard + k) for t in range(members)]
                parts = butterfly([inner[c, rows, lanes] for rows in far])
                start = (k * per_width + c) * TABLE + l * LANES
                for t in range(members):
                    out_ref[t, :, start : start + LANES] = (parts[t] * NORM).astype(out_ref.dtype)


def finish(summed, slope, table, members):
    devices, step, width = summed.shape
    return pl.pallas_call(
        finish_kernel,
        out_shape=jax.ShapeDtypeStruct((members, step, WIDTH // members), jnp.bfloat16),
        scratch_shapes=[pltpu.VMEM((width // TABLE, devices * step, TABLE), jnp.float32)],
        compiler_params=pltpu.CompilerParams(vmem_limit_bytes=VMEM_BYTES),
        cost_estimate=pl.CostEstimate(
            flops=2 * step * WIDTH * BLOCK, bytes_accessed=8 * step * WIDTH, transcendentals=0
        ),
    )(summed, slope, table)


def shards(activations, weight, grad_out):
    dp = lax.axis_size("dp")
    members = lax.axis_size("tensor")
    tokens, features = activations.shape
    width = weight.shape[0]
    place = lax.axis_index("tensor").astype(jnp.int32).reshape(1)
    sources = jnp.asarray(sources_table())[lax.axis_index("dp")]
    table = hadamard_table(TABLE)
    own, half = STEP // 2, tokens // 2
    wide_rows = lax.all_gather(activations, "tensor", axis=0, tiled=False)

    def multiply(held, pieces, slot):
        slots = [slot + 4 * n for n in range(len(pieces) // 2)]
        return product(held, pieces, slots, weight, sources, members, dp)

    below, above = send(grad_out, 0, 1), send(grad_out, 0, -1)
    top = jnp.concatenate([grad_out, below], axis=0)
    below_top, above_top = send(top, 1, 1), send(top, 1, -1)
    far = [send(below[:half], 0, 1), send(above[half:], 0, -1)]
    bottom = jnp.concatenate([above, *far], axis=0)
    below_bottom, above_bottom = send(bottom, 1, 1), send(bottom, 1, -1)
    far_top = send(below_top, 1, 1)
    near = [top, bottom]
    near_other = [other_core(block) for block in near]
    held = multiply(None, near + near_other, 0)
    below_bottom, above_bottom, held = lax.optimization_barrier(
        (below_bottom, above_bottom, held)
    )
    far_bottom = send(above_bottom, 1, -1)
    below, above = [below_top, below_bottom], [above_top, above_bottom]
    below_other = [other_core(block) for block in below]
    above_other = [other_core(block) for block in above]
    held = multiply(held, below + below_other, 8)
    held = multiply(held, above + above_other, 16)
    far_top, far_bottom, held = lax.optimization_barrier((far_top, far_bottom, held))
    far = [far_top, far_bottom]
    far_other = [other_core(block) for block in far]
    held = multiply(held, far, 24)
    partial_rows, rows_early, rows_late = multiply(held, far_other, 28)
    partial_rows, wide_rows = lax.optimization_barrier((partial_rows, wide_rows))
    summed = lax.psum_scatter(partial_rows, "tensor", scatter_dimension=0, tiled=False)
    late, slope = quantize_own(wide_rows, table, place, dp, width)
    q_own = lax.all_to_all(
        late.reshape(dp, own, width), "dp", split_axis=0, concat_axis=0, tiled=True
    )
    early = quantize(wide_rows, table, dp, width)
    q_early = lax.all_to_all(early, "dp", split_axis=0, concat_axis=0, tiled=True)
    summed, q_early, q_own = lax.optimization_barrier((summed, q_early, q_own))
    homed = lax.all_to_all(
        summed.reshape(dp, STEP, width), "dp", split_axis=0, concat_axis=0, tiled=True
    )
    q_late = lax.all_gather(q_own, "tensor", axis=1, tiled=True)
    mixed = finish(homed, slope, table, members)
    grad_input = lax.all_to_all(mixed, "tensor", split_axis=0, concat_axis=0, tiled=True)
    early_sum = gradient(q_early, rows_early)
    early_sum, q_late = lax.optimization_barrier((early_sum, q_late))
    weight_sum = early_sum + gradient(q_late, rows_late)
    return (grad_input.reshape(tokens, features), weight_sum)


def solution(mesh):
    return jax.shard_map(
        shards,
        mesh=mesh,
        in_specs=(P("dp", "tensor"), P("dp", "tensor"), P("dp", "tensor")),
        out_specs=(P("dp", "tensor"), P("dp", "tensor")),
        check_vma=False,
    )
```

time: 214 us -> 212 us (level)
  local copies, waits for them, and re-layouts: 43.1 us -> 21.9 us
  matrix products: 0 us -> 14.9 us
  waiting for transfers between devices: 24.3 us -> 33.1 us
  starting transfers between devices: 35.6 us -> 32.5 us
    unnamed x82 -> x24, local copies, waits for them, and re-layouts: 39.3 us -> 19.7 us
    dot_general x0 -> x2, matrix products: none -> 14.9 us  [gradient(): lax.dot_general(quantized.reshape(-1, quantized.shape[2]), rows.reshape(-...]
    pallas_call x5, Pallas kernels: 17 us -> 31.8 us  [product(): pl.pallas_call(functools.partial(product_kernel, count, slots), in_specs=...]
    pallas_call x3 -> x1, Pallas kernels: 19.1 us -> 5.06 us  [quantize(): pl.pallas_call(quantize_kernel, grid=(tokens // count,), in_specs=[pl.Blo...]
    all_to_all x1, waiting for transfers between devices: 4.82 us -> 16.7 us  [shards(): lax.all_to_all(mixed, 'tensor', split_axis=0, concat_axis=0, tiled=True)]
    ppermute x10, waiting for transfers between devices: 17 us -> 11.7 us  [send(): return lax.ppermute(block, 'dp', route(turn, sign))]
    reshape x2 -> x0, local copies, waits for them, and re-layouts: 3.01 us -> none  [the longest x1 1.99 us: shards(): activations.reshape(members, 2, own, features)]
  transfers between devices with their start and end apart: 23 -> 23, of which waited for: 9 -> 7; matrix products, arithmetic and copies ran while one was open for 0% -> 6% of each run, Pallas kernels for 15% -> 19%
where the time goes in v10:
time: 212 us; the launch traced here: 210 us
  blocking collectives  52.9 us (25%)
  Pallas kernels  41 us (19%)
  waiting for transfers between devices  33.1 us (16%)
  starting transfers between devices  32.5 us (15%)
  local copies, waits for them, and re-layouts  21.9 us (10%)
  matrix products  14.9 us (7%)
  between operations  14 us (7%)
    all_to_all x1, blocking collectives, shards(): lax.all_to_all(early, 'dp', split_axis=0, concat_axis=0, tiled=True)  33.8 us
    pallas_call x5, Pallas kernels, product(): pl.pallas_call(functools.partial(product_kernel, count, slots), in_specs=...  31.8 us
    unnamed x24, local copies, waits for them, and re-layouts  19.7 us
    all_to_all x1, blocking collectives, shards(): lax.all_to_all(summed.reshape(dp, STEP, width), 'dp', split_axis=0, conca...  19.1 us
    all_to_all x1, waiting for transfers between devices, shards(): lax.all_to_all(mixed, 'tensor', split_axis=0, concat_axis=0, tiled=True)  16.7 us
    dot_general x2, matrix products, gradient(): lax.dot_general(quantized.reshape(-1, quantized.shape[2]), rows.reshape(-...  14.9 us
    ppermute x10, starting transfers between devices, send(): return lax.ppermute(block, 'dp', route(turn, sign))  12.7 us
    ppermute x10, waiting for transfers between devices, send(): return lax.ppermute(block, 'dp', route(turn, sign))  11.7 us
  transfers between devices with their start and end apart: 23, of which 7 were waited for; matrix products, arithmetic and copies ran while one was open for 6% of the time, Pallas kernels for 19%

profile of v10, /device:TPU:1, one launch (start us, length us, event | category | flops | bytes accessed | tf_op | source)
XLA Modules:
  0.0 210.2 jit_solution(1366639616357678908)
XLA Ops:
  7.2 0.7 all-gather.6.cloned.1.call-update
  8.0 2.2 %collective-permute-start = (bf16[128,1536]{1,0:T(8,128)(2,1)}, bf16[128,1536]{1,0:T(8,128)(2,1)S(1)}, u32[]{:S(2)}, u32[]{:S(2)}) collective-permute-start(bf16[128,1536]{1,0:T(8,128)(2,1)} %param.7), channel_id=1, source_target_pairs={{0,64},{8,24},{16,80},{24,40},{32,96},{40,56},{48,112},{56,8},{64,... | collective-permute-start | bytes 1179656 | tf_op jit(solution)/shard_map/ppermute | solution.py:323
  10.2 1.5 collective-permute-start.3
  11.7 1.8 constant_dynamic-update-slice_fusion.1
  13.5 3.8 %collective-permute-done = bf16[128,1536]{1,0:T(8,128)(2,1)S(1)} collective-permute-done((bf16[128,1536]{1,0:T(8,128)(2,1)}, bf16[128,1536]{1,0:T(8,128)(2,1)S(1)}, u32[]{:S(2)}, u32[]{:S(2)}) %collective-permute-start) | collective-permute-done | bytes 393248 | tf_op jit(solution)/shard_map/ppermute | solution.py:323
  17.3 0.8 constant_dynamic-update-slice_fusion.refs_0_
  18.0 3.2 %collective-permute-start.8 = (bf16[256,1536]{1,0:T(8,128)(2,1)}, bf16[256,1536]{1,0:T(8,128)(2,1)S(1)}, u32[]{:S(2)}, u32[]{:S(2)}) collective-permute-start(bf16[256,1536]{1,0:T(8,128)(2,1)} %constant_dynamic-update-slice_fusion.refs_0_), channel_id=1, source_target_pairs={{0,8},{8,0},{16,24},{24,16},{32,40},{40,32},{48,56},{56,48},{64,72... | collective-permute-start | bytes 2359304 | tf_op jit(solution)/shard_map/ppermute | solution.py:327
  21.4 2.7 %collective-permute-start.5 = (bf16[64,1536]{1,0:T(8,128)(2,1)S(1)}, bf16[64,1536]{1,0:T(8,128)(2,1)S(1)}, u32[]{:S(2)}, u32[]{:S(2)}) collective-permute-start(bf16[64,1536]{1,0:T(8,128)(2,1)S(1)} %slice.9), channel_id=1, source_target_pairs={{0,192},{8,56},{16,208},{24,8},{32,224},{40,24},{48,240},{56,40},{... | collective-permute-start | bytes 589832 | tf_op jit(solution)/shard_map/ppermute | solution.py:323
  24.1 0.8 constant_dynamic-update-slice_fusion.4
  24.9 4.1 %collective-permute-done.4 = bf16[64,1536]{1,0:T(8,128)(2,1)S(1)} collective-permute-done((bf16[64,1536]{1,0:T(8,128)(2,1)S(1)}, bf16[64,1536]{1,0:T(8,128)(2,1)S(1)}, u32[]{:S(2)}, u32[]{:S(2)}) %collective-permute-start.4) | collective-permute-done | bytes 196640 | tf_op jit(solution)/shard_map/ppermute | solution.py:323
  29.0 0.7 constant_dynamic-update-slice_fusion.3
  29.7 0.7 constant_dynamic-update-slice_fusion.2.refs_1_
  30.3 1.4 collective-permute-start.9
  31.7 2.7 %collective-permute-start.7 = (bf16[256,1536]{1,0:T(8,128)(2,1)}, bf16[256,1536]{1,0:T(8,128)(2,1)S(1)}, u32[]{:S(2)}, u32[]{:S(2)}) collective-permute-start(bf16[256,1536]{1,0:T(8,128)(2,1)} %constant_dynamic-update-slice_fusion.2.refs_1_), channel_id=1, source_target_pairs={{0,48},{8,200},{16,0},{24,216},{32,16},{40,232},{48,32},{56,248},{... | collective-permute-start | bytes 2359304 | tf_op jit(solution)/shard_map/ppermute | solution.py:323
  34.4 0.9 copy-done.7
  35.3 0.8 collective-permute-start.11
  36.1 1.9 collective-permute-start.14
  37.9 0.7 dynamic-slice_bitcast_fusion.sources
  38.6 1.1 copy-done.8
  39.8 8.3 %shard_map.68 = (bf16[8,512,512]{2,1,0:T(8,128)(2,1)S(1)}, bf16[32,64,1536]{2,1,0:T(8,128)(2,1)S(1)}, bf16[32,64,1536]{2,1,0:T(8,128)(2,1)S(1)}) custom-call(s32[32]{0:T(128)S(1)} %dynamic-slice_bitcast_fusion.sources, bf16[256,1536]{1,0:T(8,128)(2,1)} %constant_dynamic-update-slice_fusion.refs_0_, ...), custom_call_target="tpu_custom_call" | custom-call | flops 1610612736 | bytes 4194304 | tf_op jit(solution)/shard_map/pallas_call | solution.py:275
  48.2 3.9 %collective-permute-done.11.refs_0_ = bf16[256,1536]{1,0:T(8,128)(2,1)} collective-permute-done((bf16[256,1536]{1,0:T(8,128)(2,1)}, bf16[256,1536]{1,0:T(8,128)(2,1)}, u32[]{:S(2)}, u32[]{:S(2)}) %collective-permute-start.11) | collective-permute-done | bytes 786464 | tf_op jit(solution)/shard_map/ppermute | solution.py:323
  52.1 1.9 collective-permute-start.12
  53.9 2.7 %collective-permute-start.10 = (bf16[256,1536]{1,0:T(8,128)(2,1)S(1)}, bf16[256,1536]{1,0:T(8,128)(2,1)S(1)}, u32[]{:S(2)}, u32[]{:S(2)}) collective-permute-start(bf16[256,1536]{1,0:T(8,128)(2,1)S(1)} %collective-permute-done.7.refs_1_), channel_id=1, source_target_pairs={{0,48},{8,200},{16,0},{24,216},{32,16},{40,232},{48,32},{56,248},{... | collective-permute-start | bytes 2359304 | tf_op jit(solution)/shard_map/ppermute | solution.py:323
  56.6 8.0 %shard_map.69 = (bf16[8,512,512]{2,1,0:T(8,128)(2,1)S(1)}, bf16[32,64,1536]{2,1,0:T(8,128)(2,1)S(1)}, bf16[32,64,1536]{2,1,0:T(8,128)(2,1)S(1)}) custom-call(s32[32]{0:T(128)S(1)} %dynamic-slice_bitcast_fusion.sources, bf16[256,1536]{1,0:T(8,128)(2,1)S(1)} %collective-permute-done.1.refs_0_, ...), custom_call_target="tpu_custom_call", output_to_operand_aliasing={{0}: (6, {}), {1}: (7, {}), {2}: (8, {})} | custom-call | flops 1610612736 | bytes 4194304 | tf_op jit(solution)/shard_map/pallas_call | solution.py:275
  64.7 7.8 %shard_map.70 = (bf16[8,512,512]{2,1,0:T(8,128)(2,1)S(1)}, bf16[32,64,1536]{2,1,0:T(8,128)(2,1)S(1)}, bf16[32,64,1536]{2,1,0:T(8,128)(2,1)S(1)}) custom-call(s32[32]{0:T(128)S(1)} %dynamic-slice_bitcast_fusion.sources, bf16[256,1536]{1,0:T(8,128)(2,1)} %collective-permute-done.11.refs_0_, ...), custom_call_target="tpu_custom_call", output_to_operand_aliasing={{0}: (6, {}), {1}: (7, {}), {2}: (8, {})} | custom-call | flops 1610612736 | bytes 4194304 | tf_op jit(solution)/shard_map/pallas_call | solution.py:275
  72.5 1.2 collective-permute-start.16
  73.8 3.9 %shard_map.71 = (bf16[8,512,512]{2,1,0:T(8,128)(2,1)S(1)}, bf16[32,64,1536]{2,1,0:T(8,128)(2,1)S(1)}, bf16[32,64,1536]{2,1,0:T(8,128)(2,1)S(1)}) custom-call(s32[32]{0:T(128)S(1)} %dynamic-slice_bitcast_fusion.sources, bf16[256,1536]{1,0:T(8,128)(2,1)S(1)} %collective-permute-done.2.refs_0_, ...), custom_call_target="tpu_custom_call", output_to_operand_aliasing={{0}: (4, {}), {1}: (5, {}), {2}: (6, {})} | custom-call | flops 805306368 | bytes 2097152 | tf_op jit(solution)/shard_map/pallas_call | solution.py:275
  77.6 3.9 %shard_map.72 = (bf16[8,512,512]{2,1,0:T(8,128)(2,1)S(1)}, bf16[32,64,1536]{2,1,0:T(8,128)(2,1)S(1)}, bf16[32,64,1536]{2,1,0:T(8,128)(2,1)S(1)}) custom-call(s32[32]{0:T(128)S(1)} %dynamic-slice_bitcast_fusion.sources, bf16[256,1536]{1,0:T(8,128)(2,1)S(1)} %collective-permute-done.16.refs_0_, ...), custom_call_target="tpu_custom_call", output_to_operand_aliasing={{0}: (4, {}), {1}: (5, {}), {2}: (6, {})} | custom-call | flops 805306368 | bytes 2097152 | tf_op jit(solution)/shard_map/pallas_call | solution.py:275
  81.5 2.7 %copy-done = bf16[32,64,1536]{2,1,0:T(8,128)(2,1)} copy-done((bf16[32,64,1536]{2,1,0:T(8,128)(2,1)}, bf16[32,64,1536]{2,1,0:T(8,128)(2,1)S(1)}, u32[]{:S(2)}) %copy-start) | copy-done | bytes 6291480
  84.2 2.0 copy-done.1
  86.2 2.6 %copy-done.2 = bf16[32,64,1536]{2,1,0:T(8,128)(2,1)} copy-done((bf16[32,64,1536]{2,1,0:T(8,128)(2,1)}, bf16[32,64,1536]{2,1,0:T(8,128)(2,1)S(1)}, u32[]{:S(2)}) %copy-start.2) | copy-done | bytes 6291480
  88.8 0.9 copy-done.6
  89.7 2.2 %copy-done.4 = bf16[1024,2048]{1,0:T(8,128)(2,1)S(1)} copy-done((bf16[1024,2048]{1,0:T(8,128)(2,1)S(1)}, bf16[1024,2048]{1,0:T(8,128)(2,1)}, u32[]{:S(2)}) %copy-start.4) | copy-done | bytes 4194328
  91.9 2.8 %shard_map.74 = (bf16[256,512]{1,0:T(8,128)(2,1)}, f32[32,16,512]{2,1,0:T(8,128)S(1)}) custom-call(s32[1]{0:T(128)} %bitcast.3.place, bf16[8,128,2048]{2,1,0:T(8,128)(2,1)S(1)} %bitcast.18, bf16[8,128,2048]{2,1,0:T(8,128)(2,1)S(1)} %bitcast.19, bf16[256,256]{1,0:T(8,128)(2,1)S(1)} %copy-done.6), custom_call_target="tpu_custom_call" | custom-call | flops 536870912 | bytes 2097152 | tf_op jit(solution)/shard_map/pallas_call | solution.py:201
  94.7 5.8 %all-to-all-start.1 = ((bf16[32,8,512]{2,1,0:T(8,128)(2,1)}), bf16[32,8,512]{2,1,0:T(8,128)(2,1)S(1)}, u32[]{:S(2)}, u32[]{:S(2)}) async-start(bf16[32,8,512]{2,1,0:T(8,128)(2,1)} %bitcast.4), calls=%async_computation.2 | async-start | bytes 524288 | tf_op jit(solution)/shard_map/all_to_all | solution.py:429
  100.6 2.2 %copy-done.5 = bf16[1024,2048]{1,0:T(8,128)(2,1)S(1)} copy-done((bf16[1024,2048]{1,0:T(8,128)(2,1)S(1)}, bf16[1024,2048]{1,0:T(8,128)(2,1)}, u32[]{:S(2)}) %copy-start.5) | copy-done | bytes 4194328
  102.8 5.1 %shard_map.73 = bf16[32,64,512]{2,1,0:T(8,128)(2,1)S(1)} custom-call(bf16[8,128,2048]{2,1,0:T(8,128)(2,1)S(1)} %bitcast.20, bf16[256,256]{1,0:T(8,128)(2,1)S(1)} %copy-done.6), custom_call_target="tpu_custom_call" | custom-call | flops 2147483648 | bytes 4194304 | tf_op jit(solution)/shard_map/pallas_call | solution.py:144
  107.9 1.6 all-to-all-done.1
  109.5 33.8 %all_to_all.20 = bf16[32,64,512]{2,1,0:T(8,128)(2,1)} all-to-all(bf16[32,64,512]{2,1,0:T(8,128)(2,1)S(1)} %shard_map.73), channel_id=1, replica_groups=mesh['dp'=32,'tensor'=8] {'dp'}, dimensions={0} | all-to-all | bytes 4194304 | tf_op jit(solution)/shard_map/all_to_all | solution.py:433
  143.4 0.9 reduce-scatter.2.cloned.1.call-done
  144.3 19.1 %all_to_all.21.summed_ref = bf16[32,16,512]{2,1,0:T(8,128)(2,1)S(1)} all-to-all(bf16[32,16,512]{2,1,0:T(8,128)(2,1)} %bitcast.21), channel_id=1, replica_groups=mesh['dp'=32,'tensor'=8] {'dp'}, dimensions={0} | all-to-all | bytes 1048576 | tf_op jit(solution)/shard_map/all_to_all | solution.py:435
  163.4 1.3 shard_map.75
  164.7 4.1 %all-to-all-start.3 = ((bf16[8,16,2048]{2,1,0:T(8,128)(2,1)}), bf16[8,16,2048]{2,1,0:T(8,128)(2,1)}, u32[]{:S(2)}, u32[]{:S(2)}) async-start(bf16[8,16,2048]{2,1,0:T(8,128)(2,1)} %shard_map.75), calls=%async_computation.4 | async-start | bytes 1048576 | tf_op jit(solution)/shard_map/all_to_all | solution.py:440
  168.9 6.3 %convolution_bitcast_fusion.1 = f32[512,1536]{1,0:T(8,128)S(1)} fusion(bf16[32,64,512]{2,1,0:T(8,128)(2,1)} %all_to_all.20, bf16[32,64,1536]{2,1,0:T(8,128)(2,1)} %copy-done.2), kind=kOutput, calls=%fused_computation.1 | convolution fusion | flops 3221225472 | bytes 11534336 | tf_op jit(solution)/shard_map/dot_general | solution.py:298
  175.2 16.7 %all-to-all-done.3 = bf16[8,16,2048]{2,1,0:T(8,128)(2,1)} async-done(((bf16[8,16,2048]{2,1,0:T(8,128)(2,1)}), bf16[8,16,2048]{2,1,0:T(8,128)(2,1)}, u32[]{:S(2)}, u32[]{:S(2)}) %all-to-all-start.3) | async-done | bytes 524320 | tf_op jit(solution)/shard_map/all_to_all | solution.py:440
  191.9 1.4 all-gather.4.cloned.1.call-done
  193.2 8.5 %fusion = f32[512,1536]{1,0:T(8,128)} fusion(f32[512,1536]{1,0:T(8,128)S(1)} %convolution_bitcast_fusion.1, bf16[32,64,512]{2,1,0:T(8,128)(2,1)} %all-gather.4.cloned.1.call-done, bf16[32,64,1536]{2,1,0:T(8,128)(2,1)} %copy-done), kind=kOutput, calls=%fused_computation.2 | convolution fusion | flops 3222011904 | bytes 14680064 | tf_op jit(solution)/shard_map/dot_general | solution.py:298
  201.8 1.9 copy.35
  (42 shorter events, 0.6 us)
Async XLA Ops:
  7.2 31.5 %copy-start.3 = (bf16[512,1536]{1,0:T(8,128)(2,1)S(1)}, bf16[512,1536]{1,0:T(8,128)(2,1)}, u32[]{:S(2)}) copy-start(bf16[512,1536]{1,0:T(8,128)(2,1)} %refs_2_.3) | copy-start | bytes 4718596
  7.2 81.6 %all-gather.6.cloned.1.call-start = ((), (), s32[]{:S(2)}) async-start(), calls=%async_computation.7 | async-start | bytes 4718592 | tf_op jit(solution)/shard_map/all_gather | solution.py:396
  7.9 136.4 %reduce-scatter.2.cloned.1.call-start = ((), (), s32[]{:S(2)}) async-start(), calls=%async_computation.5 | async-start | bytes 4718592 | tf_op jit(solution)/shard_map/reduce_scatter | solution.py:427
  8.0 9.3 %collective-permute-start = (bf16[128,1536]{1,0:T(8,128)(2,1)}, bf16[128,1536]{1,0:T(8,128)(2,1)S(1)}, u32[]{:S(2)}, u32[]{:S(2)}) collective-permute-start(bf16[128,1536]{1,0:T(8,128)(2,1)} %param.7), channel_id=1, source_target_pairs={{0,64},{8,24},{16,80},{24,40},{32,96},{40,56},{48,112},{56,8},{64,... | collective-permute-start | bytes 1179656 | tf_op jit(solution)/shard_map/ppermute | solution.py:323
  10.2 11.2 %collective-permute-start.3 = (bf16[128,1536]{1,0:T(8,128)(2,1)}, bf16[128,1536]{1,0:T(8,128)(2,1)S(1)}, u32[]{:S(2)}, u32[]{:S(2)}) collective-permute-start(bf16[128,1536]{1,0:T(8,128)(2,1)} %param.7), channel_id=1, source_target_pairs={{0,192},{8,56},{16,208},{24,8},{32,224},{40,24},{48,240},{56,40},{... | collective-permute-start | bytes 1179656 | tf_op jit(solution)/shard_map/ppermute | solution.py:323
  18.0 16.4 %collective-permute-start.8 = (bf16[256,1536]{1,0:T(8,128)(2,1)}, bf16[256,1536]{1,0:T(8,128)(2,1)S(1)}, u32[]{:S(2)}, u32[]{:S(2)}) collective-permute-start(bf16[256,1536]{1,0:T(8,128)(2,1)} %constant_dynamic-update-slice_fusion.refs_0_), channel_id=1, source_target_pairs={{0,8},{8,0},{16,24},{24,16},{32,40},{40,32},{48,56},{56,48},{64,72... | collective-permute-start | bytes 2359304 | tf_op jit(solution)/shard_map/ppermute | solution.py:327
  21.2 14.8 %collective-permute-start.1 = (bf16[256,1536]{1,0:T(8,128)(2,1)}, bf16[256,1536]{1,0:T(8,128)(2,1)S(1)}, u32[]{:S(2)}, u32[]{:S(2)}) collective-permute-start(bf16[256,1536]{1,0:T(8,128)(2,1)} %constant_dynamic-update-slice_fusion.refs_0_), channel_id=1, source_target_pairs={{0,16},{8,72},{16,32},{24,88},{32,48},{40,104},{48,0},{56,120},{64... | collective-permute-start | bytes 2359304 | tf_op jit(solution)/shard_map/ppermute | solution.py:323
  21.3 7.7 %collective-permute-start.4 = (bf16[64,1536]{1,0:T(8,128)(2,1)S(1)}, bf16[64,1536]{1,0:T(8,128)(2,1)S(1)}, u32[]{:S(2)}, u32[]{:S(2)}) collective-permute-start(bf16[64,1536]{1,0:T(8,128)(2,1)S(1)} %slice.8), channel_id=1, source_target_pairs={{0,64},{8,24},{16,80},{24,40},{32,96},{40,56},{48,112},{56,8},{64,... | collective-permute-start | bytes 589832 | tf_op jit(solution)/shard_map/ppermute | solution.py:323
  21.4 8.3 %collective-permute-start.5 = (bf16[64,1536]{1,0:T(8,128)(2,1)S(1)}, bf16[64,1536]{1,0:T(8,128)(2,1)S(1)}, u32[]{:S(2)}, u32[]{:S(2)}) collective-permute-start(bf16[64,1536]{1,0:T(8,128)(2,1)S(1)} %slice.9), channel_id=1, source_target_pairs={{0,192},{8,56},{16,208},{24,8},{32,224},{40,24},{48,240},{56,40},{... | collective-permute-start | bytes 589832 | tf_op jit(solution)/shard_map/ppermute | solution.py:323
  30.3 8.3 %collective-permute-start.9 = (bf16[256,1536]{1,0:T(8,128)(2,1)}, bf16[256,1536]{1,0:T(8,128)(2,1)}, u32[]{:S(2)}, u32[]{:S(2)}) collective-permute-start(bf16[256,1536]{1,0:T(8,128)(2,1)} %constant_dynamic-update-slice_fusion.2.refs_1_), channel_id=1, source_target_pairs={{0,8},{8,0},{16,24},{24,16},{32,40},{40,32},{48,56},{56,48},{64,72... | collective-permute-start | bytes 2359304 | tf_op jit(solution)/shard_map/ppermute | solution.py:327
  31.7 16.3 %collective-permute-start.6 = (bf16[256,1536]{1,0:T(8,128)(2,1)}, bf16[256,1536]{1,0:T(8,128)(2,1)}, u32[]{:S(2)}, u32[]{:S(2)}) collective-permute-start(bf16[256,1536]{1,0:T(8,128)(2,1)} %constant_dynamic-update-slice_fusion.2.refs_1_), channel_id=1, source_target_pairs={{0,16},{8,72},{16,32},{24,88},{32,48},{40,104},{48,0},{56,120},{64... | collective-permute-start | bytes 2359304 | tf_op jit(solution)/shard_map/ppermute | solution.py:323
  31.7 16.3 %collective-permute-start.7 = (bf16[256,1536]{1,0:T(8,128)(2,1)}, bf16[256,1536]{1,0:T(8,128)(2,1)S(1)}, u32[]{:S(2)}, u32[]{:S(2)}) collective-permute-start(bf16[256,1536]{1,0:T(8,128)(2,1)} %constant_dynamic-update-slice_fusion.2.refs_1_), channel_id=1, source_target_pairs={{0,48},{8,200},{16,0},{24,216},{32,16},{40,232},{48,32},{56,248},{... | collective-permute-start | bytes 2359304 | tf_op jit(solution)/shard_map/ppermute | solution.py:323
  34.4 0.9 copy-start.7
  35.3 16.8 %collective-permute-start.11 = (bf16[256,1536]{1,0:T(8,128)(2,1)}, bf16[256,1536]{1,0:T(8,128)(2,1)}, u32[]{:S(2)}, u32[]{:S(2)}) collective-permute-start(bf16[256,1536]{1,0:T(8,128)(2,1)} %constant_dynamic-update-slice_fusion.refs_0_), channel_id=1, source_target_pairs={{0,48},{8,200},{16,0},{24,216},{32,16},{40,232},{48,32},{56,248},{... | collective-permute-start | bytes 2359304 | tf_op jit(solution)/shard_map/ppermute | solution.py:323
  36.1 17.9 %collective-permute-start.14 = (bf16[256,1536]{1,0:T(8,128)(2,1)S(1)}, bf16[256,1536]{1,0:T(8,128)(2,1)}, u32[]{:S(2)}, u32[]{:S(2)}) collective-permute-start(bf16[256,1536]{1,0:T(8,128)(2,1)S(1)} %collective-permute-done.1.refs_0_), channel_id=1, source_target_pairs={{0,8},{8,0},{16,24},{24,16},{32,40},{40,32},{48,56},{56,48},{64,72... | collective-permute-start | bytes 2359304 | tf_op jit(solution)/shard_map/ppermute | solution.py:327
  38.6 1.1 copy-start.8
  48.1 8.6 %collective-permute-start.15 = (bf16[256,1536]{1,0:T(8,128)(2,1)}, bf16[256,1536]{1,0:T(8,128)(2,1)S(1)}, u32[]{:S(2)}, u32[]{:S(2)}) collective-permute-start(bf16[256,1536]{1,0:T(8,128)(2,1)} %collective-permute-done.6.refs_1_), channel_id=1, source_target_pairs={{0,8},{8,0},{16,24},{24,16},{32,40},{40,32},{48,56},{56,48},{64,72... | collective-permute-start | bytes 2359304 | tf_op jit(solution)/shard_map/ppermute | solution.py:327
  52.1 12.6 %collective-permute-start.12 = (bf16[256,1536]{1,0:T(8,128)(2,1)}, bf16[256,1536]{1,0:T(8,128)(2,1)S(1)}, u32[]{:S(2)}, u32[]{:S(2)}) collective-permute-start(bf16[256,1536]{1,0:T(8,128)(2,1)} %collective-permute-done.11.refs_0_), channel_id=1, source_target_pairs={{0,8},{8,0},{16,24},{24,16},{32,40},{40,32},{48,56},{56,48},{64,72... | collective-permute-start | bytes 2359304 | tf_op jit(solution)/shard_map/ppermute | solution.py:327
  53.9 10.7 %collective-permute-start.13 = (bf16[256,1536]{1,0:T(8,128)(2,1)S(1)}, bf16[256,1536]{1,0:T(8,128)(2,1)S(1)}, u32[]{:S(2)}, u32[]{:S(2)}) collective-permute-start(bf16[256,1536]{1,0:T(8,128)(2,1)S(1)} %collective-permute-done.7.refs_1_), channel_id=1, source_target_pairs={{0,8},{8,0},{16,24},{24,16},{32,40},{40,32},{48,56},{56,48},{64,72... | collective-permute-start | bytes 2359304 | tf_op jit(solution)/shard_map/ppermute | solution.py:327
  53.9 18.5 %collective-permute-start.2 = (bf16[256,1536]{1,0:T(8,128)(2,1)S(1)}, bf16[256,1536]{1,0:T(8,128)(2,1)S(1)}, u32[]{:S(2)}, u32[]{:S(2)}) collective-permute-start(bf16[256,1536]{1,0:T(8,128)(2,1)S(1)} %collective-permute-done.1.refs_0_), channel_id=1, source_target_pairs={{0,16},{8,72},{16,32},{24,88},{32,48},{40,104},{48,0},{56,120},{64... | collective-permute-start | bytes 2359304 | tf_op jit(solution)/shard_map/ppermute | solution.py:323
  53.9 18.5 %collective-permute-start.10 = (bf16[256,1536]{1,0:T(8,128)(2,1)S(1)}, bf16[256,1536]{1,0:T(8,128)(2,1)S(1)}, u32[]{:S(2)}, u32[]{:S(2)}) collective-permute-start(bf16[256,1536]{1,0:T(8,128)(2,1)S(1)} %collective-permute-done.7.refs_1_), channel_id=1, source_target_pairs={{0,48},{8,200},{16,0},{24,216},{32,16},{40,232},{48,32},{56,248},{... | collective-permute-start | bytes 2359304 | tf_op jit(solution)/shard_map/ppermute | solution.py:323
  72.5 5.1 %collective-permute-start.16 = (bf16[256,1536]{1,0:T(8,128)(2,1)S(1)}, bf16[256,1536]{1,0:T(8,128)(2,1)S(1)}, u32[]{:S(2)}, u32[]{:S(2)}) collective-permute-start(bf16[256,1536]{1,0:T(8,128)(2,1)S(1)} %collective-permute-done.2.refs_0_), channel_id=1, source_target_pairs={{0,8},{8,0},{16,24},{24,16},{32,40},{40,32},{48,56},{56,48},{64,72... | collective-permute-start | bytes 2359304 | tf_op jit(solution)/shard_map/ppermute | solution.py:327
  73.7 4.0 %collective-permute-start.17 = (bf16[256,1536]{1,0:T(8,128)(2,1)S(1)}, bf16[256,1536]{1,0:T(8,128)(2,1)S(1)}, u32[]{:S(2)}, u32[]{:S(2)}) collective-permute-start(bf16[256,1536]{1,0:T(8,128)(2,1)S(1)} %collective-permute-done.10.refs_1_), channel_id=1, source_target_pairs={{0,8},{8,0},{16,24},{24,16},{32,40},{40,32},{48,56},{56,48},{64,72... | collective-permute-start | bytes 2359304 | tf_op jit(solution)/shard_map/ppermute | solution.py:327
  81.5 2.7 %copy-start = (bf16[32,64,1536]{2,1,0:T(8,128)(2,1)}, bf16[32,64,1536]{2,1,0:T(8,128)(2,1)S(1)}, u32[]{:S(2)}) copy-start(bf16[32,64,1536]{2,1,0:T(8,128)(2,1)S(1)} %get-tuple-element.69) | copy-start | bytes 18874372
  84.2 2.0 copy-start.1
  86.2 2.6 %copy-start.2 = (bf16[32,64,1536]{2,1,0:T(8,128)(2,1)}, bf16[32,64,1536]{2,1,0:T(8,128)(2,1)S(1)}, u32[]{:S(2)}) copy-start(bf16[32,64,1536]{2,1,0:T(8,128)(2,1)S(1)} %get-tuple-element.65) | copy-start | bytes 18874372
  88.8 0.9 copy-start.6
  89.7 2.2 %copy-start.4 = (bf16[1024,2048]{1,0:T(8,128)(2,1)S(1)}, bf16[1024,2048]{1,0:T(8,128)(2,1)}, u32[]{:S(2)}) copy-start(bf16[1024,2048]{1,0:T(8,128)(2,1)} %all-gather.6.cloned.1.call-done) | copy-start | bytes 12582916
  94.7 14.8 %all-to-all-start.1 = ((bf16[32,8,512]{2,1,0:T(8,128)(2,1)}), bf16[32,8,512]{2,1,0:T(8,128)(2,1)S(1)}, u32[]{:S(2)}, u32[]{:S(2)}) async-start(bf16[32,8,512]{2,1,0:T(8,128)(2,1)} %bitcast.4), calls=%async_computation.2 | async-start | bytes 524288 | tf_op jit(solution)/shard_map/all_to_all | solution.py:429
  100.6 92.7 %all-gather.4.cloned.1.call-start = ((), (), s32[]{:S(2)}) async-start(), calls=%async_computation.6 | async-start | bytes 2359296 | tf_op jit(solution)/shard_map/all_gather | solution.py:438
  100.6 2.2 %copy-start.5 = (bf16[1024,2048]{1,0:T(8,128)(2,1)S(1)}, bf16[1024,2048]{1,0:T(8,128)(2,1)}, u32[]{:S(2)}) copy-start(bf16[1024,2048]{1,0:T(8,128)(2,1)} %all-gather.6.cloned.1.call-done) | copy-start | bytes 12582916
  109.5 34.7 %copy-start.9 = (bf16[32,8,512]{2,1,0:T(8,128)(2,1)}, bf16[32,8,512]{2,1,0:T(8,128)(2,1)S(1)}, u32[]{:S(2)}) copy-start(bf16[32,8,512]{2,1,0:T(8,128)(2,1)S(1)} %all-to-all-done.1) | copy-start | bytes 786436
  164.7 27.2 %all-to-all-start.3 = ((bf16[8,16,2048]{2,1,0:T(8,128)(2,1)}), bf16[8,16,2048]{2,1,0:T(8,128)(2,1)}, u32[]{:S(2)}, u32[]{:S(2)}) async-start(bf16[8,16,2048]{2,1,0:T(8,128)(2,1)} %shard_map.75), calls=%async_computation.4 | async-start | bytes 1048576 | tf_op jit(solution)/shard_map/all_to_all | solution.py:440
Sparse Core Ops, SparseCore 0:
  9.8 58.6 all-gather.5
  89.0 55.2 reduce-scatter.1
  146.7 46.5 all-gather.3

commit v11 on v7

--- a/solution.py
+++ b/solution.py
@@ -13,6 +13,7 @@
 TABLE = 256
 LANES = 128
 VMEM_BYTES = 60 * 1024 * 1024
+LITTLE_VMEM = 16 * 1024 * 1024
 NORM = 1.0 / math.sqrt(WIDTH)
 SIDE = 4
 STEP = 16
@@ -189,7 +190,7 @@
         out_specs=pl.BlockSpec((members, rows // members, width), lambda i: (0, position, 0)),
         out_shape=jax.ShapeDtypeStruct((members, total // members, width), jnp.bfloat16),
         input_output_aliases={0: 0} if earlier else {},
-        compiler_params=pltpu.CompilerParams(vmem_limit_bytes=VMEM_BYTES),
+        compiler_params=pltpu.CompilerParams(vmem_limit_bytes=LITTLE_VMEM),
         cost_estimate=pl.CostEstimate(
             flops=2 * rows * depth * width,
             bytes_accessed=2 * rows * (depth + width),
@@ -325,7 +326,7 @@
         finish_kernel,
         out_shape=jax.ShapeDtypeStruct((members, step, WIDTH // members), jnp.bfloat16),
         scratch_shapes=[pltpu.VMEM((width // TABLE, devices * step, TABLE), jnp.float32)],
-        compiler_params=pltpu.CompilerParams(vmem_limit_bytes=VMEM_BYTES),
+        compiler_params=pltpu.CompilerParams(vmem_limit_bytes=LITTLE_VMEM),
         cost_estimate=pl.CostEstimate(
             flops=2 * step * WIDTH * BLOCK, bytes_accessed=8 * step * WIDTH, transcendentals=0
         ),

time: 205 us -> 198 us (0.966)
  Pallas kernels: 55.4 us -> 38.4 us
  waiting for transfers between devices: 70.4 us -> 81.6 us
  local copies, waits for them, and re-layouts: 7.73 us -> 5.3 us
    pallas_call x5, Pallas kernels: 23.1 us -> 7.47 us  [product(): pl.pallas_call(product_kernel, grid=(1,), in_specs=[pl.BlockSpec(memory_s...]
    ppermute x10, waiting for transfers between devices: 16.7 us -> 26.1 us  [send(): return lax.ppermute(block, 'dp', route(turn, sign))]
    unnamed x22 -> x44, local copies, waits for them, and re-layouts: 6.44 us -> 3.97 us
  transfers between devices with their start and end apart: 22 -> 22, of which waited for: 7 -> 10; matrix products, arithmetic and copies ran while one was open for 1% -> 1% of each run, Pallas kernels for 26% -> 19%
where the time goes in v11:
time: 198 us
  waiting for transfers between devices  81.6 us (41%)
  starting transfers between devices  39.4 us (20%)
  Pallas kernels  38.4 us (19%)
  blocking collectives  18.7 us (9%)
  between operations  14.4 us (7%)
  local copies, waits for them, and re-layouts  5.3 us (3%)
    reduce_scatter x1, waiting for transfers between devices, shards(): lax.psum_scatter(partial_rows, 'tensor', scatter_dimension=0, tiled=False)  35.2 us
    ppermute x10, waiting for transfers between devices, send(): return lax.ppermute(block, 'dp', route(turn, sign))  26.1 us
    all_to_all x1, blocking collectives, shards(): lax.all_to_all(ordered, 'dp', split_axis=0, concat_axis=0, tiled=True)  18.7 us
    pallas_call x1, Pallas kernels, gradient(): pl.pallas_call(gradient_kernel, in_specs=[pl.BlockSpec(memory_space=pltpu...  14.2 us
    all_to_all x1, waiting for transfers between devices, shards(): lax.all_to_all(quantized, 'dp', split_axis=0, concat_axis=0, tiled=True)  13.9 us
    ppermute x10, starting transfers between devices, send(): return lax.ppermute(block, 'dp', route(turn, sign))  13.6 us
    pallas_call x1, Pallas kernels, quantize(): pl.pallas_call(quantize_kernel, grid_spec=pltpu.PrefetchScalarGridSpec(nu...  13.6 us
    ppermute x8, starting transfers between devices, other_core(): lax.ppermute(block, 'dp', [(d, d ^ 1) for d in range(2 * SIDE * SIDE)])  11.1 us
  transfers between devices with their start and end apart: 22, of which 10 were waited for; matrix products, arithmetic and copies ran while one was open for 1% of the time, Pallas kernels for 19%

profile of v11, /device:TPU:1, one launch (start us, length us, event | category | flops | bytes accessed | tf_op | source)
XLA Modules:
  0.0 197.8 jit_solution(18417760091099383998)
XLA Ops:
  7.2 0.0 all-gather.3.cloned.1.call-start
  7.2 0.7 all-gather.3.cloned.1.call-update
  7.9 0.0 reduce-scatter.2.cloned.1.call-start
  8.0 2.2 %collective-permute-start = (bf16[128,1536]{1,0:T(8,128)(2,1)}, bf16[128,1536]{1,0:T(8,128)(2,1)S(1)}, u32[]{:S(2)}, u32[]{:S(2)}) collective-permute-start(bf16[128,1536]{1,0:T(8,128)(2,1)} %param.7), channel_id=1, source_target_pairs={{0,64},{8,24},{16,80},{24,40},{32,96},{40,56},{48,112},{56,8},{64,... | collective-permute-start | bytes 1179656 | tf_op jit(solution)/shard_map/ppermute | solution.py:272
  10.2 1.5 collective-permute-start.3
  11.7 1.1 constant_dynamic-update-slice_fusion.1
  12.7 4.5 %collective-permute-done = bf16[128,1536]{1,0:T(8,128)(2,1)S(1)} collective-permute-done((bf16[128,1536]{1,0:T(8,128)(2,1)}, bf16[128,1536]{1,0:T(8,128)(2,1)S(1)}, u32[]{:S(2)}, u32[]{:S(2)}) %collective-permute-start) | collective-permute-done | bytes 393248 | tf_op jit(solution)/shard_map/ppermute | solution.py:272
  17.3 1.0 collective-permute-start.1
  18.3 2.4 %collective-permute-start.8 = (bf16[256,1536]{1,0:T(8,128)(2,1)S(1)}, bf16[256,1536]{1,0:T(8,128)(2,1)S(1)}, u32[]{:S(2)}, u32[]{:S(2)}) collective-permute-start(bf16[256,1536]{1,0:T(8,128)(2,1)S(1)} %constant_dynamic-update-slice_fusion.refs_0_), channel_id=1, source_target_pairs={{0,8},{8,0},{16,24},{24,16},{32,40},{40,32},{48,56},{56,48},{64,72... | collective-permute-start | bytes 2359304 | tf_op jit(solution)/shard_map/ppermute | solution.py:276
  20.7 1.1 collective-permute-start.4
  21.8 0.0 collective-permute-done.3
  21.8 1.9 collective-permute-start.5
  23.8 5.2 %collective-permute-done.4 = bf16[64,1536]{1,0:T(8,128)(2,1)S(1)} collective-permute-done((bf16[64,1536]{1,0:T(8,128)(2,1)S(1)}, bf16[64,1536]{1,0:T(8,128)(2,1)S(1)}, u32[]{:S(2)}, u32[]{:S(2)}) %collective-permute-start.4) | collective-permute-done | bytes 196640 | tf_op jit(solution)/shard_map/ppermute | solution.py:272
  29.1 0.9 collective-permute-start.9
  30.0 0.0 collective-permute-start.6
  30.0 2.7 %collective-permute-start.7 = (bf16[256,1536]{1,0:T(8,128)(2,1)S(1)}, bf16[256,1536]{1,0:T(8,128)(2,1)S(1)}, u32[]{:S(2)}, u32[]{:S(2)}) collective-permute-start(bf16[256,1536]{1,0:T(8,128)(2,1)S(1)} %constant_dynamic-update-slice_fusion.2.refs_1_), channel_id=1, source_target_pairs={{0,48},{8,200},{16,0},{24,216},{32,16},{40,232},{48,32},{56,248},{... | collective-permute-start | bytes 2359304 | tf_op jit(solution)/shard_map/ppermute | solution.py:272
  32.7 0.0 collective-permute-done.1.refs_1_.refs_4_
  32.7 0.5 collective-permute-start.13
  33.2 2.8 %collective-permute-start.11 = (bf16[256,1536]{1,0:T(8,128)(2,1)S(1)}, bf16[256,1536]{1,0:T(8,128)(2,1)S(1)}, u32[]{:S(2)}, u32[]{:S(2)}) collective-permute-start(bf16[256,1536]{1,0:T(8,128)(2,1)S(1)} %collective-permute-done.1.refs_1_.refs_4_), channel_id=1, source_target_pairs={{0,8},{8,0},{16,24},{24,16},{32,40},{40,32},{48,56},{56,48},{64,72... | collective-permute-start | bytes 2359304 | tf_op jit(solution)/shard_map/ppermute | solution.py:276
  36.0 1.8 shard_map.68.refs_0_
  37.8 4.6 %collective-permute-done.6.refs_2_.refs_5_ = bf16[256,1536]{1,0:T(8,128)(2,1)S(1)} collective-permute-done((bf16[256,1536]{1,0:T(8,128)(2,1)S(1)}, bf16[256,1536]{1,0:T(8,128)(2,1)S(1)}, u32[]{:S(2)}, u32[]{:S(2)}) %collective-permute-start.6) | collective-permute-done | bytes 786464 | tf_op jit(solution)/shard_map/ppermute | solution.py:272
  42.5 1.9 collective-permute-start.12
  44.3 5.7 %collective-permute-done.13.refs_1_.refs_8_ = bf16[256,1536]{1,0:T(8,128)(2,1)S(1)} collective-permute-done((bf16[256,1536]{1,0:T(8,128)(2,1)S(1)}, bf16[256,1536]{1,0:T(8,128)(2,1)S(1)}, u32[]{:S(2)}, u32[]{:S(2)}) %collective-permute-start.13) | collective-permute-done | bytes 786464 | tf_op jit(solution)/shard_map/ppermute | solution.py:272
  50.0 1.8 collective-permute-start.14
  51.8 2.7 %collective-permute-start.10 = (bf16[256,1536]{1,0:T(8,128)(2,1)S(1)}, bf16[256,1536]{1,0:T(8,128)(2,1)S(1)}, u32[]{:S(2)}, u32[]{:S(2)}) collective-permute-start(bf16[256,1536]{1,0:T(8,128)(2,1)S(1)} %collective-permute-done.7.refs_2_.refs_9_), channel_id=1, source_target_pairs={{0,48},{8,200},{16,0},{24,216},{32,16},{40,232},{48,32},{56,248},{... | collective-permute-start | bytes 2359304 | tf_op jit(solution)/shard_map/ppermute | solution.py:272
  54.5 1.8 shard_map.69.refs_0_
  56.4 1.8 shard_map.70.refs_0_
  58.3 6.0 %collective-permute-done.2.refs_1_.refs_12_ = bf16[256,1536]{1,0:T(8,128)(2,1)S(1)} collective-permute-done((bf16[256,1536]{1,0:T(8,128)(2,1)S(1)}, bf16[256,1536]{1,0:T(8,128)(2,1)S(1)}, u32[]{:S(2)}, u32[]{:S(2)}) %collective-permute-start.2) | collective-permute-done | bytes 786464 | tf_op jit(solution)/shard_map/ppermute | solution.py:272
  64.3 1.3 collective-permute-start.16
  65.6 0.1 collective-permute-start.17
  65.7 1.0 shard_map.71.refs_0_
  66.7 0.8 collective-permute-done.16.refs_1_.refs_14_
  67.5 1.1 collective-permute-done.17.refs_2_.refs_15_
  68.7 1.0 shard_map.72
  69.7 2.0 %copy-done = bf16[8,512,512]{2,1,0:T(8,128)(2,1)} copy-done((bf16[8,512,512]{2,1,0:T(8,128)(2,1)}, bf16[8,512,512]{2,1,0:T(8,128)(2,1)S(1)}, u32[]{:S(2)}) %copy-start) | copy-done | bytes 4194328
  71.7 0.0 reduce-scatter.2.cloned.1.call-update
  71.7 13.6 %shard_map.74 = (bf16[32,128,512]{2,1,0:T(8,128)(2,1)}, f32[32,16,512]{2,1,0:T(8,128)}) custom-call(s32[1]{0:T(128)} %bitcast.3.place, bf16[8,128,2048]{2,1,0:T(8,128)(2,1)} %bitcast.8, bf16[256,256]{1,0:T(8,128)(2,1)} %constant.18.clone.table_ref), custom_call_target="tpu_custom_call" | custom-call | flops 4294967296 | bytes 8388608 | tf_op jit(solution)/shard_map/pallas_call | solution.py:132
  85.4 6.8 %all-to-all-start = ((bf16[32,128,512]{2,1,0:T(8,128)(2,1)}), bf16[32,128,512]{2,1,0:T(8,128)(2,1)}, u32[]{:S(2)}, u32[]{:S(2)}) async-start(bf16[32,128,512]{2,1,0:T(8,128)(2,1)} %get-tuple-element.22), calls=%async_computation.1 | async-start | bytes 8388608 | tf_op jit(solution)/shard_map/all_to_all | solution.py:378
  92.2 1.3 dynamic-slice_bitcast_fusion.sources
  93.4 35.2 %reduce-scatter.2.cloned.1.call-done = bf16[1,512,512]{2,1,0:T(8,128)(2,1)} async-done(((bf16[8,512,512]{2,1,0:T(8,128)(2,1)}), bf16[1,512,512]{2,1,0:T(8,128)(2,1)}) %reduce-scatter.2.cloned.1.call-update) | async-done | bytes 524304 | tf_op jit(solution)/shard_map/reduce_scatter | solution.py:376
  128.6 1.9 shard_map.73
  130.5 13.9 %all-to-all-done.quantized_ref = bf16[32,128,512]{2,1,0:T(8,128)(2,1)} async-done(((bf16[32,128,512]{2,1,0:T(8,128)(2,1)}), bf16[32,128,512]{2,1,0:T(8,128)(2,1)}, u32[]{:S(2)}, u32[]{:S(2)}) %all-to-all-start) | async-done | bytes 4194336 | tf_op jit(solution)/shard_map/all_to_all | solution.py:378
  144.4 18.7 %all_to_all.15.summed_ref = bf16[32,16,512]{2,1,0:T(8,128)(2,1)S(1)} all-to-all(bf16[32,16,512]{2,1,0:T(8,128)(2,1)} %shard_map.73), channel_id=1, replica_groups=mesh['dp'=32,'tensor'=8] {'dp'}, dimensions={0} | all-to-all | bytes 1048576 | tf_op jit(solution)/shard_map/all_to_all | solution.py:381
  163.1 1.3 shard_map.75
  164.4 7.8 %all-to-all-start.2 = ((bf16[8,16,2048]{2,1,0:T(8,128)(2,1)}), bf16[8,16,2048]{2,1,0:T(8,128)(2,1)S(1)}, u32[]{:S(2)}, u32[]{:S(2)}) async-start(bf16[8,16,2048]{2,1,0:T(8,128)(2,1)} %shard_map.75), calls=%async_computation.3 | async-start | bytes 1048576 | tf_op jit(solution)/shard_map/all_to_all | solution.py:383
  172.2 14.2 %shard_map.76 = f32[512,1536]{1,0:T(8,128)} custom-call(s32[32]{0:T(128)} %dynamic-slice_bitcast_fusion.sources, bf16[32,128,512]{2,1,0:T(8,128)(2,1)} %all-to-all-done.quantized_ref, bf16[256,1536]{1,0:T(8,128)(2,1)} %copy-done.3, bf16[256,1536]{1,0:T(8,128)(2,1)} %copy-done.2, bf16[256,1536]{1,0:T(8,128)(2,1)} %copy-done.6, bf16[256,1536]{1,0:T(8,128)(2,1)} %copy-done.7, ...), custom_call_target="tpu_custom_call" | custom-call | flops 6442450944 | bytes 19922944 | tf_op jit(solution)/shard_map/pallas_call | solution.py:240
  186.3 3.9 %all-to-all-done.2 = bf16[8,16,2048]{2,1,0:T(8,128)(2,1)S(1)} async-done(((bf16[8,16,2048]{2,1,0:T(8,128)(2,1)}), bf16[8,16,2048]{2,1,0:T(8,128)(2,1)S(1)}, u32[]{:S(2)}, u32[]{:S(2)}) %all-to-all-start.2) | async-done | bytes 524320 | tf_op jit(solution)/shard_map/all_to_all | solution.py:383
  190.2 0.8 copy.19
  (57 shorter events, 0.2 us)
Async XLA Ops:
  7.2 28.8 %copy-start.1 = (bf16[512,1536]{1,0:T(8,128)(2,1)S(1)}, bf16[512,1536]{1,0:T(8,128)(2,1)}, u32[]{:S(2)}) copy-start(bf16[512,1536]{1,0:T(8,128)(2,1)} %refs_3_.3) | copy-start | bytes 4718596
  7.2 64.5 %all-gather.3.cloned.1.call-start = ((), (), s32[]{:S(2)}) async-start(), calls=%async_computation.5 | async-start | bytes 4718592 | tf_op jit(solution)/shard_map/all_gather | solution.py:344
  7.9 120.7 %reduce-scatter.2.cloned.1.call-start = ((), (), s32[]{:S(2)}) async-start(), calls=%async_computation.4 | async-start | bytes 4718592 | tf_op jit(solution)/shard_map/reduce_scatter | solution.py:376
  8.0 9.3 %collective-permute-start = (bf16[128,1536]{1,0:T(8,128)(2,1)}, bf16[128,1536]{1,0:T(8,128)(2,1)S(1)}, u32[]{:S(2)}, u32[]{:S(2)}) collective-permute-start(bf16[128,1536]{1,0:T(8,128)(2,1)} %param.7), channel_id=1, source_target_pairs={{0,64},{8,24},{16,80},{24,40},{32,96},{40,56},{48,112},{56,8},{64,... | collective-permute-start | bytes 1179656 | tf_op jit(solution)/shard_map/ppermute | solution.py:272
  10.2 11.7 %collective-permute-start.3 = (bf16[128,1536]{1,0:T(8,128)(2,1)}, bf16[128,1536]{1,0:T(8,128)(2,1)S(1)}, u32[]{:S(2)}, u32[]{:S(2)}) collective-permute-start(bf16[128,1536]{1,0:T(8,128)(2,1)} %param.7), channel_id=1, source_target_pairs={{0,192},{8,56},{16,208},{24,8},{32,224},{40,24},{48,240},{56,40},{... | collective-permute-start | bytes 1179656 | tf_op jit(solution)/shard_map/ppermute | solution.py:272
  17.3 20.5 %copy-start.3 = (bf16[256,1536]{1,0:T(8,128)(2,1)}, bf16[256,1536]{1,0:T(8,128)(2,1)S(1)}, u32[]{:S(2)}) copy-start(bf16[256,1536]{1,0:T(8,128)(2,1)S(1)} %constant_dynamic-update-slice_fusion.refs_0_) | copy-start | bytes 2359300
  17.3 15.4 %collective-permute-start.1 = (bf16[256,1536]{1,0:T(8,128)(2,1)S(1)}, bf16[256,1536]{1,0:T(8,128)(2,1)S(1)}, u32[]{:S(2)}, u32[]{:S(2)}) collective-permute-start(bf16[256,1536]{1,0:T(8,128)(2,1)S(1)} %constant_dynamic-update-slice_fusion.refs_0_), channel_id=1, source_target_pairs={{0,16},{8,72},{16,32},{24,88},{32,48},{40,104},{48,0},{56,120},{64... | collective-permute-start | bytes 2359304 | tf_op jit(solution)/shard_map/ppermute | solution.py:272
  18.3 14.9 %collective-permute-start.8 = (bf16[256,1536]{1,0:T(8,128)(2,1)S(1)}, bf16[256,1536]{1,0:T(8,128)(2,1)S(1)}, u32[]{:S(2)}, u32[]{:S(2)}) collective-permute-start(bf16[256,1536]{1,0:T(8,128)(2,1)S(1)} %constant_dynamic-update-slice_fusion.refs_0_), channel_id=1, source_target_pairs={{0,8},{8,0},{16,24},{24,16},{32,40},{40,32},{48,56},{56,48},{64,72... | collective-permute-start | bytes 2359304 | tf_op jit(solution)/shard_map/ppermute | solution.py:276
  20.7 8.3 %collective-permute-start.4 = (bf16[64,1536]{1,0:T(8,128)(2,1)S(1)}, bf16[64,1536]{1,0:T(8,128)(2,1)S(1)}, u32[]{:S(2)}, u32[]{:S(2)}) collective-permute-start(bf16[64,1536]{1,0:T(8,128)(2,1)S(1)} %slice.8), channel_id=1, source_target_pairs={{0,64},{8,24},{16,80},{24,40},{32,96},{40,56},{48,112},{56,8},{64,... | collective-permute-start | bytes 589832 | tf_op jit(solution)/shard_map/ppermute | solution.py:272
  21.8 7.2 %collective-permute-start.5 = (bf16[64,1536]{1,0:T(8,128)(2,1)S(1)}, bf16[64,1536]{1,0:T(8,128)(2,1)S(1)}, u32[]{:S(2)}, u32[]{:S(2)}) collective-permute-start(bf16[64,1536]{1,0:T(8,128)(2,1)S(1)} %slice.9), channel_id=1, source_target_pairs={{0,192},{8,56},{16,208},{24,8},{32,224},{40,24},{48,240},{56,40},{... | collective-permute-start | bytes 589832 | tf_op jit(solution)/shard_map/ppermute | solution.py:272
  29.1 8.7 %copy-start.2 = (bf16[256,1536]{1,0:T(8,128)(2,1)}, bf16[256,1536]{1,0:T(8,128)(2,1)S(1)}, u32[]{:S(2)}) copy-start(bf16[256,1536]{1,0:T(8,128)(2,1)S(1)} %constant_dynamic-update-slice_fusion.2.refs_1_) | copy-start | bytes 2359300
  29.1 6.9 %collective-permute-start.9 = (bf16[256,1536]{1,0:T(8,128)(2,1)S(1)}, bf16[256,1536]{1,0:T(8,128)(2,1)S(1)}, u32[]{:S(2)}, u32[]{:S(2)}) collective-permute-start(bf16[256,1536]{1,0:T(8,128)(2,1)S(1)} %constant_dynamic-update-slice_fusion.2.refs_1_), channel_id=1, source_target_pairs={{0,8},{8,0},{16,24},{24,16},{32,40},{40,32},{48,56},{56,48},{64,72... | collective-permute-start | bytes 2359304 | tf_op jit(solution)/shard_map/ppermute | solution.py:276
  30.0 12.5 %collective-permute-start.6 = (bf16[256,1536]{1,0:T(8,128)(2,1)S(1)}, bf16[256,1536]{1,0:T(8,128)(2,1)S(1)}, u32[]{:S(2)}, u32[]{:S(2)}) collective-permute-start(bf16[256,1536]{1,0:T(8,128)(2,1)S(1)} %constant_dynamic-update-slice_fusion.2.refs_1_), channel_id=1, source_target_pairs={{0,16},{8,72},{16,32},{24,88},{32,48},{40,104},{48,0},{56,120},{64... | collective-permute-start | bytes 2359304 | tf_op jit(solution)/shard_map/ppermute | solution.py:272
  30.0 12.5 %collective-permute-start.7 = (bf16[256,1536]{1,0:T(8,128)(2,1)S(1)}, bf16[256,1536]{1,0:T(8,128)(2,1)S(1)}, u32[]{:S(2)}, u32[]{:S(2)}) collective-permute-start(bf16[256,1536]{1,0:T(8,128)(2,1)S(1)} %constant_dynamic-update-slice_fusion.2.refs_1_), channel_id=1, source_target_pairs={{0,48},{8,200},{16,0},{24,216},{32,16},{40,232},{48,32},{56,248},{... | collective-permute-start | bytes 2359304 | tf_op jit(solution)/shard_map/ppermute | solution.py:272
  32.7 21.8 %copy-start.5 = (bf16[256,1536]{1,0:T(8,128)(2,1)}, bf16[256,1536]{1,0:T(8,128)(2,1)S(1)}, u32[]{:S(2)}) copy-start(bf16[256,1536]{1,0:T(8,128)(2,1)S(1)} %collective-permute-done.1.refs_1_.refs_4_) | copy-start | bytes 2359300
  32.7 17.4 %collective-permute-start.13 = (bf16[256,1536]{1,0:T(8,128)(2,1)S(1)}, bf16[256,1536]{1,0:T(8,128)(2,1)S(1)}, u32[]{:S(2)}, u32[]{:S(2)}) collective-permute-start(bf16[256,1536]{1,0:T(8,128)(2,1)S(1)} %constant_dynamic-update-slice_fusion.refs_0_), channel_id=1, source_target_pairs={{0,48},{8,200},{16,0},{24,216},{32,16},{40,232},{48,32},{56,248},{... | collective-permute-start | bytes 2359304 | tf_op jit(solution)/shard_map/ppermute | solution.py:272
  33.2 4.6 %copy-start.6 = (bf16[256,1536]{1,0:T(8,128)(2,1)}, bf16[256,1536]{1,0:T(8,128)(2,1)S(1)}, u32[]{:S(2)}) copy-start(bf16[256,1536]{1,0:T(8,128)(2,1)S(1)} %collective-permute-done.8.refs_2_) | copy-start | bytes 2359300
  33.2 18.6 %collective-permute-start.11 = (bf16[256,1536]{1,0:T(8,128)(2,1)S(1)}, bf16[256,1536]{1,0:T(8,128)(2,1)S(1)}, u32[]{:S(2)}, u32[]{:S(2)}) collective-permute-start(bf16[256,1536]{1,0:T(8,128)(2,1)S(1)} %collective-permute-done.1.refs_1_.refs_4_), channel_id=1, source_target_pairs={{0,8},{8,0},{16,24},{24,16},{32,40},{40,32},{48,56},{56,48},{64,72... | collective-permute-start | bytes 2359304 | tf_op jit(solution)/shard_map/ppermute | solution.py:276
  36.0 1.9 copy-start.7
  42.5 13.9 %copy-start.8 = (bf16[256,1536]{1,0:T(8,128)(2,1)}, bf16[256,1536]{1,0:T(8,128)(2,1)S(1)}, u32[]{:S(2)}) copy-start(bf16[256,1536]{1,0:T(8,128)(2,1)S(1)} %collective-permute-done.6.refs_2_.refs_5_) | copy-start | bytes 2359300
  42.5 13.9 %copy-start.9 = (bf16[256,1536]{1,0:T(8,128)(2,1)}, bf16[256,1536]{1,0:T(8,128)(2,1)S(1)}, u32[]{:S(2)}) copy-start(bf16[256,1536]{1,0:T(8,128)(2,1)S(1)} %collective-permute-done.7.refs_2_.refs_9_) | copy-start | bytes 2359300
  42.5 12.0 %collective-permute-start.12 = (bf16[256,1536]{1,0:T(8,128)(2,1)S(1)}, bf16[256,1536]{1,0:T(8,128)(2,1)S(1)}, u32[]{:S(2)}, u32[]{:S(2)}) collective-permute-start(bf16[256,1536]{1,0:T(8,128)(2,1)S(1)} %collective-permute-done.6.refs_2_.refs_5_), channel_id=1, source_target_pairs={{0,8},{8,0},{16,24},{24,16},{32,40},{40,32},{48,56},{56,48},{64,72... | collective-permute-start | bytes 2359304 | tf_op jit(solution)/shard_map/ppermute | solution.py:276
  50.0 6.4 %copy-start.10 = (bf16[256,1536]{1,0:T(8,128)(2,1)}, bf16[256,1536]{1,0:T(8,128)(2,1)S(1)}, u32[]{:S(2)}) copy-start(bf16[256,1536]{1,0:T(8,128)(2,1)S(1)} %collective-permute-done.13.refs_1_.refs_8_) | copy-start | bytes 2359300
  50.0 6.3 %collective-permute-start.14 = (bf16[256,1536]{1,0:T(8,128)(2,1)S(1)}, bf16[256,1536]{1,0:T(8,128)(2,1)S(1)}, u32[]{:S(2)}, u32[]{:S(2)}) collective-permute-start(bf16[256,1536]{1,0:T(8,128)(2,1)S(1)} %collective-permute-done.13.refs_1_.refs_8_), channel_id=1, source_target_pairs={{0,8},{8,0},{16,24},{24,16},{32,40},{40,32},{48,56},{56,48},{64,72... | collective-permute-start | bytes 2359304 | tf_op jit(solution)/shard_map/ppermute | solution.py:276
  51.8 4.6 %collective-permute-start.15 = (bf16[256,1536]{1,0:T(8,128)(2,1)S(1)}, bf16[256,1536]{1,0:T(8,128)(2,1)S(1)}, u32[]{:S(2)}, u32[]{:S(2)}) collective-permute-start(bf16[256,1536]{1,0:T(8,128)(2,1)S(1)} %collective-permute-done.7.refs_2_.refs_9_), channel_id=1, source_target_pairs={{0,8},{8,0},{16,24},{24,16},{32,40},{40,32},{48,56},{56,48},{64,72... | collective-permute-start | bytes 2359304 | tf_op jit(solution)/shard_map/ppermute | solution.py:276
  51.8 12.5 %collective-permute-start.2 = (bf16[256,1536]{1,0:T(8,128)(2,1)S(1)}, bf16[256,1536]{1,0:T(8,128)(2,1)S(1)}, u32[]{:S(2)}, u32[]{:S(2)}) collective-permute-start(bf16[256,1536]{1,0:T(8,128)(2,1)S(1)} %collective-permute-done.1.refs_1_.refs_4_), channel_id=1, source_target_pairs={{0,16},{8,72},{16,32},{24,88},{32,48},{40,104},{48,0},{56,120},{64... | collective-permute-start | bytes 2359304 | tf_op jit(solution)/shard_map/ppermute | solution.py:272
  51.8 4.5 %copy-start.11 = (bf16[256,1536]{1,0:T(8,128)(2,1)}, bf16[256,1536]{1,0:T(8,128)(2,1)S(1)}, u32[]{:S(2)}) copy-start(bf16[256,1536]{1,0:T(8,128)(2,1)S(1)} %collective-permute-done.11.refs_3_.refs_6_) | copy-start | bytes 2359300
  51.8 12.4 %collective-permute-start.10 = (bf16[256,1536]{1,0:T(8,128)(2,1)S(1)}, bf16[256,1536]{1,0:T(8,128)(2,1)S(1)}, u32[]{:S(2)}, u32[]{:S(2)}) collective-permute-start(bf16[256,1536]{1,0:T(8,128)(2,1)S(1)} %collective-permute-done.7.refs_2_.refs_9_), channel_id=1, source_target_pairs={{0,48},{8,200},{16,0},{24,216},{32,16},{40,232},{48,32},{56,248},{... | collective-permute-start | bytes 2359304 | tf_op jit(solution)/shard_map/ppermute | solution.py:272
  54.5 1.9 copy-start.12
  56.4 1.9 copy-start.13
  56.4 1.9 copy-start.14
  64.3 2.5 %copy-start.15 = (bf16[256,1536]{1,0:T(8,128)(2,1)}, bf16[256,1536]{1,0:T(8,128)(2,1)S(1)}, u32[]{:S(2)}) copy-start(bf16[256,1536]{1,0:T(8,128)(2,1)S(1)} %collective-permute-done.2.refs_1_.refs_12_) | copy-start | bytes 2359300
  64.3 2.5 %copy-start.16 = (bf16[256,1536]{1,0:T(8,128)(2,1)}, bf16[256,1536]{1,0:T(8,128)(2,1)S(1)}, u32[]{:S(2)}) copy-start(bf16[256,1536]{1,0:T(8,128)(2,1)S(1)} %collective-permute-done.10.refs_2_.refs_13_) | copy-start | bytes 2359300
  64.3 3.3 %collective-permute-start.16 = (bf16[256,1536]{1,0:T(8,128)(2,1)S(1)}, bf16[256,1536]{1,0:T(8,128)(2,1)S(1)}, u32[]{:S(2)}, u32[]{:S(2)}) collective-permute-start(bf16[256,1536]{1,0:T(8,128)(2,1)S(1)} %collective-permute-done.2.refs_1_.refs_12_), channel_id=1, source_target_pairs={{0,8},{8,0},{16,24},{24,16},{32,40},{40,32},{48,56},{56,48},{64,72... | collective-permute-start | bytes 2359304 | tf_op jit(solution)/shard_map/ppermute | solution.py:276
  65.6 3.0 %collective-permute-start.17 = (bf16[256,1536]{1,0:T(8,128)(2,1)S(1)}, bf16[256,1536]{1,0:T(8,128)(2,1)S(1)}, u32[]{:S(2)}, u32[]{:S(2)}) collective-permute-start(bf16[256,1536]{1,0:T(8,128)(2,1)S(1)} %collective-permute-done.10.refs_2_.refs_13_), channel_id=1, source_target_pairs={{0,8},{8,0},{16,24},{24,16},{32,40},{40,32},{48,56},{56,48},{64,72... | collective-permute-start | bytes 2359304 | tf_op jit(solution)/shard_map/ppermute | solution.py:276
  67.5 2.1 %copy-start.17 = (bf16[256,1536]{1,0:T(8,128)(2,1)}, bf16[256,1536]{1,0:T(8,128)(2,1)S(1)}, u32[]{:S(2)}) copy-start(bf16[256,1536]{1,0:T(8,128)(2,1)S(1)} %collective-permute-done.16.refs_1_.refs_14_) | copy-start | bytes 2359300
  68.7 1.0 copy-start.18
  69.7 2.0 %copy-start = (bf16[8,512,512]{2,1,0:T(8,128)(2,1)}, bf16[8,512,512]{2,1,0:T(8,128)(2,1)S(1)}, u32[]{:S(2)}) copy-start(bf16[8,512,512]{2,1,0:T(8,128)(2,1)S(1)} %shard_map.72) | copy-start | bytes 12582916
  85.4 77.7 %copy-start.4 = (f32[32,16,512]{2,1,0:T(8,128)S(1)}, f32[32,16,512]{2,1,0:T(8,128)}, u32[]{:S(2)}) copy-start(f32[32,16,512]{2,1,0:T(8,128)} %get-tuple-element.24.slope_ref) | copy-start | bytes 3145732
  85.4 77.7 %copy-start.19 = (bf16[256,256]{1,0:T(8,128)(2,1)S(1)}, bf16[256,256]{1,0:T(8,128)(2,1)}, u32[]{:S(2)}) copy-start(bf16[256,256]{1,0:T(8,128)(2,1)} %constant.18.clone.table_ref) | copy-start | bytes 393220
  85.4 59.0 %all-to-all-start = ((bf16[32,128,512]{2,1,0:T(8,128)(2,1)}), bf16[32,128,512]{2,1,0:T(8,128)(2,1)}, u32[]{:S(2)}, u32[]{:S(2)}) async-start(bf16[32,128,512]{2,1,0:T(8,128)(2,1)} %get-tuple-element.22), calls=%async_computation.1 | async-start | bytes 8388608 | tf_op jit(solution)/shard_map/all_to_all | solution.py:378
  164.4 25.8 %all-to-all-start.2 = ((bf16[8,16,2048]{2,1,0:T(8,128)(2,1)}), bf16[8,16,2048]{2,1,0:T(8,128)(2,1)S(1)}, u32[]{:S(2)}, u32[]{:S(2)}) async-start(bf16[8,16,2048]{2,1,0:T(8,128)(2,1)} %shard_map.75), calls=%async_computation.3 | async-start | bytes 1048576 | tf_op jit(solution)/shard_map/all_to_all | solution.py:383
Sparse Core Ops, SparseCore 0:
  9.8 58.6 all-gather.2
  71.8 56.6 reduce-scatter.1

commit v12 on v11

--- a/solution.py
+++ b/solution.py
@@ -1,3 +1,4 @@
+import functools
 import math
 
 import jax
@@ -14,6 +15,7 @@
 LANES = 128
 VMEM_BYTES = 60 * 1024 * 1024
 LITTLE_VMEM = 16 * 1024 * 1024
+HALVES = [slice(start, start + LANES) for start in range(0, TABLE, LANES)]
 NORM = 1.0 / math.sqrt(WIDTH)
 SIDE = 4
 STEP = 16
@@ -63,140 +65,190 @@
     return parts
 
 
-def quantize_kernel(place, rows_ref, table_ref, quantized_ref, slope_ref, inner, mixed):
-    members, count, features = rows_ref.shape
-    step, width = slope_ref.shape[1:]
-    chunks, per_shard, per_width = features // TABLE, features // width, width // TABLE
-    rows = rows_ref[...].reshape(members * count, features)
+def levels_of(largest):
+    rows = largest.shape[0]
+    peak = jnp.max(largest, axis=1, keepdims=True) * NORM
+    scale = (peak + epsilon) / levels
+    inverse = jnp.broadcast_to(NORM / scale, (rows, LANES))
+    depth = jnp.broadcast_to((ripple / (2.0 * math.pi)) * scale, (rows, LANES))
+    return inverse, depth
+
+
+def remainder(value, inverse):
+    turns = value * inverse
+    return turns - jnp.round(turns)
+
+
+def quantized_of(value, inverse, depth):
+    rest = remainder(value, inverse)
+    return value * NORM - depth * (rest * horner(SINE, rest * rest))
+
+
+def slope_of(value, inverse):
+    rest = remainder(value, inverse)
+    return 1.0 - ripple * horner(COSINE, rest * rest)
+
+
+def mix(rows, table, inner, spans):
+    chunks = inner.shape[0]
     for c in range(chunks):
         inner[c] = jnp.dot(
-            rows[:, c * TABLE : (c + 1) * TABLE],
-            table_ref[...],
-            preferred_element_type=jnp.float32,
+            rows[:, c * TABLE : (c + 1) * TABLE], table, preferred_element_type=jnp.float32
         )
-    halves = [slice(l * LANES, (l + 1) * LANES) for l in range(TABLE // LANES)]
-    for group in range(count // step):
-        spans = [
-            slice(t * count + group * step, t * count + (group + 1) * step)
-            for t in range(members)
-        ]
-        here = slice(group * step, (group + 1) * step)
-        for span in spans:
-            for lanes in halves:
-                parts = butterfly([inner[c, span, lanes] for c in range(chunks)])
-                for c in range(chunks):
-                    inner[c, span, lanes] = parts[c]
-        largest = jnp.zeros((step, LANES), jnp.float32)
-        for c in range(chunks):
-            for lanes in halves:
-                parts = butterfly([inner[c, span, lanes] for span in spans])
-                for span, part in zip(spans, parts):
-                    mixed[c, span, lanes] = part
-                    largest = jnp.maximum(largest, jnp.abs(part))
-        peak = jnp.max(largest, axis=1, keepdims=True) * NORM
-        scale = (peak + epsilon) / levels
-        inverse = jnp.broadcast_to(NORM / scale, (step, LANES))
-        depth = jnp.broadcast_to((ripple / (2.0 * math.pi)) * scale, (step, LANES))
-
-        def remainder(value):
-            turns = value * inverse
-            return turns - jnp.round(turns)
-
-        def places():
-            for t, span in enumerate(spans):
-                for c in range(chunks):
-                    for l, lanes in enumerate(halves):
-                        start = (c % per_width) * TABLE + l * LANES
-                        yield t * per_shard + c // per_width, start, mixed[c, span, lanes]
-
-        for block, start, value in places():
-            rest = remainder(value)
-            sine = rest * horner(SINE, rest * rest)
-            quantized_ref[block, here, start : start + LANES] = (
-                value * NORM - depth * sine
-            ).astype(jnp.bfloat16)
-
-        @pl.when(pl.program_id(0) * (count // step) + group == place[0])
-        def _():
-            for block, start, value in places():
-                rest = remainder(value)
-                slope_ref[block, :, start : start + LANES] = 1.0 - ripple * horner(
-                    COSINE, rest * rest
-                )
-
-
-def quantize(rows, table, place, dp, width):
+    return [mix_group(inner, group) for group in spans]
+
+
+def mix_group(inner, spans):
+    chunks = inner.shape[0]
+    rows = spans[0].stop - spans[0].start
+    for span in spans:
+        for lanes in HALVES:
+            parts = butterfly([inner[c, span, lanes] for c in range(chunks)])
+            for c in range(chunks):
+                inner[c, span, lanes] = parts[c]
+    largest = jnp.zeros((rows, LANES), jnp.float32)
+    for c in range(chunks):
+        for lanes in HALVES:
+            parts = butterfly([inner[c, span, lanes] for span in spans])
+            for span, part in zip(spans, parts):
+                inner[c, span, lanes] = part
+                largest = jnp.maximum(largest, jnp.abs(part))
+    return largest
+
+
+def quantize_kernel(rows_ref, table_ref, quantized_ref, inner):
+    members, count, features = rows_ref.shape
+    width = quantized_ref.shape[2]
+    chunks, per_shard, per_width = features // TABLE, features // width, width // TABLE
+    groups = [
+        [slice(t * count + g, t * count + g + STEP) for t in range(members)]
+        for g in range(0, count, STEP)
+    ]
+    rows = rows_ref[...].reshape(members * count, features)
+    found = mix(rows, table_ref[...], inner, groups)
+    for g, (spans, largest) in enumerate(zip(groups, found)):
+        inverse, depth = levels_of(largest)
+        here = slice(g * STEP, (g + 1) * STEP)
+        for t, span in enumerate(spans):
+            for c in range(chunks):
+                for l, lanes in enumerate(HALVES):
+                    start = (c % per_width) * TABLE + l * LANES
+                    block = t * per_shard + c // per_width
+                    quantized_ref[block, here, start : start + LANES] = quantized_of(
+                        inner[c, span, lanes], inverse, depth
+                    ).astype(jnp.bfloat16)
+
+
+def quantize(rows, table, dp, width):
     members, tokens, features = rows.shape
-    step = tokens // members
-    count = 2 * step
+    count = 2 * STEP
     return pl.pallas_call(
         quantize_kernel,
-        grid_spec=pltpu.PrefetchScalarGridSpec(
-            num_scalar_prefetch=1,
-            grid=(tokens // count,),
-            in_specs=[
-                pl.BlockSpec((members, count, features), lambda i, place: (0, i, 0)),
-                pl.BlockSpec((TABLE, TABLE), lambda i, place: (0, 0)),
-            ],
-            out_specs=[
-                pl.BlockSpec((dp, count, width), lambda i, place: (0, i, 0)),
-                pl.BlockSpec((dp, step, width), lambda i, place: (0, 0, 0)),
-            ],
-            scratch_shapes=[
-                pltpu.VMEM((features // TABLE, members * count, TABLE), jnp.float32),
-                pltpu.VMEM((features // TABLE, members * count, TABLE), jnp.float32),
-            ],
-        ),
-        out_shape=[
-            jax.ShapeDtypeStruct((dp, tokens, width), jnp.bfloat16),
-            jax.ShapeDtypeStruct((dp, step, width), jnp.float32),
+        grid=(tokens // count,),
+        in_specs=[
+            pl.BlockSpec((members, count, features), lambda i: (0, i, 0)),
+            pl.BlockSpec((TABLE, TABLE), lambda i: (0, 0)),
         ],
+        out_specs=pl.BlockSpec((dp, count, width), lambda i: (0, i, 0)),
+        scratch_shapes=[pltpu.VMEM((features // TABLE, members * count, TABLE), jnp.float32)],
+        out_shape=jax.ShapeDtypeStruct((dp, tokens, width), jnp.bfloat16),
         compiler_params=pltpu.CompilerParams(vmem_limit_bytes=VMEM_BYTES),
         cost_estimate=pl.CostEstimate(
             flops=2 * tokens * WIDTH * BLOCK, bytes_accessed=4 * tokens * WIDTH, transcendentals=0
         ),
+    )(rows, table)
+
+
+def slope_kernel(place, rows_ref, table_ref, slope_ref, inner):
+    members, _, features = rows_ref.shape
+    devices, _, width = slope_ref.shape
+    per_shard, per_width = devices // members, width // TABLE
+    spans = [slice(t * STEP, (t + 1) * STEP) for t in range(members)]
+    rows = rows_ref[...].reshape(members * STEP, features)
+    (largest,) = mix(rows, table_ref[...], inner, [spans])
+    inverse, _ = levels_of(largest)
+    for block in range(devices):
+        for k in range(per_width):
+            for l, lanes in enumerate(HALVES):
+                c = block % per_shard * per_width + k
+                start = k * TABLE + l * LANES
+                slope_ref[block, :, start : start + LANES] = slope_of(
+                    inner[c, spans[block // per_shard], lanes], inverse
+                )
+
+
+def slopes(rows, table, place, dp, width):
+    members, tokens, features = rows.shape
+    return pl.pallas_call(
+        slope_kernel,
+        grid_spec=pltpu.PrefetchScalarGridSpec(
+            num_scalar_prefetch=1,
+            grid=(1,),
+            in_specs=[
+                pl.BlockSpec((members, STEP, features), lambda i, place: (0, place[0], 0)),
+                pl.BlockSpec((TABLE, TABLE), lambda i, place: (0, 0)),
+            ],
+            out_specs=pl.BlockSpec((dp, STEP, width), lambda i, place: (0, 0, 0)),
+            scratch_shapes=[pltpu.VMEM((features // TABLE, members * STEP, TABLE), jnp.float32)],
+        ),
+        out_shape=jax.ShapeDtypeStruct((dp, STEP, width), jnp.float32),
+        compiler_params=pltpu.CompilerParams(vmem_limit_bytes=VMEM_BYTES),
+        cost_estimate=pl.CostEstimate(
+            flops=2 * STEP * WIDTH * BLOCK, bytes_accessed=8 * STEP * WIDTH, transcendentals=0
+        ),
     )(place, rows, table)
 
 
-def product_kernel(*refs):
-    weight_ref, out_ref = refs[-2:]
-    pieces = [ref for ref in refs[:-2] if len(ref.shape) == 2]
-    members, step = out_ref.shape[0], STEP
-    done = 0
-    for piece_ref in pieces:
-        rows, depth = piece_ref.shape
+def product_kernel(count, position, *refs):
+    pieces, weight_ref = refs[:count], refs[count]
+    out_ref, results, sems = refs[-3:]
+    members = out_ref.shape[0]
+    stores = []
+    for n, piece_ref in enumerate(pieces):
+        slots = piece_ref.shape[0] // (members * STEP)
         result = lax.dot_general(
             piece_ref[...],
             weight_ref[...],
             (((1,), (1,)), ((), ())),
             preferred_element_type=jnp.float32,
         ).astype(out_ref.dtype)
-        for k in range(rows // (members * step)):
+        for k in range(slots):
             for t in range(members):
-                start = (k * members + t) * step
-                out_ref[t, done * step : (done + 1) * step, :] = result[start : start + step]
-            done += 1
+                start = (k * members + t) * STEP
+                results[n, t, k * STEP : (k + 1) * STEP, :] = result[start : start + STEP]
+        place = (position * count + n) * slots * STEP
+        stores.append(
+            pltpu.make_async_copy(
+                results.at[n], out_ref.at[:, pl.ds(place, slots * STEP), :], sems.at[n]
+            )
+        )
+        stores[-1].start()
+    for store in stores:
+        store.wait()
 
 
 def product(held, pieces, weight, position, members, total):
-    rows = sum(piece.shape[0] for piece in pieces)
+    count, rows = len(pieces), pieces[0].shape[0]
     width, depth = weight.shape
-    whole = [pl.BlockSpec(memory_space=pltpu.VMEM)] * (len(pieces) + 1)
     earlier = [] if held is None else [held]
     return pl.pallas_call(
-        product_kernel,
-        grid=(1,),
-        in_specs=[pl.BlockSpec(memory_space=pl.ANY)] * len(earlier) + whole,
-        out_specs=pl.BlockSpec((members, rows // members, width), lambda i: (0, position, 0)),
+        functools.partial(product_kernel, count, position),
+        in_specs=[pl.BlockSpec(memory_space=pltpu.VMEM)] * (count + 1)
+        + [pl.BlockSpec(memory_space=pltpu.HBM)] * len(earlier),
+        out_specs=pl.BlockSpec(memory_space=pltpu.HBM),
         out_shape=jax.ShapeDtypeStruct((members, total // members, width), jnp.bfloat16),
-        input_output_aliases={0: 0} if earlier else {},
+        scratch_shapes=[
+            pltpu.VMEM((count, members, rows // members, width), jnp.bfloat16),
+            pltpu.SemaphoreType.DMA((count,)),
+        ],
+        input_output_aliases={count + 1: 0} if earlier else {},
         compiler_params=pltpu.CompilerParams(vmem_limit_bytes=LITTLE_VMEM),
         cost_estimate=pl.CostEstimate(
-            flops=2 * rows * depth * width,
-            bytes_accessed=2 * rows * (depth + width),
+            flops=2 * count * rows * depth * width,
+            bytes_accessed=2 * count * rows * (depth + width),
             transcendentals=0,
         ),
-    )(*earlier, *pieces, weight)
+    )(*pieces, weight, *earlier)
 
 
 def order_kernel(sources, rows_ref, out_ref):
@@ -374,10 +426,12 @@
     partial_rows = multiply(held, far_other, 7)
     partial_rows, wide_rows = lax.optimization_barrier((partial_rows, wide_rows))
     summed = lax.psum_scatter(partial_rows, "tensor", scatter_dimension=0, tiled=False)
-    quantized, slope = quantize(wide_rows, table, place, dp, width)
+    quantized = quantize(wide_rows, table, dp, width)
     q_block = lax.all_to_all(quantized, "dp", split_axis=0, concat_axis=0, tiled=True)
+    summed, wide_rows = lax.optimization_barrier((summed, wide_rows))
+    slope = slopes(wide_rows, table, place, dp, width)
     ordered = order(summed.reshape(dp, tokens // members, width), sources)
-    ordered, q_block = lax.optimization_barrier((ordered, q_block))
+    ordered, q_block, slope = lax.optimization_barrier((ordered, q_block, slope))
     homed = lax.all_to_all(ordered, "dp", split_axis=0, concat_axis=0, tiled=True)
     mixed = finish(homed, slope, table, members)
     grad_input = lax.all_to_all(mixed, "tensor", split_axis=0, concat_axis=0, tiled=True)

time: 198 us -> 196 us (0.990)
  waiting for transfers between devices: 81.6 us -> 74.7 us
  Pallas kernels: 38.4 us -> 42.7 us
    pallas_call x6 -> x7, Pallas kernels: 21.1 us -> 25.3 us  [the longest x1 11.9 us: quantize(): pl.pallas_call(quantize_kernel, grid=(tokens // count,), in_specs=[pl.Blo...]
    all_to_all x1, waiting for transfers between devices: 13.9 us -> 9.85 us  [shards(): lax.all_to_all(quantized, 'dp', split_axis=0, concat_axis=0, tiled=True)]
    ppermute x10, waiting for transfers between devices: 26.1 us -> 22.9 us  [send(): return lax.ppermute(block, 'dp', route(turn, sign))]
    unnamed x44 -> x46, local copies, waits for them, and re-layouts: 3.97 us -> 5.11 us
  transfers between devices with their start and end apart: 22 -> 22, of which waited for: 10 -> 12; matrix products, arithmetic and copies ran while one was open for 1% -> 1% of each run, Pallas kernels for 19% -> 21%
where the time goes in v12:
time: 196 us; the launch traced here: 195 us
  waiting for transfers between devices  74.7 us (38%)
  Pallas kernels  42.7 us (22%)
  starting transfers between devices  38.5 us (20%)
  blocking collectives  18.5 us (9%)
  between operations  14.4 us (7%)
  local copies, waits for them, and re-layouts  6.5 us (3%)
    reduce_scatter x1, waiting for transfers between devices, shards(): lax.psum_scatter(partial_rows, 'tensor', scatter_dimension=0, tiled=False)  35.8 us
    ppermute x10, waiting for transfers between devices, send(): return lax.ppermute(block, 'dp', route(turn, sign))  22.9 us
    all_to_all x1, blocking collectives, shards(): lax.all_to_all(ordered, 'dp', split_axis=0, concat_axis=0, tiled=True)  18.5 us
    pallas_call x1, Pallas kernels, gradient(): pl.pallas_call(gradient_kernel, in_specs=[pl.BlockSpec(memory_space=pltpu...  14.2 us
    ppermute x10, starting transfers between devices, send(): return lax.ppermute(block, 'dp', route(turn, sign))  13.8 us
    ppermute x8, starting transfers between devices, other_core(): lax.ppermute(block, 'dp', [(d, d ^ 1) for d in range(2 * SIDE * SIDE)])  11.9 us
    pallas_call x1, Pallas kernels, quantize(): pl.pallas_call(quantize_kernel, grid=(tokens // count,), in_specs=[pl.Blo...  11.9 us
    pallas_call x5, Pallas kernels, product(): pl.pallas_call(functools.partial(product_kernel, count, position), in_spe...  10.1 us
  transfers between devices with their start and end apart: 22, of which 12 were waited for; matrix products, arithmetic and copies ran while one was open for 1% of the time, Pallas kernels for 21%

profile of v12, /device:TPU:1, one launch (start us, length us, event | category | flops | bytes accessed | tf_op | source)
XLA Modules:
  0.0 195.4 jit_solution(8148070407429516099)
XLA Ops:
  7.2 0.0 all-gather.3.cloned.1.call-start
  7.2 0.7 all-gather.3.cloned.1.call-update
  7.9 0.0 reduce-scatter.2.cloned.1.call-start
  8.0 2.2 %collective-permute-start = (bf16[128,1536]{1,0:T(8,128)(2,1)}, bf16[128,1536]{1,0:T(8,128)(2,1)S(1)}, u32[]{:S(2)}, u32[]{:S(2)}) collective-permute-start(bf16[128,1536]{1,0:T(8,128)(2,1)} %param.7), channel_id=1, source_target_pairs={{0,64},{8,24},{16,80},{24,40},{32,96},{40,56},{48,112},{56,8},{64,... | collective-permute-start | bytes 1179656 | tf_op jit(solution)/shard_map/ppermute | solution.py:324
  10.2 1.5 collective-permute-start.3
  11.7 1.1 constant_dynamic-update-slice_fusion.1
  12.7 4.5 %collective-permute-done = bf16[128,1536]{1,0:T(8,128)(2,1)S(1)} collective-permute-done((bf16[128,1536]{1,0:T(8,128)(2,1)}, bf16[128,1536]{1,0:T(8,128)(2,1)S(1)}, u32[]{:S(2)}, u32[]{:S(2)}) %collective-permute-start) | collective-permute-done | bytes 393248 | tf_op jit(solution)/shard_map/ppermute | solution.py:324
  17.3 3.3 %collective-permute-start.8 = (bf16[256,1536]{1,0:T(8,128)(2,1)S(1)}, bf16[256,1536]{1,0:T(8,128)(2,1)S(1)}, u32[]{:S(2)}, u32[]{:S(2)}) collective-permute-start(bf16[256,1536]{1,0:T(8,128)(2,1)S(1)} %constant_dynamic-update-slice_fusion.refs_0_), channel_id=1, source_target_pairs={{0,8},{8,0},{16,24},{24,16},{32,40},{40,32},{48,56},{56,48},{64,72... | collective-permute-start | bytes 2359304 | tf_op jit(solution)/shard_map/ppermute | solution.py:328
  20.6 0.1 collective-permute-start.4
  20.7 2.7 %collective-permute-start.5 = (bf16[64,1536]{1,0:T(8,128)(2,1)S(1)}, bf16[64,1536]{1,0:T(8,128)(2,1)S(1)}, u32[]{:S(2)}, u32[]{:S(2)}) collective-permute-start(bf16[64,1536]{1,0:T(8,128)(2,1)S(1)} %slice.9), channel_id=1, source_target_pairs={{0,192},{8,56},{16,208},{24,8},{32,224},{40,24},{48,240},{56,40},{... | collective-permute-start | bytes 589832 | tf_op jit(solution)/shard_map/ppermute | solution.py:324
  23.5 4.9 %collective-permute-done.4 = bf16[64,1536]{1,0:T(8,128)(2,1)S(1)} collective-permute-done((bf16[64,1536]{1,0:T(8,128)(2,1)S(1)}, bf16[64,1536]{1,0:T(8,128)(2,1)S(1)}, u32[]{:S(2)}, u32[]{:S(2)}) %collective-permute-start.4) | collective-permute-done | bytes 196640 | tf_op jit(solution)/shard_map/ppermute | solution.py:324
  28.5 1.4 collective-permute-start.9
  29.9 1.9 collective-permute-start.7
  31.8 2.7 %collective-permute-start.11 = (bf16[256,1536]{1,0:T(8,128)(2,1)S(1)}, bf16[256,1536]{1,0:T(8,128)(2,1)S(1)}, u32[]{:S(2)}, u32[]{:S(2)}) collective-permute-start(bf16[256,1536]{1,0:T(8,128)(2,1)S(1)} %constant_dynamic-update-slice_fusion.refs_0_), channel_id=1, source_target_pairs={{0,48},{8,200},{16,0},{24,216},{32,16},{40,232},{48,32},{56,248},{... | collective-permute-start | bytes 2359304 | tf_op jit(solution)/shard_map/ppermute | solution.py:324
  34.5 0.7 collective-permute-done.1.refs_0_.refs_4_
  35.2 1.4 collective-permute-start.14
  36.6 2.5 %shard_map.68.refs_5_ = bf16[8,512,512]{2,1,0:T(8,128)(2,1)S(1)} custom-call(bf16[256,1536]{1,0:T(8,128)(2,1)S(1)} %constant_dynamic-update-slice_fusion.refs_0_, bf16[256,1536]{1,0:T(8,128)(2,1)S(1)} %constant_dynamic-update-slice_fusion.2.refs_1_, bf16[256,1536]{1,0:T(8,128)(2,1)S(1)} %collective-permute-done.8.refs_2_, ...), custom_call_target="tpu_custom_call" | custom-call | flops 1610612736 | bytes 4194304 | tf_op jit(solution)/shard_map/pallas_call | solution.py:234
  39.1 2.0 %collective-permute-done.7.refs_1_.refs_9_ = bf16[256,1536]{1,0:T(8,128)(2,1)S(1)} collective-permute-done((bf16[256,1536]{1,0:T(8,128)(2,1)S(1)}, bf16[256,1536]{1,0:T(8,128)(2,1)S(1)}, u32[]{:S(2)}, u32[]{:S(2)}) %collective-permute-start.7) | collective-permute-done | bytes 786464 | tf_op jit(solution)/shard_map/ppermute | solution.py:324
  41.1 3.1 %collective-permute-done.6.refs_1_.refs_5_ = bf16[256,1536]{1,0:T(8,128)(2,1)S(1)} collective-permute-done((bf16[256,1536]{1,0:T(8,128)(2,1)S(1)}, bf16[256,1536]{1,0:T(8,128)(2,1)S(1)}, u32[]{:S(2)}, u32[]{:S(2)}) %collective-permute-start.6) | collective-permute-done | bytes 786464 | tf_op jit(solution)/shard_map/ppermute | solution.py:324
  44.3 2.3 %collective-permute-start.15 = (bf16[256,1536]{1,0:T(8,128)(2,1)S(1)}, bf16[256,1536]{1,0:T(8,128)(2,1)S(1)}, u32[]{:S(2)}, u32[]{:S(2)}) collective-permute-start(bf16[256,1536]{1,0:T(8,128)(2,1)S(1)} %collective-permute-done.6.refs_1_.refs_5_), channel_id=1, source_target_pairs={{0,8},{8,0},{16,24},{24,16},{32,40},{40,32},{48,56},{56,48},{64,72... | collective-permute-start | bytes 2359304 | tf_op jit(solution)/shard_map/ppermute | solution.py:328
  46.5 3.0 %collective-permute-done.11.refs_0_.refs_8_ = bf16[256,1536]{1,0:T(8,128)(2,1)S(1)} collective-permute-done((bf16[256,1536]{1,0:T(8,128)(2,1)S(1)}, bf16[256,1536]{1,0:T(8,128)(2,1)S(1)}, u32[]{:S(2)}, u32[]{:S(2)}) %collective-permute-start.11) | collective-permute-done | bytes 786464 | tf_op jit(solution)/shard_map/ppermute | solution.py:324
  49.6 1.7 collective-permute-start.12
  51.3 2.7 %collective-permute-start.10 = (bf16[256,1536]{1,0:T(8,128)(2,1)S(1)}, bf16[256,1536]{1,0:T(8,128)(2,1)S(1)}, u32[]{:S(2)}, u32[]{:S(2)}) collective-permute-start(bf16[256,1536]{1,0:T(8,128)(2,1)S(1)} %collective-permute-done.7.refs_1_.refs_9_), channel_id=1, source_target_pairs={{0,48},{8,200},{16,0},{24,216},{32,16},{40,232},{48,32},{56,248},{... | collective-permute-start | bytes 2359304 | tf_op jit(solution)/shard_map/ppermute | solution.py:324
  53.9 2.5 %shard_map.69.refs_5_ = bf16[8,512,512]{2,1,0:T(8,128)(2,1)S(1)} custom-call(bf16[256,1536]{1,0:T(8,128)(2,1)S(1)} %collective-permute-done.1.refs_0_.refs_4_, bf16[256,1536]{1,0:T(8,128)(2,1)S(1)} %collective-permute-done.6.refs_1_.refs_5_, bf16[256,1536]{1,0:T(8,128)(2,1)S(1)} %collective-permute-done.14.refs_2_.refs_6_, ...), custom_call_target="tpu_custom_call", output_to_operand_aliasing={{}: (5, {})} | custom-call | flops 1610612736 | bytes 4194304 | tf_op jit(solution)/shard_map/pallas_call | solution.py:234
  56.6 2.5 %shard_map.70.refs_3_ = bf16[8,512,512]{2,1,0:T(8,128)(2,1)S(1)} custom-call(bf16[256,1536]{1,0:T(8,128)(2,1)S(1)} %collective-permute-done.11.refs_0_.refs_8_, bf16[256,1536]{1,0:T(8,128)(2,1)S(1)} %collective-permute-done.7.refs_1_.refs_9_, bf16[256,1536]{1,0:T(8,128)(2,1)S(1)} %collective-permute-done.12.refs_2_.refs_10_, ...), custom_call_target="tpu_custom_call", output_to_operand_aliasing={{}: (5, {})} | custom-call | flops 1610612736 | bytes 4194304 | tf_op jit(solution)/shard_map/pallas_call | solution.py:234
  59.1 4.6 %collective-permute-done.2.refs_0_.refs_12_ = bf16[256,1536]{1,0:T(8,128)(2,1)S(1)} collective-permute-done((bf16[256,1536]{1,0:T(8,128)(2,1)S(1)}, bf16[256,1536]{1,0:T(8,128)(2,1)S(1)}, u32[]{:S(2)}, u32[]{:S(2)}) %collective-permute-start.2) | collective-permute-done | bytes 786464 | tf_op jit(solution)/shard_map/ppermute | solution.py:324
  63.7 1.8 collective-permute-start.16
  65.5 0.1 collective-permute-start.17
  65.6 1.3 shard_map.71.refs_3_
  66.9 0.5 collective-permute-done.16.refs_0_.refs_14_
  67.4 1.1 collective-permute-done.17.refs_1_.refs_15_
  68.5 1.3 shard_map.72
  69.8 1.9 copy-done
  71.8 0.0 reduce-scatter.2.cloned.1.call-update
  71.8 11.9 %shard_map.74 = bf16[32,128,512]{2,1,0:T(8,128)(2,1)} custom-call(bf16[8,128,2048]{2,1,0:T(8,128)(2,1)} %bitcast.7, bf16[256,256]{1,0:T(8,128)(2,1)} %constant.18.clone.table_ref), custom_call_target="tpu_custom_call" | custom-call | flops 4294967296 | bytes 8388608 | tf_op jit(solution)/shard_map/pallas_call | solution.py:145
  83.6 6.3 %all-to-all-start = ((bf16[32,128,512]{2,1,0:T(8,128)(2,1)}), bf16[32,128,512]{2,1,0:T(8,128)(2,1)}, u32[]{:S(2)}, u32[]{:S(2)}) async-start(bf16[32,128,512]{2,1,0:T(8,128)(2,1)} %shard_map.74), calls=%async_computation.1 | async-start | bytes 8388608 | tf_op jit(solution)/shard_map/all_to_all | solution.py:430
  90.0 1.3 dynamic-slice_bitcast_fusion.sources
  91.3 35.8 %reduce-scatter.2.cloned.1.call-done = bf16[1,512,512]{2,1,0:T(8,128)(2,1)} async-done(((bf16[8,512,512]{2,1,0:T(8,128)(2,1)}), bf16[1,512,512]{2,1,0:T(8,128)(2,1)}) %reduce-scatter.2.cloned.1.call-update) | async-done | bytes 524304 | tf_op jit(solution)/shard_map/reduce_scatter | solution.py:428
  127.1 1.9 shard_map.73
  128.9 3.4 %shard_map.75.slope_ref = f32[32,16,512]{2,1,0:T(8,128)} custom-call(s32[1]{0:T(128)} %bitcast.4.place, bf16[8,128,2048]{2,1,0:T(8,128)(2,1)} %bitcast.8, bf16[256,256]{1,0:T(8,128)(2,1)} %constant.18.clone.table_ref), custom_call_target="tpu_custom_call" | custom-call | flops 536870912 | bytes 2097152 | tf_op jit(solution)/shard_map/pallas_call | solution.py:182
  132.3 9.9 %all-to-all-done.quantized_ref = bf16[32,128,512]{2,1,0:T(8,128)(2,1)} async-done(((bf16[32,128,512]{2,1,0:T(8,128)(2,1)}), bf16[32,128,512]{2,1,0:T(8,128)(2,1)}, u32[]{:S(2)}, u32[]{:S(2)}) %all-to-all-start) | async-done | bytes 4194336 | tf_op jit(solution)/shard_map/all_to_all | solution.py:430
  142.2 18.5 %all_to_all.15.summed_ref = bf16[32,16,512]{2,1,0:T(8,128)(2,1)S(1)} all-to-all(bf16[32,16,512]{2,1,0:T(8,128)(2,1)S(1)} %copy-done.20), channel_id=1, replica_groups=mesh['dp'=32,'tensor'=8] {'dp'}, dimensions={0} | all-to-all | bytes 1048576 | tf_op jit(solution)/shard_map/all_to_all | solution.py:435
  160.7 1.2 copy-done.2
  161.9 1.3 shard_map.76
  163.2 6.5 %all-to-all-start.2 = ((bf16[8,16,2048]{2,1,0:T(8,128)(2,1)}), bf16[8,16,2048]{2,1,0:T(8,128)(2,1)S(1)}, u32[]{:S(2)}, u32[]{:S(2)}) async-start(bf16[8,16,2048]{2,1,0:T(8,128)(2,1)} %shard_map.76), calls=%async_computation.3 | async-start | bytes 1048576 | tf_op jit(solution)/shard_map/all_to_all | solution.py:437
  169.7 14.2 %shard_map.77 = f32[512,1536]{1,0:T(8,128)} custom-call(s32[32]{0:T(128)} %dynamic-slice_bitcast_fusion.sources, bf16[32,128,512]{2,1,0:T(8,128)(2,1)} %all-to-all-done.quantized_ref, bf16[256,1536]{1,0:T(8,128)(2,1)} %copy-done.4, bf16[256,1536]{1,0:T(8,128)(2,1)} %copy-done.3, bf16[256,1536]{1,0:T(8,128)(2,1)} %copy-done.5, bf16[256,1536]{1,0:T(8,128)(2,1)} %copy-done.7, ...), custom_call_target="tpu_custom_call" | custom-call | flops 6442450944 | bytes 19922944 | tf_op jit(solution)/shard_map/pallas_call | solution.py:292
  183.9 3.9 %all-to-all-done.2 = bf16[8,16,2048]{2,1,0:T(8,128)(2,1)S(1)} async-done(((bf16[8,16,2048]{2,1,0:T(8,128)(2,1)}), bf16[8,16,2048]{2,1,0:T(8,128)(2,1)S(1)}, u32[]{:S(2)}, u32[]{:S(2)}) %all-to-all-start.2) | async-done | bytes 524320 | tf_op jit(solution)/shard_map/all_to_all | solution.py:437
  187.8 0.8 copy.19
  (60 shorter events, 0.2 us)
Async XLA Ops:
  7.2 29.4 %copy-start.1 = (bf16[512,1536]{1,0:T(8,128)(2,1)S(1)}, bf16[512,1536]{1,0:T(8,128)(2,1)}, u32[]{:S(2)}) copy-start(bf16[512,1536]{1,0:T(8,128)(2,1)} %refs_2_.3) | copy-start | bytes 4718596
  7.2 64.6 %all-gather.3.cloned.1.call-start = ((), (), s32[]{:S(2)}) async-start(), calls=%async_computation.5 | async-start | bytes 4718592 | tf_op jit(solution)/shard_map/all_gather | solution.py:396
  7.9 119.2 %reduce-scatter.2.cloned.1.call-start = ((), (), s32[]{:S(2)}) async-start(), calls=%async_computation.4 | async-start | bytes 4718592 | tf_op jit(solution)/shard_map/reduce_scatter | solution.py:428
  8.0 9.3 %collective-permute-start = (bf16[128,1536]{1,0:T(8,128)(2,1)}, bf16[128,1536]{1,0:T(8,128)(2,1)S(1)}, u32[]{:S(2)}, u32[]{:S(2)}) collective-permute-start(bf16[128,1536]{1,0:T(8,128)(2,1)} %param.7), channel_id=1, source_target_pairs={{0,64},{8,24},{16,80},{24,40},{32,96},{40,56},{48,112},{56,8},{64,... | collective-permute-start | bytes 1179656 | tf_op jit(solution)/shard_map/ppermute | solution.py:324
  10.2 10.6 %collective-permute-start.3 = (bf16[128,1536]{1,0:T(8,128)(2,1)}, bf16[128,1536]{1,0:T(8,128)(2,1)S(1)}, u32[]{:S(2)}, u32[]{:S(2)}) collective-permute-start(bf16[128,1536]{1,0:T(8,128)(2,1)} %param.7), channel_id=1, source_target_pairs={{0,192},{8,56},{16,208},{24,8},{32,224},{40,24},{48,240},{56,40},{... | collective-permute-start | bytes 1179656 | tf_op jit(solution)/shard_map/ppermute | solution.py:324
  17.3 21.8 %copy-start.4 = (bf16[256,1536]{1,0:T(8,128)(2,1)}, bf16[256,1536]{1,0:T(8,128)(2,1)S(1)}, u32[]{:S(2)}) copy-start(bf16[256,1536]{1,0:T(8,128)(2,1)S(1)} %constant_dynamic-update-slice_fusion.refs_0_) | copy-start | bytes 2359300
  17.3 14.5 %collective-permute-start.8 = (bf16[256,1536]{1,0:T(8,128)(2,1)S(1)}, bf16[256,1536]{1,0:T(8,128)(2,1)S(1)}, u32[]{:S(2)}, u32[]{:S(2)}) collective-permute-start(bf16[256,1536]{1,0:T(8,128)(2,1)S(1)} %constant_dynamic-update-slice_fusion.refs_0_), channel_id=1, source_target_pairs={{0,8},{8,0},{16,24},{24,16},{32,40},{40,32},{48,56},{56,48},{64,72... | collective-permute-start | bytes 2359304 | tf_op jit(solution)/shard_map/ppermute | solution.py:328
  20.6 14.6 %collective-permute-start.1 = (bf16[256,1536]{1,0:T(8,128)(2,1)S(1)}, bf16[256,1536]{1,0:T(8,128)(2,1)S(1)}, u32[]{:S(2)}, u32[]{:S(2)}) collective-permute-start(bf16[256,1536]{1,0:T(8,128)(2,1)S(1)} %constant_dynamic-update-slice_fusion.refs_0_), channel_id=1, source_target_pairs={{0,16},{8,72},{16,32},{24,88},{32,48},{40,104},{48,0},{56,120},{64... | collective-permute-start | bytes 2359304 | tf_op jit(solution)/shard_map/ppermute | solution.py:324
  20.6 7.8 %collective-permute-start.4 = (bf16[64,1536]{1,0:T(8,128)(2,1)S(1)}, bf16[64,1536]{1,0:T(8,128)(2,1)S(1)}, u32[]{:S(2)}, u32[]{:S(2)}) collective-permute-start(bf16[64,1536]{1,0:T(8,128)(2,1)S(1)} %slice.8), channel_id=1, source_target_pairs={{0,64},{8,24},{16,80},{24,40},{32,96},{40,56},{48,112},{56,8},{64,... | collective-permute-start | bytes 589832 | tf_op jit(solution)/shard_map/ppermute | solution.py:324
  20.7 7.7 %collective-permute-start.5 = (bf16[64,1536]{1,0:T(8,128)(2,1)S(1)}, bf16[64,1536]{1,0:T(8,128)(2,1)S(1)}, u32[]{:S(2)}, u32[]{:S(2)}) collective-permute-start(bf16[64,1536]{1,0:T(8,128)(2,1)S(1)} %slice.9), channel_id=1, source_target_pairs={{0,192},{8,56},{16,208},{24,8},{32,224},{40,24},{48,240},{56,40},{... | collective-permute-start | bytes 589832 | tf_op jit(solution)/shard_map/ppermute | solution.py:324
  28.5 10.6 %copy-start.3 = (bf16[256,1536]{1,0:T(8,128)(2,1)}, bf16[256,1536]{1,0:T(8,128)(2,1)S(1)}, u32[]{:S(2)}) copy-start(bf16[256,1536]{1,0:T(8,128)(2,1)S(1)} %constant_dynamic-update-slice_fusion.2.refs_1_) | copy-start | bytes 2359300
  28.5 8.1 %collective-permute-start.9 = (bf16[256,1536]{1,0:T(8,128)(2,1)S(1)}, bf16[256,1536]{1,0:T(8,128)(2,1)S(1)}, u32[]{:S(2)}, u32[]{:S(2)}) collective-permute-start(bf16[256,1536]{1,0:T(8,128)(2,1)S(1)} %constant_dynamic-update-slice_fusion.2.refs_1_), channel_id=1, source_target_pairs={{0,8},{8,0},{16,24},{24,16},{32,40},{40,32},{48,56},{56,48},{64,72... | collective-permute-start | bytes 2359304 | tf_op jit(solution)/shard_map/ppermute | solution.py:328
  29.9 11.2 %collective-permute-start.7 = (bf16[256,1536]{1,0:T(8,128)(2,1)S(1)}, bf16[256,1536]{1,0:T(8,128)(2,1)S(1)}, u32[]{:S(2)}, u32[]{:S(2)}) collective-permute-start(bf16[256,1536]{1,0:T(8,128)(2,1)S(1)} %constant_dynamic-update-slice_fusion.2.refs_1_), channel_id=1, source_target_pairs={{0,48},{8,200},{16,0},{24,216},{32,16},{40,232},{48,32},{56,248},{... | collective-permute-start | bytes 2359304 | tf_op jit(solution)/shard_map/ppermute | solution.py:324
  31.8 12.5 %collective-permute-start.6 = (bf16[256,1536]{1,0:T(8,128)(2,1)S(1)}, bf16[256,1536]{1,0:T(8,128)(2,1)S(1)}, u32[]{:S(2)}, u32[]{:S(2)}) collective-permute-start(bf16[256,1536]{1,0:T(8,128)(2,1)S(1)} %constant_dynamic-update-slice_fusion.2.refs_1_), channel_id=1, source_target_pairs={{0,16},{8,72},{16,32},{24,88},{32,48},{40,104},{48,0},{56,120},{64... | collective-permute-start | bytes 2359304 | tf_op jit(solution)/shard_map/ppermute | solution.py:324
  31.8 7.3 %copy-start.5 = (bf16[256,1536]{1,0:T(8,128)(2,1)}, bf16[256,1536]{1,0:T(8,128)(2,1)S(1)}, u32[]{:S(2)}) copy-start(bf16[256,1536]{1,0:T(8,128)(2,1)S(1)} %collective-permute-done.8.refs_2_) | copy-start | bytes 2359300
  31.8 17.7 %collective-permute-start.11 = (bf16[256,1536]{1,0:T(8,128)(2,1)S(1)}, bf16[256,1536]{1,0:T(8,128)(2,1)S(1)}, u32[]{:S(2)}, u32[]{:S(2)}) collective-permute-start(bf16[256,1536]{1,0:T(8,128)(2,1)S(1)} %constant_dynamic-update-slice_fusion.refs_0_), channel_id=1, source_target_pairs={{0,48},{8,200},{16,0},{24,216},{32,16},{40,232},{48,32},{56,248},{... | collective-permute-start | bytes 2359304 | tf_op jit(solution)/shard_map/ppermute | solution.py:324
  35.2 18.8 %copy-start.6 = (bf16[256,1536]{1,0:T(8,128)(2,1)}, bf16[256,1536]{1,0:T(8,128)(2,1)S(1)}, u32[]{:S(2)}) copy-start(bf16[256,1536]{1,0:T(8,128)(2,1)S(1)} %collective-permute-done.1.refs_0_.refs_4_) | copy-start | bytes 2359300
  35.2 16.1 %collective-permute-start.14 = (bf16[256,1536]{1,0:T(8,128)(2,1)S(1)}, bf16[256,1536]{1,0:T(8,128)(2,1)S(1)}, u32[]{:S(2)}, u32[]{:S(2)}) collective-permute-start(bf16[256,1536]{1,0:T(8,128)(2,1)S(1)} %collective-permute-done.1.refs_0_.refs_4_), channel_id=1, source_target_pairs={{0,8},{8,0},{16,24},{24,16},{32,40},{40,32},{48,56},{56,48},{64,72... | collective-permute-start | bytes 2359304 | tf_op jit(solution)/shard_map/ppermute | solution.py:328
  36.6 2.6 %copy-start.7 = (bf16[256,1536]{1,0:T(8,128)(2,1)}, bf16[256,1536]{1,0:T(8,128)(2,1)S(1)}, u32[]{:S(2)}) copy-start(bf16[256,1536]{1,0:T(8,128)(2,1)S(1)} %collective-permute-done.9.refs_3_) | copy-start | bytes 2359300
  41.1 15.4 %copy-start.8 = (bf16[256,1536]{1,0:T(8,128)(2,1)}, bf16[256,1536]{1,0:T(8,128)(2,1)S(1)}, u32[]{:S(2)}) copy-start(bf16[256,1536]{1,0:T(8,128)(2,1)S(1)} %collective-permute-done.7.refs_1_.refs_9_) | copy-start | bytes 2359300
  44.3 12.2 %copy-start.9 = (bf16[256,1536]{1,0:T(8,128)(2,1)}, bf16[256,1536]{1,0:T(8,128)(2,1)S(1)}, u32[]{:S(2)}) copy-start(bf16[256,1536]{1,0:T(8,128)(2,1)S(1)} %collective-permute-done.6.refs_1_.refs_5_) | copy-start | bytes 2359300
  44.3 9.7 %collective-permute-start.15 = (bf16[256,1536]{1,0:T(8,128)(2,1)S(1)}, bf16[256,1536]{1,0:T(8,128)(2,1)S(1)}, u32[]{:S(2)}, u32[]{:S(2)}) collective-permute-start(bf16[256,1536]{1,0:T(8,128)(2,1)S(1)} %collective-permute-done.6.refs_1_.refs_5_), channel_id=1, source_target_pairs={{0,8},{8,0},{16,24},{24,16},{32,40},{40,32},{48,56},{56,48},{64,72... | collective-permute-start | bytes 2359304 | tf_op jit(solution)/shard_map/ppermute | solution.py:328
  49.6 7.0 %copy-start.10 = (bf16[256,1536]{1,0:T(8,128)(2,1)}, bf16[256,1536]{1,0:T(8,128)(2,1)S(1)}, u32[]{:S(2)}) copy-start(bf16[256,1536]{1,0:T(8,128)(2,1)S(1)} %collective-permute-done.11.refs_0_.refs_8_) | copy-start | bytes 2359300
  49.6 7.0 %collective-permute-start.12 = (bf16[256,1536]{1,0:T(8,128)(2,1)S(1)}, bf16[256,1536]{1,0:T(8,128)(2,1)S(1)}, u32[]{:S(2)}, u32[]{:S(2)}) collective-permute-start(bf16[256,1536]{1,0:T(8,128)(2,1)S(1)} %collective-permute-done.11.refs_0_.refs_8_), channel_id=1, source_target_pairs={{0,8},{8,0},{16,24},{24,16},{32,40},{40,32},{48,56},{56,48},{64,72... | collective-permute-start | bytes 2359304 | tf_op jit(solution)/shard_map/ppermute | solution.py:328
  51.2 5.3 %collective-permute-start.13 = (bf16[256,1536]{1,0:T(8,128)(2,1)S(1)}, bf16[256,1536]{1,0:T(8,128)(2,1)S(1)}, u32[]{:S(2)}, u32[]{:S(2)}) collective-permute-start(bf16[256,1536]{1,0:T(8,128)(2,1)S(1)} %collective-permute-done.7.refs_1_.refs_9_), channel_id=1, source_target_pairs={{0,8},{8,0},{16,24},{24,16},{32,40},{40,32},{48,56},{56,48},{64,72... | collective-permute-start | bytes 2359304 | tf_op jit(solution)/shard_map/ppermute | solution.py:328
  51.3 12.5 %collective-permute-start.2 = (bf16[256,1536]{1,0:T(8,128)(2,1)S(1)}, bf16[256,1536]{1,0:T(8,128)(2,1)S(1)}, u32[]{:S(2)}, u32[]{:S(2)}) collective-permute-start(bf16[256,1536]{1,0:T(8,128)(2,1)S(1)} %collective-permute-done.1.refs_0_.refs_4_), channel_id=1, source_target_pairs={{0,16},{8,72},{16,32},{24,88},{32,48},{40,104},{48,0},{56,120},{64... | collective-permute-start | bytes 2359304 | tf_op jit(solution)/shard_map/ppermute | solution.py:324
  51.3 5.2 %copy-start.11 = (bf16[256,1536]{1,0:T(8,128)(2,1)}, bf16[256,1536]{1,0:T(8,128)(2,1)S(1)}, u32[]{:S(2)}) copy-start(bf16[256,1536]{1,0:T(8,128)(2,1)S(1)} %collective-permute-done.14.refs_2_.refs_6_) | copy-start | bytes 2359300
  51.3 12.4 %collective-permute-start.10 = (bf16[256,1536]{1,0:T(8,128)(2,1)S(1)}, bf16[256,1536]{1,0:T(8,128)(2,1)S(1)}, u32[]{:S(2)}, u32[]{:S(2)}) collective-permute-start(bf16[256,1536]{1,0:T(8,128)(2,1)S(1)} %collective-permute-done.7.refs_1_.refs_9_), channel_id=1, source_target_pairs={{0,48},{8,200},{16,0},{24,216},{32,16},{40,232},{48,32},{56,248},{... | collective-permute-start | bytes 2359304 | tf_op jit(solution)/shard_map/ppermute | solution.py:324
  53.9 2.6 %copy-start.12 = (bf16[256,1536]{1,0:T(8,128)(2,1)}, bf16[256,1536]{1,0:T(8,128)(2,1)S(1)}, u32[]{:S(2)}) copy-start(bf16[256,1536]{1,0:T(8,128)(2,1)S(1)} %collective-permute-done.15.refs_3_.refs_7_) | copy-start | bytes 2359300
  56.5 2.6 %copy-start.13 = (bf16[256,1536]{1,0:T(8,128)(2,1)}, bf16[256,1536]{1,0:T(8,128)(2,1)S(1)}, u32[]{:S(2)}) copy-start(bf16[256,1536]{1,0:T(8,128)(2,1)S(1)} %collective-permute-done.12.refs_2_.refs_10_) | copy-start | bytes 2359300
  56.6 2.6 %copy-start.14 = (bf16[256,1536]{1,0:T(8,128)(2,1)}, bf16[256,1536]{1,0:T(8,128)(2,1)S(1)}, u32[]{:S(2)}) copy-start(bf16[256,1536]{1,0:T(8,128)(2,1)S(1)} %collective-permute-done.13.refs_3_.refs_11_) | copy-start | bytes 2359300
  63.7 3.2 %copy-start.15 = (bf16[256,1536]{1,0:T(8,128)(2,1)}, bf16[256,1536]{1,0:T(8,128)(2,1)S(1)}, u32[]{:S(2)}) copy-start(bf16[256,1536]{1,0:T(8,128)(2,1)S(1)} %collective-permute-done.2.refs_0_.refs_12_) | copy-start | bytes 2359300
  63.7 3.2 %copy-start.16 = (bf16[256,1536]{1,0:T(8,128)(2,1)}, bf16[256,1536]{1,0:T(8,128)(2,1)S(1)}, u32[]{:S(2)}) copy-start(bf16[256,1536]{1,0:T(8,128)(2,1)S(1)} %collective-permute-done.10.refs_1_.refs_13_) | copy-start | bytes 2359300
  63.7 3.7 %collective-permute-start.16 = (bf16[256,1536]{1,0:T(8,128)(2,1)S(1)}, bf16[256,1536]{1,0:T(8,128)(2,1)S(1)}, u32[]{:S(2)}, u32[]{:S(2)}) collective-permute-start(bf16[256,1536]{1,0:T(8,128)(2,1)S(1)} %collective-permute-done.2.refs_0_.refs_12_), channel_id=1, source_target_pairs={{0,8},{8,0},{16,24},{24,16},{32,40},{40,32},{48,56},{56,48},{64,72... | collective-permute-start | bytes 2359304 | tf_op jit(solution)/shard_map/ppermute | solution.py:328
  65.5 3.0 %collective-permute-start.17 = (bf16[256,1536]{1,0:T(8,128)(2,1)S(1)}, bf16[256,1536]{1,0:T(8,128)(2,1)S(1)}, u32[]{:S(2)}, u32[]{:S(2)}) collective-permute-start(bf16[256,1536]{1,0:T(8,128)(2,1)S(1)} %collective-permute-done.10.refs_1_.refs_13_), channel_id=1, source_target_pairs={{0,8},{8,0},{16,24},{24,16},{32,40},{40,32},{48,56},{56,48},{64,72... | collective-permute-start | bytes 2359304 | tf_op jit(solution)/shard_map/ppermute | solution.py:328
  67.4 2.4 %copy-start.17 = (bf16[256,1536]{1,0:T(8,128)(2,1)}, bf16[256,1536]{1,0:T(8,128)(2,1)S(1)}, u32[]{:S(2)}) copy-start(bf16[256,1536]{1,0:T(8,128)(2,1)S(1)} %collective-permute-done.16.refs_0_.refs_14_) | copy-start | bytes 2359300
  68.5 1.3 copy-start.18
  69.8 1.9 copy-start
  83.6 58.5 %all-to-all-start = ((bf16[32,128,512]{2,1,0:T(8,128)(2,1)}), bf16[32,128,512]{2,1,0:T(8,128)(2,1)}, u32[]{:S(2)}, u32[]{:S(2)}) async-start(bf16[32,128,512]{2,1,0:T(8,128)(2,1)} %shard_map.74), calls=%async_computation.1 | async-start | bytes 8388608 | tf_op jit(solution)/shard_map/all_to_all | solution.py:430
  89.9 70.7 %copy-start.19 = (bf16[256,256]{1,0:T(8,128)(2,1)S(1)}, bf16[256,256]{1,0:T(8,128)(2,1)}, u32[]{:S(2)}) copy-start(bf16[256,256]{1,0:T(8,128)(2,1)} %constant.18.clone.table_ref) | copy-start | bytes 393220
  128.9 13.2 %copy-start.20 = (bf16[32,16,512]{2,1,0:T(8,128)(2,1)S(1)}, bf16[32,16,512]{2,1,0:T(8,128)(2,1)}, u32[]{:S(2)}) copy-start(bf16[32,16,512]{2,1,0:T(8,128)(2,1)} %shard_map.73) | copy-start | bytes 1572868
  160.7 1.2 copy-start.2
  163.2 24.5 %all-to-all-start.2 = ((bf16[8,16,2048]{2,1,0:T(8,128)(2,1)}), bf16[8,16,2048]{2,1,0:T(8,128)(2,1)S(1)}, u32[]{:S(2)}, u32[]{:S(2)}) async-start(bf16[8,16,2048]{2,1,0:T(8,128)(2,1)} %shard_map.76), calls=%async_computation.3 | async-start | bytes 1048576 | tf_op jit(solution)/shard_map/all_to_all | solution.py:437
Sparse Core Ops, SparseCore 0:
  9.8 58.6 all-gather.2
  71.9 55.0 reduce-scatter.1

commit v13 on v12

--- a/solution.py
+++ b/solution.py
@@ -41,7 +41,7 @@
     return [float(c) for c in scaled.convert(kind=np.polynomial.Polynomial).coef]
 
 
-SINE = fit(True, 6)
+SINE = [ripple / (2.0 * math.pi) * c for c in fit(True, 5)]
 COSINE = fit(False, 7)
 
 
@@ -70,8 +70,7 @@
     peak = jnp.max(largest, axis=1, keepdims=True) * NORM
     scale = (peak + epsilon) / levels
     inverse = jnp.broadcast_to(NORM / scale, (rows, LANES))
-    depth = jnp.broadcast_to((ripple / (2.0 * math.pi)) * scale, (rows, LANES))
-    return inverse, depth
+    return inverse, jnp.broadcast_to(scale, (rows, LANES))
 
 
 def remainder(value, inverse):
@@ -79,9 +78,10 @@
     return turns - jnp.round(turns)
 
 
-def quantized_of(value, inverse, depth):
-    rest = remainder(value, inverse)
-    return value * NORM - depth * (rest * horner(SINE, rest * rest))
+def quantized_of(value, inverse, scale):
+    turns = value * inverse
+    rest = turns - jnp.round(turns)
+    return scale * (turns - rest * horner(SINE, rest * rest))
 
 
 def slope_of(value, inverse):
@@ -127,7 +127,7 @@
     rows = rows_ref[...].reshape(members * count, features)
     found = mix(rows, table_ref[...], inner, groups)
     for g, (spans, largest) in enumerate(zip(groups, found)):
-        inverse, depth = levels_of(largest)
+        inverse, scale = levels_of(largest)
         here = slice(g * STEP, (g + 1) * STEP)
         for t, span in enumerate(spans):
             for c in range(chunks):
@@ -135,7 +135,7 @@
                     start = (c % per_width) * TABLE + l * LANES
                     block = t * per_shard + c // per_width
                     quantized_ref[block, here, start : start + LANES] = quantized_of(
-                        inner[c, span, lanes], inverse, depth
+                        inner[c, span, lanes], inverse, scale
                     ).astype(jnp.bfloat16)
 
 
@@ -174,7 +174,7 @@
                 start = k * TABLE + l * LANES
                 slope_ref[block, :, start : start + LANES] = slope_of(
                     inner[c, spans[block // per_shard], lanes], inverse
-                )
+                ).astype(slope_ref.dtype)
 
 
 def slopes(rows, table, place, dp, width):
@@ -191,7 +191,7 @@
             out_specs=pl.BlockSpec((dp, STEP, width), lambda i, place: (0, 0, 0)),
             scratch_shapes=[pltpu.VMEM((features // TABLE, members * STEP, TABLE), jnp.float32)],
         ),
-        out_shape=jax.ShapeDtypeStruct((dp, STEP, width), jnp.float32),
+        out_shape=jax.ShapeDtypeStruct((dp, STEP, width), jnp.bfloat16),
         compiler_params=pltpu.CompilerParams(vmem_limit_bytes=VMEM_BYTES),
         cost_estimate=pl.CostEstimate(
             flops=2 * STEP * WIDTH * BLOCK, bytes_accessed=8 * STEP * WIDTH, transcendentals=0
@@ -236,7 +236,7 @@
         in_specs=[pl.BlockSpec(memory_space=pltpu.VMEM)] * (count + 1)
         + [pl.BlockSpec(memory_space=pltpu.HBM)] * len(earlier),
         out_specs=pl.BlockSpec(memory_space=pltpu.HBM),
-        out_shape=jax.ShapeDtypeStruct((members, total // members, width), jnp.bfloat16),
+        out_shape=pltpu.HBM((members, total // members, width), jnp.bfloat16),
         scratch_shapes=[
             pltpu.VMEM((count, members, rows // members, width), jnp.bfloat16),
             pltpu.SemaphoreType.DMA((count,)),
@@ -347,7 +347,8 @@
     devices, step, width = summed_ref.shape
     members, per_width = out_ref.shape[0], width // TABLE
     per_shard = devices // members
-    upstream = (summed_ref[...].astype(jnp.float32) * slope_ref[...]).astype(jnp.bfloat16)
+    upstream = summed_ref[...].astype(jnp.float32) * slope_ref[...].astype(jnp.float32)
+    upstream = upstream.astype(jnp.bfloat16)
     upstream = upstream.reshape(devices * step, width)
     for c in range(per_width):
         inner[c] = jnp.dot(

time: 196 us -> 193 us (0.985)
  local copies, waits for them, and re-layouts: 6.5 us -> 4.4 us
    unnamed x46 -> x44, local copies, waits for them, and re-layouts: 5.11 us -> 3.01 us
where the time goes in v13:
time: 193 us
  waiting for transfers between devices  74.3 us (38%)
  Pallas kernels  42.5 us (22%)
  starting transfers between devices  38.6 us (20%)
  blocking collectives  18.5 us (10%)
  between operations  14.4 us (7%)
  local copies, waits for them, and re-layouts  4.4 us (2%)
    reduce_scatter x1, waiting for transfers between devices, shards(): lax.psum_scatter(partial_rows, 'tensor', scatter_dimension=0, tiled=False)  36.8 us
    ppermute x10, waiting for transfers between devices, send(): return lax.ppermute(block, 'dp', route(turn, sign))  22.8 us
    all_to_all x1, blocking collectives, shards(): lax.all_to_all(ordered, 'dp', split_axis=0, concat_axis=0, tiled=True)  18.5 us
    pallas_call x1, Pallas kernels, gradient(): pl.pallas_call(gradient_kernel, in_specs=[pl.BlockSpec(memory_space=pltpu...  14.2 us
    ppermute x10, starting transfers between devices, send(): return lax.ppermute(block, 'dp', route(turn, sign))  13.8 us
    ppermute x8, starting transfers between devices, other_core(): lax.ppermute(block, 'dp', [(d, d ^ 1) for d in range(2 * SIDE * SIDE)])  11.9 us
    pallas_call x5, Pallas kernels, product(): pl.pallas_call(functools.partial(product_kernel, count, position), in_spe...  11.2 us
    pallas_call x1, Pallas kernels, quantize(): pl.pallas_call(quantize_kernel, grid=(tokens // count,), in_specs=[pl.Blo...  10.8 us
  transfers between devices with their start and end apart: 22, of which 12 were waited for; matrix products, arithmetic and copies ran while one was open for 1% of the time, Pallas kernels for 21%

profile of v13, /device:TPU:1, one launch (start us, length us, event | category | flops | bytes accessed | tf_op | source)
XLA Modules:
  0.0 192.7 jit_solution(13917309272286969906)
XLA Ops:
  7.2 0.0 all-gather.3.cloned.1.call-start
  7.2 0.7 all-gather.3.cloned.1.call-update
  7.9 0.0 reduce-scatter.2.cloned.1.call-start
  8.0 2.2 %collective-permute-start = (bf16[128,1536]{1,0:T(8,128)(2,1)}, bf16[128,1536]{1,0:T(8,128)(2,1)S(1)}, u32[]{:S(2)}, u32[]{:S(2)}) collective-permute-start(bf16[128,1536]{1,0:T(8,128)(2,1)} %param.7), channel_id=1, source_target_pairs={{0,64},{8,24},{16,80},{24,40},{32,96},{40,56},{48,112},{56,8},{64,... | collective-permute-start | bytes 1179656 | tf_op jit(solution)/shard_map/ppermute | solution.py:324
  10.2 1.5 collective-permute-start.3
  11.7 1.1 constant_dynamic-update-slice_fusion.1
  12.7 4.5 %collective-permute-done = bf16[128,1536]{1,0:T(8,128)(2,1)S(1)} collective-permute-done((bf16[128,1536]{1,0:T(8,128)(2,1)}, bf16[128,1536]{1,0:T(8,128)(2,1)S(1)}, u32[]{:S(2)}, u32[]{:S(2)}) %collective-permute-start) | collective-permute-done | bytes 393248 | tf_op jit(solution)/shard_map/ppermute | solution.py:324
  17.3 3.3 %collective-permute-start.8 = (bf16[256,1536]{1,0:T(8,128)(2,1)S(1)}, bf16[256,1536]{1,0:T(8,128)(2,1)S(1)}, u32[]{:S(2)}, u32[]{:S(2)}) collective-permute-start(bf16[256,1536]{1,0:T(8,128)(2,1)S(1)} %constant_dynamic-update-slice_fusion.refs_0_), channel_id=1, source_target_pairs={{0,8},{8,0},{16,24},{24,16},{32,40},{40,32},{48,56},{56,48},{64,72... | collective-permute-start | bytes 2359304 | tf_op jit(solution)/shard_map/ppermute | solution.py:328
  20.6 0.1 collective-permute-start.4
  20.7 2.7 %collective-permute-start.5 = (bf16[64,1536]{1,0:T(8,128)(2,1)S(1)}, bf16[64,1536]{1,0:T(8,128)(2,1)S(1)}, u32[]{:S(2)}, u32[]{:S(2)}) collective-permute-start(bf16[64,1536]{1,0:T(8,128)(2,1)S(1)} %slice.9), channel_id=1, source_target_pairs={{0,192},{8,56},{16,208},{24,8},{32,224},{40,24},{48,240},{56,40},{... | collective-permute-start | bytes 589832 | tf_op jit(solution)/shard_map/ppermute | solution.py:324
  23.5 4.9 %collective-permute-done.4 = bf16[64,1536]{1,0:T(8,128)(2,1)S(1)} collective-permute-done((bf16[64,1536]{1,0:T(8,128)(2,1)S(1)}, bf16[64,1536]{1,0:T(8,128)(2,1)S(1)}, u32[]{:S(2)}, u32[]{:S(2)}) %collective-permute-start.4) | collective-permute-done | bytes 196640 | tf_op jit(solution)/shard_map/ppermute | solution.py:324
  28.5 1.4 collective-permute-start.9
  29.9 1.9 collective-permute-start.7
  31.8 2.7 %collective-permute-start.11 = (bf16[256,1536]{1,0:T(8,128)(2,1)S(1)}, bf16[256,1536]{1,0:T(8,128)(2,1)S(1)}, u32[]{:S(2)}, u32[]{:S(2)}) collective-permute-start(bf16[256,1536]{1,0:T(8,128)(2,1)S(1)} %constant_dynamic-update-slice_fusion.refs_0_), channel_id=1, source_target_pairs={{0,48},{8,200},{16,0},{24,216},{32,16},{40,232},{48,32},{56,248},{... | collective-permute-start | bytes 2359304 | tf_op jit(solution)/shard_map/ppermute | solution.py:324
  34.5 0.7 collective-permute-done.1.refs_0_.refs_4_
  35.2 1.4 collective-permute-start.14
  36.6 2.6 %shard_map.68.refs_5_ = bf16[8,512,512]{2,1,0:T(8,128)(2,1)} custom-call(bf16[256,1536]{1,0:T(8,128)(2,1)S(1)} %constant_dynamic-update-slice_fusion.refs_0_, bf16[256,1536]{1,0:T(8,128)(2,1)S(1)} %constant_dynamic-update-slice_fusion.2.refs_1_, bf16[256,1536]{1,0:T(8,128)(2,1)S(1)} %collective-permute-done.8.refs_2_, ...), custom_call_target="tpu_custom_call" | custom-call | flops 1610612736 | bytes 4194304 | tf_op jit(solution)/shard_map/pallas_call | solution.py:234
  39.2 2.0 %collective-permute-done.7.refs_1_.refs_9_ = bf16[256,1536]{1,0:T(8,128)(2,1)S(1)} collective-permute-done((bf16[256,1536]{1,0:T(8,128)(2,1)S(1)}, bf16[256,1536]{1,0:T(8,128)(2,1)S(1)}, u32[]{:S(2)}, u32[]{:S(2)}) %collective-permute-start.7) | collective-permute-done | bytes 786464 | tf_op jit(solution)/shard_map/ppermute | solution.py:324
  41.1 3.1 %collective-permute-done.6.refs_1_.refs_5_ = bf16[256,1536]{1,0:T(8,128)(2,1)S(1)} collective-permute-done((bf16[256,1536]{1,0:T(8,128)(2,1)S(1)}, bf16[256,1536]{1,0:T(8,128)(2,1)S(1)}, u32[]{:S(2)}, u32[]{:S(2)}) %collective-permute-start.6) | collective-permute-done | bytes 786464 | tf_op jit(solution)/shard_map/ppermute | solution.py:324
  44.3 2.3 %collective-permute-start.15 = (bf16[256,1536]{1,0:T(8,128)(2,1)S(1)}, bf16[256,1536]{1,0:T(8,128)(2,1)S(1)}, u32[]{:S(2)}, u32[]{:S(2)}) collective-permute-start(bf16[256,1536]{1,0:T(8,128)(2,1)S(1)} %collective-permute-done.6.refs_1_.refs_5_), channel_id=1, source_target_pairs={{0,8},{8,0},{16,24},{24,16},{32,40},{40,32},{48,56},{56,48},{64,72... | collective-permute-start | bytes 2359304 | tf_op jit(solution)/shard_map/ppermute | solution.py:328
  46.5 3.0 %collective-permute-done.11.refs_0_.refs_8_ = bf16[256,1536]{1,0:T(8,128)(2,1)S(1)} collective-permute-done((bf16[256,1536]{1,0:T(8,128)(2,1)S(1)}, bf16[256,1536]{1,0:T(8,128)(2,1)S(1)}, u32[]{:S(2)}, u32[]{:S(2)}) %collective-permute-start.11) | collective-permute-done | bytes 786464 | tf_op jit(solution)/shard_map/ppermute | solution.py:324
  49.6 1.7 collective-permute-start.12
  51.3 2.7 %collective-permute-start.10 = (bf16[256,1536]{1,0:T(8,128)(2,1)S(1)}, bf16[256,1536]{1,0:T(8,128)(2,1)S(1)}, u32[]{:S(2)}, u32[]{:S(2)}) collective-permute-start(bf16[256,1536]{1,0:T(8,128)(2,1)S(1)} %collective-permute-done.7.refs_1_.refs_9_), channel_id=1, source_target_pairs={{0,48},{8,200},{16,0},{24,216},{32,16},{40,232},{48,32},{56,248},{... | collective-permute-start | bytes 2359304 | tf_op jit(solution)/shard_map/ppermute | solution.py:324
  53.9 2.6 %shard_map.69.refs_5_ = bf16[8,512,512]{2,1,0:T(8,128)(2,1)} custom-call(bf16[256,1536]{1,0:T(8,128)(2,1)S(1)} %collective-permute-done.1.refs_0_.refs_4_, bf16[256,1536]{1,0:T(8,128)(2,1)S(1)} %collective-permute-done.6.refs_1_.refs_5_, bf16[256,1536]{1,0:T(8,128)(2,1)S(1)} %collective-permute-done.14.refs_2_.refs_6_, ...), custom_call_target="tpu_custom_call", output_to_operand_aliasing={{}: (5, {})} | custom-call | flops 1610612736 | bytes 4194304 | tf_op jit(solution)/shard_map/pallas_call | solution.py:234
  56.6 2.6 %shard_map.70.refs_3_ = bf16[8,512,512]{2,1,0:T(8,128)(2,1)} custom-call(bf16[256,1536]{1,0:T(8,128)(2,1)S(1)} %collective-permute-done.11.refs_0_.refs_8_, bf16[256,1536]{1,0:T(8,128)(2,1)S(1)} %collective-permute-done.7.refs_1_.refs_9_, bf16[256,1536]{1,0:T(8,128)(2,1)S(1)} %collective-permute-done.12.refs_2_.refs_10_, ...), custom_call_target="tpu_custom_call", output_to_operand_aliasing={{}: (5, {})} | custom-call | flops 1610612736 | bytes 4194304 | tf_op jit(solution)/shard_map/pallas_call | solution.py:234
  59.2 4.5 %collective-permute-done.2.refs_0_.refs_12_ = bf16[256,1536]{1,0:T(8,128)(2,1)S(1)} collective-permute-done((bf16[256,1536]{1,0:T(8,128)(2,1)S(1)}, bf16[256,1536]{1,0:T(8,128)(2,1)S(1)}, u32[]{:S(2)}, u32[]{:S(2)}) %collective-permute-start.2) | collective-permute-done | bytes 786464 | tf_op jit(solution)/shard_map/ppermute | solution.py:324
  63.7 1.8 collective-permute-start.16
  65.5 0.1 collective-permute-start.17
  65.6 1.7 shard_map.71.refs_3_
  67.4 0.1 collective-permute-done.16.refs_0_.refs_14_
  67.4 1.1 collective-permute-done.17.refs_1_.refs_15_
  68.5 1.7 shard_map.72
  70.3 0.0 all-gather.3.cloned.1.call-done
  70.3 0.0 reduce-scatter.2.cloned.1.call-update
  70.4 10.8 %shard_map.74 = bf16[32,128,512]{2,1,0:T(8,128)(2,1)} custom-call(bf16[8,128,2048]{2,1,0:T(8,128)(2,1)} %bitcast.7, bf16[256,256]{1,0:T(8,128)(2,1)} %constant.18.clone.table_ref), custom_call_target="tpu_custom_call" | custom-call | flops 4294967296 | bytes 8388608 | tf_op jit(solution)/shard_map/pallas_call | solution.py:145
  81.1 6.3 %all-to-all-start = ((bf16[32,128,512]{2,1,0:T(8,128)(2,1)}), bf16[32,128,512]{2,1,0:T(8,128)(2,1)}, u32[]{:S(2)}, u32[]{:S(2)}) async-start(bf16[32,128,512]{2,1,0:T(8,128)(2,1)} %shard_map.74), calls=%async_computation.1 | async-start | bytes 8388608 | tf_op jit(solution)/shard_map/all_to_all | solution.py:431
  87.5 1.3 dynamic-slice_bitcast_fusion.sources
  88.8 36.8 %reduce-scatter.2.cloned.1.call-done = bf16[1,512,512]{2,1,0:T(8,128)(2,1)} async-done(((bf16[8,512,512]{2,1,0:T(8,128)(2,1)}), bf16[1,512,512]{2,1,0:T(8,128)(2,1)}) %reduce-scatter.2.cloned.1.call-update) | async-done | bytes 524304 | tf_op jit(solution)/shard_map/reduce_scatter | solution.py:429
  125.6 1.9 shard_map.73
  127.5 3.2 %shard_map.75.slope_ref = bf16[32,16,512]{2,1,0:T(8,128)(2,1)} custom-call(s32[1]{0:T(128)} %bitcast.4.place, bf16[8,128,2048]{2,1,0:T(8,128)(2,1)} %bitcast.8, bf16[256,256]{1,0:T(8,128)(2,1)} %constant.18.clone.table_ref), custom_call_target="tpu_custom_call" | custom-call | flops 536870912 | bytes 2097152 | tf_op jit(solution)/shard_map/pallas_call | solution.py:182
  130.7 8.9 %all-to-all-done.quantized_ref = bf16[32,128,512]{2,1,0:T(8,128)(2,1)} async-done(((bf16[32,128,512]{2,1,0:T(8,128)(2,1)}), bf16[32,128,512]{2,1,0:T(8,128)(2,1)}, u32[]{:S(2)}, u32[]{:S(2)}) %all-to-all-start) | async-done | bytes 4194336 | tf_op jit(solution)/shard_map/all_to_all | solution.py:431
  139.7 18.5 %all_to_all.15.summed_ref = bf16[32,16,512]{2,1,0:T(8,128)(2,1)S(1)} all-to-all(bf16[32,16,512]{2,1,0:T(8,128)(2,1)S(1)} %copy-done.19), channel_id=1, replica_groups=mesh['dp'=32,'tensor'=8] {'dp'}, dimensions={0} | all-to-all | bytes 1048576 | tf_op jit(solution)/shard_map/all_to_all | solution.py:436
  158.2 1.0 copy-done.17
  159.2 1.3 shard_map.76
  160.5 6.5 %all-to-all-start.2 = ((bf16[8,16,2048]{2,1,0:T(8,128)(2,1)}), bf16[8,16,2048]{2,1,0:T(8,128)(2,1)S(1)}, u32[]{:S(2)}, u32[]{:S(2)}) async-start(bf16[8,16,2048]{2,1,0:T(8,128)(2,1)} %shard_map.76), calls=%async_computation.3 | async-start | bytes 1048576 | tf_op jit(solution)/shard_map/all_to_all | solution.py:438
  167.0 14.2 %shard_map.77 = f32[512,1536]{1,0:T(8,128)} custom-call(s32[32]{0:T(128)} %dynamic-slice_bitcast_fusion.sources, bf16[32,128,512]{2,1,0:T(8,128)(2,1)} %all-to-all-done.quantized_ref, bf16[256,1536]{1,0:T(8,128)(2,1)} %copy-done.2, bf16[256,1536]{1,0:T(8,128)(2,1)} %copy-done.1, bf16[256,1536]{1,0:T(8,128)(2,1)} %copy-done.3, bf16[256,1536]{1,0:T(8,128)(2,1)} %copy-done.5, ...), custom_call_target="tpu_custom_call" | custom-call | flops 6442450944 | bytes 19922944 | tf_op jit(solution)/shard_map/pallas_call | solution.py:292
  181.2 3.9 %all-to-all-done.2 = bf16[8,16,2048]{2,1,0:T(8,128)(2,1)S(1)} async-done(((bf16[8,16,2048]{2,1,0:T(8,128)(2,1)}), bf16[8,16,2048]{2,1,0:T(8,128)(2,1)S(1)}, u32[]{:S(2)}, u32[]{:S(2)}) %all-to-all-start.2) | async-done | bytes 524320 | tf_op jit(solution)/shard_map/all_to_all | solution.py:438
  185.1 0.8 copy.19
  (58 shorter events, 0.2 us)
Async XLA Ops:
  7.2 29.4 %copy-start = (bf16[512,1536]{1,0:T(8,128)(2,1)S(1)}, bf16[512,1536]{1,0:T(8,128)(2,1)}, u32[]{:S(2)}) copy-start(bf16[512,1536]{1,0:T(8,128)(2,1)} %refs_2_.3) | copy-start | bytes 4718596
  7.2 63.2 %all-gather.3.cloned.1.call-start = ((), (), s32[]{:S(2)}) async-start(), calls=%async_computation.5 | async-start | bytes 4718592 | tf_op jit(solution)/shard_map/all_gather | solution.py:397
  7.9 117.7 %reduce-scatter.2.cloned.1.call-start = ((), (), s32[]{:S(2)}) async-start(), calls=%async_computation.4 | async-start | bytes 4718592 | tf_op jit(solution)/shard_map/reduce_scatter | solution.py:429
  8.0 9.3 %collective-permute-start = (bf16[128,1536]{1,0:T(8,128)(2,1)}, bf16[128,1536]{1,0:T(8,128)(2,1)S(1)}, u32[]{:S(2)}, u32[]{:S(2)}) collective-permute-start(bf16[128,1536]{1,0:T(8,128)(2,1)} %param.7), channel_id=1, source_target_pairs={{0,64},{8,24},{16,80},{24,40},{32,96},{40,56},{48,112},{56,8},{64,... | collective-permute-start | bytes 1179656 | tf_op jit(solution)/shard_map/ppermute | solution.py:324
  10.2 10.6 %collective-permute-start.3 = (bf16[128,1536]{1,0:T(8,128)(2,1)}, bf16[128,1536]{1,0:T(8,128)(2,1)S(1)}, u32[]{:S(2)}, u32[]{:S(2)}) collective-permute-start(bf16[128,1536]{1,0:T(8,128)(2,1)} %param.7), channel_id=1, source_target_pairs={{0,192},{8,56},{16,208},{24,8},{32,224},{40,24},{48,240},{56,40},{... | collective-permute-start | bytes 1179656 | tf_op jit(solution)/shard_map/ppermute | solution.py:324
  17.3 21.8 %copy-start.2 = (bf16[256,1536]{1,0:T(8,128)(2,1)}, bf16[256,1536]{1,0:T(8,128)(2,1)S(1)}, u32[]{:S(2)}) copy-start(bf16[256,1536]{1,0:T(8,128)(2,1)S(1)} %constant_dynamic-update-slice_fusion.refs_0_) | copy-start | bytes 2359300
  17.3 14.5 %collective-permute-start.8 = (bf16[256,1536]{1,0:T(8,128)(2,1)S(1)}, bf16[256,1536]{1,0:T(8,128)(2,1)S(1)}, u32[]{:S(2)}, u32[]{:S(2)}) collective-permute-start(bf16[256,1536]{1,0:T(8,128)(2,1)S(1)} %constant_dynamic-update-slice_fusion.refs_0_), channel_id=1, source_target_pairs={{0,8},{8,0},{16,24},{24,16},{32,40},{40,32},{48,56},{56,48},{64,72... | collective-permute-start | bytes 2359304 | tf_op jit(solution)/shard_map/ppermute | solution.py:328
  20.6 14.6 %collective-permute-start.1 = (bf16[256,1536]{1,0:T(8,128)(2,1)S(1)}, bf16[256,1536]{1,0:T(8,128)(2,1)S(1)}, u32[]{:S(2)}, u32[]{:S(2)}) collective-permute-start(bf16[256,1536]{1,0:T(8,128)(2,1)S(1)} %constant_dynamic-update-slice_fusion.refs_0_), channel_id=1, source_target_pairs={{0,16},{8,72},{16,32},{24,88},{32,48},{40,104},{48,0},{56,120},{64... | collective-permute-start | bytes 2359304 | tf_op jit(solution)/shard_map/ppermute | solution.py:324
  20.6 7.8 %collective-permute-start.4 = (bf16[64,1536]{1,0:T(8,128)(2,1)S(1)}, bf16[64,1536]{1,0:T(8,128)(2,1)S(1)}, u32[]{:S(2)}, u32[]{:S(2)}) collective-permute-start(bf16[64,1536]{1,0:T(8,128)(2,1)S(1)} %slice.8), channel_id=1, source_target_pairs={{0,64},{8,24},{16,80},{24,40},{32,96},{40,56},{48,112},{56,8},{64,... | collective-permute-start | bytes 589832 | tf_op jit(solution)/shard_map/ppermute | solution.py:324
  20.7 7.7 %collective-permute-start.5 = (bf16[64,1536]{1,0:T(8,128)(2,1)S(1)}, bf16[64,1536]{1,0:T(8,128)(2,1)S(1)}, u32[]{:S(2)}, u32[]{:S(2)}) collective-permute-start(bf16[64,1536]{1,0:T(8,128)(2,1)S(1)} %slice.9), channel_id=1, source_target_pairs={{0,192},{8,56},{16,208},{24,8},{32,224},{40,24},{48,240},{56,40},{... | collective-permute-start | bytes 589832 | tf_op jit(solution)/shard_map/ppermute | solution.py:324
  28.5 10.6 %copy-start.1 = (bf16[256,1536]{1,0:T(8,128)(2,1)}, bf16[256,1536]{1,0:T(8,128)(2,1)S(1)}, u32[]{:S(2)}) copy-start(bf16[256,1536]{1,0:T(8,128)(2,1)S(1)} %constant_dynamic-update-slice_fusion.2.refs_1_) | copy-start | bytes 2359300
  28.5 8.1 %collective-permute-start.9 = (bf16[256,1536]{1,0:T(8,128)(2,1)S(1)}, bf16[256,1536]{1,0:T(8,128)(2,1)S(1)}, u32[]{:S(2)}, u32[]{:S(2)}) collective-permute-start(bf16[256,1536]{1,0:T(8,128)(2,1)S(1)} %constant_dynamic-update-slice_fusion.2.refs_1_), channel_id=1, source_target_pairs={{0,8},{8,0},{16,24},{24,16},{32,40},{40,32},{48,56},{56,48},{64,72... | collective-permute-start | bytes 2359304 | tf_op jit(solution)/shard_map/ppermute | solution.py:328
  29.9 11.2 %collective-permute-start.7 = (bf16[256,1536]{1,0:T(8,128)(2,1)S(1)}, bf16[256,1536]{1,0:T(8,128)(2,1)S(1)}, u32[]{:S(2)}, u32[]{:S(2)}) collective-permute-start(bf16[256,1536]{1,0:T(8,128)(2,1)S(1)} %constant_dynamic-update-slice_fusion.2.refs_1_), channel_id=1, source_target_pairs={{0,48},{8,200},{16,0},{24,216},{32,16},{40,232},{48,32},{56,248},{... | collective-permute-start | bytes 2359304 | tf_op jit(solution)/shard_map/ppermute | solution.py:324
  31.8 12.5 %collective-permute-start.6 = (bf16[256,1536]{1,0:T(8,128)(2,1)S(1)}, bf16[256,1536]{1,0:T(8,128)(2,1)S(1)}, u32[]{:S(2)}, u32[]{:S(2)}) collective-permute-start(bf16[256,1536]{1,0:T(8,128)(2,1)S(1)} %constant_dynamic-update-slice_fusion.2.refs_1_), channel_id=1, source_target_pairs={{0,16},{8,72},{16,32},{24,88},{32,48},{40,104},{48,0},{56,120},{64... | collective-permute-start | bytes 2359304 | tf_op jit(solution)/shard_map/ppermute | solution.py:324
  31.8 7.3 %copy-start.3 = (bf16[256,1536]{1,0:T(8,128)(2,1)}, bf16[256,1536]{1,0:T(8,128)(2,1)S(1)}, u32[]{:S(2)}) copy-start(bf16[256,1536]{1,0:T(8,128)(2,1)S(1)} %collective-permute-done.8.refs_2_) | copy-start | bytes 2359300
  31.8 17.7 %collective-permute-start.11 = (bf16[256,1536]{1,0:T(8,128)(2,1)S(1)}, bf16[256,1536]{1,0:T(8,128)(2,1)S(1)}, u32[]{:S(2)}, u32[]{:S(2)}) collective-permute-start(bf16[256,1536]{1,0:T(8,128)(2,1)S(1)} %constant_dynamic-update-slice_fusion.refs_0_), channel_id=1, source_target_pairs={{0,48},{8,200},{16,0},{24,216},{32,16},{40,232},{48,32},{56,248},{... | collective-permute-start | bytes 2359304 | tf_op jit(solution)/shard_map/ppermute | solution.py:324
  35.2 18.8 %copy-start.4 = (bf16[256,1536]{1,0:T(8,128)(2,1)}, bf16[256,1536]{1,0:T(8,128)(2,1)S(1)}, u32[]{:S(2)}) copy-start(bf16[256,1536]{1,0:T(8,128)(2,1)S(1)} %collective-permute-done.1.refs_0_.refs_4_) | copy-start | bytes 2359300
  35.2 16.1 %collective-permute-start.14 = (bf16[256,1536]{1,0:T(8,128)(2,1)S(1)}, bf16[256,1536]{1,0:T(8,128)(2,1)S(1)}, u32[]{:S(2)}, u32[]{:S(2)}) collective-permute-start(bf16[256,1536]{1,0:T(8,128)(2,1)S(1)} %collective-permute-done.1.refs_0_.refs_4_), channel_id=1, source_target_pairs={{0,8},{8,0},{16,24},{24,16},{32,40},{40,32},{48,56},{56,48},{64,72... | collective-permute-start | bytes 2359304 | tf_op jit(solution)/shard_map/ppermute | solution.py:328
  36.6 2.6 %copy-start.5 = (bf16[256,1536]{1,0:T(8,128)(2,1)}, bf16[256,1536]{1,0:T(8,128)(2,1)S(1)}, u32[]{:S(2)}) copy-start(bf16[256,1536]{1,0:T(8,128)(2,1)S(1)} %collective-permute-done.9.refs_3_) | copy-start | bytes 2359300
  41.1 15.5 %copy-start.6 = (bf16[256,1536]{1,0:T(8,128)(2,1)}, bf16[256,1536]{1,0:T(8,128)(2,1)S(1)}, u32[]{:S(2)}) copy-start(bf16[256,1536]{1,0:T(8,128)(2,1)S(1)} %collective-permute-done.7.refs_1_.refs_9_) | copy-start | bytes 2359300
  44.3 12.3 %copy-start.7 = (bf16[256,1536]{1,0:T(8,128)(2,1)}, bf16[256,1536]{1,0:T(8,128)(2,1)S(1)}, u32[]{:S(2)}) copy-start(bf16[256,1536]{1,0:T(8,128)(2,1)S(1)} %collective-permute-done.6.refs_1_.refs_5_) | copy-start | bytes 2359300
  44.3 9.7 %collective-permute-start.15 = (bf16[256,1536]{1,0:T(8,128)(2,1)S(1)}, bf16[256,1536]{1,0:T(8,128)(2,1)S(1)}, u32[]{:S(2)}, u32[]{:S(2)}) collective-permute-start(bf16[256,1536]{1,0:T(8,128)(2,1)S(1)} %collective-permute-done.6.refs_1_.refs_5_), channel_id=1, source_target_pairs={{0,8},{8,0},{16,24},{24,16},{32,40},{40,32},{48,56},{56,48},{64,72... | collective-permute-start | bytes 2359304 | tf_op jit(solution)/shard_map/ppermute | solution.py:328
  49.6 7.0 %copy-start.8 = (bf16[256,1536]{1,0:T(8,128)(2,1)}, bf16[256,1536]{1,0:T(8,128)(2,1)S(1)}, u32[]{:S(2)}) copy-start(bf16[256,1536]{1,0:T(8,128)(2,1)S(1)} %collective-permute-done.11.refs_0_.refs_8_) | copy-start | bytes 2359300
  49.6 7.0 %collective-permute-start.12 = (bf16[256,1536]{1,0:T(8,128)(2,1)S(1)}, bf16[256,1536]{1,0:T(8,128)(2,1)S(1)}, u32[]{:S(2)}, u32[]{:S(2)}) collective-permute-start(bf16[256,1536]{1,0:T(8,128)(2,1)S(1)} %collective-permute-done.11.refs_0_.refs_8_), channel_id=1, source_target_pairs={{0,8},{8,0},{16,24},{24,16},{32,40},{40,32},{48,56},{56,48},{64,72... | collective-permute-start | bytes 2359304 | tf_op jit(solution)/shard_map/ppermute | solution.py:328
  51.2 5.3 %collective-permute-start.13 = (bf16[256,1536]{1,0:T(8,128)(2,1)S(1)}, bf16[256,1536]{1,0:T(8,128)(2,1)S(1)}, u32[]{:S(2)}, u32[]{:S(2)}) collective-permute-start(bf16[256,1536]{1,0:T(8,128)(2,1)S(1)} %collective-permute-done.7.refs_1_.refs_9_), channel_id=1, source_target_pairs={{0,8},{8,0},{16,24},{24,16},{32,40},{40,32},{48,56},{56,48},{64,72... | collective-permute-start | bytes 2359304 | tf_op jit(solution)/shard_map/ppermute | solution.py:328
  51.3 12.5 %collective-permute-start.2 = (bf16[256,1536]{1,0:T(8,128)(2,1)S(1)}, bf16[256,1536]{1,0:T(8,128)(2,1)S(1)}, u32[]{:S(2)}, u32[]{:S(2)}) collective-permute-start(bf16[256,1536]{1,0:T(8,128)(2,1)S(1)} %collective-permute-done.1.refs_0_.refs_4_), channel_id=1, source_target_pairs={{0,16},{8,72},{16,32},{24,88},{32,48},{40,104},{48,0},{56,120},{64... | collective-permute-start | bytes 2359304 | tf_op jit(solution)/shard_map/ppermute | solution.py:324
  51.3 5.3 %copy-start.9 = (bf16[256,1536]{1,0:T(8,128)(2,1)}, bf16[256,1536]{1,0:T(8,128)(2,1)S(1)}, u32[]{:S(2)}) copy-start(bf16[256,1536]{1,0:T(8,128)(2,1)S(1)} %collective-permute-done.14.refs_2_.refs_6_) | copy-start | bytes 2359300
  51.3 12.4 %collective-permute-start.10 = (bf16[256,1536]{1,0:T(8,128)(2,1)S(1)}, bf16[256,1536]{1,0:T(8,128)(2,1)S(1)}, u32[]{:S(2)}, u32[]{:S(2)}) collective-permute-start(bf16[256,1536]{1,0:T(8,128)(2,1)S(1)} %collective-permute-done.7.refs_1_.refs_9_), channel_id=1, source_target_pairs={{0,48},{8,200},{16,0},{24,216},{32,16},{40,232},{48,32},{56,248},{... | collective-permute-start | bytes 2359304 | tf_op jit(solution)/shard_map/ppermute | solution.py:324
  53.9 2.6 %copy-start.10 = (bf16[256,1536]{1,0:T(8,128)(2,1)}, bf16[256,1536]{1,0:T(8,128)(2,1)S(1)}, u32[]{:S(2)}) copy-start(bf16[256,1536]{1,0:T(8,128)(2,1)S(1)} %collective-permute-done.15.refs_3_.refs_7_) | copy-start | bytes 2359300
  56.6 2.6 %copy-start.11 = (bf16[256,1536]{1,0:T(8,128)(2,1)}, bf16[256,1536]{1,0:T(8,128)(2,1)S(1)}, u32[]{:S(2)}) copy-start(bf16[256,1536]{1,0:T(8,128)(2,1)S(1)} %collective-permute-done.12.refs_2_.refs_10_) | copy-start | bytes 2359300
  56.6 2.6 %copy-start.12 = (bf16[256,1536]{1,0:T(8,128)(2,1)}, bf16[256,1536]{1,0:T(8,128)(2,1)S(1)}, u32[]{:S(2)}) copy-start(bf16[256,1536]{1,0:T(8,128)(2,1)S(1)} %collective-permute-done.13.refs_3_.refs_11_) | copy-start | bytes 2359300
  63.7 3.6 %copy-start.13 = (bf16[256,1536]{1,0:T(8,128)(2,1)}, bf16[256,1536]{1,0:T(8,128)(2,1)S(1)}, u32[]{:S(2)}) copy-start(bf16[256,1536]{1,0:T(8,128)(2,1)S(1)} %collective-permute-done.2.refs_0_.refs_12_) | copy-start | bytes 2359300
  63.7 3.6 %copy-start.14 = (bf16[256,1536]{1,0:T(8,128)(2,1)}, bf16[256,1536]{1,0:T(8,128)(2,1)S(1)}, u32[]{:S(2)}) copy-start(bf16[256,1536]{1,0:T(8,128)(2,1)S(1)} %collective-permute-done.10.refs_1_.refs_13_) | copy-start | bytes 2359300
  63.7 3.7 %collective-permute-start.16 = (bf16[256,1536]{1,0:T(8,128)(2,1)S(1)}, bf16[256,1536]{1,0:T(8,128)(2,1)S(1)}, u32[]{:S(2)}, u32[]{:S(2)}) collective-permute-start(bf16[256,1536]{1,0:T(8,128)(2,1)S(1)} %collective-permute-done.2.refs_0_.refs_12_), channel_id=1, source_target_pairs={{0,8},{8,0},{16,24},{24,16},{32,40},{40,32},{48,56},{56,48},{64,72... | collective-permute-start | bytes 2359304 | tf_op jit(solution)/shard_map/ppermute | solution.py:328
  65.5 3.0 %collective-permute-start.17 = (bf16[256,1536]{1,0:T(8,128)(2,1)S(1)}, bf16[256,1536]{1,0:T(8,128)(2,1)S(1)}, u32[]{:S(2)}, u32[]{:S(2)}) collective-permute-start(bf16[256,1536]{1,0:T(8,128)(2,1)S(1)} %collective-permute-done.10.refs_1_.refs_13_), channel_id=1, source_target_pairs={{0,8},{8,0},{16,24},{24,16},{32,40},{40,32},{48,56},{56,48},{64,72... | collective-permute-start | bytes 2359304 | tf_op jit(solution)/shard_map/ppermute | solution.py:328
  67.4 2.9 %copy-start.15 = (bf16[256,1536]{1,0:T(8,128)(2,1)}, bf16[256,1536]{1,0:T(8,128)(2,1)S(1)}, u32[]{:S(2)}) copy-start(bf16[256,1536]{1,0:T(8,128)(2,1)S(1)} %collective-permute-done.16.refs_0_.refs_14_) | copy-start | bytes 2359300
  68.5 1.8 copy-start.16
  81.1 58.5 %all-to-all-start = ((bf16[32,128,512]{2,1,0:T(8,128)(2,1)}), bf16[32,128,512]{2,1,0:T(8,128)(2,1)}, u32[]{:S(2)}, u32[]{:S(2)}) async-start(bf16[32,128,512]{2,1,0:T(8,128)(2,1)} %shard_map.74), calls=%async_computation.1 | async-start | bytes 8388608 | tf_op jit(solution)/shard_map/all_to_all | solution.py:431
  87.4 70.7 %copy-start.18 = (bf16[256,256]{1,0:T(8,128)(2,1)S(1)}, bf16[256,256]{1,0:T(8,128)(2,1)}, u32[]{:S(2)}) copy-start(bf16[256,256]{1,0:T(8,128)(2,1)} %constant.18.clone.table_ref) | copy-start | bytes 393220
  127.5 12.1 %copy-start.19 = (bf16[32,16,512]{2,1,0:T(8,128)(2,1)S(1)}, bf16[32,16,512]{2,1,0:T(8,128)(2,1)}, u32[]{:S(2)}) copy-start(bf16[32,16,512]{2,1,0:T(8,128)(2,1)} %shard_map.73) | copy-start | bytes 1572868
  158.2 1.0 copy-start.17
  160.5 24.5 %all-to-all-start.2 = ((bf16[8,16,2048]{2,1,0:T(8,128)(2,1)}), bf16[8,16,2048]{2,1,0:T(8,128)(2,1)S(1)}, u32[]{:S(2)}, u32[]{:S(2)}) async-start(bf16[8,16,2048]{2,1,0:T(8,128)(2,1)} %shard_map.76), calls=%async_computation.3 | async-start | bytes 1048576 | tf_op jit(solution)/shard_map/all_to_all | solution.py:438
Sparse Core Ops, SparseCore 0:
  9.8 58.6 all-gather.2
  71.0 54.5 reduce-scatter.1

commit v14 on v13

--- a/solution.py
+++ b/solution.py
@@ -199,7 +199,7 @@
     )(place, rows, table)
 
 
-def product_kernel(count, position, *refs):
+def product_kernel(count, positions, *refs):
     pieces, weight_ref = refs[:count], refs[count]
     out_ref, results, sems = refs[-3:]
     members = out_ref.shape[0]
@@ -216,7 +216,7 @@
             for t in range(members):
                 start = (k * members + t) * STEP
                 results[n, t, k * STEP : (k + 1) * STEP, :] = result[start : start + STEP]
-        place = (position * count + n) * slots * STEP
+        place = positions[n] * slots * STEP
         stores.append(
             pltpu.make_async_copy(
                 results.at[n], out_ref.at[:, pl.ds(place, slots * STEP), :], sems.at[n]
@@ -227,12 +227,12 @@
         store.wait()
 
 
-def product(held, pieces, weight, position, members, total):
+def product(held, pieces, weight, positions, members, total):
     count, rows = len(pieces), pieces[0].shape[0]
     width, depth = weight.shape
     earlier = [] if held is None else [held]
     return pl.pallas_call(
-        functools.partial(product_kernel, count, position),
+        functools.partial(product_kernel, count, positions),
         in_specs=[pl.BlockSpec(memory_space=pltpu.VMEM)] * (count + 1)
         + [pl.BlockSpec(memory_space=pltpu.HBM)] * len(earlier),
         out_specs=pl.BlockSpec(memory_space=pltpu.HBM),
@@ -397,8 +397,8 @@
     wide_rows = lax.all_gather(activations, "tensor", axis=0, tiled=False)
     total = dp * tokens
 
-    def multiply(held, pieces, position):
-        return product(held, pieces, weight, position, members, total)
+    def multiply(held, pieces, positions):
+        return product(held, pieces, weight, positions, members, total)
 
     half = tokens // 2
     below, above = send(grad_out, 0, 1), send(grad_out, 0, -1)
@@ -410,7 +410,7 @@
     far_top = send(below_top, 1, 1)
     near = [top, bottom]
     near_other = [other_core(block) for block in near]
-    held = multiply(None, near + near_other, 0)
+    held = multiply(None, near + near_other, range(0, 4))
     below_bottom, above_bottom, held = lax.optimization_barrier(
         (below_bottom, above_bottom, held)
     )
@@ -418,13 +418,16 @@
     below, above = [below_top, below_bottom], [above_top, above_bottom]
     below_other = [other_core(block) for block in below]
     above_other = [other_core(block) for block in above]
-    held = multiply(held, below + below_other, 1)
-    held = multiply(held, above + above_other, 2)
-    far_top, far_bottom, held = lax.optimization_barrier((far_top, far_bottom, held))
-    far = [far_top, far_bottom]
-    far_other = [other_core(block) for block in far]
-    held = multiply(held, far, 6)
-    partial_rows = multiply(held, far_other, 7)
+    held = multiply(held, below + below_other, range(4, 8))
+    held = multiply(held, above + above_other, range(8, 12))
+    far_top, held = lax.optimization_barrier((far_top, held))
+    top_other = other_core(far_top)
+    held = multiply(held, [far_top, top_other], (12, 14))
+    far_bottom, held = lax.optimization_barrier((far_bottom, held))
+    bottom_other = other_core(far_bottom)
+    held = multiply(held, [far_bottom], (13,))
+    partial_rows = multiply(held, [bottom_other], (15,))
+    far, far_other = [far_top, far_bottom], [top_other, bottom_other]
     partial_rows, wide_rows = lax.optimization_barrier((partial_rows, wide_rows))
     summed = lax.psum_scatter(partial_rows, "tensor", scatter_dimension=0, tiled=False)
     quantized = quantize(wide_rows, table, dp, width)

time: 193 us -> 205 us (1.062)
  waiting for transfers between devices: 74.3 us -> 89.5 us
  starting transfers between devices: 38.6 us -> 34.3 us
    ppermute x10, waiting for transfers between devices: 22.8 us -> 36.5 us  [send(): return lax.ppermute(block, 'dp', route(turn, sign))]
    ppermute x10, starting transfers between devices: 13.8 us -> 10.6 us  [send(): return lax.ppermute(block, 'dp', route(turn, sign))]
    pallas_call x5 -> x6, Pallas kernels: 11.2 us -> 12 us  [product(): pl.pallas_call(functools.partial(product_kernel, count, positions), in_sp...]
  transfers between devices with their start and end apart: 22 -> 22, of which waited for: 12 -> 13; matrix products, arithmetic and copies ran while one was open for 1% -> 1% of each run, Pallas kernels for 21% -> 21%
where the time goes in v14:
time: 205 us
  waiting for transfers between devices  89.5 us (44%)
  Pallas kernels  43.4 us (21%)
  starting transfers between devices  34.3 us (17%)
  blocking collectives  18.5 us (9%)
  between operations  14.4 us (7%)
  local copies, waits for them, and re-layouts  4.4 us (2%)
    reduce_scatter x1, waiting for transfers between devices, shards(): lax.psum_scatter(partial_rows, 'tensor', scatter_dimension=0, tiled=False)  38.1 us
    ppermute x10, waiting for transfers between devices, send(): return lax.ppermute(block, 'dp', route(turn, sign))  36.5 us
    all_to_all x1, blocking collectives, shards(): lax.all_to_all(ordered, 'dp', split_axis=0, concat_axis=0, tiled=True)  18.5 us
    pallas_call x1, Pallas kernels, gradient(): pl.pallas_call(gradient_kernel, in_specs=[pl.BlockSpec(memory_space=pltpu...  14.2 us
    pallas_call x6, Pallas kernels, product(): pl.pallas_call(functools.partial(product_kernel, count, positions), in_sp...  12 us
    ppermute x8, starting transfers between devices, other_core(): lax.ppermute(block, 'dp', [(d, d ^ 1) for d in range(2 * SIDE * SIDE)])  10.9 us
    pallas_call x1, Pallas kernels, quantize(): pl.pallas_call(quantize_kernel, grid=(tokens // count,), in_specs=[pl.Blo...  10.8 us
    ppermute x10, starting transfers between devices, send(): return lax.ppermute(block, 'dp', route(turn, sign))  10.6 us
  transfers between devices with their start and end apart: 22, of which 13 were waited for; matrix products, arithmetic and copies ran while one was open for 1% of the time, Pallas kernels for 21%

profile of v14, /device:TPU:1, one launch (start us, length us, event | category | flops | bytes accessed | tf_op | source)
XLA Modules:
  0.0 204.6 jit_solution(6144698125190959562)
XLA Ops:
  7.2 0.7 all-gather.3.cloned.1.call-update
  7.9 0.0 reduce-scatter.2.cloned.1.call-start
  8.0 2.2 %collective-permute-start.1 = (bf16[128,1536]{1,0:T(8,128)(2,1)}, bf16[128,1536]{1,0:T(8,128)(2,1)S(1)}, u32[]{:S(2)}, u32[]{:S(2)}) collective-permute-start(bf16[128,1536]{1,0:T(8,128)(2,1)} %param.7), channel_id=1, source_target_pairs={{0,64},{8,24},{16,80},{24,40},{32,96},{40,56},{48,112},{56,8},{64,... | collective-permute-start | bytes 1179656 | tf_op jit(solution)/shard_map/ppermute | solution.py:324
  10.2 1.5 collective-permute-start
  11.7 1.1 constant_dynamic-update-slice_fusion.4
  12.7 4.5 %collective-permute-done.1 = bf16[128,1536]{1,0:T(8,128)(2,1)S(1)} collective-permute-done((bf16[128,1536]{1,0:T(8,128)(2,1)}, bf16[128,1536]{1,0:T(8,128)(2,1)S(1)}, u32[]{:S(2)}, u32[]{:S(2)}) %collective-permute-start.1) | collective-permute-done | bytes 393248 | tf_op jit(solution)/shard_map/ppermute | solution.py:324
  17.3 1.0 collective-permute-start.9
  18.3 2.4 %collective-permute-start.6 = (bf16[256,1536]{1,0:T(8,128)(2,1)S(1)}, bf16[256,1536]{1,0:T(8,128)(2,1)S(1)}, u32[]{:S(2)}, u32[]{:S(2)}) collective-permute-start(bf16[256,1536]{1,0:T(8,128)(2,1)S(1)} %constant_dynamic-update-slice_fusion.3.refs_0_), channel_id=1, source_target_pairs={{0,8},{8,0},{16,24},{24,16},{32,40},{40,32},{48,56},{56,48},{64,72... | collective-permute-start | bytes 2359304 | tf_op jit(solution)/shard_map/ppermute | solution.py:328
  20.7 2.9 %collective-permute-start.3 = (bf16[64,1536]{1,0:T(8,128)(2,1)S(1)}, bf16[64,1536]{1,0:T(8,128)(2,1)S(1)}, u32[]{:S(2)}, u32[]{:S(2)}) collective-permute-start(bf16[64,1536]{1,0:T(8,128)(2,1)S(1)} %slice.9), channel_id=1, source_target_pairs={{0,192},{8,56},{16,208},{24,8},{32,224},{40,24},{48,240},{56,40},{... | collective-permute-start | bytes 589832 | tf_op jit(solution)/shard_map/ppermute | solution.py:324
  23.7 0.1 collective-permute-start.2
  23.8 8.3 %collective-permute-done.2 = bf16[64,1536]{1,0:T(8,128)(2,1)S(1)} collective-permute-done((bf16[64,1536]{1,0:T(8,128)(2,1)S(1)}, bf16[64,1536]{1,0:T(8,128)(2,1)S(1)}, u32[]{:S(2)}, u32[]{:S(2)}) %collective-permute-start.2) | collective-permute-done | bytes 196640 | tf_op jit(solution)/shard_map/ppermute | solution.py:324
  32.1 0.3 collective-permute-start.7
  32.4 1.5 collective-permute-start.4
  33.9 1.2 collective-permute-start.11
  35.1 2.4 %collective-permute-start.14 = (bf16[256,1536]{1,0:T(8,128)(2,1)S(1)}, bf16[256,1536]{1,0:T(8,128)(2,1)S(1)}, u32[]{:S(2)}, u32[]{:S(2)}) collective-permute-start(bf16[256,1536]{1,0:T(8,128)(2,1)S(1)} %collective-permute-done.9.refs_0_.refs_4_), channel_id=1, source_target_pairs={{0,8},{8,0},{16,24},{24,16},{32,40},{40,32},{48,56},{56,48},{64,72... | collective-permute-start | bytes 2359304 | tf_op jit(solution)/shard_map/ppermute | solution.py:328
  37.5 2.6 %shard_map.68.refs_5_ = bf16[8,512,512]{2,1,0:T(8,128)(2,1)} custom-call(bf16[256,1536]{1,0:T(8,128)(2,1)S(1)} %constant_dynamic-update-slice_fusion.3.refs_0_, bf16[256,1536]{1,0:T(8,128)(2,1)S(1)} %constant_dynamic-update-slice_fusion.refs_1_, bf16[256,1536]{1,0:T(8,128)(2,1)S(1)} %collective-permute-done.6.refs_2_, ...), custom_call_target="tpu_custom_call" | custom-call | flops 1610612736 | bytes 4194304 | tf_op jit(solution)/shard_map/pallas_call | solution.py:234
  40.1 3.5 %collective-permute-done.5.refs_1_.refs_9_ = bf16[256,1536]{1,0:T(8,128)(2,1)S(1)} collective-permute-done((bf16[256,1536]{1,0:T(8,128)(2,1)S(1)}, bf16[256,1536]{1,0:T(8,128)(2,1)S(1)}, u32[]{:S(2)}, u32[]{:S(2)}) %collective-permute-start.5) | collective-permute-done | bytes 786464 | tf_op jit(solution)/shard_map/ppermute | solution.py:324
  43.6 1.2 collective-permute-done.4.refs_1_.refs_5_
  44.8 2.6 %collective-permute-start.15 = (bf16[256,1536]{1,0:T(8,128)(2,1)S(1)}, bf16[256,1536]{1,0:T(8,128)(2,1)S(1)}, u32[]{:S(2)}, u32[]{:S(2)}) collective-permute-start(bf16[256,1536]{1,0:T(8,128)(2,1)S(1)} %collective-permute-done.4.refs_1_.refs_5_), channel_id=1, source_target_pairs={{0,8},{8,0},{16,24},{24,16},{32,40},{40,32},{48,56},{56,48},{64,72... | collective-permute-start | bytes 2359304 | tf_op jit(solution)/shard_map/ppermute | solution.py:328
  47.4 4.6 %collective-permute-done.11.refs_0_.refs_8_ = bf16[256,1536]{1,0:T(8,128)(2,1)S(1)} collective-permute-done((bf16[256,1536]{1,0:T(8,128)(2,1)S(1)}, bf16[256,1536]{1,0:T(8,128)(2,1)S(1)}, u32[]{:S(2)}, u32[]{:S(2)}) %collective-permute-start.11) | collective-permute-done | bytes 786464 | tf_op jit(solution)/shard_map/ppermute | solution.py:324
  52.1 1.1 collective-permute-start.12
  53.2 2.6 %shard_map.69.refs_5_ = bf16[8,512,512]{2,1,0:T(8,128)(2,1)} custom-call(bf16[256,1536]{1,0:T(8,128)(2,1)S(1)} %collective-permute-done.9.refs_0_.refs_4_, bf16[256,1536]{1,0:T(8,128)(2,1)S(1)} %collective-permute-done.4.refs_1_.refs_5_, bf16[256,1536]{1,0:T(8,128)(2,1)S(1)} %collective-permute-done.14.refs_2_.refs_6_, ...), custom_call_target="tpu_custom_call", output_to_operand_aliasing={{}: (5, {})} | custom-call | flops 1610612736 | bytes 4194304 | tf_op jit(solution)/shard_map/pallas_call | solution.py:234
  55.8 0.3 collective-permute-done.13.refs_3_.refs_11_
  56.2 2.6 %shard_map.70.refs_3_ = bf16[8,512,512]{2,1,0:T(8,128)(2,1)} custom-call(bf16[256,1536]{1,0:T(8,128)(2,1)S(1)} %collective-permute-done.11.refs_0_.refs_8_, bf16[256,1536]{1,0:T(8,128)(2,1)S(1)} %collective-permute-done.5.refs_1_.refs_9_, bf16[256,1536]{1,0:T(8,128)(2,1)S(1)} %collective-permute-done.12.refs_2_.refs_10_, ...), custom_call_target="tpu_custom_call", output_to_operand_aliasing={{}: (5, {})} | custom-call | flops 1610612736 | bytes 4194304 | tf_op jit(solution)/shard_map/pallas_call | solution.py:234
  58.7 6.8 %collective-permute-done.10.refs_0_.refs_12_ = bf16[256,1536]{1,0:T(8,128)(2,1)S(1)} collective-permute-done((bf16[256,1536]{1,0:T(8,128)(2,1)S(1)}, bf16[256,1536]{1,0:T(8,128)(2,1)S(1)}, u32[]{:S(2)}, u32[]{:S(2)}) %collective-permute-start.10) | collective-permute-done | bytes 786464 | tf_op jit(solution)/shard_map/ppermute | solution.py:324
  65.6 1.3 collective-permute-start.16
  66.8 0.1 collective-permute-start.8
  67.0 1.8 collective-permute-done.16.refs_1_.refs_14_
  68.7 1.7 shard_map.71.refs_2_
  70.5 7.5 %collective-permute-done.8.refs_0_.refs_13_ = bf16[256,1536]{1,0:T(8,128)(2,1)S(1)} collective-permute-done((bf16[256,1536]{1,0:T(8,128)(2,1)S(1)}, bf16[256,1536]{1,0:T(8,128)(2,1)S(1)}, u32[]{:S(2)}, u32[]{:S(2)}) %collective-permute-start.8) | collective-permute-done | bytes 786464 | tf_op jit(solution)/shard_map/ppermute | solution.py:324
  78.0 0.9 collective-permute-start.17
  78.9 1.3 shard_map.72.refs_2_
  80.2 0.6 collective-permute-done.17.refs_0_.refs_15_
  80.8 1.3 shard_map.73
  82.2 10.8 %shard_map.75 = bf16[32,128,512]{2,1,0:T(8,128)(2,1)} custom-call(bf16[8,128,2048]{2,1,0:T(8,128)(2,1)} %bitcast.7, bf16[256,256]{1,0:T(8,128)(2,1)} %constant.18.clone.table_ref), custom_call_target="tpu_custom_call" | custom-call | flops 4294967296 | bytes 8388608 | tf_op jit(solution)/shard_map/pallas_call | solution.py:145
  93.0 5.0 %all-to-all-start = ((bf16[32,128,512]{2,1,0:T(8,128)(2,1)}), bf16[32,128,512]{2,1,0:T(8,128)(2,1)}, u32[]{:S(2)}, u32[]{:S(2)}) async-start(bf16[32,128,512]{2,1,0:T(8,128)(2,1)} %shard_map.75), calls=%async_computation.1 | async-start | bytes 8388608 | tf_op jit(solution)/shard_map/all_to_all | solution.py:434
  98.0 1.3 dynamic-slice_bitcast_fusion.sources
  99.3 38.1 %reduce-scatter.2.cloned.1.call-done = bf16[1,512,512]{2,1,0:T(8,128)(2,1)} async-done(((bf16[8,512,512]{2,1,0:T(8,128)(2,1)}), bf16[1,512,512]{2,1,0:T(8,128)(2,1)}) %reduce-scatter.2.cloned.1.call-update) | async-done | bytes 524304 | tf_op jit(solution)/shard_map/reduce_scatter | solution.py:432
  137.4 1.9 shard_map.74
  139.3 3.2 %shard_map.76.slope_ref = bf16[32,16,512]{2,1,0:T(8,128)(2,1)} custom-call(s32[1]{0:T(128)} %bitcast.4.place, bf16[8,128,2048]{2,1,0:T(8,128)(2,1)} %bitcast.8, bf16[256,256]{1,0:T(8,128)(2,1)} %constant.18.clone.table_ref), custom_call_target="tpu_custom_call" | custom-call | flops 536870912 | bytes 2097152 | tf_op jit(solution)/shard_map/pallas_call | solution.py:182
  142.6 7.6 %all-to-all-done.quantized_ref = bf16[32,128,512]{2,1,0:T(8,128)(2,1)} async-done(((bf16[32,128,512]{2,1,0:T(8,128)(2,1)}), bf16[32,128,512]{2,1,0:T(8,128)(2,1)}, u32[]{:S(2)}, u32[]{:S(2)}) %all-to-all-start) | async-done | bytes 4194336 | tf_op jit(solution)/shard_map/all_to_all | solution.py:434
  150.2 18.5 %all_to_all.15.summed_ref = bf16[32,16,512]{2,1,0:T(8,128)(2,1)S(1)} all-to-all(bf16[32,16,512]{2,1,0:T(8,128)(2,1)S(1)} %copy-done.19), channel_id=1, replica_groups=mesh['dp'=32,'tensor'=8] {'dp'}, dimensions={0} | all-to-all | bytes 1048576 | tf_op jit(solution)/shard_map/all_to_all | solution.py:439
  168.7 1.0 copy-done.17
  169.8 1.3 shard_map.77
  171.1 7.8 %all-to-all-start.2 = ((bf16[8,16,2048]{2,1,0:T(8,128)(2,1)}), bf16[8,16,2048]{2,1,0:T(8,128)(2,1)S(1)}, u32[]{:S(2)}, u32[]{:S(2)}) async-start(bf16[8,16,2048]{2,1,0:T(8,128)(2,1)} %shard_map.77), calls=%async_computation.3 | async-start | bytes 1048576 | tf_op jit(solution)/shard_map/all_to_all | solution.py:441
  178.9 14.2 %shard_map.78 = f32[512,1536]{1,0:T(8,128)} custom-call(s32[32]{0:T(128)} %dynamic-slice_bitcast_fusion.sources, bf16[32,128,512]{2,1,0:T(8,128)(2,1)} %all-to-all-done.quantized_ref, bf16[256,1536]{1,0:T(8,128)(2,1)} %copy-done.2, bf16[256,1536]{1,0:T(8,128)(2,1)} %copy-done.1, bf16[256,1536]{1,0:T(8,128)(2,1)} %copy-done.4, bf16[256,1536]{1,0:T(8,128)(2,1)} %copy-done.5, ...), custom_call_target="tpu_custom_call" | custom-call | flops 6442450944 | bytes 19922944 | tf_op jit(solution)/shard_map/pallas_call | solution.py:292
  193.0 3.9 %all-to-all-done.2 = bf16[8,16,2048]{2,1,0:T(8,128)(2,1)S(1)} async-done(((bf16[8,16,2048]{2,1,0:T(8,128)(2,1)}), bf16[8,16,2048]{2,1,0:T(8,128)(2,1)S(1)}, u32[]{:S(2)}, u32[]{:S(2)}) %all-to-all-start.2) | async-done | bytes 524320 | tf_op jit(solution)/shard_map/all_to_all | solution.py:441
  196.9 0.8 copy.21
  (59 shorter events, 0.3 us)
Async XLA Ops:
  7.2 30.3 %copy-start = (bf16[512,1536]{1,0:T(8,128)(2,1)S(1)}, bf16[512,1536]{1,0:T(8,128)(2,1)}, u32[]{:S(2)}) copy-start(bf16[512,1536]{1,0:T(8,128)(2,1)} %refs_1_.3) | copy-start | bytes 4718596
  7.2 75.0 %all-gather.3.cloned.1.call-start = ((), (), s32[]{:S(2)}) async-start(), calls=%async_computation.5 | async-start | bytes 4718592 | tf_op jit(solution)/shard_map/all_gather | solution.py:397
  7.9 129.5 %reduce-scatter.2.cloned.1.call-start = ((), (), s32[]{:S(2)}) async-start(), calls=%async_computation.4 | async-start | bytes 4718592 | tf_op jit(solution)/shard_map/reduce_scatter | solution.py:432
  8.0 9.3 %collective-permute-start.1 = (bf16[128,1536]{1,0:T(8,128)(2,1)}, bf16[128,1536]{1,0:T(8,128)(2,1)S(1)}, u32[]{:S(2)}, u32[]{:S(2)}) collective-permute-start(bf16[128,1536]{1,0:T(8,128)(2,1)} %param.7), channel_id=1, source_target_pairs={{0,64},{8,24},{16,80},{24,40},{32,96},{40,56},{48,112},{56,8},{64,... | collective-permute-start | bytes 1179656 | tf_op jit(solution)/shard_map/ppermute | solution.py:324
  10.2 10.5 %collective-permute-start = (bf16[128,1536]{1,0:T(8,128)(2,1)}, bf16[128,1536]{1,0:T(8,128)(2,1)S(1)}, u32[]{:S(2)}, u32[]{:S(2)}) collective-permute-start(bf16[128,1536]{1,0:T(8,128)(2,1)} %param.7), channel_id=1, source_target_pairs={{0,192},{8,56},{16,208},{24,8},{32,224},{40,24},{48,240},{56,40},{... | collective-permute-start | bytes 1179656 | tf_op jit(solution)/shard_map/ppermute | solution.py:324
  17.3 22.7 %copy-start.2 = (bf16[256,1536]{1,0:T(8,128)(2,1)}, bf16[256,1536]{1,0:T(8,128)(2,1)S(1)}, u32[]{:S(2)}) copy-start(bf16[256,1536]{1,0:T(8,128)(2,1)S(1)} %constant_dynamic-update-slice_fusion.3.refs_0_) | copy-start | bytes 2359300
  17.3 16.5 %collective-permute-start.9 = (bf16[256,1536]{1,0:T(8,128)(2,1)S(1)}, bf16[256,1536]{1,0:T(8,128)(2,1)S(1)}, u32[]{:S(2)}, u32[]{:S(2)}) collective-permute-start(bf16[256,1536]{1,0:T(8,128)(2,1)S(1)} %constant_dynamic-update-slice_fusion.3.refs_0_), channel_id=1, source_target_pairs={{0,16},{8,72},{16,32},{24,88},{32,48},{40,104},{48,0},{56,120},{64... | collective-permute-start | bytes 2359304 | tf_op jit(solution)/shard_map/ppermute | solution.py:324
  18.3 16.8 %collective-permute-start.6 = (bf16[256,1536]{1,0:T(8,128)(2,1)S(1)}, bf16[256,1536]{1,0:T(8,128)(2,1)S(1)}, u32[]{:S(2)}, u32[]{:S(2)}) collective-permute-start(bf16[256,1536]{1,0:T(8,128)(2,1)S(1)} %constant_dynamic-update-slice_fusion.3.refs_0_), channel_id=1, source_target_pairs={{0,8},{8,0},{16,24},{24,16},{32,40},{40,32},{48,56},{56,48},{64,72... | collective-permute-start | bytes 2359304 | tf_op jit(solution)/shard_map/ppermute | solution.py:328
  20.7 11.3 %collective-permute-start.3 = (bf16[64,1536]{1,0:T(8,128)(2,1)S(1)}, bf16[64,1536]{1,0:T(8,128)(2,1)S(1)}, u32[]{:S(2)}, u32[]{:S(2)}) collective-permute-start(bf16[64,1536]{1,0:T(8,128)(2,1)S(1)} %slice.9), channel_id=1, source_target_pairs={{0,192},{8,56},{16,208},{24,8},{32,224},{40,24},{48,240},{56,40},{... | collective-permute-start | bytes 589832 | tf_op jit(solution)/shard_map/ppermute | solution.py:324
  23.7 8.4 %collective-permute-start.2 = (bf16[64,1536]{1,0:T(8,128)(2,1)S(1)}, bf16[64,1536]{1,0:T(8,128)(2,1)S(1)}, u32[]{:S(2)}, u32[]{:S(2)}) collective-permute-start(bf16[64,1536]{1,0:T(8,128)(2,1)S(1)} %slice.8), channel_id=1, source_target_pairs={{0,64},{8,24},{16,80},{24,40},{32,96},{40,56},{48,112},{56,8},{64,... | collective-permute-start | bytes 589832 | tf_op jit(solution)/shard_map/ppermute | solution.py:324
  32.1 8.0 %copy-start.1 = (bf16[256,1536]{1,0:T(8,128)(2,1)}, bf16[256,1536]{1,0:T(8,128)(2,1)S(1)}, u32[]{:S(2)}) copy-start(bf16[256,1536]{1,0:T(8,128)(2,1)S(1)} %constant_dynamic-update-slice_fusion.refs_1_) | copy-start | bytes 2359300
  32.1 5.4 %collective-permute-start.7 = (bf16[256,1536]{1,0:T(8,128)(2,1)S(1)}, bf16[256,1536]{1,0:T(8,128)(2,1)S(1)}, u32[]{:S(2)}, u32[]{:S(2)}) collective-permute-start(bf16[256,1536]{1,0:T(8,128)(2,1)S(1)} %constant_dynamic-update-slice_fusion.refs_1_), channel_id=1, source_target_pairs={{0,8},{8,0},{16,24},{24,16},{32,40},{40,32},{48,56},{56,48},{64,72... | collective-permute-start | bytes 2359304 | tf_op jit(solution)/shard_map/ppermute | solution.py:328
  32.4 11.2 %collective-permute-start.5 = (bf16[256,1536]{1,0:T(8,128)(2,1)S(1)}, bf16[256,1536]{1,0:T(8,128)(2,1)S(1)}, u32[]{:S(2)}, u32[]{:S(2)}) collective-permute-start(bf16[256,1536]{1,0:T(8,128)(2,1)S(1)} %constant_dynamic-update-slice_fusion.refs_1_), channel_id=1, source_target_pairs={{0,48},{8,200},{16,0},{24,216},{32,16},{40,232},{48,32},{56,248},{... | collective-permute-start | bytes 2359304 | tf_op jit(solution)/shard_map/ppermute | solution.py:324
  32.4 12.5 %collective-permute-start.4 = (bf16[256,1536]{1,0:T(8,128)(2,1)S(1)}, bf16[256,1536]{1,0:T(8,128)(2,1)S(1)}, u32[]{:S(2)}, u32[]{:S(2)}) collective-permute-start(bf16[256,1536]{1,0:T(8,128)(2,1)S(1)} %constant_dynamic-update-slice_fusion.refs_1_), channel_id=1, source_target_pairs={{0,16},{8,72},{16,32},{24,88},{32,48},{40,104},{48,0},{56,120},{64... | collective-permute-start | bytes 2359304 | tf_op jit(solution)/shard_map/ppermute | solution.py:324
  33.9 19.3 %copy-start.3 = (bf16[256,1536]{1,0:T(8,128)(2,1)}, bf16[256,1536]{1,0:T(8,128)(2,1)S(1)}, u32[]{:S(2)}) copy-start(bf16[256,1536]{1,0:T(8,128)(2,1)S(1)} %collective-permute-done.9.refs_0_.refs_4_) | copy-start | bytes 2359300
  33.9 18.2 %collective-permute-start.11 = (bf16[256,1536]{1,0:T(8,128)(2,1)S(1)}, bf16[256,1536]{1,0:T(8,128)(2,1)S(1)}, u32[]{:S(2)}, u32[]{:S(2)}) collective-permute-start(bf16[256,1536]{1,0:T(8,128)(2,1)S(1)} %constant_dynamic-update-slice_fusion.3.refs_0_), channel_id=1, source_target_pairs={{0,48},{8,200},{16,0},{24,216},{32,16},{40,232},{48,32},{56,248},{... | collective-permute-start | bytes 2359304 | tf_op jit(solution)/shard_map/ppermute | solution.py:324
  35.1 5.0 %copy-start.4 = (bf16[256,1536]{1,0:T(8,128)(2,1)}, bf16[256,1536]{1,0:T(8,128)(2,1)S(1)}, u32[]{:S(2)}) copy-start(bf16[256,1536]{1,0:T(8,128)(2,1)S(1)} %collective-permute-done.6.refs_2_) | copy-start | bytes 2359300
  35.1 18.1 %collective-permute-start.14 = (bf16[256,1536]{1,0:T(8,128)(2,1)S(1)}, bf16[256,1536]{1,0:T(8,128)(2,1)S(1)}, u32[]{:S(2)}, u32[]{:S(2)}) collective-permute-start(bf16[256,1536]{1,0:T(8,128)(2,1)S(1)} %collective-permute-done.9.refs_0_.refs_4_), channel_id=1, source_target_pairs={{0,8},{8,0},{16,24},{24,16},{32,40},{40,32},{48,56},{56,48},{64,72... | collective-permute-start | bytes 2359304 | tf_op jit(solution)/shard_map/ppermute | solution.py:328
  37.5 2.6 %copy-start.5 = (bf16[256,1536]{1,0:T(8,128)(2,1)}, bf16[256,1536]{1,0:T(8,128)(2,1)S(1)}, u32[]{:S(2)}) copy-start(bf16[256,1536]{1,0:T(8,128)(2,1)S(1)} %collective-permute-done.7.refs_3_) | copy-start | bytes 2359300
  43.6 23.2 %copy-start.6 = (bf16[256,1536]{1,0:T(8,128)(2,1)}, bf16[256,1536]{1,0:T(8,128)(2,1)S(1)}, u32[]{:S(2)}) copy-start(bf16[256,1536]{1,0:T(8,128)(2,1)S(1)} %collective-permute-done.5.refs_1_.refs_9_) | copy-start | bytes 2359300
  44.8 10.9 %copy-start.7 = (bf16[256,1536]{1,0:T(8,128)(2,1)}, bf16[256,1536]{1,0:T(8,128)(2,1)S(1)}, u32[]{:S(2)}) copy-start(bf16[256,1536]{1,0:T(8,128)(2,1)S(1)} %collective-permute-done.4.refs_1_.refs_5_) | copy-start | bytes 2359300
  44.8 8.3 %collective-permute-start.15 = (bf16[256,1536]{1,0:T(8,128)(2,1)S(1)}, bf16[256,1536]{1,0:T(8,128)(2,1)S(1)}, u32[]{:S(2)}, u32[]{:S(2)}) collective-permute-start(bf16[256,1536]{1,0:T(8,128)(2,1)S(1)} %collective-permute-done.4.refs_1_.refs_5_), channel_id=1, source_target_pairs={{0,8},{8,0},{16,24},{24,16},{32,40},{40,32},{48,56},{56,48},{64,72... | collective-permute-start | bytes 2359304 | tf_op jit(solution)/shard_map/ppermute | solution.py:328
  52.0 4.1 %copy-start.8 = (bf16[256,1536]{1,0:T(8,128)(2,1)}, bf16[256,1536]{1,0:T(8,128)(2,1)S(1)}, u32[]{:S(2)}) copy-start(bf16[256,1536]{1,0:T(8,128)(2,1)S(1)} %collective-permute-done.11.refs_0_.refs_8_) | copy-start | bytes 2359300
  52.1 3.7 %collective-permute-start.12 = (bf16[256,1536]{1,0:T(8,128)(2,1)S(1)}, bf16[256,1536]{1,0:T(8,128)(2,1)S(1)}, u32[]{:S(2)}, u32[]{:S(2)}) collective-permute-start(bf16[256,1536]{1,0:T(8,128)(2,1)S(1)} %collective-permute-done.11.refs_0_.refs_8_), channel_id=1, source_target_pairs={{0,8},{8,0},{16,24},{24,16},{32,40},{40,32},{48,56},{56,48},{64,72... | collective-permute-start | bytes 2359304 | tf_op jit(solution)/shard_map/ppermute | solution.py:328
  53.1 3.0 %collective-permute-start.13 = (bf16[256,1536]{1,0:T(8,128)(2,1)S(1)}, bf16[256,1536]{1,0:T(8,128)(2,1)S(1)}, u32[]{:S(2)}, u32[]{:S(2)}) collective-permute-start(bf16[256,1536]{1,0:T(8,128)(2,1)S(1)} %collective-permute-done.5.refs_1_.refs_9_), channel_id=1, source_target_pairs={{0,8},{8,0},{16,24},{24,16},{32,40},{40,32},{48,56},{56,48},{64,72... | collective-permute-start | bytes 2359304 | tf_op jit(solution)/shard_map/ppermute | solution.py:328
  53.1 12.5 %collective-permute-start.10 = (bf16[256,1536]{1,0:T(8,128)(2,1)S(1)}, bf16[256,1536]{1,0:T(8,128)(2,1)S(1)}, u32[]{:S(2)}, u32[]{:S(2)}) collective-permute-start(bf16[256,1536]{1,0:T(8,128)(2,1)S(1)} %collective-permute-done.9.refs_0_.refs_4_), channel_id=1, source_target_pairs={{0,16},{8,72},{16,32},{24,88},{32,48},{40,104},{48,0},{56,120},{64... | collective-permute-start | bytes 2359304 | tf_op jit(solution)/shard_map/ppermute | solution.py:324
  53.1 2.6 %copy-start.9 = (bf16[256,1536]{1,0:T(8,128)(2,1)}, bf16[256,1536]{1,0:T(8,128)(2,1)S(1)}, u32[]{:S(2)}) copy-start(bf16[256,1536]{1,0:T(8,128)(2,1)S(1)} %collective-permute-done.14.refs_2_.refs_6_) | copy-start | bytes 2359300
  53.2 2.6 %copy-start.10 = (bf16[256,1536]{1,0:T(8,128)(2,1)}, bf16[256,1536]{1,0:T(8,128)(2,1)S(1)}, u32[]{:S(2)}) copy-start(bf16[256,1536]{1,0:T(8,128)(2,1)S(1)} %collective-permute-done.15.refs_3_.refs_7_) | copy-start | bytes 2359300
  55.8 2.9 %copy-start.11 = (bf16[256,1536]{1,0:T(8,128)(2,1)}, bf16[256,1536]{1,0:T(8,128)(2,1)S(1)}, u32[]{:S(2)}) copy-start(bf16[256,1536]{1,0:T(8,128)(2,1)S(1)} %collective-permute-done.12.refs_2_.refs_10_) | copy-start | bytes 2359300
  56.2 2.6 %copy-start.12 = (bf16[256,1536]{1,0:T(8,128)(2,1)}, bf16[256,1536]{1,0:T(8,128)(2,1)S(1)}, u32[]{:S(2)}) copy-start(bf16[256,1536]{1,0:T(8,128)(2,1)S(1)} %collective-permute-done.13.refs_3_.refs_11_) | copy-start | bytes 2359300
  65.6 4.9 %copy-start.13 = (bf16[256,1536]{1,0:T(8,128)(2,1)}, bf16[256,1536]{1,0:T(8,128)(2,1)S(1)}, u32[]{:S(2)}) copy-start(bf16[256,1536]{1,0:T(8,128)(2,1)S(1)} %collective-permute-done.10.refs_0_.refs_12_) | copy-start | bytes 2359300
  65.6 3.2 %collective-permute-start.16 = (bf16[256,1536]{1,0:T(8,128)(2,1)S(1)}, bf16[256,1536]{1,0:T(8,128)(2,1)S(1)}, u32[]{:S(2)}, u32[]{:S(2)}) collective-permute-start(bf16[256,1536]{1,0:T(8,128)(2,1)S(1)} %collective-permute-done.10.refs_0_.refs_12_), channel_id=1, source_target_pairs={{0,8},{8,0},{16,24},{24,16},{32,40},{40,32},{48,56},{56,48},{64,72... | collective-permute-start | bytes 2359304 | tf_op jit(solution)/shard_map/ppermute | solution.py:328
  66.8 11.1 %collective-permute-start.8 = (bf16[256,1536]{1,0:T(8,128)(2,1)S(1)}, bf16[256,1536]{1,0:T(8,128)(2,1)S(1)}, u32[]{:S(2)}, u32[]{:S(2)}) collective-permute-start(bf16[256,1536]{1,0:T(8,128)(2,1)S(1)} %collective-permute-done.5.refs_1_.refs_9_), channel_id=1, source_target_pairs={{0,48},{8,200},{16,0},{24,216},{32,16},{40,232},{48,32},{56,248},{... | collective-permute-start | bytes 2359304 | tf_op jit(solution)/shard_map/ppermute | solution.py:324
  68.7 1.7 copy-start.14
  78.0 2.3 %copy-start.15 = (bf16[256,1536]{1,0:T(8,128)(2,1)}, bf16[256,1536]{1,0:T(8,128)(2,1)S(1)}, u32[]{:S(2)}) copy-start(bf16[256,1536]{1,0:T(8,128)(2,1)S(1)} %collective-permute-done.8.refs_0_.refs_13_) | copy-start | bytes 2359300
  78.0 2.9 %collective-permute-start.17 = (bf16[256,1536]{1,0:T(8,128)(2,1)S(1)}, bf16[256,1536]{1,0:T(8,128)(2,1)S(1)}, u32[]{:S(2)}, u32[]{:S(2)}) collective-permute-start(bf16[256,1536]{1,0:T(8,128)(2,1)S(1)} %collective-permute-done.8.refs_0_.refs_13_), channel_id=1, source_target_pairs={{0,8},{8,0},{16,24},{24,16},{32,40},{40,32},{48,56},{56,48},{64,72... | collective-permute-start | bytes 2359304 | tf_op jit(solution)/shard_map/ppermute | solution.py:328
  80.8 1.3 copy-start.16
  93.0 57.2 %all-to-all-start = ((bf16[32,128,512]{2,1,0:T(8,128)(2,1)}), bf16[32,128,512]{2,1,0:T(8,128)(2,1)}, u32[]{:S(2)}, u32[]{:S(2)}) async-start(bf16[32,128,512]{2,1,0:T(8,128)(2,1)} %shard_map.75), calls=%async_computation.1 | async-start | bytes 8388608 | tf_op jit(solution)/shard_map/all_to_all | solution.py:434
  98.0 70.7 %copy-start.18 = (bf16[256,256]{1,0:T(8,128)(2,1)S(1)}, bf16[256,256]{1,0:T(8,128)(2,1)}, u32[]{:S(2)}) copy-start(bf16[256,256]{1,0:T(8,128)(2,1)} %constant.18.clone.table_ref) | copy-start | bytes 393220
  139.3 10.9 %copy-start.19 = (bf16[32,16,512]{2,1,0:T(8,128)(2,1)S(1)}, bf16[32,16,512]{2,1,0:T(8,128)(2,1)}, u32[]{:S(2)}) copy-start(bf16[32,16,512]{2,1,0:T(8,128)(2,1)} %shard_map.74) | copy-start | bytes 1572868
  168.7 1.0 copy-start.17
  171.1 25.9 %all-to-all-start.2 = ((bf16[8,16,2048]{2,1,0:T(8,128)(2,1)}), bf16[8,16,2048]{2,1,0:T(8,128)(2,1)S(1)}, u32[]{:S(2)}, u32[]{:S(2)}) async-start(bf16[8,16,2048]{2,1,0:T(8,128)(2,1)} %shard_map.77), calls=%async_computation.3 | async-start | bytes 1048576 | tf_op jit(solution)/shard_map/all_to_all | solution.py:441
Sparse Core Ops, SparseCore 0:
  9.8 58.6 all-gather.2
  82.3 55.0 reduce-scatter.1

commit v15 on v13

--- a/solution.py
+++ b/solution.py
@@ -400,12 +400,10 @@
     def multiply(held, pieces, position):
         return product(held, pieces, weight, position, members, total)
 
-    half = tokens // 2
     below, above = send(grad_out, 0, 1), send(grad_out, 0, -1)
     top = jnp.concatenate([grad_out, below], axis=0)
     below_top, above_top = send(top, 1, 1), send(top, 1, -1)
-    far = [send(below[:half], 0, 1), send(above[half:], 0, -1)]
-    bottom = jnp.concatenate([above, *far], axis=0)
+    bottom = jnp.concatenate([above, send(grad_out, 0, 2)], axis=0)
     below_bottom, above_bottom = send(bottom, 1, 1), send(bottom, 1, -1)
     far_top = send(below_top, 1, 1)
     near = [top, bottom]

time: 193 us -> 190 us (0.984)
    ppermute x10 -> x9, waiting for transfers between devices: 22.8 us -> 18.2 us  [send(): return lax.ppermute(block, 'dp', route(turn, sign))]
    all_gather x1, waiting for transfers between devices: 0.02 us -> 3.03 us  [shards(): wide_rows = lax.all_gather(activations, 'tensor', axis=0, tiled=False)]
    all_to_all x1, starting transfers between devices: 6.48 us -> 4.1 us  [shards(): lax.all_to_all(mixed, 'tensor', split_axis=0, concat_axis=0, tiled=True)]
    ppermute x10 -> x9, starting transfers between devices: 13.8 us -> 13.6 us  [send(): return lax.ppermute(block, 'dp', route(turn, sign))]
  transfers between devices with their start and end apart: 22 -> 21, of which waited for: 12 -> 9; matrix products, arithmetic and copies ran while one was open for 1% -> 1% of each run, Pallas kernels for 21% -> 22%
where the time goes in v15:
time: 190 us
  waiting for transfers between devices  72.8 us (38%)
  Pallas kernels  42.7 us (22%)
  starting transfers between devices  37.1 us (20%)
  blocking collectives  18.5 us (10%)
  between operations  14.3 us (8%)
  local copies, waits for them, and re-layouts  4.3 us (2%)
    reduce_scatter x1, waiting for transfers between devices, shards(): lax.psum_scatter(partial_rows, 'tensor', scatter_dimension=0, tiled=False)  36.8 us
    all_to_all x1, blocking collectives, shards(): lax.all_to_all(ordered, 'dp', split_axis=0, concat_axis=0, tiled=True)  18.5 us
    ppermute x9, waiting for transfers between devices, send(): return lax.ppermute(block, 'dp', route(turn, sign))  18.2 us
    pallas_call x1, Pallas kernels, gradient(): pl.pallas_call(gradient_kernel, in_specs=[pl.BlockSpec(memory_space=pltpu...  14.2 us
    ppermute x9, starting transfers between devices, send(): return lax.ppermute(block, 'dp', route(turn, sign))  13.6 us
    ppermute x8, starting transfers between devices, other_core(): lax.ppermute(block, 'dp', [(d, d ^ 1) for d in range(2 * SIDE * SIDE)])  11.7 us
    pallas_call x5, Pallas kernels, product(): pl.pallas_call(functools.partial(product_kernel, count, position), in_spe...  11.3 us
    pallas_call x1, Pallas kernels, quantize(): pl.pallas_call(quantize_kernel, grid=(tokens // count,), in_specs=[pl.Blo...  10.8 us
  transfers between devices with their start and end apart: 21, of which 9 were waited for; matrix products, arithmetic and copies ran while one was open for 1% of the time, Pallas kernels for 22%

profile of v15, /device:TPU:1, one launch (start us, length us, event | category | flops | bytes accessed | tf_op | source)
XLA Modules:
  0.0 189.8 jit_solution(1940016727886762623)
XLA Ops:
  7.2 0.0 all-gather.3.cloned.1.call-start
  7.2 0.7 all-gather.3.cloned.1.call-update
  7.9 0.0 reduce-scatter.2.cloned.1.call-start
  8.0 2.2 %collective-permute-start = (bf16[128,1536]{1,0:T(8,128)(2,1)}, bf16[128,1536]{1,0:T(8,128)(2,1)S(1)}, u32[]{:S(2)}, u32[]{:S(2)}) collective-permute-start(bf16[128,1536]{1,0:T(8,128)(2,1)} %param.7), channel_id=1, source_target_pairs={{0,64},{8,24},{16,80},{24,40},{32,96},{40,56},{48,112},{56,8},{64,... | collective-permute-start | bytes 1179656 | tf_op jit(solution)/shard_map/ppermute | solution.py:324
  10.2 2.6 %collective-permute-start.4 = (bf16[128,1536]{1,0:T(8,128)(2,1)}, bf16[128,1536]{1,0:T(8,128)(2,1)S(1)}, u32[]{:S(2)}, u32[]{:S(2)}) collective-permute-start(bf16[128,1536]{1,0:T(8,128)(2,1)} %param.7), channel_id=1, source_target_pairs={{0,128},{8,40},{16,144},{24,56},{32,160},{40,8},{48,176},{56,24},{... | collective-permute-start | bytes 1179656 | tf_op jit(solution)/shard_map/ppermute | solution.py:324
  12.8 1.1 collective-permute-start.3
  13.8 1.1 constant_dynamic-update-slice_fusion.1
  14.9 2.4 %collective-permute-done = bf16[128,1536]{1,0:T(8,128)(2,1)S(1)} collective-permute-done((bf16[128,1536]{1,0:T(8,128)(2,1)}, bf16[128,1536]{1,0:T(8,128)(2,1)S(1)}, u32[]{:S(2)}, u32[]{:S(2)}) %collective-permute-start) | collective-permute-done | bytes 393248 | tf_op jit(solution)/shard_map/ppermute | solution.py:324
  17.3 7.5 %collective-permute-start.7 = (bf16[256,1536]{1,0:T(8,128)(2,1)S(1)}, bf16[256,1536]{1,0:T(8,128)(2,1)S(1)}, u32[]{:S(2)}, u32[]{:S(2)}) collective-permute-start(bf16[256,1536]{1,0:T(8,128)(2,1)S(1)} %constant_dynamic-update-slice_fusion.refs_0_), channel_id=1, source_target_pairs={{0,8},{8,0},{16,24},{24,16},{32,40},{40,32},{48,56},{56,48},{64,72... | collective-permute-start | bytes 2359304 | tf_op jit(solution)/shard_map/ppermute | solution.py:328
  24.8 0.0 collective-permute-start.1
  24.8 0.0 collective-permute-done.3
  24.9 0.9 collective-permute-start.8
  25.8 2.3 %collective-permute-start.6 = (bf16[256,1536]{1,0:T(8,128)(2,1)S(1)}, bf16[256,1536]{1,0:T(8,128)(2,1)S(1)}, u32[]{:S(2)}, u32[]{:S(2)}) collective-permute-start(bf16[256,1536]{1,0:T(8,128)(2,1)S(1)} %constant_dynamic-update-slice_fusion.2.refs_1_), channel_id=1, source_target_pairs={{0,48},{8,200},{16,0},{24,216},{32,16},{40,232},{48,32},{56,248},{... | collective-permute-start | bytes 2359304 | tf_op jit(solution)/shard_map/ppermute | solution.py:324
  28.1 2.7 %collective-permute-start.10 = (bf16[256,1536]{1,0:T(8,128)(2,1)S(1)}, bf16[256,1536]{1,0:T(8,128)(2,1)S(1)}, u32[]{:S(2)}, u32[]{:S(2)}) collective-permute-start(bf16[256,1536]{1,0:T(8,128)(2,1)S(1)} %constant_dynamic-update-slice_fusion.refs_0_), channel_id=1, source_target_pairs={{0,48},{8,200},{16,0},{24,216},{32,16},{40,232},{48,32},{56,248},{... | collective-permute-start | bytes 2359304 | tf_op jit(solution)/shard_map/ppermute | solution.py:324
  30.8 6.5 %collective-permute-done.1.refs_0_.refs_4_ = bf16[256,1536]{1,0:T(8,128)(2,1)S(1)} collective-permute-done((bf16[256,1536]{1,0:T(8,128)(2,1)S(1)}, bf16[256,1536]{1,0:T(8,128)(2,1)S(1)}, u32[]{:S(2)}, u32[]{:S(2)}) %collective-permute-start.1) | collective-permute-done | bytes 786464 | tf_op jit(solution)/shard_map/ppermute | solution.py:324
  37.3 0.8 collective-permute-start.13
  38.1 2.6 %shard_map.68.refs_5_ = bf16[8,512,512]{2,1,0:T(8,128)(2,1)} custom-call(bf16[256,1536]{1,0:T(8,128)(2,1)S(1)} %constant_dynamic-update-slice_fusion.refs_0_, bf16[256,1536]{1,0:T(8,128)(2,1)S(1)} %constant_dynamic-update-slice_fusion.2.refs_1_, bf16[256,1536]{1,0:T(8,128)(2,1)S(1)} %collective-permute-done.7.refs_2_, ...), custom_call_target="tpu_custom_call" | custom-call | flops 1610612736 | bytes 4194304 | tf_op jit(solution)/shard_map/pallas_call | solution.py:234
  40.8 4.9 %collective-permute-done.5.refs_1_.refs_5_ = bf16[256,1536]{1,0:T(8,128)(2,1)S(1)} collective-permute-done((bf16[256,1536]{1,0:T(8,128)(2,1)S(1)}, bf16[256,1536]{1,0:T(8,128)(2,1)S(1)}, u32[]{:S(2)}, u32[]{:S(2)}) %collective-permute-start.5) | collective-permute-done | bytes 786464 | tf_op jit(solution)/shard_map/ppermute | solution.py:324
  45.7 0.8 collective-permute-start.14
  46.5 0.1 collective-permute-start.11
  46.6 0.4 collective-permute-start.12
  47.1 2.7 %collective-permute-start.9 = (bf16[256,1536]{1,0:T(8,128)(2,1)S(1)}, bf16[256,1536]{1,0:T(8,128)(2,1)S(1)}, u32[]{:S(2)}, u32[]{:S(2)}) collective-permute-start(bf16[256,1536]{1,0:T(8,128)(2,1)S(1)} %collective-permute-done.6.refs_1_.refs_9_), channel_id=1, source_target_pairs={{0,48},{8,200},{16,0},{24,216},{32,16},{40,232},{48,32},{56,248},{... | collective-permute-start | bytes 2359304 | tf_op jit(solution)/shard_map/ppermute | solution.py:324
  49.8 2.6 %shard_map.69.refs_5_ = bf16[8,512,512]{2,1,0:T(8,128)(2,1)} custom-call(bf16[256,1536]{1,0:T(8,128)(2,1)S(1)} %collective-permute-done.1.refs_0_.refs_4_, bf16[256,1536]{1,0:T(8,128)(2,1)S(1)} %collective-permute-done.5.refs_1_.refs_5_, bf16[256,1536]{1,0:T(8,128)(2,1)S(1)} %collective-permute-done.13.refs_2_.refs_6_, ...), custom_call_target="tpu_custom_call", output_to_operand_aliasing={{}: (5, {})} | custom-call | flops 1610612736 | bytes 4194304 | tf_op jit(solution)/shard_map/pallas_call | solution.py:234
  52.5 2.6 %shard_map.70.refs_3_ = bf16[8,512,512]{2,1,0:T(8,128)(2,1)} custom-call(bf16[256,1536]{1,0:T(8,128)(2,1)S(1)} %collective-permute-done.10.refs_0_.refs_8_, bf16[256,1536]{1,0:T(8,128)(2,1)S(1)} %collective-permute-done.6.refs_1_.refs_9_, bf16[256,1536]{1,0:T(8,128)(2,1)S(1)} %collective-permute-done.11.refs_2_.refs_10_, ...), custom_call_target="tpu_custom_call", output_to_operand_aliasing={{}: (5, {})} | custom-call | flops 1610612736 | bytes 4194304 | tf_op jit(solution)/shard_map/pallas_call | solution.py:234
  55.1 4.4 %collective-permute-done.2.refs_0_.refs_12_ = bf16[256,1536]{1,0:T(8,128)(2,1)S(1)} collective-permute-done((bf16[256,1536]{1,0:T(8,128)(2,1)S(1)}, bf16[256,1536]{1,0:T(8,128)(2,1)S(1)}, u32[]{:S(2)}, u32[]{:S(2)}) %collective-permute-start.2) | collective-permute-done | bytes 786464 | tf_op jit(solution)/shard_map/ppermute | solution.py:324
  59.5 1.1 collective-permute-start.15
  60.6 0.1 collective-permute-start.16
  60.7 1.8 shard_map.71.refs_3_
  62.5 0.0 collective-permute-done.15.refs_0_.refs_14_
  62.5 1.1 collective-permute-done.16.refs_1_.refs_15_
  63.6 1.7 shard_map.72
  65.4 3.0 %all-gather.3.cloned.1.call-done = bf16[1024,2048]{1,0:T(8,128)(2,1)} async-done(((bf16[128,2048]{1,0:T(8,128)(2,1)}), bf16[1024,2048]{1,0:T(8,128)(2,1)}) %all-gather.3.cloned.1.call-update) | async-done | bytes 4194320 | tf_op jit(solution)/shard_map/all_gather | solution.py:397
  68.5 0.0 reduce-scatter.2.cloned.1.call-update
  68.5 10.8 %shard_map.74 = bf16[32,128,512]{2,1,0:T(8,128)(2,1)} custom-call(bf16[8,128,2048]{2,1,0:T(8,128)(2,1)} %bitcast.7, bf16[256,256]{1,0:T(8,128)(2,1)} %constant.18.clone.table_ref), custom_call_target="tpu_custom_call" | custom-call | flops 4294967296 | bytes 8388608 | tf_op jit(solution)/shard_map/pallas_call | solution.py:145
  79.3 7.6 %all-to-all-start = ((bf16[32,128,512]{2,1,0:T(8,128)(2,1)}), bf16[32,128,512]{2,1,0:T(8,128)(2,1)}, u32[]{:S(2)}, u32[]{:S(2)}) async-start(bf16[32,128,512]{2,1,0:T(8,128)(2,1)} %shard_map.74), calls=%async_computation.1 | async-start | bytes 8388608 | tf_op jit(solution)/shard_map/all_to_all | solution.py:429
  86.9 0.0 copy-start.18
  86.9 1.2 dynamic-slice_bitcast_fusion.sources
  88.2 36.8 %reduce-scatter.2.cloned.1.call-done = bf16[1,512,512]{2,1,0:T(8,128)(2,1)} async-done(((bf16[8,512,512]{2,1,0:T(8,128)(2,1)}), bf16[1,512,512]{2,1,0:T(8,128)(2,1)}) %reduce-scatter.2.cloned.1.call-update) | async-done | bytes 524304 | tf_op jit(solution)/shard_map/reduce_scatter | solution.py:427
  125.0 1.9 shard_map.73
  126.9 3.2 %shard_map.75.slope_ref = bf16[32,16,512]{2,1,0:T(8,128)(2,1)} custom-call(s32[1]{0:T(128)} %bitcast.4.place, bf16[8,128,2048]{2,1,0:T(8,128)(2,1)} %bitcast.8, bf16[256,256]{1,0:T(8,128)(2,1)} %constant.18.clone.table_ref), custom_call_target="tpu_custom_call" | custom-call | flops 536870912 | bytes 2097152 | tf_op jit(solution)/shard_map/pallas_call | solution.py:182
  130.1 9.0 %all-to-all-done.quantized_ref = bf16[32,128,512]{2,1,0:T(8,128)(2,1)} async-done(((bf16[32,128,512]{2,1,0:T(8,128)(2,1)}), bf16[32,128,512]{2,1,0:T(8,128)(2,1)}, u32[]{:S(2)}, u32[]{:S(2)}) %all-to-all-start) | async-done | bytes 4194336 | tf_op jit(solution)/shard_map/all_to_all | solution.py:429
  139.1 18.5 %all_to_all.15.summed_ref = bf16[32,16,512]{2,1,0:T(8,128)(2,1)S(1)} all-to-all(bf16[32,16,512]{2,1,0:T(8,128)(2,1)S(1)} %copy-done.19), channel_id=1, replica_groups=mesh['dp'=32,'tensor'=8] {'dp'}, dimensions={0} | all-to-all | bytes 1048576 | tf_op jit(solution)/shard_map/all_to_all | solution.py:434
  157.7 1.0 copy-done.17
  158.7 1.3 shard_map.76
  160.0 4.1 %all-to-all-start.2 = ((bf16[8,16,2048]{2,1,0:T(8,128)(2,1)}), bf16[8,16,2048]{2,1,0:T(8,128)(2,1)S(1)}, u32[]{:S(2)}, u32[]{:S(2)}) async-start(bf16[8,16,2048]{2,1,0:T(8,128)(2,1)} %shard_map.76), calls=%async_computation.3 | async-start | bytes 1048576 | tf_op jit(solution)/shard_map/all_to_all | solution.py:436
  164.1 14.2 %shard_map.77 = f32[512,1536]{1,0:T(8,128)} custom-call(s32[32]{0:T(128)} %dynamic-slice_bitcast_fusion.sources, bf16[32,128,512]{2,1,0:T(8,128)(2,1)} %all-to-all-done.quantized_ref, bf16[256,1536]{1,0:T(8,128)(2,1)} %copy-done.2, bf16[256,1536]{1,0:T(8,128)(2,1)} %copy-done.1, bf16[256,1536]{1,0:T(8,128)(2,1)} %copy-done.3, bf16[256,1536]{1,0:T(8,128)(2,1)} %copy-done.5, ...), custom_call_target="tpu_custom_call" | custom-call | flops 6442450944 | bytes 19922944 | tf_op jit(solution)/shard_map/pallas_call | solution.py:292
  178.3 3.9 %all-to-all-done.2 = bf16[8,16,2048]{2,1,0:T(8,128)(2,1)S(1)} async-done(((bf16[8,16,2048]{2,1,0:T(8,128)(2,1)}), bf16[8,16,2048]{2,1,0:T(8,128)(2,1)S(1)}, u32[]{:S(2)}, u32[]{:S(2)}) %all-to-all-start.2) | async-done | bytes 524320 | tf_op jit(solution)/shard_map/all_to_all | solution.py:436
  182.2 0.8 copy.18
  (53 shorter events, 0.2 us)
Async XLA Ops:
  7.2 30.9 %copy-start = (bf16[512,1536]{1,0:T(8,128)(2,1)S(1)}, bf16[512,1536]{1,0:T(8,128)(2,1)}, u32[]{:S(2)}) copy-start(bf16[512,1536]{1,0:T(8,128)(2,1)} %refs_2_.3) | copy-start | bytes 4718596
  7.2 61.3 %all-gather.3.cloned.1.call-start = ((), (), s32[]{:S(2)}) async-start(), calls=%async_computation.5 | async-start | bytes 4718592 | tf_op jit(solution)/shard_map/all_gather | solution.py:397
  7.9 117.1 %reduce-scatter.2.cloned.1.call-start = ((), (), s32[]{:S(2)}) async-start(), calls=%async_computation.4 | async-start | bytes 4718592 | tf_op jit(solution)/shard_map/reduce_scatter | solution.py:427
  8.0 9.3 %collective-permute-start = (bf16[128,1536]{1,0:T(8,128)(2,1)}, bf16[128,1536]{1,0:T(8,128)(2,1)S(1)}, u32[]{:S(2)}, u32[]{:S(2)}) collective-permute-start(bf16[128,1536]{1,0:T(8,128)(2,1)} %param.7), channel_id=1, source_target_pairs={{0,64},{8,24},{16,80},{24,40},{32,96},{40,56},{48,112},{56,8},{64,... | collective-permute-start | bytes 1179656 | tf_op jit(solution)/shard_map/ppermute | solution.py:324
  10.2 14.7 %collective-permute-start.4 = (bf16[128,1536]{1,0:T(8,128)(2,1)}, bf16[128,1536]{1,0:T(8,128)(2,1)S(1)}, u32[]{:S(2)}, u32[]{:S(2)}) collective-permute-start(bf16[128,1536]{1,0:T(8,128)(2,1)} %param.7), channel_id=1, source_target_pairs={{0,128},{8,40},{16,144},{24,56},{32,160},{40,8},{48,176},{56,24},{... | collective-permute-start | bytes 1179656 | tf_op jit(solution)/shard_map/ppermute | solution.py:324
  12.8 12.0 %collective-permute-start.3 = (bf16[128,1536]{1,0:T(8,128)(2,1)}, bf16[128,1536]{1,0:T(8,128)(2,1)S(1)}, u32[]{:S(2)}, u32[]{:S(2)}) collective-permute-start(bf16[128,1536]{1,0:T(8,128)(2,1)} %param.7), channel_id=1, source_target_pairs={{0,192},{8,56},{16,208},{24,8},{32,224},{40,24},{48,240},{56,40},{... | collective-permute-start | bytes 1179656 | tf_op jit(solution)/shard_map/ppermute | solution.py:324
  17.3 23.4 %copy-start.2 = (bf16[256,1536]{1,0:T(8,128)(2,1)}, bf16[256,1536]{1,0:T(8,128)(2,1)S(1)}, u32[]{:S(2)}) copy-start(bf16[256,1536]{1,0:T(8,128)(2,1)S(1)} %constant_dynamic-update-slice_fusion.refs_0_) | copy-start | bytes 2359300
  17.3 10.8 %collective-permute-start.7 = (bf16[256,1536]{1,0:T(8,128)(2,1)S(1)}, bf16[256,1536]{1,0:T(8,128)(2,1)S(1)}, u32[]{:S(2)}, u32[]{:S(2)}) collective-permute-start(bf16[256,1536]{1,0:T(8,128)(2,1)S(1)} %constant_dynamic-update-slice_fusion.refs_0_), channel_id=1, source_target_pairs={{0,8},{8,0},{16,24},{24,16},{32,40},{40,32},{48,56},{56,48},{64,72... | collective-permute-start | bytes 2359304 | tf_op jit(solution)/shard_map/ppermute | solution.py:328
  24.8 12.5 %collective-permute-start.1 = (bf16[256,1536]{1,0:T(8,128)(2,1)S(1)}, bf16[256,1536]{1,0:T(8,128)(2,1)S(1)}, u32[]{:S(2)}, u32[]{:S(2)}) collective-permute-start(bf16[256,1536]{1,0:T(8,128)(2,1)S(1)} %constant_dynamic-update-slice_fusion.refs_0_), channel_id=1, source_target_pairs={{0,16},{8,72},{16,32},{24,88},{32,48},{40,104},{48,0},{56,120},{64... | collective-permute-start | bytes 2359304 | tf_op jit(solution)/shard_map/ppermute | solution.py:324
  24.9 15.8 %copy-start.1 = (bf16[256,1536]{1,0:T(8,128)(2,1)}, bf16[256,1536]{1,0:T(8,128)(2,1)S(1)}, u32[]{:S(2)}) copy-start(bf16[256,1536]{1,0:T(8,128)(2,1)S(1)} %constant_dynamic-update-slice_fusion.2.refs_1_) | copy-start | bytes 2359300
  24.9 13.2 %collective-permute-start.8 = (bf16[256,1536]{1,0:T(8,128)(2,1)S(1)}, bf16[256,1536]{1,0:T(8,128)(2,1)S(1)}, u32[]{:S(2)}, u32[]{:S(2)}) collective-permute-start(bf16[256,1536]{1,0:T(8,128)(2,1)S(1)} %constant_dynamic-update-slice_fusion.2.refs_1_), channel_id=1, source_target_pairs={{0,8},{8,0},{16,24},{24,16},{32,40},{40,32},{48,56},{56,48},{64,72... | collective-permute-start | bytes 2359304 | tf_op jit(solution)/shard_map/ppermute | solution.py:328
  25.8 15.0 %collective-permute-start.6 = (bf16[256,1536]{1,0:T(8,128)(2,1)S(1)}, bf16[256,1536]{1,0:T(8,128)(2,1)S(1)}, u32[]{:S(2)}, u32[]{:S(2)}) collective-permute-start(bf16[256,1536]{1,0:T(8,128)(2,1)S(1)} %constant_dynamic-update-slice_fusion.2.refs_1_), channel_id=1, source_target_pairs={{0,48},{8,200},{16,0},{24,216},{32,16},{40,232},{48,32},{56,248},{... | collective-permute-start | bytes 2359304 | tf_op jit(solution)/shard_map/ppermute | solution.py:324
  28.1 17.6 %collective-permute-start.5 = (bf16[256,1536]{1,0:T(8,128)(2,1)S(1)}, bf16[256,1536]{1,0:T(8,128)(2,1)S(1)}, u32[]{:S(2)}, u32[]{:S(2)}) collective-permute-start(bf16[256,1536]{1,0:T(8,128)(2,1)S(1)} %constant_dynamic-update-slice_fusion.2.refs_1_), channel_id=1, source_target_pairs={{0,16},{8,72},{16,32},{24,88},{32,48},{40,104},{48,0},{56,120},{64... | collective-permute-start | bytes 2359304 | tf_op jit(solution)/shard_map/ppermute | solution.py:324
  28.1 12.6 %copy-start.3 = (bf16[256,1536]{1,0:T(8,128)(2,1)}, bf16[256,1536]{1,0:T(8,128)(2,1)S(1)}, u32[]{:S(2)}) copy-start(bf16[256,1536]{1,0:T(8,128)(2,1)S(1)} %collective-permute-done.7.refs_2_) | copy-start | bytes 2359300
  28.1 18.4 %collective-permute-start.10 = (bf16[256,1536]{1,0:T(8,128)(2,1)S(1)}, bf16[256,1536]{1,0:T(8,128)(2,1)S(1)}, u32[]{:S(2)}, u32[]{:S(2)}) collective-permute-start(bf16[256,1536]{1,0:T(8,128)(2,1)S(1)} %constant_dynamic-update-slice_fusion.refs_0_), channel_id=1, source_target_pairs={{0,48},{8,200},{16,0},{24,216},{32,16},{40,232},{48,32},{56,248},{... | collective-permute-start | bytes 2359304 | tf_op jit(solution)/shard_map/ppermute | solution.py:324
  37.3 12.5 %copy-start.4 = (bf16[256,1536]{1,0:T(8,128)(2,1)}, bf16[256,1536]{1,0:T(8,128)(2,1)S(1)}, u32[]{:S(2)}) copy-start(bf16[256,1536]{1,0:T(8,128)(2,1)S(1)} %collective-permute-done.1.refs_0_.refs_4_) | copy-start | bytes 2359300
  37.3 9.8 %collective-permute-start.13 = (bf16[256,1536]{1,0:T(8,128)(2,1)S(1)}, bf16[256,1536]{1,0:T(8,128)(2,1)S(1)}, u32[]{:S(2)}, u32[]{:S(2)}) collective-permute-start(bf16[256,1536]{1,0:T(8,128)(2,1)S(1)} %collective-permute-done.1.refs_0_.refs_4_), channel_id=1, source_target_pairs={{0,8},{8,0},{16,24},{24,16},{32,40},{40,32},{48,56},{56,48},{64,72... | collective-permute-start | bytes 2359304 | tf_op jit(solution)/shard_map/ppermute | solution.py:328
  38.1 2.6 %copy-start.5 = (bf16[256,1536]{1,0:T(8,128)(2,1)}, bf16[256,1536]{1,0:T(8,128)(2,1)S(1)}, u32[]{:S(2)}) copy-start(bf16[256,1536]{1,0:T(8,128)(2,1)S(1)} %collective-permute-done.8.refs_3_) | copy-start | bytes 2359300
  40.8 11.7 %copy-start.6 = (bf16[256,1536]{1,0:T(8,128)(2,1)}, bf16[256,1536]{1,0:T(8,128)(2,1)S(1)}, u32[]{:S(2)}) copy-start(bf16[256,1536]{1,0:T(8,128)(2,1)S(1)} %collective-permute-done.6.refs_1_.refs_9_) | copy-start | bytes 2359300
  45.7 6.7 %copy-start.7 = (bf16[256,1536]{1,0:T(8,128)(2,1)}, bf16[256,1536]{1,0:T(8,128)(2,1)S(1)}, u32[]{:S(2)}) copy-start(bf16[256,1536]{1,0:T(8,128)(2,1)S(1)} %collective-permute-done.5.refs_1_.refs_5_) | copy-start | bytes 2359300
  45.7 4.1 %collective-permute-start.14 = (bf16[256,1536]{1,0:T(8,128)(2,1)S(1)}, bf16[256,1536]{1,0:T(8,128)(2,1)S(1)}, u32[]{:S(2)}, u32[]{:S(2)}) collective-permute-start(bf16[256,1536]{1,0:T(8,128)(2,1)S(1)} %collective-permute-done.5.refs_1_.refs_5_), channel_id=1, source_target_pairs={{0,8},{8,0},{16,24},{24,16},{32,40},{40,32},{48,56},{56,48},{64,72... | collective-permute-start | bytes 2359304 | tf_op jit(solution)/shard_map/ppermute | solution.py:328
  46.5 5.9 %copy-start.8 = (bf16[256,1536]{1,0:T(8,128)(2,1)}, bf16[256,1536]{1,0:T(8,128)(2,1)S(1)}, u32[]{:S(2)}) copy-start(bf16[256,1536]{1,0:T(8,128)(2,1)S(1)} %collective-permute-done.10.refs_0_.refs_8_) | copy-start | bytes 2359300
  46.5 5.9 %collective-permute-start.11 = (bf16[256,1536]{1,0:T(8,128)(2,1)S(1)}, bf16[256,1536]{1,0:T(8,128)(2,1)S(1)}, u32[]{:S(2)}, u32[]{:S(2)}) collective-permute-start(bf16[256,1536]{1,0:T(8,128)(2,1)S(1)} %collective-permute-done.10.refs_0_.refs_8_), channel_id=1, source_target_pairs={{0,8},{8,0},{16,24},{24,16},{32,40},{40,32},{48,56},{56,48},{64,72... | collective-permute-start | bytes 2359304 | tf_op jit(solution)/shard_map/ppermute | solution.py:328
  46.6 5.8 %collective-permute-start.12 = (bf16[256,1536]{1,0:T(8,128)(2,1)S(1)}, bf16[256,1536]{1,0:T(8,128)(2,1)S(1)}, u32[]{:S(2)}, u32[]{:S(2)}) collective-permute-start(bf16[256,1536]{1,0:T(8,128)(2,1)S(1)} %collective-permute-done.6.refs_1_.refs_9_), channel_id=1, source_target_pairs={{0,8},{8,0},{16,24},{24,16},{32,40},{40,32},{48,56},{56,48},{64,72... | collective-permute-start | bytes 2359304 | tf_op jit(solution)/shard_map/ppermute | solution.py:328
  47.0 12.5 %collective-permute-start.2 = (bf16[256,1536]{1,0:T(8,128)(2,1)S(1)}, bf16[256,1536]{1,0:T(8,128)(2,1)S(1)}, u32[]{:S(2)}, u32[]{:S(2)}) collective-permute-start(bf16[256,1536]{1,0:T(8,128)(2,1)S(1)} %collective-permute-done.1.refs_0_.refs_4_), channel_id=1, source_target_pairs={{0,16},{8,72},{16,32},{24,88},{32,48},{40,104},{48,0},{56,120},{64... | collective-permute-start | bytes 2359304 | tf_op jit(solution)/shard_map/ppermute | solution.py:324
  47.1 5.3 %copy-start.9 = (bf16[256,1536]{1,0:T(8,128)(2,1)}, bf16[256,1536]{1,0:T(8,128)(2,1)S(1)}, u32[]{:S(2)}) copy-start(bf16[256,1536]{1,0:T(8,128)(2,1)S(1)} %collective-permute-done.13.refs_2_.refs_6_) | copy-start | bytes 2359300
  47.1 12.4 %collective-permute-start.9 = (bf16[256,1536]{1,0:T(8,128)(2,1)S(1)}, bf16[256,1536]{1,0:T(8,128)(2,1)S(1)}, u32[]{:S(2)}, u32[]{:S(2)}) collective-permute-start(bf16[256,1536]{1,0:T(8,128)(2,1)S(1)} %collective-permute-done.6.refs_1_.refs_9_), channel_id=1, source_target_pairs={{0,48},{8,200},{16,0},{24,216},{32,16},{40,232},{48,32},{56,248},{... | collective-permute-start | bytes 2359304 | tf_op jit(solution)/shard_map/ppermute | solution.py:324
  49.8 2.6 %copy-start.10 = (bf16[256,1536]{1,0:T(8,128)(2,1)}, bf16[256,1536]{1,0:T(8,128)(2,1)S(1)}, u32[]{:S(2)}) copy-start(bf16[256,1536]{1,0:T(8,128)(2,1)S(1)} %collective-permute-done.14.refs_3_.refs_7_) | copy-start | bytes 2359300
  52.4 2.6 %copy-start.11 = (bf16[256,1536]{1,0:T(8,128)(2,1)}, bf16[256,1536]{1,0:T(8,128)(2,1)S(1)}, u32[]{:S(2)}) copy-start(bf16[256,1536]{1,0:T(8,128)(2,1)S(1)} %collective-permute-done.11.refs_2_.refs_10_) | copy-start | bytes 2359300
  52.4 2.6 %copy-start.12 = (bf16[256,1536]{1,0:T(8,128)(2,1)}, bf16[256,1536]{1,0:T(8,128)(2,1)S(1)}, u32[]{:S(2)}) copy-start(bf16[256,1536]{1,0:T(8,128)(2,1)S(1)} %collective-permute-done.12.refs_3_.refs_11_) | copy-start | bytes 2359300
  59.5 3.0 %copy-start.13 = (bf16[256,1536]{1,0:T(8,128)(2,1)}, bf16[256,1536]{1,0:T(8,128)(2,1)S(1)}, u32[]{:S(2)}) copy-start(bf16[256,1536]{1,0:T(8,128)(2,1)S(1)} %collective-permute-done.2.refs_0_.refs_12_) | copy-start | bytes 2359300
  59.5 3.0 %copy-start.14 = (bf16[256,1536]{1,0:T(8,128)(2,1)}, bf16[256,1536]{1,0:T(8,128)(2,1)S(1)}, u32[]{:S(2)}) copy-start(bf16[256,1536]{1,0:T(8,128)(2,1)S(1)} %collective-permute-done.9.refs_1_.refs_13_) | copy-start | bytes 2359300
  59.5 3.0 %collective-permute-start.15 = (bf16[256,1536]{1,0:T(8,128)(2,1)S(1)}, bf16[256,1536]{1,0:T(8,128)(2,1)S(1)}, u32[]{:S(2)}, u32[]{:S(2)}) collective-permute-start(bf16[256,1536]{1,0:T(8,128)(2,1)S(1)} %collective-permute-done.2.refs_0_.refs_12_), channel_id=1, source_target_pairs={{0,8},{8,0},{16,24},{24,16},{32,40},{40,32},{48,56},{56,48},{64,72... | collective-permute-start | bytes 2359304 | tf_op jit(solution)/shard_map/ppermute | solution.py:328
  60.6 3.0 %collective-permute-start.16 = (bf16[256,1536]{1,0:T(8,128)(2,1)S(1)}, bf16[256,1536]{1,0:T(8,128)(2,1)S(1)}, u32[]{:S(2)}, u32[]{:S(2)}) collective-permute-start(bf16[256,1536]{1,0:T(8,128)(2,1)S(1)} %collective-permute-done.9.refs_1_.refs_13_), channel_id=1, source_target_pairs={{0,8},{8,0},{16,24},{24,16},{32,40},{40,32},{48,56},{56,48},{64,72... | collective-permute-start | bytes 2359304 | tf_op jit(solution)/shard_map/ppermute | solution.py:328
  62.5 2.9 %copy-start.15 = (bf16[256,1536]{1,0:T(8,128)(2,1)}, bf16[256,1536]{1,0:T(8,128)(2,1)S(1)}, u32[]{:S(2)}) copy-start(bf16[256,1536]{1,0:T(8,128)(2,1)S(1)} %collective-permute-done.15.refs_0_.refs_14_) | copy-start | bytes 2359300
  63.6 1.8 copy-start.16
  79.3 59.8 %all-to-all-start = ((bf16[32,128,512]{2,1,0:T(8,128)(2,1)}), bf16[32,128,512]{2,1,0:T(8,128)(2,1)}, u32[]{:S(2)}, u32[]{:S(2)}) async-start(bf16[32,128,512]{2,1,0:T(8,128)(2,1)} %shard_map.74), calls=%async_computation.1 | async-start | bytes 8388608 | tf_op jit(solution)/shard_map/all_to_all | solution.py:429
  86.9 70.7 %copy-start.18 = (bf16[256,256]{1,0:T(8,128)(2,1)S(1)}, bf16[256,256]{1,0:T(8,128)(2,1)}, u32[]{:S(2)}) copy-start(bf16[256,256]{1,0:T(8,128)(2,1)} %constant.18.clone.table_ref) | copy-start | bytes 393220
  126.9 12.2 %copy-start.19 = (bf16[32,16,512]{2,1,0:T(8,128)(2,1)S(1)}, bf16[32,16,512]{2,1,0:T(8,128)(2,1)}, u32[]{:S(2)}) copy-start(bf16[32,16,512]{2,1,0:T(8,128)(2,1)} %shard_map.73) | copy-start | bytes 1572868
  157.7 1.0 copy-start.17
  160.0 22.2 %all-to-all-start.2 = ((bf16[8,16,2048]{2,1,0:T(8,128)(2,1)}), bf16[8,16,2048]{2,1,0:T(8,128)(2,1)S(1)}, u32[]{:S(2)}, u32[]{:S(2)}) async-start(bf16[8,16,2048]{2,1,0:T(8,128)(2,1)} %shard_map.76), calls=%async_computation.3 | async-start | bytes 1048576 | tf_op jit(solution)/shard_map/all_to_all | solution.py:436
Sparse Core Ops, SparseCore 0:
  9.8 58.6 all-gather.2
  71.0 53.9 reduce-scatter.1
